TPU v7x, 32 devices: a whole 2x2x4 slice. The times are simulated.
32 devices in a mesh: branch: 2 (over x), head: 4 (over y, core), tokens: 4 (over z).
Axes of the slice: x: 2, y: 2, z: 4, core: 2. Of those that a mesh axis runs over, the one named last changes fastest.
Arguments:
- queries: bfloat16 [2, 4608, 1536], P('branch', 'tokens', 'head'), may hold values from -128 to 128
- keys: bfloat16 [2, 4608, 1536], P('branch', 'tokens', 'head'), may hold values from -4 to 4
- values: bfloat16 [2, 4608, 1536], P('branch', 'tokens', 'head'), may hold values from -96 to 96
- residual: bfloat16 [2, 4608, 2, 1536], P('branch', 'tokens', None, 'head'), may hold values from -3 to 3
- gate: bfloat16 [2, 2, 1536], replicated, may hold values from 0.099609375 to 1.8984375
- out_weight: bfloat16 [1536, 3072], P('head'), may hold values from -0.15625 to 0.15625
- time_offsets: int32 [3, 4], replicated, may hold values from 0 to 1
- guidance_index: int32 [18], replicated, may hold values from 0 to 7
Outputs:
- guided: bfloat16 [4608, 3072], P('tokens', ('branch', 'head'))
All inputs are finite; a program needn't handle non-finite values.
Results may differ from a plain program's by a relative error of at most 0.0051.
Values may be sent and summed in bfloat16 or wider, within the bound.
No kernel may reach another device: no remote copies, remote signals or barrier semaphores. Data moves between devices by JAX's collectives and lax.ppermute only.
A program may use at most 128 MiB of HBM per device.

v0:
```python
import math

import jax
import jax.numpy as jnp
from jax import lax
from jax.sharding import PartitionSpec as P

HD = 128
TT = 6
TH = 8
TW = 8


def with_halo(block, sides, width):
    for axis, dim in sides:
        count = lax.axis_size(axis)
        forward = [(i, i + 1) for i in range(count - 1)]
        backward = [(target, source) for source, target in forward]
        low = lax.ppermute(
            lax.slice_in_dim(block, block.shape[dim] - width, None, axis=dim), axis, forward
        )
        high = lax.ppermute(lax.slice_in_dim(block, 0, width, axis=dim), axis, backward)
        block = jnp.concatenate([low, block, high], axis=dim)
    return block


def partner_2(value, axis, bit):
    return lax.ppermute(value, axis, [(i, i ^ 1 << bit) for i in range(lax.axis_size(axis))])


def local(queries, keys, values, residual, gate, out_weight, time_offsets, guidance_index):
    tile_size = TT * TH * TW
    query_rows = queries[0]
    row_count = query_rows.shape[0]
    feature_count = query_rows.shape[1]
    tiles_time = time_offsets.shape[0]
    tiles_wide = time_offsets.shape[1]
    column = tiles_time * tile_size
    local_width = row_count // column
    width_pos = lax.axis_index("tokens")
    key_value = jnp.stack([keys[0], values[0]])
    region = with_halo(key_value, (("tokens", 1),), column)
    near_steps = jnp.arange(3, dtype=jnp.int32) - 1
    time_range = jnp.arange(tiles_time, dtype=jnp.int32)
    width_grid = jnp.arange(tiles_wide, dtype=jnp.int32)
    score_scale = 1.0 / math.sqrt(HD)
    heads_dev = feature_count // HD
    width_query = width_pos * local_width + 0
    width_key = width_query + near_steps
    width_ok = (width_key >= 0) & (width_key < tiles_wide)
    offset = jnp.sum(jnp.where(width_grid[None, :] == width_query, time_offsets, 0), axis=1)
    lower = time_range[:, None] - offset[:, None]
    time_ok = (time_range[None, :] >= lower) & (time_range[None, :] <= lower + 1)
    allowed = width_ok[None, :, None, None] & time_ok[:, None, :, None]
    allowed = jnp.broadcast_to(allowed, (tiles_time, 3, tiles_time, tile_size)).reshape(
        tiles_time, 1, 3 * column
    )
    key_rows = region[0, 0 : 3 * column]
    value_rows = region[1, 0 : 3 * column]
    head_pieces = []
    for head_index in range(heads_dev):
        first = head_index * HD
        scores = (
            lax.dot_general(
                query_rows[:, first : first + HD],
                key_rows[:, first : first + HD],
                (((1,), (1,)), ((), ())),
                preferred_element_type=jnp.float32,
            )
            * score_scale
        )
        scores = scores.reshape(tiles_time, tile_size, 3 * column)
        masked = jnp.where(allowed, scores, -1e30)
        row_max = jnp.max(masked, axis=2, keepdims=True)
        weights = jnp.where(allowed, jnp.exp(masked - row_max), 0.0)
        norm_total = jnp.sum(weights, axis=2, keepdims=True)
        blended = jnp.einsum(
            "aqk,kd->aqd",
            weights.astype(jnp.bfloat16),
            value_rows[:, first : first + HD],
            preferred_element_type=jnp.float32,
        )
        head_pieces.append((blended / norm_total).reshape(column, HD).astype(jnp.bfloat16))
    pieces = jnp.concatenate(head_pieces, axis=1)
    head_count = lax.axis_size("head")
    head_pos = lax.axis_index("head")
    branch_pos = lax.axis_index("branch")
    half_full = gate.shape[2]
    half_width = half_full // head_count
    is_cond = branch_pos == 0
    guide_scale = 1.0 + 0.5 * guidance_index.astype(jnp.float32)
    token_scale = jnp.broadcast_to(
        guide_scale[None, :, None], (local_width, guidance_index.shape[0], TH * TW)
    ).reshape(row_count)
    weight_order = out_weight.reshape(out_weight.shape[0], 2, head_count, half_width)
    weight_order = jnp.transpose(weight_order, (0, 2, 1, 3)).reshape(
        out_weight.shape[0], 2 * head_count * half_width
    )
    own_share = lax.psum_scatter(
        lax.dot_general(
            weight_order, pieces, (((0,), (1,)), ((), ())), preferred_element_type=jnp.float32
        ),
        "head",
        scatter_dimension=0,
        tiled=True,
    )
    projected = own_share.T.reshape(row_count, 2, half_width)
    gate_mine = lax.dynamic_index_in_dim(gate, branch_pos, 0, keepdims=False)
    gate_block = lax.dynamic_slice_in_dim(gate_mine, head_pos * half_width, half_width, 1).astype(
        jnp.float32
    )
    hidden = residual[0].astype(jnp.float32) + gate_block[None, :, :] * projected
    mine = jnp.where(is_cond, hidden[:, 0], hidden[:, 1])
    outgoing = jnp.where(is_cond, hidden[:, 1], hidden[:, 0])
    partner = partner_2(outgoing, "branch", 0)
    conditional = jnp.where(is_cond, mine, partner)
    unconditional = jnp.where(is_cond, partner, mine)
    guided = unconditional + token_scale[:, None] * (conditional - unconditional)
    return guided.astype(jnp.bfloat16)


def solution(mesh):
    return jax.shard_map(
        local,
        mesh=mesh,
        in_specs=(
            P("branch", "tokens", "head"),
            P("branch", "tokens", "head"),
            P("branch", "tokens", "head"),
            P("branch", "tokens", None, "head"),
            P(),
            P("head", None),
            P(),
            P(),
        ),
        out_specs=P("tokens", ("branch", "head")),
        check_vma=False,
    )
```

profile of v0, /device:TPU:9, one launch (start us, length us, event | category | flops | bytes accessed | tf_op | source)
XLA Modules:
  0.0 300.6 jit_solution(7033405109282335135)
XLA Ops:
  6.5 0.0 reduce-scatter.2.cloned.1.call-start
  6.5 2.2 constant_dynamic-update-slice_fusion.1
  8.7 2.2 constant_dynamic-update-slice_fusion
  10.9 3.2 %collective-permute-start = (bf16[2,1152,384]{2,1,0:T(8,128)(2,1)}, bf16[2,1152,384]{2,1,0:T(8,128)(2,1)}, u32[]{:S(2)}, u32[]{:S(2)}) collective-permute-start(bf16[2,1152,384]{2,1,0:T(8,128)(2,1)} %constant_dynamic-update-slice_fusion), channel_id=1, source_target_pairs={{0,1},{1,2},{2,3},{4,5},{5,6},{6,7},{8,9},{9,10},{10,11},{12,13},{... | collective-permute-start | bytes 5308424 | tf_op jit(solution)/shard_map/ppermute | solution.py:19
  14.1 3.3 %collective-permute-start.1 = (bf16[2,1152,384]{2,1,0:T(8,128)(2,1)}, bf16[2,1152,384]{2,1,0:T(8,128)(2,1)}, u32[]{:S(2)}, u32[]{:S(2)}) collective-permute-start(bf16[2,1152,384]{2,1,0:T(8,128)(2,1)} %constant_dynamic-update-slice_fusion), channel_id=1, source_target_pairs={{1,0},{2,1},{3,2},{5,4},{6,5},{7,6},{9,8},{10,9},{11,10},{13,12},{... | collective-permute-start | bytes 5308424 | tf_op jit(solution)/shard_map/ppermute | solution.py:22
  17.4 0.8 select_reduce_fusion
  18.2 0.1 fusion.34
  18.3 0.1 broadcast_and_fusion
  18.4 0.1 broadcast_in_dim.83
  18.5 3.0 copy.14
  21.5 1.6 copy.15
  23.2 29.4 %collective-permute-done = bf16[2,1152,384]{2,1,0:T(8,128)(2,1)} collective-permute-done((bf16[2,1152,384]{2,1,0:T(8,128)(2,1)}, bf16[2,1152,384]{2,1,0:T(8,128)(2,1)}, u32[]{:S(2)}, u32[]{:S(2)}) %collective-permute-start) | collective-permute-done | bytes 1769504 | tf_op jit(solution)/shard_map/ppermute | solution.py:19
  52.6 2.9 collective-permute-done.1
  55.5 3.5 %pad_maximum_fusion = bf16[2,3456,384]{2,1,0:T(8,128)(2,1)S(1)} fusion(bf16[2,1152,384]{2,1,0:T(8,128)(2,1)} %collective-permute-done.1, bf16[2,1152,384]{2,1,0:T(8,128)(2,1)} %constant_dynamic-update-slice_fusion, bf16[2,1152,384]{2,1,0:T(8,128)(2,1)} %collective-permute-done), kind=kLoop, calls=%fused_computation.25 | loop fusion | flops 15925248 | bytes 10616832 | tf_op jit(solution)/shard_map/concatenate | solution.py:23
  59.0 0.0 copy-start.3
  59.0 2.0 slice_bitcast_fusion
  61.0 0.0 copy-done.3
  61.0 2.2 convolution_multiply_fusion
  63.3 0.0 copy-start
  63.3 10.6 %fusion.3 = (f32[1152]{0:T(1024)}, f32[1152]{0:T(1024)}, f32[3456,1152]{0,1:T(8,128)}) fusion(pred[3,3456]{1,0:T(4,128)(4,1)S(1)} %broadcast_in_dim.84, f32[3456,1152]{0,1:T(8,128)S(1)} %convolution_multiply_fusion, bf16[1152,384]{1,0:T(8,128)(2,1)S(1)} %bitcast.109, bf16[3456,384]{1,0:T(8,128)(2,1)S(1)} %get-tuple-element.11), kind=kOutput, calls=%fused_computation.15 | convolution fusion | flops 1039120128 | bytes 33053184 | tf_op jit(solution)/shard_map/dot_general | solution.py:64
  73.9 0.0 copy-done
  73.9 1.3 sub.64
  75.2 1.3 sub.74
  76.5 21.3 %fusion = (f32[1152]{0:T(1024)}, f32[1152]{0:T(1024)}, f32[1152]{0:T(1024)}, f32[3456,1152]{0,1:T(8,128)}) fusion(f32[3456,1152]{0,1:T(8,128)} %get-tuple-element.14, f32[1152]{0:T(1024)} %get-tuple-element.8, pred[3,3456]{1,0:T(4,128)(4,1)S(1)} %broadcast_in_dim.84, f32[1152]{0:T(1024)} %get-tuple-element.9, f32[3456,1152]{0,1:T(8,128)} %copy-done, ...), kind=kOutput, calls=%fused_computation.9 | convolution fusion | flops 1063006848 | bytes 48992256 | tf_op jit(solution)/shard_map/dot_general | solution.py:64
  97.8 0.7 div.30
  98.5 0.7 sub.69
  99.2 0.0 copy-start.4
  99.2 0.0 copy-start.2
  99.2 0.0 copy-start.6
  99.2 9.5 %fusion.1 = f32[1152]{0:T(1024)S(1)} fusion(f32[3456,1152]{0,1:T(8,128)} %get-tuple-element.15, f32[1152]{0:T(1024)} %get-tuple-element.6, pred[3,3456]{1,0:T(4,128)(4,1)S(1)} %broadcast_in_dim.84), kind=kLoop, calls=%fused_computation.10 | loop fusion | flops 15924096 | bytes 15944832 | tf_op jit(solution)/shard_map/reduce_sum | solution.py:76
  108.8 0.0 copy-done.4
  108.8 0.0 copy-done.2
  108.8 0.0 copy-done.6
  108.8 0.0 slice-start
  108.8 0.0 slice-start.1
  108.9 8.3 %fusion.22 = bf16[3,384,128]{2,1,0:T(8,128)(2,1)S(1)} fusion(f32[3,384,3456]{2,1,0:T(8,128)} %bitcast.103, f32[3,384]{1,0:T(4,128)S(1)} %copy-done.6, pred[3,3456]{1,0:T(4,128)(4,1)S(1)} %broadcast_in_dim.84, bf16[3456,384]{1,0:T(8,128)(2,1)S(1)} %copy-done.2, f32[3,384]{1,0:T(4,128)S(1)} %div.30), kind=kOutput, calls=%fused_computation.42 | convolution fusion | flops 1035436032 | bytes 17131008 | tf_op jit(solution)/shard_map/aqk,kd->aqd/dot_general | solution.py:77
  117.2 0.0 slice-start.2
  117.2 0.0 slice-start.3
  117.2 0.0 copy-start.5
  117.2 8.3 %fusion.20 = bf16[3,384,128]{2,1,0:T(8,128)(2,1)S(1)} fusion(f32[3,384,3456]{2,1,0:T(8,128)} %bitcast.104, f32[3,384]{1,0:T(4,128)S(1)} %sub.69, pred[3,3456]{1,0:T(4,128)(4,1)S(1)} %broadcast_in_dim.84, bf16[3456,384]{1,0:T(8,128)(2,1)S(1)} %copy-done.2, f32[3,384]{1,0:T(4,128)S(1)} %div.33), kind=kOutput, calls=%fused_computation.40 | convolution fusion | flops 1035436032 | bytes 17131008 | tf_op jit(solution)/shard_map/aqk,kd->aqd/dot_general | solution.py:77
  125.6 0.0 slice-done
  125.6 0.0 slice-done.1
  125.6 0.0 slice-done.2
  125.6 0.0 slice-done.3
  125.6 0.0 copy-done.5
  125.6 0.0 copy-start.1
  125.7 3.1 %fusion.18 = bf16[3,384,128]{2,1,0:T(8,128)(2,1)S(1)} fusion(f32[3,384,3456]{2,1,0:T(8,128)S(1)} %bitcast.102, f32[3,384]{1,0:T(4,128)S(1)} %copy-done.5, pred[3,3456]{1,0:T(4,128)(4,1)S(1)} %broadcast_in_dim.84, bf16[3456,384]{1,0:T(8,128)(2,1)S(1)} %copy-done.2, f32[3,384]{1,0:T(4,128)S(1)} %div.36), kind=kOutput, calls=%fused_computation.38 | convolution fusion | flops 1035436032 | bytes 17131008 | tf_op jit(solution)/shard_map/aqk,kd->aqd/dot_general | solution.py:77
  128.8 0.0 copy-done.1
  128.8 7.2 %convolution_bitcast_fusion = f32[3072,1152]{0,1:T(8,128)} fusion(bf16[384,3072]{0,1:T(8,128)(2,1)S(1)} %bitcast.106, bf16[1152,128]{1,0:T(8,128)(2,1)S(1)} %bitcast.113, bf16[1152,128]{1,0:T(8,128)(2,1)S(1)} %bitcast.112, bf16[1152,128]{1,0:T(8,128)(2,1)S(1)} %bitcast.111), kind=kOutput, calls=%fused_computation.18 | convolution fusion | flops 2720563200 | bytes 17399808 | tf_op jit(solution)/shard_map/dot_general | solution.py:100
  135.9 0.0 reduce-scatter.2.cloned.1.call-update
  136.0 0.0 copy-start.7
  136.0 0.8 bitcast_convert_fusion
  136.7 110.1 %reduce-scatter.2.cloned.1.call-done = f32[768,1152]{0,1:T(8,128)} async-done(((f32[3072,1152]{0,1:T(8,128)}), f32[768,1152]{0,1:T(8,128)}) %reduce-scatter.2.cloned.1.call-update) | async-done | bytes 3538960 | tf_op jit(solution)/shard_map/reduce_scatter | solution.py:99
  246.8 2.9 fusion.12
  249.7 1.4 select_bitcast_fusion
  251.1 1.2 collective-permute-start.2
  252.3 0.0 copy-done.7
  252.3 0.1 broadcast_in_dim.91
  252.4 0.7 broadcast_in_dim.92
  253.0 37.9 %collective-permute-done.2 = f32[1152,384]{1,0:T(8,128)} collective-permute-done((f32[1152,384]{1,0:T(8,128)}, f32[1152,384]{1,0:T(8,128)}, u32[]{:S(2)}, u32[]{:S(2)}) %collective-permute-start.2) | collective-permute-done | bytes 1769504 | tf_op jit(solution)/shard_map/ppermute | solution.py:28
  290.9 2.8 fusion.16
  (8 shorter events, 0.1 us)
Async XLA Ops:
  6.5 240.3 %reduce-scatter.2.cloned.1.call-start = ((), (), s32[]{:S(2)}) async-start(), calls=%async_computation.1 | async-start | bytes 17694720 | tf_op jit(solution)/shard_map/reduce_scatter | solution.py:99
  10.9 41.7 %collective-permute-start = (bf16[2,1152,384]{2,1,0:T(8,128)(2,1)}, bf16[2,1152,384]{2,1,0:T(8,128)(2,1)}, u32[]{:S(2)}, u32[]{:S(2)}) collective-permute-start(bf16[2,1152,384]{2,1,0:T(8,128)(2,1)} %constant_dynamic-update-slice_fusion), channel_id=1, source_target_pairs={{0,1},{1,2},{2,3},{4,5},{5,6},{6,7},{8,9},{9,10},{10,11},{12,13},{... | collective-permute-start | bytes 5308424 | tf_op jit(solution)/shard_map/ppermute | solution.py:19
  14.1 41.4 %collective-permute-start.1 = (bf16[2,1152,384]{2,1,0:T(8,128)(2,1)}, bf16[2,1152,384]{2,1,0:T(8,128)(2,1)}, u32[]{:S(2)}, u32[]{:S(2)}) collective-permute-start(bf16[2,1152,384]{2,1,0:T(8,128)(2,1)} %constant_dynamic-update-slice_fusion), channel_id=1, source_target_pairs={{1,0},{2,1},{3,2},{5,4},{6,5},{7,6},{9,8},{10,9},{11,10},{13,12},{... | collective-permute-start | bytes 5308424 | tf_op jit(solution)/shard_map/ppermute | solution.py:22
  59.0 2.0 copy-start.3
  63.3 10.6 %copy-start = (f32[3456,1152]{0,1:T(8,128)}, f32[3456,1152]{0,1:T(8,128)S(1)}, u32[]{:S(2)}) copy-start(f32[3456,1152]{0,1:T(8,128)S(1)} %convolution_multiply_fusion) | copy-start | bytes 47775748
  99.2 9.6 %copy-start.4 = (f32[1152]{0:T(1024)S(1)}, f32[1152]{0:T(1024)}, u32[]{:S(2)}) copy-start(f32[1152]{0:T(1024)} %get-tuple-element.7) | copy-start | bytes 13828
  99.2 9.6 %copy-start.2 = (bf16[3456,384]{1,0:T(8,128)(2,1)S(1)}, bf16[3456,384]{1,0:T(8,128)(2,1)}, u32[]{:S(2)}) copy-start(bf16[3456,384]{1,0:T(8,128)(2,1)} %get-tuple-element.10) | copy-start | bytes 7962628
  99.2 9.6 %copy-start.6 = (f32[3,384]{1,0:T(4,128)S(1)}, f32[3,384]{1,0:T(4,128)}, u32[]{:S(2)}) copy-start(f32[3,384]{1,0:T(4,128)} %sub.64) | copy-start | bytes 13828
  108.8 16.8 %slice-start = ((s8[15925248]{0:T(1024)(128)(4,1)}), s8[4194304]{0:T(1024)(128)(4,1)S(1)}, s32[]{:S(2)}) async-start(s8[15925248]{0:T(1024)(128)(4,1)} %bitcast.100), calls=%async_computation.2 | async-start | bytes 8388608
  108.8 16.8 %slice-start.1 = ((s8[15925248]{0:T(1024)(128)(4,1)}), s8[4194304]{0:T(1024)(128)(4,1)S(1)}, s32[]{:S(2)}) async-start(s8[15925248]{0:T(1024)(128)(4,1)} %bitcast.100), calls=%async_computation.3 | async-start | bytes 8388608
  117.2 8.4 %slice-start.2 = ((s8[15925248]{0:T(1024)(128)(4,1)}), s8[4194304]{0:T(1024)(128)(4,1)S(1)}, s32[]{:S(2)}) async-start(s8[15925248]{0:T(1024)(128)(4,1)} %bitcast.100), calls=%async_computation.4 | async-start | bytes 8388608
  117.2 8.4 %slice-start.3 = ((s8[15925248]{0:T(1024)(128)(4,1)}), s8[3342336]{0:T(1024)(128)(4,1)S(1)}, s32[]{:S(2)}) async-start(s8[15925248]{0:T(1024)(128)(4,1)} %bitcast.100), calls=%async_computation.5 | async-start | bytes 6684672
  117.2 8.4 %copy-start.5 = (f32[3,384]{1,0:T(4,128)S(1)}, f32[3,384]{1,0:T(4,128)}, u32[]{:S(2)}) copy-start(f32[3,384]{1,0:T(4,128)} %sub.74) | copy-start | bytes 13828
  125.6 3.1 %copy-start.1 = (bf16[384,4,2,384]{0,3,2,1:T(8,128)(2,1)S(1)}, bf16[384,4,2,384]{0,3,2,1:T(8,128)(2,1)}, u32[]{:S(2)}) copy-start(bf16[384,4,2,384]{0,3,2,1:T(8,128)(2,1)} %copy.15) | copy-start | bytes 7077892
  136.0 116.3 %copy-start.7 = (s32[18]{0:T(128)S(1)}, s32[18]{0:T(128)}, u32[]{:S(2)}) copy-start(s32[18]{0:T(128)} %param.15) | copy-start | bytes 220
  251.1 39.8 %collective-permute-start.2 = (f32[1152,384]{1,0:T(8,128)}, f32[1152,384]{1,0:T(8,128)}, u32[]{:S(2)}, u32[]{:S(2)}) collective-permute-start(f32[1152,384]{1,0:T(8,128)} %select_bitcast_fusion), channel_id=1, source_target_pairs={{0,16},{16,0},{1,17},{17,1},{2,18},{18,2},{3,19},{19,3},{4,20},{20... | collective-permute-start | bytes 5308424 | tf_op jit(solution)/shard_map/ppermute | solution.py:28
Sparse Core Ops, SparseCore 0:
  136.1 110.7 reduce-scatter.1
where the time goes:
time: 304 us; the launch traced here: 301 us
  waiting for transfers between devices  180 us (59%)
  matrix products  61.1 us (20%)
  other arithmetic  21.9 us (7%)
  local copies, waits for them, and re-layouts  15.9 us (5%)
  between operations  13.7 us (5%)
  starting transfers between devices  7.64 us (3%)
    reduce_scatter x1, waiting for transfers between devices, local(): lax.psum_scatter(lax.dot_general(weight_order, pieces, (((0,), (1,)), (()...  110 us
    ppermute x1, waiting for transfers between devices, partner_2(): lax.ppermute(value, axis, [(i, i ^ 1 << bit) for i in range(lax.axis_size...  37.9 us
    dot_general x3, matrix products, local(): lax.dot_general(query_rows[:, first:first + HD], key_rows[:, first:first...  34.2 us
    ppermute x1, waiting for transfers between devices, with_halo(): lax.ppermute(lax.slice_in_dim(block, block.shape[dim] - width, None, axis...  29.4 us
    dot_general x3, matrix products, local(): jnp.einsum('aqk,kd->aqd', weights.astype(jnp.bfloat16), value_rows[:, fir...  19.8 us
    reduce_sum x1, other arithmetic, local(): norm_total = jnp.sum(weights, axis=2, keepdims=True)  9.55 us
    dot_general x1, matrix products, local(): lax.dot_general(weight_order, pieces, (((0,), (1,)), ((), ())), preferred...  7.16 us
  transfers between devices with their start and end apart: 4, of which 4 were waited for; matrix products, arithmetic and copies ran while one was open for 2% of the time, Pallas kernels for 0%

commit v1 on v0

v1 whole, which is shorter than its diff:
```python
import functools
import math

import jax
import jax.numpy as jnp
from jax import lax
from jax.experimental import pallas as pl
from jax.experimental.pallas import tpu as pltpu
from jax.sharding import PartitionSpec as P

HD = 128
FRAME = 64
FAR = 1e30
EXP2_SCALE = math.log2(math.e) / math.sqrt(HD)
VMEM_LIMIT = 40 * 1024 * 1024


def attention_kernel(info_ref, q_ref, k_ref, v_ref, low_ref, high_ref, out_ref):
    tiles_time = pl.num_programs(0)
    tile = q_ref.shape[0]
    time_tile = pl.program_id(0)
    first = time_tile - info_ref[time_tile]
    query = q_ref[...]
    ones = jnp.ones((tile, HD), jnp.bfloat16)
    sides = (
        (lambda rows: k_ref[rows, :], lambda rows: v_ref[rows, :], None),
        (lambda rows: low_ref[0, rows, :], lambda rows: low_ref[1, rows, :], info_ref[tiles_time]),
        (lambda rows: high_ref[0, rows, :], lambda rows: high_ref[1, rows, :], info_ref[tiles_time + 1]),
    )
    blocks = []
    row_max = None
    for step in range(2):
        key_tile = first + step
        inside = (key_tile >= 0) & (key_tile < tiles_time)
        start = jnp.clip(key_tile, 0, tiles_time - 1) * tile
        rows = pl.ds(pl.multiple_of(start, tile), tile)
        for keys_of, values_of, width_ok in sides:
            allowed = inside if width_ok is None else inside & (width_ok == 1)
            scores = lax.dot_general(
                query, keys_of(rows), (((1,), (1,)), ((), ())), preferred_element_type=jnp.float32
            )
            block_max = jnp.where(allowed, jnp.max(scores, axis=1, keepdims=True), -FAR)
            row_max = block_max if row_max is None else jnp.maximum(row_max, block_max)
            blocks.append((scores, values_of, rows, allowed))
    shift = row_max * EXP2_SCALE
    total = jnp.zeros((tile, 2 * HD), jnp.float32)
    for scores, values_of, rows, allowed in blocks:
        weights = jnp.exp2(scores * EXP2_SCALE - jnp.where(allowed, shift, FAR))
        total += jnp.dot(
            weights.astype(jnp.bfloat16),
            jnp.concatenate([values_of(rows), ones], axis=1),
            preferred_element_type=jnp.float32,
        )
    out_ref[...] = (total[:, :HD] / total[:, HD:]).astype(jnp.bfloat16)


def attention(info, queries, keys, values, low, high, head, tile):
    count = queries.shape[0]
    side = pl.BlockSpec((2, count, HD), lambda t, info: (0, 0, 0))
    whole = pl.BlockSpec((count, HD), lambda t, info: (0, head))
    pairs = count * 6 * tile
    return pl.pallas_call(
        attention_kernel,
        out_shape=jax.ShapeDtypeStruct((count, HD), jnp.bfloat16),
        grid_spec=pltpu.PrefetchScalarGridSpec(
            num_scalar_prefetch=1,
            grid=(count // tile,),
            in_specs=[pl.BlockSpec((tile, HD), lambda t, info: (t, head)), whole, whole, side, side],
            out_specs=pl.BlockSpec((tile, HD), lambda t, info: (t, 0)),
        ),
        compiler_params=pltpu.CompilerParams(vmem_limit_bytes=VMEM_LIMIT),
        cost_estimate=pl.CostEstimate(
            flops=4 * pairs * HD, bytes_accessed=8 * count * HD * 2, transcendentals=pairs
        ),
        name="attention",
    )(info, queries, keys, values, low, high)


def projection_kernel(head_count, info_ref, *refs):
    *pieces, w_ref, gate_ref, mine_ref, other_ref, out_ref = refs
    tile = out_ref.shape[0]
    frames = tile // FRAME
    time_tile = pl.program_id(0)
    branch = info_ref[0]
    weights = w_ref[...].reshape(-1, w_ref.shape[-1])
    hidden = []
    for which in range(2):
        rows = jnp.concatenate(
            [piece[which * head_count + h] for h in range(head_count) for piece in pieces], axis=1
        )
        projected = jnp.dot(rows, weights, preferred_element_type=jnp.float32)
        gate = jnp.where(branch == 0, gate_ref[which, 0:1, :], gate_ref[which, 1:2, :])
        base = jnp.where(branch == which, mine_ref[...], other_ref[...])
        hidden.append(base.astype(jnp.float32) + gate.astype(jnp.float32) * projected)
    for frame in range(frames):
        rows = slice(frame * FRAME, (frame + 1) * FRAME)
        step = info_ref[1 + time_tile * frames + frame].astype(jnp.float32)
        guide = 1.0 + 0.5 * step
        cond, uncond = hidden[0][rows], hidden[1][rows]
        out_ref[rows, :] = (uncond + guide * (cond - uncond)).astype(jnp.bfloat16)


def project(info, pieces, weights, gate, mine, other, tile, head_count):
    count, width = mine.shape
    rows = pl.BlockSpec((tile, width), lambda t, info: (t, 0))
    piece = pl.BlockSpec((2 * head_count, tile, HD), lambda t, info: (0, t, 0))
    return pl.pallas_call(
        functools.partial(projection_kernel, head_count),
        out_shape=jax.ShapeDtypeStruct((count, width), jnp.bfloat16),
        grid_spec=pltpu.PrefetchScalarGridSpec(
            num_scalar_prefetch=1,
            grid=(count // tile,),
            in_specs=[piece] * len(pieces)
            + [
                pl.BlockSpec(weights.shape, lambda t, info: (0, 0, 0)),
                pl.BlockSpec(gate.shape, lambda t, info: (0, 0, 0)),
                rows,
                rows,
            ],
            out_specs=rows,
        ),
        compiler_params=pltpu.CompilerParams(vmem_limit_bytes=VMEM_LIMIT),
        cost_estimate=pl.CostEstimate(
            flops=4 * count * width * len(pieces) * head_count * HD,
            bytes_accessed=2 * count * (3 * width + 2 * len(pieces) * head_count * HD),
            transcendentals=0,
        ),
        name="projection",
    )(info, *pieces, weights, gate, mine, other)


def local(queries, keys, values, residual, gate, out_weight, time_offsets, guidance_index):
    tiles_time, tiles_wide = time_offsets.shape
    count, features = queries.shape[1:]
    tile = count // tiles_time
    heads = features // HD
    head_count = lax.axis_size("head")
    columns = lax.axis_size("tokens")
    branch_pos = lax.axis_index("branch")
    head_pos = lax.axis_index("head")
    width_pos = lax.axis_index("tokens")
    width = gate.shape[2] // head_count

    up = [(i, i + 1) for i in range(columns - 1)]
    down = [(i + 1, i) for i in range(columns - 1)]
    swap = [(0, 1), (1, 0)]

    low, high = [], []
    for head in range(heads):
        cols = slice(head * HD, (head + 1) * HD)
        key_value = jnp.stack([keys[0, :, cols], values[0, :, cols]])
        low.append(lax.ppermute(key_value, "tokens", up))
        high.append(lax.ppermute(key_value, "tokens", down))

    half = lax.dynamic_index_in_dim(residual[0], branch_pos, 1, keepdims=False)
    other_half = lax.dynamic_index_in_dim(residual[0], 1 - branch_pos, 1, keepdims=False)
    partner_half = lax.ppermute(other_half, "branch", swap)
    gate_block = lax.dynamic_slice_in_dim(gate, head_pos * width, width, 2)

    branch_weight = lax.dynamic_slice_in_dim(out_weight, branch_pos * gate.shape[2], gate.shape[2], 1)
    branch_weight = branch_weight.reshape(features, head_count, width).transpose(1, 0, 2)
    weights = lax.all_to_all(branch_weight, "head", 0, 0)

    offsets = lax.dynamic_index_in_dim(time_offsets, width_pos, 1, keepdims=False)
    edges = jnp.stack([width_pos > 0, width_pos < tiles_wide - 1]).astype(jnp.int32)
    attention_info = jnp.concatenate([offsets, edges])
    projection_info = jnp.concatenate([branch_pos[None].astype(jnp.int32), guidance_index])

    pieces = []
    for head in range(heads):
        own = attention(
            attention_info, queries[0], keys[0], values[0], low[head], high[head], head, tile
        )
        pieces.append(lax.all_gather(own, ("branch", "head")))
    return project(
        projection_info, pieces, weights, gate_block, half, partner_half, tile, head_count
    )


def solution(mesh):
    return jax.shard_map(
        local,
        mesh=mesh,
        in_specs=(
            P("branch", "tokens", "head"),
            P("branch", "tokens", "head"),
            P("branch", "tokens", "head"),
            P("branch", "tokens", None, "head"),
            P(),
            P("head", None),
            P(),
            P(),
        ),
        out_specs=P("tokens", ("branch", "head")),
        check_vma=False,
    )
```

time: 304 us -> 163 us (0.54)
  waiting for transfers between devices: 180 us -> 56 us
  matrix products: 61.1 us -> 0 us
  Pallas kernels: 0 us -> 31.1 us
  other arithmetic: 21.9 us -> 3.22 us
  starting transfers between devices: 7.64 us -> 25.9 us
  local copies, waits for them, and re-layouts: 15.9 us -> 30.4 us
    reduce_scatter x1 -> x0, waiting for transfers between devices: 110 us -> none  [local(): lax.psum_scatter(lax.dot_general(weight_order, pieces, (((0,), (1,)), (()...]
    dot_general x7 -> x0, matrix products: 61.1 us -> none  [the longest x3 34.2 us: local(): lax.dot_general(query_rows[:, first:first + HD], key_rows[:, first:first...]
    pallas_call x0 -> x4, Pallas kernels: none -> 31.1 us  [the longest x3 24.2 us: attention(): pl.pallas_call(attention_kernel, out_shape=jax.ShapeDtypeStruct((count, H...]
    ppermute x3 -> x7, waiting for transfers between devices: 70.2 us -> 39.8 us  [the longest x3 27.9 us: local(): low.append(lax.ppermute(key_value, 'tokens', up))]
    unnamed x26 -> x31, local copies, waits for them, and re-layouts: 5.25 us -> 18.3 us
    all_to_all x0 -> x1, waiting for transfers between devices: none -> 10.8 us  [local(): weights = lax.all_to_all(branch_weight, 'head', 0, 0)]
    reduce_sum x2 -> x0, other arithmetic: 10.3 us -> none  [the longest x1 9.55 us: local(): norm_total = jnp.sum(weights, axis=2, keepdims=True)]
    ppermute x3 -> x7, starting transfers between devices: 7.64 us -> 17.9 us  [the longest x3 8.6 us: local(): low.append(lax.ppermute(key_value, 'tokens', up))]
  transfers between devices with their start and end apart: 4 -> 11, of which waited for: 4 -> 9; matrix products, arithmetic and copies ran while one was open for 2% -> 11% of each run, Pallas kernels for 0% -> 10%
where the time goes in v1:
time: 163 us; the launch traced here: 160 us
  waiting for transfers between devices  56 us (34%)
  Pallas kernels  31.1 us (19%)
  local copies, waits for them, and re-layouts  30.4 us (19%)
  starting transfers between devices  25.9 us (16%)
  between operations  13.2 us (8%)
  other arithmetic  3.22 us (2%)
    ppermute x3, waiting for transfers between devices, local(): low.append(lax.ppermute(key_value, 'tokens', up))  27.9 us
    pallas_call x3, Pallas kernels, attention(): pl.pallas_call(attention_kernel, out_shape=jax.ShapeDtypeStruct((count, H...  24.2 us
    unnamed x31, local copies, waits for them, and re-layouts  18.3 us
    all_to_all x1, waiting for transfers between devices, local(): weights = lax.all_to_all(branch_weight, 'head', 0, 0)  10.8 us
    ppermute x3, starting transfers between devices, local(): low.append(lax.ppermute(key_value, 'tokens', up))  8.6 us
    ppermute x3, starting transfers between devices, local(): high.append(lax.ppermute(key_value, 'tokens', down))  8.1 us
    all_to_all x1, starting transfers between devices, local(): weights = lax.all_to_all(branch_weight, 'head', 0, 0)  7.94 us
    ppermute x3, waiting for transfers between devices, local(): high.append(lax.ppermute(key_value, 'tokens', down))  7.77 us
  transfers between devices with their start and end apart: 11, of which 9 were waited for; matrix products, arithmetic and copies ran while one was open for 11% of the time, Pallas kernels for 10%

profile of v1, /device:TPU:9, one launch (start us, length us, event | category | flops | bytes accessed | tf_op | source)
XLA Modules:
  0.0 159.9 jit_solution(12724782636267493834)
XLA Ops:
  6.5 0.0 copy-start
  6.5 0.0 copy-start.12
  6.5 0.0 all-gather.11.cloned.1.call-start
  6.5 2.5 %fusion = (bf16[1,1152,128]{2,1,0:T(8,128)(2,1)S(1)}, bf16[1,1152,128]{2,1,0:T(8,128)(2,1)S(1)}, bf16[1,1152,128]{2,1,0:T(8,128)(2,1)}, bf16[1,1152,128]{2,1,0:T...) fusion(bf16[1,1152,384]{2,1,0:T(8,128)(2,1)} %param.9, bf16[1,1152,384]{2,1,0:T(8,128)(2,1)} %param.10), kind=kLoop, calls=%fused_computation.13 | loop fusion | bytes 3538944 | tf_op jit(solution)/shard_map/slice | solution.py:151
  9.1 0.9 pad_maximum_fusion.2
  10.0 3.2 %collective-permute-start.4 = (bf16[2,1152,128]{2,1,0:T(8,128)(2,1)}, bf16[2,1152,128]{2,1,0:T(8,128)(2,1)}, u32[]{:S(2)}, u32[]{:S(2)}) collective-permute-start(bf16[2,1152,128]{2,1,0:T(8,128)(2,1)} %pad_maximum_fusion.2), channel_id=1, source_target_pairs={{0,1},{1,2},{2,3},{4,5},{5,6},{6,7},{8,9},{9,10},{10,11},{12,13},{... | collective-permute-start | bytes 1769480 | tf_op jit(solution)/shard_map/ppermute | solution.py:152
  13.2 2.9 %collective-permute-start.5 = (bf16[2,1152,128]{2,1,0:T(8,128)(2,1)}, bf16[2,1152,128]{2,1,0:T(8,128)(2,1)}, u32[]{:S(2)}, u32[]{:S(2)}) collective-permute-start(bf16[2,1152,128]{2,1,0:T(8,128)(2,1)} %pad_maximum_fusion.2), channel_id=1, source_target_pairs={{1,0},{2,1},{3,2},{5,4},{6,5},{7,6},{9,8},{10,9},{11,10},{13,12},{... | collective-permute-start | bytes 1769480 | tf_op jit(solution)/shard_map/ppermute | solution.py:153
  16.1 0.0 copy-done.12
  16.1 0.2 dynamic-slice_reduce_fusion
  16.2 0.1 add_convert_fusion
  16.3 0.1 pad_add_fusion.1.info_ref
  16.4 10.0 %collective-permute-done.4.low_ref = bf16[2,1152,128]{2,1,0:T(8,128)(2,1)} collective-permute-done((bf16[2,1152,128]{2,1,0:T(8,128)(2,1)}, bf16[2,1152,128]{2,1,0:T(8,128)(2,1)}, u32[]{:S(2)}, u32[]{:S(2)}) %collective-permute-start.4) | collective-permute-done | bytes 589856 | tf_op jit(solution)/shard_map/ppermute | solution.py:152
  26.4 2.9 %collective-permute-done.5.high_ref = bf16[2,1152,128]{2,1,0:T(8,128)(2,1)} collective-permute-done((bf16[2,1152,128]{2,1,0:T(8,128)(2,1)}, bf16[2,1152,128]{2,1,0:T(8,128)(2,1)}, u32[]{:S(2)}, u32[]{:S(2)}) %collective-permute-start.5) | collective-permute-done | bytes 589856 | tf_op jit(solution)/shard_map/ppermute | solution.py:153
  29.2 0.0 copy-done.5
  29.3 0.0 copy-start.6
  29.3 1.2 copy-done.6
  30.4 0.0 copy-start.9
  30.4 1.2 copy-done.9
  31.6 8.9 %attention.5 = bf16[1152,128]{1,0:T(8,128)(2,1)} custom-call(s32[5]{0:T(128)S(1)} %pad_add_fusion.1.info_ref, bf16[1152,384]{1,0:T(8,128)(2,1)S(1)} %bitcast.27, bf16[1152,384]{1,0:T(8,128)(2,1)S(1)} %bitcast.21, bf16[1152,384]{1,0:T(8,128)(2,1)S(1)} %bitcast.24, bf16[2,1152,128]{2,1,0:T(8,128)(2,1)} %collective-permute-done.4.low_ref, ...), custom_call_target="tpu_custom_call" | custom-call | flops 1358954496 | bytes 2359296 | tf_op jit(solution)/shard_map/attention/pallas_call | solution.py:62
  40.5 0.0 all-gather.11.cloned.1.call-update
  40.5 0.0 all-gather.9.cloned.1.call-start
  40.6 1.1 pad_maximum_fusion.1
  41.7 3.2 %collective-permute-start.2 = (bf16[2,1152,128]{2,1,0:T(8,128)(2,1)S(1)}, bf16[2,1152,128]{2,1,0:T(8,128)(2,1)S(1)}, u32[]{:S(2)}, u32[]{:S(2)}) collective-permute-start(bf16[2,1152,128]{2,1,0:T(8,128)(2,1)S(1)} %pad_maximum_fusion.1), channel_id=1, source_target_pairs={{0,1},{1,2},{2,3},{4,5},{5,6},{6,7},{8,9},{9,10},{10,11},{12,13},{... | collective-permute-start | bytes 1769480 | tf_op jit(solution)/shard_map/ppermute | solution.py:152
  44.9 2.1 %collective-permute-start.3 = (bf16[2,1152,128]{2,1,0:T(8,128)(2,1)S(1)}, bf16[2,1152,128]{2,1,0:T(8,128)(2,1)S(1)}, u32[]{:S(2)}, u32[]{:S(2)}) collective-permute-start(bf16[2,1152,128]{2,1,0:T(8,128)(2,1)S(1)} %pad_maximum_fusion.1), channel_id=1, source_target_pairs={{1,0},{2,1},{3,2},{5,4},{6,5},{7,6},{9,8},{10,9},{11,10},{13,12},{... | collective-permute-start | bytes 1769480 | tf_op jit(solution)/shard_map/ppermute | solution.py:153
  47.0 9.5 %collective-permute-done.2.low_ref = bf16[2,1152,128]{2,1,0:T(8,128)(2,1)S(1)} collective-permute-done((bf16[2,1152,128]{2,1,0:T(8,128)(2,1)S(1)}, bf16[2,1152,128]{2,1,0:T(8,128)(2,1)S(1)}, u32[]{:S(2)}, u32[]{:S(2)}) %collective-permute-start.2) | collective-permute-done | bytes 589856 | tf_op jit(solution)/shard_map/ppermute | solution.py:152
  56.5 2.9 %collective-permute-done.3.high_ref = bf16[2,1152,128]{2,1,0:T(8,128)(2,1)S(1)} collective-permute-done((bf16[2,1152,128]{2,1,0:T(8,128)(2,1)S(1)}, bf16[2,1152,128]{2,1,0:T(8,128)(2,1)S(1)}, u32[]{:S(2)}, u32[]{:S(2)}) %collective-permute-start.3) | collective-permute-done | bytes 589856 | tf_op jit(solution)/shard_map/ppermute | solution.py:153
  59.4 0.0 copy-start.7
  59.4 1.2 copy-done.7
  60.6 0.0 copy-start.10
  60.6 1.2 copy-done.10
  61.8 7.7 %attention.4 = bf16[1152,128]{1,0:T(8,128)(2,1)} custom-call(s32[5]{0:T(128)S(1)} %pad_add_fusion.1.info_ref, bf16[1152,384]{1,0:T(8,128)(2,1)S(1)} %bitcast.28, bf16[1152,384]{1,0:T(8,128)(2,1)S(1)} %bitcast.22, bf16[1152,384]{1,0:T(8,128)(2,1)S(1)} %bitcast.25, bf16[2,1152,128]{2,1,0:T(8,128)(2,1)S(1)} %collective-permute-done.2.low_ref, ...), custom_call_target="tpu_custom_call" | custom-call | flops 1358954496 | bytes 2359296 | tf_op jit(solution)/shard_map/attention/pallas_call | solution.py:62
  69.4 0.0 all-gather.9.cloned.1.call-update
  69.5 0.0 all-gather.7.cloned.1.call-start
  69.5 1.0 pad_maximum_fusion
  70.5 2.2 %collective-permute-start = (bf16[2,1152,128]{2,1,0:T(8,128)(2,1)S(1)}, bf16[2,1152,128]{2,1,0:T(8,128)(2,1)S(1)}, u32[]{:S(2)}, u32[]{:S(2)}) collective-permute-start(bf16[2,1152,128]{2,1,0:T(8,128)(2,1)S(1)} %pad_maximum_fusion), channel_id=1, source_target_pairs={{0,1},{1,2},{2,3},{4,5},{5,6},{6,7},{8,9},{9,10},{10,11},{12,13},{... | collective-permute-start | bytes 1769480 | tf_op jit(solution)/shard_map/ppermute | solution.py:152
  72.7 3.1 %collective-permute-start.1 = (bf16[2,1152,128]{2,1,0:T(8,128)(2,1)S(1)}, bf16[2,1152,128]{2,1,0:T(8,128)(2,1)S(1)}, u32[]{:S(2)}, u32[]{:S(2)}) collective-permute-start(bf16[2,1152,128]{2,1,0:T(8,128)(2,1)S(1)} %pad_maximum_fusion), channel_id=1, source_target_pairs={{1,0},{2,1},{3,2},{5,4},{6,5},{7,6},{9,8},{10,9},{11,10},{13,12},{... | collective-permute-start | bytes 1769480 | tf_op jit(solution)/shard_map/ppermute | solution.py:153
  75.9 8.4 %collective-permute-done.low_ref = bf16[2,1152,128]{2,1,0:T(8,128)(2,1)S(1)} collective-permute-done((bf16[2,1152,128]{2,1,0:T(8,128)(2,1)S(1)}, bf16[2,1152,128]{2,1,0:T(8,128)(2,1)S(1)}, u32[]{:S(2)}, u32[]{:S(2)}) %collective-permute-start) | collective-permute-done | bytes 589856 | tf_op jit(solution)/shard_map/ppermute | solution.py:152
  84.3 1.9 %collective-permute-done.1.high_ref = bf16[2,1152,128]{2,1,0:T(8,128)(2,1)S(1)} collective-permute-done((bf16[2,1152,128]{2,1,0:T(8,128)(2,1)S(1)}, bf16[2,1152,128]{2,1,0:T(8,128)(2,1)S(1)}, u32[]{:S(2)}, u32[]{:S(2)}) %collective-permute-start.1) | collective-permute-done | bytes 589856 | tf_op jit(solution)/shard_map/ppermute | solution.py:153
  86.2 0.0 copy-start.8
  86.2 1.2 copy-done.8
  87.4 0.0 copy-start.11
  87.4 1.2 copy-done.11
  88.6 7.7 %attention.3 = bf16[1152,128]{1,0:T(8,128)(2,1)} custom-call(s32[5]{0:T(128)S(1)} %pad_add_fusion.1.info_ref, bf16[1152,384]{1,0:T(8,128)(2,1)S(1)} %bitcast.29, bf16[1152,384]{1,0:T(8,128)(2,1)S(1)} %bitcast.23, bf16[1152,384]{1,0:T(8,128)(2,1)S(1)} %bitcast.26, bf16[2,1152,128]{2,1,0:T(8,128)(2,1)S(1)} %collective-permute-done.low_ref, ...), custom_call_target="tpu_custom_call" | custom-call | flops 1358954496 | bytes 2359296 | tf_op jit(solution)/shard_map/attention/pallas_call | solution.py:62
  96.2 0.0 all-gather.7.cloned.1.call-update
  96.3 6.3 %constant_dynamic-slice_fusion = (bf16[1,1152,1,384]{3,2,1,0:T(2,128)(2,1)S(1)}, bf16[1,1152,1,384]{3,2,1,0:T(2,128)(2,1)}) fusion(bf16[1,1152,2,384]{3,2,1,0:T(2,128)(2,1)} %param.11, s32[]{:T(128)S(6)} %select_n.21, s32[]{:T(128)S(6)} %select_n.20), kind=kLoop, calls=%fused_computation.7 | loop fusion | bytes 3538952 | tf_op jit(solution)/shard_map/jit(dynamic_index_in_dim)/dynamic_slice | solution.py:156
  102.6 1.1 copy.18
  103.7 1.2 collective-permute-start.6
  104.9 0.0 copy-done
  104.9 0.1 constant_dynamic-slice_fusion.3
  105.0 1.4 copy.13
  106.4 2.4 %copy.10 = bf16[384,4,384]{2,0,1:T(8,128)(2,1)} copy(bf16[384,4,384]{0,2,1:T(8,128)(2,1)} %bitcast.31) | data formatting | bytes 2359296 | tf_op jit(solution)/shard_map/reshape | solution.py:161
  108.8 7.9 %all-to-all-start = ((bf16[4,384,384]{2,1,0:T(8,128)(2,1)}), bf16[4,384,384]{2,1,0:T(8,128)(2,1)S(1)}, u32[]{:S(2)}, u32[]{:S(2)}) async-start(bf16[4,384,384]{2,1,0:T(8,128)(2,1)} %bitcast.30), calls=%async_computation | async-start | bytes 2359296 | tf_op jit(solution)/shard_map/all_to_all | solution.py:162
  116.7 2.5 %copy.19 = bf16[1,1152,1,384]{3,1,2,0:T(8,128)(2,1)} copy(bf16[1,1152,1,384]{3,2,1,0:T(2,128)(2,1)} %get-tuple-element.6) | data formatting | bytes 1769472
  119.2 0.0 copy-done.13
  119.2 0.1 pad_add_fusion.info_ref
  119.3 0.7 constant_dynamic-slice_fusion.2.refs_4_
  120.0 4.2 %collective-permute-done.6.refs_6_ = bf16[1152,384]{1,0:T(8,128)(2,1)} collective-permute-done((bf16[1152,384]{1,0:T(8,128)(2,1)}, bf16[1152,384]{1,0:T(8,128)(2,1)}, u32[]{:S(2)}, u32[]{:S(2)}) %collective-permute-start.6) | collective-permute-done | bytes 884768 | tf_op jit(solution)/shard_map/ppermute | solution.py:157
  124.2 10.8 %all-to-all-done.refs_3_ = bf16[4,384,384]{2,1,0:T(8,128)(2,1)S(1)} async-done(((bf16[4,384,384]{2,1,0:T(8,128)(2,1)}), bf16[4,384,384]{2,1,0:T(8,128)(2,1)S(1)}, u32[]{:S(2)}, u32[]{:S(2)}) %all-to-all-start) | async-done | bytes 1179680 | tf_op jit(solution)/shard_map/all_to_all | solution.py:162
  135.0 5.3 %all-gather.7.cloned.1.call-done = bf16[9216,128]{1,0:T(8,128)(2,1)} async-done(((bf16[1152,128]{1,0:T(8,128)(2,1)}), bf16[9216,128]{1,0:T(8,128)(2,1)}) %all-gather.7.cloned.1.call-update) | async-done | bytes 2359312 | tf_op jit(solution)/shard_map/all_gather | solution.py:174
  140.3 1.2 copy-done.1
  141.4 1.7 %copy-done.2 = bf16[9216,128]{1,0:T(8,128)(2,1)S(1)} copy-done((bf16[9216,128]{1,0:T(8,128)(2,1)S(1)}, bf16[9216,128]{1,0:T(8,128)(2,1)}, u32[]{:S(2)}) %copy-start.2) | copy-done | bytes 2359320
  143.1 1.7 %copy-done.3 = bf16[9216,128]{1,0:T(8,128)(2,1)S(1)} copy-done((bf16[9216,128]{1,0:T(8,128)(2,1)S(1)}, bf16[9216,128]{1,0:T(8,128)(2,1)}, u32[]{:S(2)}) %copy-start.3) | copy-done | bytes 2359320
  144.8 1.7 %copy-done.4 = bf16[9216,128]{1,0:T(8,128)(2,1)S(1)} copy-done((bf16[9216,128]{1,0:T(8,128)(2,1)S(1)}, bf16[9216,128]{1,0:T(8,128)(2,1)}, u32[]{:S(2)}) %copy-start.4) | copy-done | bytes 2359320
  146.4 6.9 %projection.1 = bf16[1152,384]{1,0:T(8,128)(2,1)} custom-call(s32[19]{0:T(128)S(1)} %pad_add_fusion.info_ref, bf16[8,1152,128]{2,1,0:T(8,128)(2,1)S(1)} %bitcast.20, bf16[8,1152,128]{2,1,0:T(8,128)(2,1)S(1)} %bitcast.19, bf16[8,1152,128]{2,1,0:T(8,128)(2,1)S(1)} %bitcast.18, bf16[4,384,384]{2,1,0:T(8,128)(2,1)S(1)} %all-to-all-done.refs_3_, ...), custom_call_target="tpu_custom_call" | custom-call | flops 2717908992 | bytes 9732096 | tf_op jit(solution)/shard_map/projection/pallas_call | solution.py:107
  (8 shorter events, 0.0 us)
Async XLA Ops:
  6.5 98.4 %copy-start = (bf16[384,3072]{1,0:T(8,128)(2,1)S(1)}, bf16[384,3072]{1,0:T(8,128)(2,1)}, u32[]{:S(2)}) copy-start(bf16[384,3072]{1,0:T(8,128)(2,1)} %param.13) | copy-start | bytes 7077892
  6.5 22.7 %copy-start.5 = (bf16[1,1152,384]{2,1,0:T(8,128)(2,1)S(1)}, bf16[1,1152,384]{2,1,0:T(8,128)(2,1)}, u32[]{:S(2)}) copy-start(bf16[1,1152,384]{2,1,0:T(8,128)(2,1)} %param.9) | copy-start | bytes 2654212
  6.5 9.5 %copy-start.12 = (s32[3,4]{1,0:T(4,128)S(1)}, s32[3,4]{1,0:T(4,128)}, u32[]{:S(2)}) copy-start(s32[3,4]{1,0:T(4,128)} %param.14) | copy-start | bytes 148
  6.5 128.5 %all-gather.11.cloned.1.call-start = ((), (), s32[]{:S(2)}) async-start(), calls=%async_computation.3 | async-start | bytes 2654208 | tf_op jit(solution)/shard_map/all_gather | solution.py:174
  10.0 16.4 %collective-permute-start.4 = (bf16[2,1152,128]{2,1,0:T(8,128)(2,1)}, bf16[2,1152,128]{2,1,0:T(8,128)(2,1)}, u32[]{:S(2)}, u32[]{:S(2)}) collective-permute-start(bf16[2,1152,128]{2,1,0:T(8,128)(2,1)} %pad_maximum_fusion.2), channel_id=1, source_target_pairs={{0,1},{1,2},{2,3},{4,5},{5,6},{6,7},{8,9},{9,10},{10,11},{12,13},{... | collective-permute-start | bytes 1769480 | tf_op jit(solution)/shard_map/ppermute | solution.py:152
  13.2 16.1 %collective-permute-start.5 = (bf16[2,1152,128]{2,1,0:T(8,128)(2,1)}, bf16[2,1152,128]{2,1,0:T(8,128)(2,1)}, u32[]{:S(2)}, u32[]{:S(2)}) collective-permute-start(bf16[2,1152,128]{2,1,0:T(8,128)(2,1)} %pad_maximum_fusion.2), channel_id=1, source_target_pairs={{1,0},{2,1},{3,2},{5,4},{6,5},{7,6},{9,8},{10,9},{11,10},{13,12},{... | collective-permute-start | bytes 1769480 | tf_op jit(solution)/shard_map/ppermute | solution.py:153
  29.3 1.2 copy-start.6
  30.4 1.2 copy-start.9
  40.5 94.5 %all-gather.9.cloned.1.call-start = ((), (), s32[]{:S(2)}) async-start(), calls=%async_computation.2 | async-start | bytes 2654208 | tf_op jit(solution)/shard_map/all_gather | solution.py:174
  41.7 14.8 %collective-permute-start.2 = (bf16[2,1152,128]{2,1,0:T(8,128)(2,1)S(1)}, bf16[2,1152,128]{2,1,0:T(8,128)(2,1)S(1)}, u32[]{:S(2)}, u32[]{:S(2)}) collective-permute-start(bf16[2,1152,128]{2,1,0:T(8,128)(2,1)S(1)} %pad_maximum_fusion.1), channel_id=1, source_target_pairs={{0,1},{1,2},{2,3},{4,5},{5,6},{6,7},{8,9},{9,10},{10,11},{12,13},{... | collective-permute-start | bytes 1769480 | tf_op jit(solution)/shard_map/ppermute | solution.py:152
  44.9 14.6 %collective-permute-start.3 = (bf16[2,1152,128]{2,1,0:T(8,128)(2,1)S(1)}, bf16[2,1152,128]{2,1,0:T(8,128)(2,1)S(1)}, u32[]{:S(2)}, u32[]{:S(2)}) collective-permute-start(bf16[2,1152,128]{2,1,0:T(8,128)(2,1)S(1)} %pad_maximum_fusion.1), channel_id=1, source_target_pairs={{1,0},{2,1},{3,2},{5,4},{6,5},{7,6},{9,8},{10,9},{11,10},{13,12},{... | collective-permute-start | bytes 1769480 | tf_op jit(solution)/shard_map/ppermute | solution.py:153
  59.4 1.2 copy-start.7
  60.6 1.2 copy-start.10
  69.5 70.8 %all-gather.7.cloned.1.call-start = ((), (), s32[]{:S(2)}) async-start(), calls=%async_computation.1 | async-start | bytes 2654208 | tf_op jit(solution)/shard_map/all_gather | solution.py:174
  70.5 13.7 %collective-permute-start = (bf16[2,1152,128]{2,1,0:T(8,128)(2,1)S(1)}, bf16[2,1152,128]{2,1,0:T(8,128)(2,1)S(1)}, u32[]{:S(2)}, u32[]{:S(2)}) collective-permute-start(bf16[2,1152,128]{2,1,0:T(8,128)(2,1)S(1)} %pad_maximum_fusion), channel_id=1, source_target_pairs={{0,1},{1,2},{2,3},{4,5},{5,6},{6,7},{8,9},{9,10},{10,11},{12,13},{... | collective-permute-start | bytes 1769480 | tf_op jit(solution)/shard_map/ppermute | solution.py:152
  72.7 13.5 %collective-permute-start.1 = (bf16[2,1152,128]{2,1,0:T(8,128)(2,1)S(1)}, bf16[2,1152,128]{2,1,0:T(8,128)(2,1)S(1)}, u32[]{:S(2)}, u32[]{:S(2)}) collective-permute-start(bf16[2,1152,128]{2,1,0:T(8,128)(2,1)S(1)} %pad_maximum_fusion), channel_id=1, source_target_pairs={{1,0},{2,1},{3,2},{5,4},{6,5},{7,6},{9,8},{10,9},{11,10},{13,12},{... | collective-permute-start | bytes 1769480 | tf_op jit(solution)/shard_map/ppermute | solution.py:153
  86.2 1.2 copy-start.8
  87.4 1.2 copy-start.11
  103.7 20.5 %collective-permute-start.6 = (bf16[1152,384]{1,0:T(8,128)(2,1)}, bf16[1152,384]{1,0:T(8,128)(2,1)}, u32[]{:S(2)}, u32[]{:S(2)}) collective-permute-start(bf16[1152,384]{1,0:T(8,128)(2,1)} %bitcast.15), channel_id=1, source_target_pairs={{0,16},{16,0},{1,17},{17,1},{2,18},{18,2},{3,19},{19,3},{4,20},{20... | collective-permute-start | bytes 2654216 | tf_op jit(solution)/shard_map/ppermute | solution.py:157
  108.8 26.3 %all-to-all-start = ((bf16[4,384,384]{2,1,0:T(8,128)(2,1)}), bf16[4,384,384]{2,1,0:T(8,128)(2,1)S(1)}, u32[]{:S(2)}, u32[]{:S(2)}) async-start(bf16[4,384,384]{2,1,0:T(8,128)(2,1)} %bitcast.30), calls=%async_computation | async-start | bytes 2359296 | tf_op jit(solution)/shard_map/all_to_all | solution.py:162
  116.7 2.5 %copy-start.13 = (s32[18]{0:T(128)S(1)}, s32[18]{0:T(128)}, u32[]{:S(2)}) copy-start(s32[18]{0:T(128)} %param.15) | copy-start | bytes 220
  140.3 1.2 copy-start.1
  141.4 1.7 %copy-start.2 = (bf16[9216,128]{1,0:T(8,128)(2,1)S(1)}, bf16[9216,128]{1,0:T(8,128)(2,1)}, u32[]{:S(2)}) copy-start(bf16[9216,128]{1,0:T(8,128)(2,1)} %all-gather.11.cloned.1.call-done) | copy-start | bytes 7077892
  143.1 1.7 %copy-start.3 = (bf16[9216,128]{1,0:T(8,128)(2,1)S(1)}, bf16[9216,128]{1,0:T(8,128)(2,1)}, u32[]{:S(2)}) copy-start(bf16[9216,128]{1,0:T(8,128)(2,1)} %all-gather.9.cloned.1.call-done) | copy-start | bytes 7077892
  144.8 1.7 %copy-start.4 = (bf16[9216,128]{1,0:T(8,128)(2,1)S(1)}, bf16[9216,128]{1,0:T(8,128)(2,1)}, u32[]{:S(2)}) copy-start(bf16[9216,128]{1,0:T(8,128)(2,1)} %all-gather.7.cloned.1.call-done) | copy-start | bytes 7077892
Sparse Core Ops, SparseCore 0:
  40.6 30.7 all-gather.10
  73.3 29.0 all-gather.8
  104.3 35.9 all-gather.6

commit v2 on v1

v2 whole, which is shorter than its diff:
```python
import functools
import math

import jax
import jax.numpy as jnp
from jax import lax
from jax.experimental import pallas as pl
from jax.experimental.pallas import tpu as pltpu
from jax.sharding import PartitionSpec as P

HD = 128
FRAME = 64
FAR = 1e30
EXP2_SCALE = math.log2(math.e) / math.sqrt(HD)
VMEM_LIMIT = 40 * 1024 * 1024


def attention_kernel(info_ref, q_ref, k_ref, v_ref, low_ref, high_ref, out_ref):
    tiles_time = pl.num_programs(0)
    tile = q_ref.shape[0]
    first = pl.program_id(0) - info_ref[pl.program_id(0)]
    base = jnp.clip(first, 0, tiles_time - 2)
    rows = pl.ds(pl.multiple_of(base * tile, tile), 2 * tile)
    inside = [(base + step >= first) & (base + step <= first + 1) for step in range(2)]
    query = q_ref[...]
    sides = (
        (k_ref[rows, :], v_ref[rows, :], None),
        (low_ref[0, rows, :], low_ref[1, rows, :], info_ref[tiles_time] == 1),
        (high_ref[0, rows, :], high_ref[1, rows, :], info_ref[tiles_time + 1] == 1),
    )
    blocks = []
    row_max = None
    for keys, _, width_ok in sides:
        scores = lax.dot_general(
            query, keys, (((1,), (1,)), ((), ())), preferred_element_type=jnp.float32
        )
        for step in range(2):
            allowed = inside[step] if width_ok is None else inside[step] & width_ok
            block = scores[:, step * tile : (step + 1) * tile]
            block_max = jnp.where(allowed, jnp.max(block, axis=1, keepdims=True), -FAR)
            row_max = block_max if row_max is None else jnp.maximum(row_max, block_max)
            blocks.append((block, allowed))
    shift = row_max * EXP2_SCALE
    weights = [
        jnp.exp2(block * EXP2_SCALE - jnp.where(allowed, shift, FAR)).astype(jnp.bfloat16)
        for block, allowed in blocks
    ]
    values = jnp.concatenate([side[1] for side in sides], axis=0)
    total = jnp.dot(
        jnp.concatenate(weights, axis=1),
        jnp.concatenate([values, jnp.ones_like(values)], axis=1),
        preferred_element_type=jnp.float32,
    )
    out_ref[...] = (total[:, :HD] / total[:, HD:]).astype(jnp.bfloat16)


def attention(info, queries, keys, values, low, high, head, tile):
    count = queries.shape[0]
    side = pl.BlockSpec((2, count, HD), lambda t, info: (0, 0, 0))
    whole = pl.BlockSpec((count, HD), lambda t, info: (0, head))
    pairs = count * 6 * tile
    return pl.pallas_call(
        attention_kernel,
        out_shape=jax.ShapeDtypeStruct((count, HD), jnp.bfloat16),
        grid_spec=pltpu.PrefetchScalarGridSpec(
            num_scalar_prefetch=1,
            grid=(count // tile,),
            in_specs=[pl.BlockSpec((tile, HD), lambda t, info: (t, head)), whole, whole, side, side],
            out_specs=pl.BlockSpec((tile, HD), lambda t, info: (t, 0)),
        ),
        compiler_params=pltpu.CompilerParams(vmem_limit_bytes=VMEM_LIMIT),
        cost_estimate=pl.CostEstimate(
            flops=4 * pairs * HD, bytes_accessed=8 * count * HD * 2, transcendentals=pairs
        ),
        name="attention",
    )(info, queries, keys, values, low, high)


def projection_kernel(info_ref, *refs):
    *pieces, gate_ref, mine_ref, other_ref, out_ref = refs
    weight_count = info_weights(pieces)
    weight_refs, pieces = pieces[:weight_count], pieces[weight_count:]
    tile = out_ref.shape[0]
    frames = tile // FRAME
    time_tile = pl.program_id(0)
    own_first = info_ref[0] == 0
    weights = jnp.concatenate([ref[...] for ref in weight_refs], axis=0)
    half = len(pieces) // 2
    hidden = []
    for which, base_ref in enumerate((mine_ref, other_ref)):
        rows = jnp.concatenate(
            [piece[...] for piece in pieces[which * half : (which + 1) * half]], axis=1
        )
        projected = jnp.dot(rows, weights, preferred_element_type=jnp.float32)
        hidden.append(base_ref[...].astype(jnp.float32) + gate_ref[which] * projected)
    for frame in range(frames):
        rows = slice(frame * FRAME, (frame + 1) * FRAME)
        step = info_ref[1 + time_tile * frames + frame].astype(jnp.float32)
        guide = 1.0 + 0.5 * step
        cond = jnp.where(own_first, hidden[0][rows], hidden[1][rows])
        uncond = jnp.where(own_first, hidden[1][rows], hidden[0][rows])
        out_ref[rows, :] = (uncond + guide * (cond - uncond)).astype(jnp.bfloat16)


def info_weights(operands):
    return 4


def project(info, weights, pieces, gate, mine, other, tile):
    count, width = mine.shape
    rows = pl.BlockSpec((tile, width), lambda t, info: (t, 0))
    piece = pl.BlockSpec((tile, HD), lambda t, info: (t, 0))
    return pl.pallas_call(
        projection_kernel,
        out_shape=jax.ShapeDtypeStruct((count, width), jnp.bfloat16),
        grid_spec=pltpu.PrefetchScalarGridSpec(
            num_scalar_prefetch=1,
            grid=(count // tile,),
            in_specs=[pl.BlockSpec(w.shape, lambda t, info: (0, 0)) for w in weights]
            + [piece] * len(pieces)
            + [pl.BlockSpec(gate.shape, lambda t, info: (0, 0, 0)), rows, rows],
            out_specs=rows,
        ),
        compiler_params=pltpu.CompilerParams(vmem_limit_bytes=VMEM_LIMIT),
        cost_estimate=pl.CostEstimate(
            flops=2 * count * width * len(pieces) * HD,
            bytes_accessed=2 * count * (3 * width + len(pieces) * HD),
            transcendentals=0,
        ),
        name="projection",
    )(info, *weights, *pieces, gate, mine, other)


def pack_kernel(k_ref, v_ref, *out_refs):
    for head, out_ref in enumerate(out_refs):
        cols = slice(head * HD, (head + 1) * HD)
        out_ref[0] = k_ref[:, cols]
        out_ref[1] = v_ref[:, cols]


def pack_heads(keys, values, tile):
    count, features = keys.shape
    heads = features // HD
    rows = pl.BlockSpec((tile, features), lambda t: (t, 0))
    return pl.pallas_call(
        pack_kernel,
        out_shape=[jax.ShapeDtypeStruct((2, count, HD), jnp.bfloat16)] * heads,
        grid=(count // tile,),
        in_specs=[rows, rows],
        out_specs=[pl.BlockSpec((2, tile, HD), lambda t: (0, t, 0))] * heads,
        cost_estimate=pl.CostEstimate(
            flops=0, bytes_accessed=8 * count * features, transcendentals=0
        ),
        name="pack_heads",
    )(keys, values)


def split_kernel(info_ref, w_ref, *out_refs):
    for index, out_ref in enumerate(out_refs):

        @pl.when(pl.program_id(0) == index)
        def _():
            out_ref[...] = w_ref[...]


def split_weight(info, weight, width, head_count):
    rows = weight.shape[0]
    return pl.pallas_call(
        split_kernel,
        out_shape=[jax.ShapeDtypeStruct((rows, width), jnp.bfloat16)] * head_count,
        grid_spec=pltpu.PrefetchScalarGridSpec(
            num_scalar_prefetch=1,
            grid=(head_count,),
            in_specs=[pl.BlockSpec((rows, width), lambda i, info: (0, info[i]))],
            out_specs=[pl.BlockSpec((rows, width), lambda i, info: (0, 0))] * head_count,
        ),
        cost_estimate=pl.CostEstimate(
            flops=0, bytes_accessed=4 * rows * width * head_count, transcendentals=0
        ),
        name="split_weight",
    )(info, weight)


def local(queries, keys, values, residual, gate, out_weight, time_offsets, guidance_index):
    tiles_time, tiles_wide = time_offsets.shape
    count, features = queries.shape[1:]
    tile = count // tiles_time
    heads = features // HD
    head_count = lax.axis_size("head")
    columns = lax.axis_size("tokens")
    branch_pos = lax.axis_index("branch")
    head_pos = lax.axis_index("head")
    width_pos = lax.axis_index("tokens")
    width = gate.shape[2] // head_count

    up = [(i, i + 1) for i in range(columns - 1)]
    down = [(i + 1, i) for i in range(columns - 1)]

    def swap(value, branch_bit, head_bits):
        if not head_bits:
            return lax.ppermute(value, "branch", [(0, 1), (1, 0)])
        if not branch_bit:
            return lax.ppermute(value, "head", [(i, i ^ head_bits) for i in range(head_count)])
        flip = head_count + head_bits
        return lax.ppermute(
            value, ("branch", "head"), [(i, i ^ flip) for i in range(2 * head_count)]
        )

    packed = pack_heads(keys[0], values[0], tile)
    packed, residual, out_weight = lax.optimization_barrier((packed, residual, out_weight))
    low, high = [], []
    for key_value in packed:
        low.append(lax.ppermute(key_value, "tokens", up))
        high.append(lax.ppermute(key_value, "tokens", down))

    first_half, second_half = residual[0, :, 0], residual[0, :, 1]
    mine = jnp.where(branch_pos == 0, first_half, second_half)
    other = swap(jnp.where(branch_pos == 0, second_half, first_half), 1, 0)
    gate_block = lax.dynamic_slice(
        gate, (0, branch_pos, head_pos * width), (2, 1, width)
    ).astype(jnp.float32)
    gate_block = jnp.where(branch_pos == 0, gate_block, gate_block[::-1])

    distances = jnp.arange(head_count, dtype=jnp.int32)
    blocks = split_weight(
        branch_pos * head_count + (head_pos ^ distances), out_weight, width, head_count
    )
    weights = [blocks[0]] + [swap(blocks[bits], 0, bits) for bits in range(1, head_count)]

    offsets = lax.dynamic_index_in_dim(time_offsets, width_pos, 1, keepdims=False)
    edges = jnp.stack([width_pos > 0, width_pos < tiles_wide - 1]).astype(jnp.int32)
    attention_info = jnp.concatenate([offsets, edges])
    projection_info = jnp.concatenate([branch_pos[None].astype(jnp.int32), guidance_index])

    pieces = {}
    for head in range(heads):
        own = attention(
            attention_info, queries[0], keys[0], values[0], low[head], high[head], head, tile
        )
        pieces[0, 0, head] = own
        pieces[1, 0, head] = swap(own, 1, 0)
        pieces[0, 2, head] = swap(own, 0, 2)
        pieces[1, 2, head] = swap(own, 1, 2)
        for branch_bit in range(2):
            for bits in (0, 2):
                pieces[branch_bit, bits + 1, head] = swap(pieces[branch_bit, bits, head], 0, 1)
    ordered = [
        pieces[branch_bit, bits, head]
        for branch_bit in range(2)
        for bits in range(head_count)
        for head in range(heads)
    ]
    return project(projection_info, weights, ordered, gate_block, mine, other, tile)


def solution(mesh):
    return jax.shard_map(
        local,
        mesh=mesh,
        in_specs=(
            P("branch", "tokens", "head"),
            P("branch", "tokens", "head"),
            P("branch", "tokens", "head"),
            P("branch", "tokens", None, "head"),
            P(),
            P("head", None),
            P(),
            P(),
        ),
        out_specs=P("tokens", ("branch", "head")),
        check_vma=False,
    )
```

time: 163 us -> 131 us (0.80)
  waiting for transfers between devices: 56 us -> 27.3 us
  between operations: 13.2 us -> 0.27 us
  starting transfers between devices: 25.9 us -> 38 us
  local copies, waits for them, and re-layouts: 30.4 us -> 22 us
  Pallas kernels: 31.1 us -> 38.9 us
    ppermute x3, waiting for transfers between devices: 27.9 us -> 0.01 us  [local(): low.append(lax.ppermute(key_value, 'tokens', up))]
    ppermute x1 -> x25, waiting for transfers between devices: 4.16 us -> 27.3 us  [the longest x3 16.7 us: swap(): lax.ppermute(value, ('branch', 'head'), [(i, i ^ flip) for i in range(2 *...]
    ppermute x1 -> x25, starting transfers between devices: 1.22 us -> 21.5 us  [the longest x18 13.1 us: swap(): lax.ppermute(value, 'head', [(i, i ^ head_bits) for i in range(head_count)])]
    all_to_all x1 -> x0, waiting for transfers between devices: 10.8 us -> none  [local(): weights = lax.all_to_all(branch_weight, 'head', 0, 0)]
    all_to_all x1 -> x0, starting transfers between devices: 7.94 us -> none  [local(): weights = lax.all_to_all(branch_weight, 'head', 0, 0)]
    ppermute x3, waiting for transfers between devices: 7.77 us -> 0.01 us  [local(): high.append(lax.ppermute(key_value, 'tokens', down))]
    pallas_call x1 -> x3, Pallas kernels: 6.9 us -> 14.3 us  [the longest x1 6.91 us: project(): pl.pallas_call(projection_kernel, out_shape=jax.ShapeDtypeStruct((count,...]
    dynamic_slice x3 -> x0, local copies, waits for them, and re-layouts: 7.07 us -> none  [the longest x1 6.31 us: local(): lax.dynamic_index_in_dim(residual[0], 1 - branch_pos, 1, keepdims=False)]
  transfers between devices with their start and end apart: 11 -> 31, of which waited for: 9 -> 10; matrix products, arithmetic and copies ran while one was open for 11% -> 5% of each run, Pallas kernels for 10% -> 22%
where the time goes in v2:
time: 131 us; the launch traced here: 129 us
  Pallas kernels  38.9 us (30%)
  starting transfers between devices  38 us (29%)
  waiting for transfers between devices  27.3 us (21%)
  local copies, waits for them, and re-layouts  22 us (17%)
  other arithmetic  2.55 us (2%)
    pallas_call x3, Pallas kernels, attention(): pl.pallas_call(attention_kernel, out_shape=jax.ShapeDtypeStruct((count, H...  24.6 us
    unnamed x64, local copies, waits for them, and re-layouts  18.7 us
    ppermute x3, waiting for transfers between devices, swap(): lax.ppermute(value, ('branch', 'head'), [(i, i ^ flip) for i in range(2 *...  16.7 us
    ppermute x18, starting transfers between devices, swap(): lax.ppermute(value, 'head', [(i, i ^ head_bits) for i in range(head_count)])  13.1 us
    ppermute x3, starting transfers between devices, local(): low.append(lax.ppermute(key_value, 'tokens', up))  9.93 us
    ppermute x4, waiting for transfers between devices, swap(): return lax.ppermute(value, 'branch', [(0, 1), (1, 0)])  8.58 us
    pallas_call x1, Pallas kernels, project(): pl.pallas_call(projection_kernel, out_shape=jax.ShapeDtypeStruct((count,...  6.91 us
    ppermute x3, starting transfers between devices, local(): high.append(lax.ppermute(key_value, 'tokens', down))  6.54 us
  transfers between devices with their start and end apart: 31, of which 10 were waited for; matrix products, arithmetic and copies ran while one was open for 5% of the time, Pallas kernels for 22%

profile of v2, /device:TPU:9, one launch (start us, length us, event | category | flops | bytes accessed | tf_op | source)
XLA Modules:
  0.0 129.0 jit_solution(16225257153703757760)
XLA Ops:
  0.0 3.6 %pack_heads.1 = (bf16[2,1152,128]{2,1,0:T(8,128)(2,1)}, bf16[2,1152,128]{2,1,0:T(8,128)(2,1)}, bf16[2,1152,128]{2,1,0:T(8,128)(2,1)}) custom-call(bf16[1152,384]{1,0:T(8,128)(2,1)} %bitcast.10, bf16[1152,384]{1,0:T(8,128)(2,1)} %bitcast.14), custom_call_target="tpu_custom_call" | custom-call | bytes 3538944 | tf_op jit(solution)/shard_map/pack_heads/pallas_call | solution.py:145
  3.6 1.9 %collective-permute-start.4 = (bf16[2,1152,128]{2,1,0:T(8,128)(2,1)}, bf16[2,1152,128]{2,1,0:T(8,128)(2,1)S(1)}, u32[]{:S(2)}, u32[]{:S(2)}) collective-permute-start(bf16[2,1152,128]{2,1,0:T(8,128)(2,1)} %get-tuple-element.25), channel_id=1, source_target_pairs={{1,0},{2,1},{3,2},{5,4},{6,5},{7,6},{9,8},{10,9},{11,10},{13,12},{... | collective-permute-start | bytes 1769480 | tf_op jit(solution)/shard_map/ppermute | solution.py:214
  5.5 3.4 %collective-permute-start.3 = (bf16[2,1152,128]{2,1,0:T(8,128)(2,1)}, bf16[2,1152,128]{2,1,0:T(8,128)(2,1)S(1)}, u32[]{:S(2)}, u32[]{:S(2)}) collective-permute-start(bf16[2,1152,128]{2,1,0:T(8,128)(2,1)} %get-tuple-element.25), channel_id=1, source_target_pairs={{0,1},{1,2},{2,3},{4,5},{5,6},{6,7},{8,9},{9,10},{10,11},{12,13},{... | collective-permute-start | bytes 1769480 | tf_op jit(solution)/shard_map/ppermute | solution.py:213
  8.9 0.5 xor_add_fusion.info_ref
  9.4 3.8 %split_weight.1 = (bf16[384,384]{1,0:T(8,128)(2,1)}, bf16[384,384]{1,0:T(8,128)(2,1)}, bf16[384,384]{1,0:T(8,128)(2,1)}, bf16[384,384]{1,0:T(8,128)(2,1)}) custom-call(s32[4]{0:T(128)} %xor_add_fusion.info_ref, bf16[384,3072]{1,0:T(8,128)(2,1)} %w_ref), custom_call_target="tpu_custom_call" | custom-call | bytes 2359296 | tf_op jit(solution)/shard_map/split_weight/pallas_call | solution.py:168
  13.2 1.2 collective-permute-start
  14.4 1.9 %collective-permute-start.6 = (bf16[2,1152,128]{2,1,0:T(8,128)(2,1)}, bf16[2,1152,128]{2,1,0:T(8,128)(2,1)}, u32[]{:S(2)}, u32[]{:S(2)}) collective-permute-start(bf16[2,1152,128]{2,1,0:T(8,128)(2,1)} %get-tuple-element.26), channel_id=1, source_target_pairs={{1,0},{2,1},{3,2},{5,4},{6,5},{7,6},{9,8},{10,9},{11,10},{13,12},{... | collective-permute-start | bytes 1769480 | tf_op jit(solution)/shard_map/ppermute | solution.py:214
  16.3 3.4 %collective-permute-start.5 = (bf16[2,1152,128]{2,1,0:T(8,128)(2,1)}, bf16[2,1152,128]{2,1,0:T(8,128)(2,1)}, u32[]{:S(2)}, u32[]{:S(2)}) collective-permute-start(bf16[2,1152,128]{2,1,0:T(8,128)(2,1)} %get-tuple-element.26), channel_id=1, source_target_pairs={{0,1},{1,2},{2,3},{4,5},{5,6},{6,7},{8,9},{9,10},{10,11},{12,13},{... | collective-permute-start | bytes 1769480 | tf_op jit(solution)/shard_map/ppermute | solution.py:213
  19.7 0.7 copy-done.4
  20.4 2.7 %collective-permute-start.8 = (bf16[2,1152,128]{2,1,0:T(8,128)(2,1)}, bf16[2,1152,128]{2,1,0:T(8,128)(2,1)}, u32[]{:S(2)}, u32[]{:S(2)}) collective-permute-start(bf16[2,1152,128]{2,1,0:T(8,128)(2,1)} %get-tuple-element.27), channel_id=1, source_target_pairs={{1,0},{2,1},{3,2},{5,4},{6,5},{7,6},{9,8},{10,9},{11,10},{13,12},{... | collective-permute-start | bytes 1769480 | tf_op jit(solution)/shard_map/ppermute | solution.py:214
  23.2 0.8 copy-done.26
  24.0 1.4 %collective-permute-start.1 = (bf16[384,384]{1,0:T(8,128)(2,1)}, bf16[384,384]{1,0:T(8,128)(2,1)S(1)}, u32[]{:S(2)}, u32[]{:S(2)}) collective-permute-start(bf16[384,384]{1,0:T(8,128)(2,1)} %get-tuple-element.23), channel_id=1, source_target_pairs={{0,8},{4,12},{8,0},{12,4},{1,9},{5,13},{9,1},{13,5},{2,10},{6,14},... | collective-permute-start | bytes 884744 | tf_op jit(solution)/shard_map/ppermute | solution.py:203
  25.4 0.8 copy-done.28
  26.2 0.8 collective-permute-start.2
  27.1 3.1 %copy.9 = bf16[1,1152,2,384]{3,1,2,0:T(8,128)(2,1)} copy(bf16[1,1152,2,384]{3,2,1,0:T(2,128)(2,1)} %param.11) | data formatting | bytes 3538944 | tf_op jit(solution)/shard_map/optimization_barrier | solution.py:210
  30.5 1.1 copy-done.27
  31.6 1.1 copy-done.29
  32.6 7.4 %attention.3.refs_4_ = bf16[1152,128]{1,0:T(8,128)(2,1)S(1)} custom-call(s32[5]{0:T(128)S(1)} %pad_add_fusion.1.info_ref, bf16[1152,384]{1,0:T(8,128)(2,1)S(1)} %bitcast.18, bf16[1152,384]{1,0:T(8,128)(2,1)S(1)} %bitcast.11, bf16[1152,384]{1,0:T(8,128)(2,1)S(1)} %bitcast.15, bf16[2,1152,128]{2,1,0:T(8,128)(2,1)S(1)} %copy-done.29, ...), custom_call_target="tpu_custom_call" | custom-call | flops 1358954496 | bytes 2359296 | tf_op jit(solution)/shard_map/attention/pallas_call | solution.py:62
  40.1 0.7 copy-done.6
  40.8 3.2 %collective-permute-start.7 = (bf16[2,1152,128]{2,1,0:T(8,128)(2,1)}, bf16[2,1152,128]{2,1,0:T(8,128)(2,1)S(1)}, u32[]{:S(2)}, u32[]{:S(2)}) collective-permute-start(bf16[2,1152,128]{2,1,0:T(8,128)(2,1)} %get-tuple-element.27), channel_id=1, source_target_pairs={{0,1},{1,2},{2,3},{4,5},{5,6},{6,7},{8,9},{9,10},{10,11},{12,13},{... | collective-permute-start | bytes 1769480 | tf_op jit(solution)/shard_map/ppermute | solution.py:213
  44.1 0.7 copy-done.8
  44.8 2.2 %collective-permute-start.24 = (bf16[1152,128]{1,0:T(8,128)(2,1)S(1)}, bf16[1152,128]{1,0:T(8,128)(2,1)}, u32[]{:S(2)}, u32[]{:S(2)}) collective-permute-start(bf16[1152,128]{1,0:T(8,128)(2,1)S(1)} %attention.3.refs_4_), channel_id=1, source_target_pairs={{0,24},{4,28},{8,16},{12,20},{16,8},{20,12},{24,0},{28,4},{1,25},{... | collective-permute-start | bytes 884744 | tf_op jit(solution)/shard_map/ppermute | solution.py:205
  47.4 1.0 collective-permute-start.9
  48.4 0.7 copy-done.10
  49.1 1.1 select_bitcast_fusion
  50.2 8.7 %attention.4.refs_5_ = bf16[1152,128]{1,0:T(8,128)(2,1)S(1)} custom-call(s32[5]{0:T(128)S(1)} %pad_add_fusion.1.info_ref, bf16[1152,384]{1,0:T(8,128)(2,1)S(1)} %bitcast.19, bf16[1152,384]{1,0:T(8,128)(2,1)S(1)} %bitcast.12, bf16[1152,384]{1,0:T(8,128)(2,1)S(1)} %bitcast.16, bf16[2,1152,128]{2,1,0:T(8,128)(2,1)} %collective-permute-done.5.low_ref, ...), custom_call_target="tpu_custom_call" | custom-call | flops 1358954496 | bytes 2359296 | tf_op jit(solution)/shard_map/attention/pallas_call | solution.py:62
  58.9 1.3 %collective-permute-start.30 = (bf16[1152,384]{1,0:T(8,128)(2,1)}, bf16[1152,384]{1,0:T(8,128)(2,1)S(1)}, u32[]{:S(2)}, u32[]{:S(2)}) collective-permute-start(bf16[1152,384]{1,0:T(8,128)(2,1)} %get-tuple-element.29), channel_id=1, source_target_pairs={{0,16},{16,0},{1,17},{17,1},{2,18},{18,2},{3,19},{19,3},{4,20},{20... | collective-permute-start | bytes 2654216 | tf_op jit(solution)/shard_map/ppermute | solution.py:201
  60.2 1.0 collective-permute-start.25
  61.2 1.2 collective-permute-start.19
  62.4 0.5 collective-permute-start.13
  62.9 1.2 collective-permute-start.10
  64.1 8.5 %attention.5.refs_6_ = bf16[1152,128]{1,0:T(8,128)(2,1)S(1)} custom-call(s32[5]{0:T(128)S(1)} %pad_add_fusion.1.info_ref, bf16[1152,384]{1,0:T(8,128)(2,1)S(1)} %bitcast.20, bf16[1152,384]{1,0:T(8,128)(2,1)S(1)} %bitcast.13, bf16[1152,384]{1,0:T(8,128)(2,1)S(1)} %bitcast.17, bf16[2,1152,128]{2,1,0:T(8,128)(2,1)S(1)} %collective-permute-done.7.low_ref, ...), custom_call_target="tpu_custom_call" | custom-call | flops 1358954496 | bytes 2359296 | tf_op jit(solution)/shard_map/attention/pallas_call | solution.py:62
  72.6 15.0 %collective-permute-done.25.refs_23_ = bf16[1152,128]{1,0:T(8,128)(2,1)} collective-permute-done((bf16[1152,128]{1,0:T(8,128)(2,1)S(1)}, bf16[1152,128]{1,0:T(8,128)(2,1)}, u32[]{:S(2)}, u32[]{:S(2)}) %collective-permute-start.25) | collective-permute-done | bytes 294944 | tf_op jit(solution)/shard_map/ppermute | solution.py:205
  87.7 1.3 %collective-permute-start.26 = (bf16[1152,128]{1,0:T(8,128)(2,1)S(1)}, bf16[1152,128]{1,0:T(8,128)(2,1)S(1)}, u32[]{:S(2)}, u32[]{:S(2)}) collective-permute-start(bf16[1152,128]{1,0:T(8,128)(2,1)S(1)} %attention.5.refs_6_), channel_id=1, source_target_pairs={{0,24},{4,28},{8,16},{12,20},{16,8},{20,12},{24,0},{28,4},{1,25},{... | collective-permute-start | bytes 884744 | tf_op jit(solution)/shard_map/ppermute | solution.py:205
  89.0 4.2 %collective-permute-done.19.refs_17_ = bf16[1152,128]{1,0:T(8,128)(2,1)S(1)} collective-permute-done((bf16[1152,128]{1,0:T(8,128)(2,1)S(1)}, bf16[1152,128]{1,0:T(8,128)(2,1)S(1)}, u32[]{:S(2)}, u32[]{:S(2)}) %collective-permute-start.19) | collective-permute-done | bytes 294944 | tf_op jit(solution)/shard_map/ppermute | solution.py:201
  93.1 1.1 collective-permute-start.20
  94.3 1.1 collective-permute-start.14
  95.4 0.7 copy-done.20
  96.1 1.7 %collective-permute-start.11 = (bf16[1152,128]{1,0:T(8,128)(2,1)S(1)}, bf16[1152,128]{1,0:T(8,128)(2,1)S(1)}, u32[]{:S(2)}, u32[]{:S(2)}) collective-permute-start(bf16[1152,128]{1,0:T(8,128)(2,1)S(1)} %attention.5.refs_6_), channel_id=1, source_target_pairs={{0,4},{4,0},{8,12},{12,8},{1,5},{5,1},{9,13},{13,9},{2,6},{6,2},{1... | collective-permute-start | bytes 884744 | tf_op jit(solution)/shard_map/ppermute | solution.py:203
  97.8 0.7 copy-done.22
  98.6 1.7 %collective-permute-done.26.refs_24_ = bf16[1152,128]{1,0:T(8,128)(2,1)S(1)} collective-permute-done((bf16[1152,128]{1,0:T(8,128)(2,1)S(1)}, bf16[1152,128]{1,0:T(8,128)(2,1)S(1)}, u32[]{:S(2)}, u32[]{:S(2)}) %collective-permute-start.26) | collective-permute-done | bytes 294944 | tf_op jit(solution)/shard_map/ppermute | solution.py:205
  100.2 1.2 collective-permute-start.27
  101.4 4.4 %collective-permute-done.20.refs_18_ = bf16[1152,128]{1,0:T(8,128)(2,1)S(1)} collective-permute-done((bf16[1152,128]{1,0:T(8,128)(2,1)S(1)}, bf16[1152,128]{1,0:T(8,128)(2,1)S(1)}, u32[]{:S(2)}, u32[]{:S(2)}) %collective-permute-start.20) | collective-permute-done | bytes 294944 | tf_op jit(solution)/shard_map/ppermute | solution.py:201
  105.8 0.8 collective-permute-start.21
  106.8 0.5 collective-permute-start.15
  107.3 0.8 dynamic-slice_convert_fusion
  108.1 0.5 collective-permute-start.22
  108.7 0.4 collective-permute-start.29
  109.3 0.4 collective-permute-start.17
  110.0 0.4 collective-permute-done.16.refs_14_
  110.6 0.4 collective-permute-done.23.refs_21_
  111.1 0.4 collective-permute-done.17.refs_15_
  111.5 1.0 copy-done.3
  112.4 1.0 copy-done.5
  113.4 1.0 copy-done.7
  114.4 1.0 copy-done.9
  115.3 1.0 copy-done.11
  116.3 1.0 copy-done.13
  117.3 1.0 copy-done.15
  118.2 1.0 copy-done.17
  119.2 1.0 copy-done.19
  120.1 1.0 copy-done.21
  121.1 1.0 copy-done.23
  122.1 6.9 %projection.1 = bf16[1152,384]{1,0:T(8,128)(2,1)} custom-call(s32[19]{0:T(128)S(1)} %pad_add_fusion.info_ref, bf16[384,384]{1,0:T(8,128)(2,1)S(1)} %copy-done.3, bf16[384,384]{1,0:T(8,128)(2,1)S(1)} %copy-done.5, bf16[384,384]{1,0:T(8,128)(2,1)S(1)} %copy-done.7, bf16[384,384]{1,0:T(8,128)(2,1)S(1)} %copy-done.9, bf16[1152,128]{1,0:T(8,128)(2,1)S(1)} %copy-done.11, ...), custom_call_target="tpu_custom_call" | custom-call | flops 2717908992 | bytes 9732096 | tf_op jit(solution)/shard_map/projection/pallas_call | solution.py:113
  (77 shorter events, 2.0 us)
Async XLA Ops:
  0.0 30.2 %copy-start = (s32[3,4]{1,0:T(4,128)S(1)}, s32[3,4]{1,0:T(4,128)}, u32[]{:S(2)}) copy-start(s32[3,4]{1,0:T(4,128)} %param.14) | copy-start | bytes 148
  3.6 19.6 %collective-permute-start.4 = (bf16[2,1152,128]{2,1,0:T(8,128)(2,1)}, bf16[2,1152,128]{2,1,0:T(8,128)(2,1)S(1)}, u32[]{:S(2)}, u32[]{:S(2)}) collective-permute-start(bf16[2,1152,128]{2,1,0:T(8,128)(2,1)} %get-tuple-element.25), channel_id=1, source_target_pairs={{1,0},{2,1},{3,2},{5,4},{6,5},{7,6},{9,8},{10,9},{11,10},{13,12},{... | collective-permute-start | bytes 1769480 | tf_op jit(solution)/shard_map/ppermute | solution.py:214
  5.5 19.9 %collective-permute-start.3 = (bf16[2,1152,128]{2,1,0:T(8,128)(2,1)}, bf16[2,1152,128]{2,1,0:T(8,128)(2,1)S(1)}, u32[]{:S(2)}, u32[]{:S(2)}) collective-permute-start(bf16[2,1152,128]{2,1,0:T(8,128)(2,1)} %get-tuple-element.25), channel_id=1, source_target_pairs={{0,1},{1,2},{2,3},{4,5},{5,6},{6,7},{8,9},{9,10},{10,11},{12,13},{... | collective-permute-start | bytes 1769480 | tf_op jit(solution)/shard_map/ppermute | solution.py:213
  13.2 6.5 %collective-permute-start = (bf16[384,384]{1,0:T(8,128)(2,1)}, bf16[384,384]{1,0:T(8,128)(2,1)S(1)}, u32[]{:S(2)}, u32[]{:S(2)}) collective-permute-start(bf16[384,384]{1,0:T(8,128)(2,1)} %get-tuple-element.22), channel_id=1, source_target_pairs={{0,4},{4,0},{8,12},{12,8},{1,5},{5,1},{9,13},{13,9},{2,6},{6,2},{1... | collective-permute-start | bytes 884744 | tf_op jit(solution)/shard_map/ppermute | solution.py:203
  14.4 32.5 %collective-permute-start.6 = (bf16[2,1152,128]{2,1,0:T(8,128)(2,1)}, bf16[2,1152,128]{2,1,0:T(8,128)(2,1)}, u32[]{:S(2)}, u32[]{:S(2)}) collective-permute-start(bf16[2,1152,128]{2,1,0:T(8,128)(2,1)} %get-tuple-element.26), channel_id=1, source_target_pairs={{1,0},{2,1},{3,2},{5,4},{6,5},{7,6},{9,8},{10,9},{11,10},{13,12},{... | collective-permute-start | bytes 1769480 | tf_op jit(solution)/shard_map/ppermute | solution.py:214
  16.3 30.9 %collective-permute-start.5 = (bf16[2,1152,128]{2,1,0:T(8,128)(2,1)}, bf16[2,1152,128]{2,1,0:T(8,128)(2,1)}, u32[]{:S(2)}, u32[]{:S(2)}) collective-permute-start(bf16[2,1152,128]{2,1,0:T(8,128)(2,1)} %get-tuple-element.26), channel_id=1, source_target_pairs={{0,1},{1,2},{2,3},{4,5},{5,6},{6,7},{8,9},{9,10},{10,11},{12,13},{... | collective-permute-start | bytes 1769480 | tf_op jit(solution)/shard_map/ppermute | solution.py:213
  19.7 0.7 copy-start.4
  20.4 27.0 %collective-permute-start.8 = (bf16[2,1152,128]{2,1,0:T(8,128)(2,1)}, bf16[2,1152,128]{2,1,0:T(8,128)(2,1)}, u32[]{:S(2)}, u32[]{:S(2)}) collective-permute-start(bf16[2,1152,128]{2,1,0:T(8,128)(2,1)} %get-tuple-element.27), channel_id=1, source_target_pairs={{1,0},{2,1},{3,2},{5,4},{6,5},{7,6},{9,8},{10,9},{11,10},{13,12},{... | collective-permute-start | bytes 1769480 | tf_op jit(solution)/shard_map/ppermute | solution.py:214
  23.2 0.8 copy-start.26
  24.0 16.1 %collective-permute-start.1 = (bf16[384,384]{1,0:T(8,128)(2,1)}, bf16[384,384]{1,0:T(8,128)(2,1)S(1)}, u32[]{:S(2)}, u32[]{:S(2)}) collective-permute-start(bf16[384,384]{1,0:T(8,128)(2,1)} %get-tuple-element.23), channel_id=1, source_target_pairs={{0,8},{4,12},{8,0},{12,4},{1,9},{5,13},{9,1},{13,5},{2,10},{6,14},... | collective-permute-start | bytes 884744 | tf_op jit(solution)/shard_map/ppermute | solution.py:203
  25.4 0.8 copy-start.28
  26.2 17.8 %collective-permute-start.2 = (bf16[384,384]{1,0:T(8,128)(2,1)}, bf16[384,384]{1,0:T(8,128)(2,1)S(1)}, u32[]{:S(2)}, u32[]{:S(2)}) collective-permute-start(bf16[384,384]{1,0:T(8,128)(2,1)} %get-tuple-element.24), channel_id=1, source_target_pairs={{0,12},{4,8},{8,4},{12,0},{1,13},{5,9},{9,5},{13,1},{2,14},{6,10},... | collective-permute-start | bytes 884744 | tf_op jit(solution)/shard_map/ppermute | solution.py:203
  27.1 3.4 %copy-start.1 = (bf16[1,1152,384]{2,1,0:T(8,128)(2,1)S(1)}, bf16[1,1152,384]{2,1,0:T(8,128)(2,1)}, u32[]{:S(2)}) copy-start(bf16[1,1152,384]{2,1,0:T(8,128)(2,1)} %param.9) | copy-start | bytes 2654212
  27.1 3.4 %copy-start.2 = (bf16[1,1152,384]{2,1,0:T(8,128)(2,1)S(1)}, bf16[1,1152,384]{2,1,0:T(8,128)(2,1)}, u32[]{:S(2)}) copy-start(bf16[1,1152,384]{2,1,0:T(8,128)(2,1)} %param.10) | copy-start | bytes 2654212
  27.1 3.4 %copy-start.24 = (bf16[1,1152,384]{2,1,0:T(8,128)(2,1)S(1)}, bf16[1,1152,384]{2,1,0:T(8,128)(2,1)}, u32[]{:S(2)}) copy-start(bf16[1,1152,384]{2,1,0:T(8,128)(2,1)} %param.8) | copy-start | bytes 2654212
  30.5 1.1 copy-start.27
  31.6 1.1 copy-start.29
  32.6 16.5 %copy-start.30 = (bf16[1,1152,2,384]{3,1,2,0:T(8,128)(2,1)S(1)}, bf16[1,1152,2,384]{3,1,2,0:T(8,128)(2,1)}, u32[]{:S(2)}) copy-start(bf16[1,1152,2,384]{3,1,2,0:T(8,128)(2,1)} %copy.9) | copy-start | bytes 5308420
  40.1 10.1 %copy-start.25 = (bf16[1,1152,384]{2,1,0:T(8,128)(2,1)S(1)}, bf16[1,1152,384]{2,1,0:T(8,128)(2,1)}, u32[]{:S(2)}) copy-start(bf16[1,1152,384]{2,1,0:T(8,128)(2,1)} %param.8) | copy-start | bytes 2654212
  40.1 0.7 copy-start.6
  40.8 18.1 %collective-permute-start.7 = (bf16[2,1152,128]{2,1,0:T(8,128)(2,1)}, bf16[2,1152,128]{2,1,0:T(8,128)(2,1)S(1)}, u32[]{:S(2)}, u32[]{:S(2)}) collective-permute-start(bf16[2,1152,128]{2,1,0:T(8,128)(2,1)} %get-tuple-element.27), channel_id=1, source_target_pairs={{0,1},{1,2},{2,3},{4,5},{5,6},{6,7},{8,9},{9,10},{10,11},{12,13},{... | collective-permute-start | bytes 1769480 | tf_op jit(solution)/shard_map/ppermute | solution.py:213
  44.0 0.7 copy-start.8
  44.8 15.5 %collective-permute-start.24 = (bf16[1152,128]{1,0:T(8,128)(2,1)S(1)}, bf16[1152,128]{1,0:T(8,128)(2,1)}, u32[]{:S(2)}, u32[]{:S(2)}) collective-permute-start(bf16[1152,128]{1,0:T(8,128)(2,1)S(1)} %attention.3.refs_4_), channel_id=1, source_target_pairs={{0,24},{4,28},{8,16},{12,20},{16,8},{20,12},{24,0},{28,4},{1,25},{... | collective-permute-start | bytes 884744 | tf_op jit(solution)/shard_map/ppermute | solution.py:205
  46.9 14.3 %collective-permute-start.18 = (bf16[1152,128]{1,0:T(8,128)(2,1)S(1)}, bf16[1152,128]{1,0:T(8,128)(2,1)}, u32[]{:S(2)}, u32[]{:S(2)}) collective-permute-start(bf16[1152,128]{1,0:T(8,128)(2,1)S(1)} %attention.3.refs_4_), channel_id=1, source_target_pairs={{0,16},{16,0},{1,17},{17,1},{2,18},{18,2},{3,19},{19,3},{4,20},{20... | collective-permute-start | bytes 884744 | tf_op jit(solution)/shard_map/ppermute | solution.py:201
  47.2 15.2 %collective-permute-start.12 = (bf16[1152,128]{1,0:T(8,128)(2,1)S(1)}, bf16[1152,128]{1,0:T(8,128)(2,1)}, u32[]{:S(2)}, u32[]{:S(2)}) collective-permute-start(bf16[1152,128]{1,0:T(8,128)(2,1)S(1)} %attention.3.refs_4_), channel_id=1, source_target_pairs={{0,8},{4,12},{8,0},{12,4},{1,9},{5,13},{9,1},{13,5},{2,10},{6,14},... | collective-permute-start | bytes 884744 | tf_op jit(solution)/shard_map/ppermute | solution.py:203
  47.4 15.5 %collective-permute-start.9 = (bf16[1152,128]{1,0:T(8,128)(2,1)S(1)}, bf16[1152,128]{1,0:T(8,128)(2,1)S(1)}, u32[]{:S(2)}, u32[]{:S(2)}) collective-permute-start(bf16[1152,128]{1,0:T(8,128)(2,1)S(1)} %attention.3.refs_4_), channel_id=1, source_target_pairs={{0,4},{4,0},{8,12},{12,8},{1,5},{5,1},{9,13},{13,9},{2,6},{6,2},{1... | collective-permute-start | bytes 884744 | tf_op jit(solution)/shard_map/ppermute | solution.py:203
  48.4 0.7 copy-start.10
  58.9 13.7 %copy-start.14 = (bf16[1152,128]{1,0:T(8,128)(2,1)}, bf16[1152,128]{1,0:T(8,128)(2,1)S(1)}, u32[]{:S(2)}) copy-start(bf16[1152,128]{1,0:T(8,128)(2,1)S(1)} %attention.4.refs_5_) | copy-start | bytes 884740
  58.9 50.7 %copy-start.31 = (s32[18]{0:T(128)S(1)}, s32[18]{0:T(128)}, u32[]{:S(2)}) copy-start(s32[18]{0:T(128)} %param.15) | copy-start | bytes 220
  58.9 49.1 %collective-permute-start.30 = (bf16[1152,384]{1,0:T(8,128)(2,1)}, bf16[1152,384]{1,0:T(8,128)(2,1)S(1)}, u32[]{:S(2)}, u32[]{:S(2)}) collective-permute-start(bf16[1152,384]{1,0:T(8,128)(2,1)} %get-tuple-element.29), channel_id=1, source_target_pairs={{0,16},{16,0},{1,17},{17,1},{2,18},{18,2},{3,19},{19,3},{4,20},{20... | collective-permute-start | bytes 2654216 | tf_op jit(solution)/shard_map/ppermute | solution.py:201
  60.2 27.4 %collective-permute-start.25 = (bf16[1152,128]{1,0:T(8,128)(2,1)S(1)}, bf16[1152,128]{1,0:T(8,128)(2,1)}, u32[]{:S(2)}, u32[]{:S(2)}) collective-permute-start(bf16[1152,128]{1,0:T(8,128)(2,1)S(1)} %attention.4.refs_5_), channel_id=1, source_target_pairs={{0,24},{4,28},{8,16},{12,20},{16,8},{20,12},{24,0},{28,4},{1,25},{... | collective-permute-start | bytes 884744 | tf_op jit(solution)/shard_map/ppermute | solution.py:205
  61.2 31.9 %collective-permute-start.19 = (bf16[1152,128]{1,0:T(8,128)(2,1)S(1)}, bf16[1152,128]{1,0:T(8,128)(2,1)S(1)}, u32[]{:S(2)}, u32[]{:S(2)}) collective-permute-start(bf16[1152,128]{1,0:T(8,128)(2,1)S(1)} %attention.4.refs_5_), channel_id=1, source_target_pairs={{0,16},{16,0},{1,17},{17,1},{2,18},{18,2},{3,19},{19,3},{4,20},{20... | collective-permute-start | bytes 884744 | tf_op jit(solution)/shard_map/ppermute | solution.py:201
  62.4 31.9 %collective-permute-start.13 = (bf16[1152,128]{1,0:T(8,128)(2,1)S(1)}, bf16[1152,128]{1,0:T(8,128)(2,1)S(1)}, u32[]{:S(2)}, u32[]{:S(2)}) collective-permute-start(bf16[1152,128]{1,0:T(8,128)(2,1)S(1)} %attention.4.refs_5_), channel_id=1, source_target_pairs={{0,8},{4,12},{8,0},{12,4},{1,9},{5,13},{9,1},{13,5},{2,10},{6,14},... | collective-permute-start | bytes 884744 | tf_op jit(solution)/shard_map/ppermute | solution.py:203
  62.9 9.7 %copy-start.12 = (bf16[1152,128]{1,0:T(8,128)(2,1)}, bf16[1152,128]{1,0:T(8,128)(2,1)S(1)}, u32[]{:S(2)}) copy-start(bf16[1152,128]{1,0:T(8,128)(2,1)S(1)} %collective-permute-done.9.refs_7_) | copy-start | bytes 884740
  62.9 32.5 %collective-permute-start.10 = (bf16[1152,128]{1,0:T(8,128)(2,1)S(1)}, bf16[1152,128]{1,0:T(8,128)(2,1)S(1)}, u32[]{:S(2)}, u32[]{:S(2)}) collective-permute-start(bf16[1152,128]{1,0:T(8,128)(2,1)S(1)} %attention.4.refs_5_), channel_id=1, source_target_pairs={{0,4},{4,0},{8,12},{12,8},{1,5},{5,1},{9,13},{13,9},{2,6},{6,2},{1... | collective-permute-start | bytes 884744 | tf_op jit(solution)/shard_map/ppermute | solution.py:203
  87.7 12.6 %collective-permute-start.26 = (bf16[1152,128]{1,0:T(8,128)(2,1)S(1)}, bf16[1152,128]{1,0:T(8,128)(2,1)S(1)}, u32[]{:S(2)}, u32[]{:S(2)}) collective-permute-start(bf16[1152,128]{1,0:T(8,128)(2,1)S(1)} %attention.5.refs_6_), channel_id=1, source_target_pairs={{0,24},{4,28},{8,16},{12,20},{16,8},{20,12},{24,0},{28,4},{1,25},{... | collective-permute-start | bytes 884744 | tf_op jit(solution)/shard_map/ppermute | solution.py:205
  93.1 2.2 %copy-start.16 = (bf16[1152,128]{1,0:T(8,128)(2,1)}, bf16[1152,128]{1,0:T(8,128)(2,1)S(1)}, u32[]{:S(2)}) copy-start(bf16[1152,128]{1,0:T(8,128)(2,1)S(1)} %collective-permute-done.19.refs_17_) | copy-start | bytes 884740
  93.1 12.7 %collective-permute-start.20 = (bf16[1152,128]{1,0:T(8,128)(2,1)S(1)}, bf16[1152,128]{1,0:T(8,128)(2,1)S(1)}, u32[]{:S(2)}, u32[]{:S(2)}) collective-permute-start(bf16[1152,128]{1,0:T(8,128)(2,1)S(1)} %attention.5.refs_6_), channel_id=1, source_target_pairs={{0,16},{16,0},{1,17},{17,1},{2,18},{18,2},{3,19},{19,3},{4,20},{20... | collective-permute-start | bytes 884744 | tf_op jit(solution)/shard_map/ppermute | solution.py:201
  94.3 3.6 %copy-start.18 = (bf16[1152,128]{1,0:T(8,128)(2,1)}, bf16[1152,128]{1,0:T(8,128)(2,1)S(1)}, u32[]{:S(2)}) copy-start(bf16[1152,128]{1,0:T(8,128)(2,1)S(1)} %collective-permute-done.13.refs_11_) | copy-start | bytes 884740
  94.3 12.5 %collective-permute-start.14 = (bf16[1152,128]{1,0:T(8,128)(2,1)S(1)}, bf16[1152,128]{1,0:T(8,128)(2,1)S(1)}, u32[]{:S(2)}, u32[]{:S(2)}) collective-permute-start(bf16[1152,128]{1,0:T(8,128)(2,1)S(1)} %attention.5.refs_6_), channel_id=1, source_target_pairs={{0,8},{4,12},{8,0},{12,4},{1,9},{5,13},{9,1},{13,5},{2,10},{6,14},... | collective-permute-start | bytes 884744 | tf_op jit(solution)/shard_map/ppermute | solution.py:203
  95.4 0.7 copy-start.20
  96.1 11.2 %collective-permute-start.11 = (bf16[1152,128]{1,0:T(8,128)(2,1)S(1)}, bf16[1152,128]{1,0:T(8,128)(2,1)S(1)}, u32[]{:S(2)}, u32[]{:S(2)}) collective-permute-start(bf16[1152,128]{1,0:T(8,128)(2,1)S(1)} %attention.5.refs_6_), channel_id=1, source_target_pairs={{0,4},{4,0},{8,12},{12,8},{1,5},{5,1},{9,13},{13,9},{2,6},{6,2},{1... | collective-permute-start | bytes 884744 | tf_op jit(solution)/shard_map/ppermute | solution.py:203
  97.8 0.7 copy-start.22
  100.2 8.4 %collective-permute-start.27 = (bf16[1152,128]{1,0:T(8,128)(2,1)}, bf16[1152,128]{1,0:T(8,128)(2,1)S(1)}, u32[]{:S(2)}, u32[]{:S(2)}) collective-permute-start(bf16[1152,128]{1,0:T(8,128)(2,1)} %collective-permute-done.24.refs_22_), channel_id=1, source_target_pairs={{0,4},{4,0},{8,12},{12,8},{1,5},{5,1},{9,13},{13,9},{2,6},{6,2},{1... | collective-permute-start | bytes 884744 | tf_op jit(solution)/shard_map/ppermute | solution.py:203
  105.8 2.9 %collective-permute-start.21 = (bf16[1152,128]{1,0:T(8,128)(2,1)}, bf16[1152,128]{1,0:T(8,128)(2,1)S(1)}, u32[]{:S(2)}, u32[]{:S(2)}) collective-permute-start(bf16[1152,128]{1,0:T(8,128)(2,1)} %collective-permute-done.18.refs_16_), channel_id=1, source_target_pairs={{0,4},{4,0},{8,12},{12,8},{1,5},{5,1},{9,13},{13,9},{2,6},{6,2},{1... | collective-permute-start | bytes 884744 | tf_op jit(solution)/shard_map/ppermute | solution.py:203
  106.8 2.3 %collective-permute-start.15 = (bf16[1152,128]{1,0:T(8,128)(2,1)}, bf16[1152,128]{1,0:T(8,128)(2,1)}, u32[]{:S(2)}, u32[]{:S(2)}) collective-permute-start(bf16[1152,128]{1,0:T(8,128)(2,1)} %collective-permute-done.12.refs_10_), channel_id=1, source_target_pairs={{0,4},{4,0},{8,12},{12,8},{1,5},{5,1},{9,13},{13,9},{2,6},{6,2},{1... | collective-permute-start | bytes 884744 | tf_op jit(solution)/shard_map/ppermute | solution.py:203
  107.3 2.0 %collective-permute-start.28 = (bf16[1152,128]{1,0:T(8,128)(2,1)}, bf16[1152,128]{1,0:T(8,128)(2,1)}, u32[]{:S(2)}, u32[]{:S(2)}) collective-permute-start(bf16[1152,128]{1,0:T(8,128)(2,1)} %collective-permute-done.25.refs_23_), channel_id=1, source_target_pairs={{0,4},{4,0},{8,12},{12,8},{1,5},{5,1},{9,13},{13,9},{2,6},{6,2},{1... | collective-permute-start | bytes 884744 | tf_op jit(solution)/shard_map/ppermute | solution.py:203
  108.1 1.9 %collective-permute-start.22 = (bf16[1152,128]{1,0:T(8,128)(2,1)}, bf16[1152,128]{1,0:T(8,128)(2,1)S(1)}, u32[]{:S(2)}, u32[]{:S(2)}) collective-permute-start(bf16[1152,128]{1,0:T(8,128)(2,1)} %copy-done.16), channel_id=1, source_target_pairs={{0,4},{4,0},{8,12},{12,8},{1,5},{5,1},{9,13},{13,9},{2,6},{6,2},{1... | collective-permute-start | bytes 884744 | tf_op jit(solution)/shard_map/ppermute | solution.py:203
  108.6 1.8 %collective-permute-start.16 = (bf16[1152,128]{1,0:T(8,128)(2,1)}, bf16[1152,128]{1,0:T(8,128)(2,1)S(1)}, u32[]{:S(2)}, u32[]{:S(2)}) collective-permute-start(bf16[1152,128]{1,0:T(8,128)(2,1)} %copy-done.18), channel_id=1, source_target_pairs={{0,4},{4,0},{8,12},{12,8},{1,5},{5,1},{9,13},{13,9},{2,6},{6,2},{1... | collective-permute-start | bytes 884744 | tf_op jit(solution)/shard_map/ppermute | solution.py:203
  108.7 2.0 %collective-permute-start.29 = (bf16[1152,128]{1,0:T(8,128)(2,1)S(1)}, bf16[1152,128]{1,0:T(8,128)(2,1)S(1)}, u32[]{:S(2)}, u32[]{:S(2)}) collective-permute-start(bf16[1152,128]{1,0:T(8,128)(2,1)S(1)} %collective-permute-done.26.refs_24_), channel_id=1, source_target_pairs={{0,4},{4,0},{8,12},{12,8},{1,5},{5,1},{9,13},{13,9},{2,6},{6,2},{1... | collective-permute-start | bytes 884744 | tf_op jit(solution)/shard_map/ppermute | solution.py:203
  109.1 2.0 %collective-permute-start.23 = (bf16[1152,128]{1,0:T(8,128)(2,1)S(1)}, bf16[1152,128]{1,0:T(8,128)(2,1)S(1)}, u32[]{:S(2)}, u32[]{:S(2)}) collective-permute-start(bf16[1152,128]{1,0:T(8,128)(2,1)S(1)} %collective-permute-done.20.refs_18_), channel_id=1, source_target_pairs={{0,4},{4,0},{8,12},{12,8},{1,5},{5,1},{9,13},{13,9},{2,6},{6,2},{1... | collective-permute-start | bytes 884744 | tf_op jit(solution)/shard_map/ppermute | solution.py:203
  109.3 2.2 %collective-permute-start.17 = (bf16[1152,128]{1,0:T(8,128)(2,1)S(1)}, bf16[1152,128]{1,0:T(8,128)(2,1)S(1)}, u32[]{:S(2)}, u32[]{:S(2)}) collective-permute-start(bf16[1152,128]{1,0:T(8,128)(2,1)S(1)} %collective-permute-done.14.refs_12_), channel_id=1, source_target_pairs={{0,4},{4,0},{8,12},{12,8},{1,5},{5,1},{9,13},{13,9},{2,6},{6,2},{1... | collective-permute-start | bytes 884744 | tf_op jit(solution)/shard_map/ppermute | solution.py:203
  111.5 1.0 copy-start.3
  112.4 1.0 copy-start.5
  113.4 1.0 copy-start.7
  114.4 1.0 copy-start.9
  115.3 1.0 copy-start.11
  116.3 1.0 copy-start.13
  117.3 1.0 copy-start.15
  118.2 1.0 copy-start.17
  119.2 1.0 copy-start.19
  120.1 1.0 copy-start.21
  121.1 1.0 copy-start.23

commit v3 on v2

v3 whole, which is shorter than its diff:
```python
import functools
import math

import jax
import jax.numpy as jnp
from jax import lax
from jax.experimental import pallas as pl
from jax.experimental.pallas import tpu as pltpu
from jax.sharding import PartitionSpec as P

HD = 128
FRAME = 64
FAR = 1e30
EXP2_SCALE = math.log2(math.e) / math.sqrt(HD)
VMEM_LIMIT = 24 * 1024 * 1024


def attention_kernel(info_ref, q_ref, k_ref, v_ref, low_ref, high_ref, out_ref):
    tiles_time = info_ref.shape[0] - 2
    tile = q_ref.shape[0] // tiles_time
    width_oks = (None, info_ref[tiles_time] == 1, info_ref[tiles_time + 1] == 1)

    def window(t):
        first = t - info_ref[t]
        base = jnp.clip(first, 0, tiles_time - 2)
        inside = [(base + step >= first) & (base + step <= first + 1) for step in range(2)]
        return pl.ds(pl.multiple_of(base * tile, tile), 2 * tile), inside

    def score(t):
        rows, inside = window(t)
        query = q_ref[t * tile : (t + 1) * tile, :]
        blocks = []
        row_max = None
        for keys, width_ok in zip(
            (k_ref[rows, :], low_ref[0, rows, :], high_ref[0, rows, :]), width_oks
        ):
            scores = lax.dot_general(
                query, keys, (((1,), (1,)), ((), ())), preferred_element_type=jnp.float32
            )
            for step in range(2):
                allowed = inside[step] if width_ok is None else inside[step] & width_ok
                block = scores[:, step * tile : (step + 1) * tile]
                lanes = block[:, :HD]
                for first in range(HD, tile, HD):
                    lanes = jnp.maximum(lanes, block[:, first : first + HD])
                lanes = jnp.where(allowed, lanes, -FAR)
                row_max = lanes if row_max is None else jnp.maximum(row_max, lanes)
                blocks.append((block, allowed))
        return blocks, jnp.max(row_max, axis=1, keepdims=True) * EXP2_SCALE

    def blend(t, blocks, shift):
        rows, _ = window(t)
        weights = [
            jnp.exp2(block * EXP2_SCALE - jnp.where(allowed, shift, FAR)).astype(jnp.bfloat16)
            for block, allowed in blocks
        ]
        values = jnp.concatenate([v_ref[rows, :], low_ref[1, rows, :], high_ref[1, rows, :]], axis=0)
        total = jnp.dot(
            jnp.concatenate(weights, axis=1),
            jnp.concatenate([values, jnp.ones_like(values)], axis=1),
            preferred_element_type=jnp.float32,
        )
        out_ref[t * tile : (t + 1) * tile, :] = (total[:, :HD] / total[:, HD:]).astype(jnp.bfloat16)

    ready = score(0)
    for t in range(tiles_time):
        later = score(t + 1) if t + 1 < tiles_time else None
        blend(t, *ready)
        ready = later


def attention(info, queries, keys, values, low, high, head, tile):
    count = queries.shape[0]
    side = pl.BlockSpec((2, count, HD), lambda i, info: (0, 0, 0))
    whole = pl.BlockSpec((count, HD), lambda i, info: (0, head))
    pairs = count * 6 * tile
    return pl.pallas_call(
        attention_kernel,
        out_shape=jax.ShapeDtypeStruct((count, HD), jnp.bfloat16),
        grid_spec=pltpu.PrefetchScalarGridSpec(
            num_scalar_prefetch=1,
            grid=(1,),
            in_specs=[whole, whole, whole, side, side],
            out_specs=pl.BlockSpec((count, HD), lambda i, info: (0, 0)),
        ),
        compiler_params=pltpu.CompilerParams(vmem_limit_bytes=VMEM_LIMIT),
        cost_estimate=pl.CostEstimate(
            flops=4 * pairs * HD, bytes_accessed=8 * count * HD * 2, transcendentals=pairs
        ),
        name="attention",
    )(info, queries, keys, values, low, high)


def partial_kernel(first, own_cols, info_ref, *refs):
    near_ref, far_ref, *pieces, gate_ref, base_own_ref, base_other_ref, own_ref, other_ref = refs
    tile = own_ref.shape[0]
    frames = tile // FRAME
    time_tile = pl.program_id(0)
    cond_first = info_ref[0] == 0
    weights = jnp.concatenate([near_ref[...], far_ref[...]], axis=0)
    half = len(pieces) // 2
    parts = []
    for which in range(2):
        rows = jnp.concatenate(
            [piece[...] for piece in pieces[which * half : (which + 1) * half]], axis=1
        )
        projected = jnp.dot(rows, weights, preferred_element_type=jnp.float32)
        parts.append(gate_ref[which] * projected)
    for frame in range(frames):
        rows = slice(frame * FRAME, (frame + 1) * FRAME)
        guide = 1.0 + 0.5 * info_ref[1 + time_tile * frames + frame].astype(jnp.float32)
        scales = (jnp.where(cond_first, guide, 1.0 - guide), jnp.where(cond_first, 1.0 - guide, guide))
        total = scales[0] * parts[0][rows] + scales[1] * parts[1][rows]
        own, other = total[:, :own_cols], total[:, own_cols:]
        if first:
            own += scales[0] * base_own_ref[rows, :].astype(jnp.float32)
            own += scales[1] * base_other_ref[rows, :].astype(jnp.float32)
        else:
            own += base_own_ref[rows, :]
            other += base_other_ref[rows, :]
        own_ref[rows, :] = own
        other_ref[rows, :] = other.astype(other_ref.dtype)


def partial_projection(info, weights, pieces, gate, base, tile, group):
    count, width = base[0].shape
    first = group.start == 0
    depth = len(group) * HD
    weight = pl.BlockSpec((depth, 2 * width), lambda t, info: (group.start // len(group), 0))
    rows = pl.BlockSpec((tile, width), lambda t, info: (t, 0))
    piece = pl.BlockSpec((tile, HD), lambda t, info: (t, 0))
    return pl.pallas_call(
        functools.partial(partial_kernel, first, width),
        out_shape=[
            jax.ShapeDtypeStruct((count, width), jnp.float32),
            jax.ShapeDtypeStruct((count, width), jnp.float32 if first else jnp.bfloat16),
        ],
        grid_spec=pltpu.PrefetchScalarGridSpec(
            num_scalar_prefetch=1,
            grid=(count // tile,),
            in_specs=[weight] * 2
            + [piece] * len(pieces)
            + [pl.BlockSpec(gate.shape, lambda t, info: (0, 0, 0)), rows, rows],
            out_specs=[rows, rows],
        ),
        compiler_params=pltpu.CompilerParams(vmem_limit_bytes=VMEM_LIMIT),
        cost_estimate=pl.CostEstimate(
            flops=4 * count * width * len(pieces) * HD,
            bytes_accessed=2 * count * (6 * width + len(pieces) * HD),
            transcendentals=0,
        ),
        name="partial_projection",
    )(info, *weights, *pieces, gate, *base)


def pack_kernel(k_ref, v_ref, *out_refs):
    for head, out_ref in enumerate(out_refs):
        cols = slice(head * HD, (head + 1) * HD)
        out_ref[0] = k_ref[:, cols]
        out_ref[1] = v_ref[:, cols]


def pack_heads(keys, values, first, heads, tile):
    count = keys.shape[0]
    rows = pl.BlockSpec((tile, heads * HD), lambda t: (t, first // heads))
    return pl.pallas_call(
        pack_kernel,
        out_shape=[jax.ShapeDtypeStruct((2, count, HD), jnp.bfloat16)] * heads,
        grid=(count // tile,),
        in_specs=[rows, rows],
        out_specs=[pl.BlockSpec((2, tile, HD), lambda t: (0, t, 0))] * heads,
        cost_estimate=pl.CostEstimate(
            flops=0, bytes_accessed=8 * count * heads * HD, transcendentals=0
        ),
        name="pack_heads",
    )(keys, values)


def split_kernel(info_ref, w_ref, near_ref, far_ref):
    cols = near_ref.shape[1]
    for index, out_ref in enumerate((near_ref, far_ref)):
        for side in range(2):

            @pl.when(pl.program_id(0) == 2 * index + side)
            def _():
                out_ref[:, side * (cols // 2) : (side + 1) * (cols // 2)] = w_ref[...]


def split_weight(info, weight, width):
    rows = weight.shape[0]
    whole = pl.BlockSpec((rows, 2 * width), lambda i, info: (0, 0))
    return pl.pallas_call(
        split_kernel,
        out_shape=[jax.ShapeDtypeStruct((rows, 2 * width), jnp.bfloat16)] * 2,
        grid_spec=pltpu.PrefetchScalarGridSpec(
            num_scalar_prefetch=1,
            grid=(4,),
            in_specs=[pl.BlockSpec((rows, width), lambda i, info: (0, info[i]))],
            out_specs=[whole, whole],
        ),
        cost_estimate=pl.CostEstimate(
            flops=0, bytes_accessed=16 * rows * width, transcendentals=0
        ),
        name="split_weight",
    )(info, weight)


def local(queries, keys, values, residual, gate, out_weight, time_offsets, guidance_index):
    tiles_time, tiles_wide = time_offsets.shape
    count, features = queries.shape[1:]
    tile = count // tiles_time
    heads = features // HD
    head_count = lax.axis_size("head")
    columns = lax.axis_size("tokens")
    branch_pos = lax.axis_index("branch")
    head_pos = lax.axis_index("head")
    width_pos = lax.axis_index("tokens")
    width = gate.shape[2] // head_count

    up = [(i, i + 1) for i in range(columns - 1)]
    down = [(i + 1, i) for i in range(columns - 1)]

    def swap(value, branch_bit, head_bits):
        if not branch_bit and not head_bits:
            return value
        if not head_bits:
            return lax.ppermute(value, "branch", [(0, 1), (1, 0)])
        if not branch_bit:
            return lax.ppermute(value, "head", [(i, i ^ head_bits) for i in range(head_count)])
        flip = head_count + head_bits
        return lax.ppermute(
            value, ("branch", "head"), [(i, i ^ flip) for i in range(2 * head_count)]
        )

    packed = pack_heads(keys[0], values[0], 0, 1, tile)
    (packed, late_keys, late_values, residual, out_weight) = lax.optimization_barrier(
        (packed, keys[0], values[0], residual, out_weight)
    )
    for head in range(1, heads):
        packed += pack_heads(late_keys, late_values, head, 1, tile)
    low = [lax.ppermute(key_value, "tokens", up) for key_value in packed]
    high = [lax.ppermute(key_value, "tokens", down) for key_value in packed]

    first_half, second_half = residual[0, :, 0], residual[0, :, 1]
    mine = jnp.where(branch_pos == 0, first_half, second_half)
    other = swap(jnp.where(branch_pos == 0, second_half, first_half), 1, 0)
    gate_block = jnp.concatenate(
        [
            lax.dynamic_slice(gate, (0, branch_pos, place * width), (2, 1, width))
            for place in (head_pos, head_pos ^ 1)
        ],
        axis=2,
    ).astype(jnp.float32)
    gate_block = jnp.where(branch_pos == 0, gate_block, gate_block[::-1])

    distances = jnp.arange(4, dtype=jnp.int32)
    near, far = split_weight(
        branch_pos * head_count + (head_pos ^ distances), out_weight, width
    )
    far = swap(far, 0, 2)

    offsets = lax.dynamic_index_in_dim(time_offsets, width_pos, 1, keepdims=False)
    edges = jnp.stack([width_pos > 0, width_pos < tiles_wide - 1]).astype(jnp.int32)
    attention_info = jnp.concatenate([offsets, edges])
    projection_info = jnp.concatenate([branch_pos[None].astype(jnp.int32), guidance_index])

    pieces = {}
    head_queries = queries[0]
    for head in range(heads):
        if head == 1:
            head_queries, other = lax.optimization_barrier((head_queries, other))
        own = attention(
            attention_info, head_queries, keys[0], values[0], low[head], high[head], head, tile
        )
        for branch_bit in range(2):
            for bits in (0, 2):
                pieces[branch_bit, bits, head] = swap(own, branch_bit, bits)

    base = (mine, other)
    for group in (range(heads - 1), range(heads - 1, heads)):
        ordered = [pieces[bit, bits, head] for bit in range(2) for bits in (0, 2) for head in group]
        base = partial_projection(
            projection_info, (near, far), ordered, gate_block, base, tile, group
        )
    return (base[0] + swap(base[1], 0, 1).astype(jnp.float32)).astype(jnp.bfloat16)


def solution(mesh):
    return jax.shard_map(
        local,
        mesh=mesh,
        in_specs=(
            P("branch", "tokens", "head"),
            P("branch", "tokens", "head"),
            P("branch", "tokens", "head"),
            P("branch", "tokens", None, "head"),
            P(),
            P("head", None),
            P(),
            P(),
        ),
        out_specs=P("tokens", ("branch", "head")),
        check_vma=False,
    )
```

time: 131 us -> 94.8 us (0.72); the launches traced: 129 us -> 94.1 us
  local copies, waits for them, and re-layouts: 22 us -> 0.54 us
  waiting for transfers between devices: 27.3 us -> 19.3 us
  Pallas kernels: 38.9 us -> 35.3 us
  starting transfers between devices: 38 us -> 35.7 us
    unnamed x64 -> x16, local copies, waits for them, and re-layouts: 18.7 us -> 0.04 us
    ppermute x18 -> x5, waiting for transfers between devices: 2.02 us -> 19.3 us  [swap(): lax.ppermute(value, 'head', [(i, i ^ head_bits) for i in range(head_count)])]
    ppermute x3, waiting for transfers between devices: 16.7 us -> 0.01 us  [swap(): lax.ppermute(value, ('branch', 'head'), [(i, i ^ flip) for i in range(2 *...]
    ppermute x4, waiting for transfers between devices: 8.58 us -> 0.01 us  [swap(): return lax.ppermute(value, 'branch', [(0, 1), (1, 0)])]
    pallas_call x3, Pallas kernels: 24.6 us -> 16.6 us  [attention(): pl.pallas_call(attention_kernel, out_shape=jax.ShapeDtypeStruct((count, H...]
    pallas_call x1 -> x3, Pallas kernels: 3.57 us -> 8.51 us  [pack_heads(): pl.pallas_call(pack_kernel, out_shape=[jax.ShapeDtypeStruct((2, count, HD...]
    ppermute x18 -> x5, starting transfers between devices: 13.1 us -> 10.1 us  [swap(): lax.ppermute(value, 'head', [(i, i ^ head_bits) for i in range(head_count)])]
    optimization_barrier x1, local copies, waits for them, and re-layouts: 3.1 us -> 0.23 us  [local(): lax.optimization_barrier((packed, keys[0], values[0], residual, out_weight))]
  transfers between devices with their start and end apart: 31 -> 18, of which waited for: 10 -> 4; matrix products, arithmetic and copies ran while one was open for 5% -> 2% of each run, Pallas kernels for 22% -> 32%
where the time goes in v3:
time: 94.8 us; the launch traced here: 94.1 us
  starting transfers between devices  35.7 us (38%)
  Pallas kernels  35.3 us (37%)
  waiting for transfers between devices  19.3 us (20%)
  other arithmetic  2.96 us (3%)
    ppermute x5, waiting for transfers between devices, swap(): lax.ppermute(value, 'head', [(i, i ^ head_bits) for i in range(head_count)])  19.3 us
    pallas_call x3, Pallas kernels, attention(): pl.pallas_call(attention_kernel, out_shape=jax.ShapeDtypeStruct((count, H...  16.6 us
    ppermute x5, starting transfers between devices, swap(): lax.ppermute(value, 'head', [(i, i ^ head_bits) for i in range(head_count)])  10.1 us
    ppermute x3, starting transfers between devices, local(): low = [lax.ppermute(key_value, 'tokens', up) for key_value in packed]  9.89 us
    pallas_call x3, Pallas kernels, pack_heads(): pl.pallas_call(pack_kernel, out_shape=[jax.ShapeDtypeStruct((2, count, HD...  8.51 us
    ppermute x3, starting transfers between devices, local(): high = [lax.ppermute(key_value, 'tokens', down) for key_value in packed]  7.7 us
    pallas_call x2, Pallas kernels, partial_projection(): pl.pallas_call(functools.partial(partial_kernel, first, width), out_shape...  6.43 us
    ppermute x3, starting transfers between devices, swap(): lax.ppermute(value, ('branch', 'head'), [(i, i ^ flip) for i in range(2 *...  4.19 us
  transfers between devices with their start and end apart: 18, of which 4 were waited for; matrix products, arithmetic and copies ran while one was open for 2% of the time, Pallas kernels for 32%

profile of v3, /device:TPU:9, one launch (start us, length us, event | category | flops | bytes accessed | tf_op | source)
XLA Modules:
  0.0 94.1 jit_solution(10802222170951098678)
XLA Ops:
  0.0 0.0 copy-start
  0.0 2.9 %pack_heads.3 = bf16[2,1152,128]{2,1,0:T(8,128)(2,1)} custom-call(bf16[1152,384]{1,0:T(8,128)(2,1)} %bitcast.10, bf16[1152,384]{1,0:T(8,128)(2,1)} %bitcast.16), custom_call_target="tpu_custom_call" | custom-call | bytes 1179648 | tf_op jit(solution)/shard_map/pack_heads/pallas_call | solution.py:166
  2.9 3.2 %collective-permute-start.7 = (bf16[2,1152,128]{2,1,0:T(8,128)(2,1)}, bf16[2,1152,128]{2,1,0:T(8,128)(2,1)}, u32[]{:S(2)}, u32[]{:S(2)}) collective-permute-start(bf16[2,1152,128]{2,1,0:T(8,128)(2,1)} %pack_heads.3), channel_id=1, source_target_pairs={{0,1},{1,2},{2,3},{4,5},{5,6},{6,7},{8,9},{9,10},{10,11},{12,13},{... | collective-permute-start | bytes 1769480 | tf_op jit(solution)/shard_map/ppermute | solution.py:241
  6.1 2.9 %collective-permute-start.8 = (bf16[2,1152,128]{2,1,0:T(8,128)(2,1)}, bf16[2,1152,128]{2,1,0:T(8,128)(2,1)}, u32[]{:S(2)}, u32[]{:S(2)}) collective-permute-start(bf16[2,1152,128]{2,1,0:T(8,128)(2,1)} %pack_heads.3), channel_id=1, source_target_pairs={{1,0},{2,1},{3,2},{5,4},{6,5},{7,6},{9,8},{10,9},{11,10},{13,12},{... | collective-permute-start | bytes 1769480 | tf_op jit(solution)/shard_map/ppermute | solution.py:242
  9.0 0.0 copy-done.5
  9.0 0.2 copy.9
  9.3 1.1 %select_bitcast_fusion = (bf16[1152,384]{1,0:T(8,128)(2,1)S(1)}, bf16[1152,384]{1,0:T(8,128)(2,1)}) fusion(pred[]{:T(512)S(6)} %eq.2, bf16[1,1152,2,384]{3,1,2,0:T(8,128)(2,1)S(1)} %copy.9), kind=kLoop, calls=%fused_computation.1 | loop fusion | flops 884736 | bytes 3538945 | tf_op jit(solution)/shard_map/jit(_where)/select_n | solution.py:245
  10.4 1.2 %collective-permute-start.1 = (bf16[1152,384]{1,0:T(8,128)(2,1)}, bf16[1152,384]{1,0:T(8,128)(2,1)}, u32[]{:S(2)}, u32[]{:S(2)}) collective-permute-start(bf16[1152,384]{1,0:T(8,128)(2,1)} %get-tuple-element.32), channel_id=1, source_target_pairs={{0,16},{16,0},{1,17},{17,1},{2,18},{18,2},{3,19},{19,3},{4,20},{20... | collective-permute-start | bytes 2654216 | tf_op jit(solution)/shard_map/ppermute | solution.py:227
  11.6 2.8 %pack_heads.5 = bf16[2,1152,128]{2,1,0:T(8,128)(2,1)} custom-call(bf16[1152,384]{1,0:T(8,128)(2,1)} %bitcast.11, bf16[1152,384]{1,0:T(8,128)(2,1)} %bitcast.17), custom_call_target="tpu_custom_call" | custom-call | bytes 1179648 | tf_op jit(solution)/shard_map/pack_heads/pallas_call | solution.py:166
  14.3 1.9 %collective-permute-start.10 = (bf16[2,1152,128]{2,1,0:T(8,128)(2,1)}, bf16[2,1152,128]{2,1,0:T(8,128)(2,1)}, u32[]{:S(2)}, u32[]{:S(2)}) collective-permute-start(bf16[2,1152,128]{2,1,0:T(8,128)(2,1)} %pack_heads.5), channel_id=1, source_target_pairs={{1,0},{2,1},{3,2},{5,4},{6,5},{7,6},{9,8},{10,9},{11,10},{13,12},{... | collective-permute-start | bytes 1769480 | tf_op jit(solution)/shard_map/ppermute | solution.py:242
  16.2 3.4 %collective-permute-start.9 = (bf16[2,1152,128]{2,1,0:T(8,128)(2,1)}, bf16[2,1152,128]{2,1,0:T(8,128)(2,1)}, u32[]{:S(2)}, u32[]{:S(2)}) collective-permute-start(bf16[2,1152,128]{2,1,0:T(8,128)(2,1)} %pack_heads.5), channel_id=1, source_target_pairs={{0,1},{1,2},{2,3},{4,5},{5,6},{6,7},{8,9},{9,10},{10,11},{12,13},{... | collective-permute-start | bytes 1769480 | tf_op jit(solution)/shard_map/ppermute | solution.py:241
  19.6 0.0 copy-start.4
  19.6 2.9 %pack_heads.4 = bf16[2,1152,128]{2,1,0:T(8,128)(2,1)} custom-call(bf16[1152,384]{1,0:T(8,128)(2,1)} %bitcast.12, bf16[1152,384]{1,0:T(8,128)(2,1)} %bitcast.18), custom_call_target="tpu_custom_call" | custom-call | bytes 1179648 | tf_op jit(solution)/shard_map/pack_heads/pallas_call | solution.py:166
  22.5 0.0 copy-done
  22.5 0.2 dynamic-slice_reduce_fusion
  22.7 0.0 collective-permute-done.7.low_ref
  22.7 3.3 %collective-permute-start.2 = (bf16[2,1152,128]{2,1,0:T(8,128)(2,1)}, bf16[2,1152,128]{2,1,0:T(8,128)(2,1)}, u32[]{:S(2)}, u32[]{:S(2)}) collective-permute-start(bf16[2,1152,128]{2,1,0:T(8,128)(2,1)} %pack_heads.4), channel_id=1, source_target_pairs={{0,1},{1,2},{2,3},{4,5},{5,6},{6,7},{8,9},{9,10},{10,11},{12,13},{... | collective-permute-start | bytes 1769480 | tf_op jit(solution)/shard_map/ppermute | solution.py:241
  26.0 0.0 collective-permute-done.8.high_ref
  26.0 2.9 %collective-permute-start.3 = (bf16[2,1152,128]{2,1,0:T(8,128)(2,1)}, bf16[2,1152,128]{2,1,0:T(8,128)(2,1)}, u32[]{:S(2)}, u32[]{:S(2)}) collective-permute-start(bf16[2,1152,128]{2,1,0:T(8,128)(2,1)} %pack_heads.4), channel_id=1, source_target_pairs={{1,0},{2,1},{3,2},{5,4},{6,5},{7,6},{9,8},{10,9},{11,10},{13,12},{... | collective-permute-start | bytes 1769480 | tf_op jit(solution)/shard_map/ppermute | solution.py:242
  28.9 0.5 xor_add_fusion.info_ref
  29.5 3.8 %split_weight.1 = (bf16[384,768]{1,0:T(8,128)(2,1)}, bf16[384,768]{1,0:T(8,128)(2,1)}) custom-call(s32[4]{0:T(128)} %xor_add_fusion.info_ref, bf16[384,3072]{1,0:T(8,128)(2,1)} %w_ref), custom_call_target="tpu_custom_call" | custom-call | bytes 2359296 | tf_op jit(solution)/shard_map/split_weight/pallas_call | solution.py:192
  33.3 0.1 add_convert_fusion.1
  33.4 0.1 pad_add_fusion.1.info_ref
  33.4 0.0 collective-permute-done.1.refs_12_
  33.4 1.2 %collective-permute-start = (bf16[384,768]{1,0:T(8,128)(2,1)}, bf16[384,768]{1,0:T(8,128)(2,1)S(1)}, u32[]{:S(2)}, u32[]{:S(2)}) collective-permute-start(bf16[384,768]{1,0:T(8,128)(2,1)} %get-tuple-element.20), channel_id=1, source_target_pairs={{0,8},{4,12},{8,0},{12,4},{1,9},{5,13},{9,1},{13,5},{2,10},{6,14},... | collective-permute-start | bytes 1769480 | tf_op jit(solution)/shard_map/ppermute | solution.py:229
  34.7 0.0 copy-done.4
  34.7 0.0 copy-done.1
  34.7 0.0 copy-done.2
  34.7 5.5 %attention.4.refs_2_ = bf16[1152,128]{1,0:T(8,128)(2,1)S(1)} custom-call(s32[5]{0:T(128)S(1)} %pad_add_fusion.1.info_ref, bf16[1152,384]{1,0:T(8,128)(2,1)S(1)} %bitcast.22, bf16[1152,384]{1,0:T(8,128)(2,1)S(1)} %bitcast.13, bf16[1152,384]{1,0:T(8,128)(2,1)S(1)} %bitcast.19, bf16[2,1152,128]{2,1,0:T(8,128)(2,1)} %collective-permute-done.7.low_ref, ...), custom_call_target="tpu_custom_call" | custom-call | flops 1358954496 | bytes 2359296 | tf_op jit(solution)/shard_map/attention/pallas_call | solution.py:77
  40.2 0.0 copy-start.6
  40.2 0.0 collective-permute-done.10.high_ref
  40.2 0.3 collective-permute-start.11
  40.5 0.0 collective-permute-done.9.low_ref
  40.5 0.3 collective-permute-start.13
  40.8 5.5 %attention.5.refs_3_ = bf16[1152,128]{1,0:T(8,128)(2,1)S(1)} custom-call(s32[5]{0:T(128)S(1)} %pad_add_fusion.1.info_ref, bf16[1152,384]{1,0:T(8,128)(2,1)S(1)} %bitcast.23, bf16[1152,384]{1,0:T(8,128)(2,1)S(1)} %bitcast.14, bf16[1152,384]{1,0:T(8,128)(2,1)S(1)} %bitcast.20, bf16[2,1152,128]{2,1,0:T(8,128)(2,1)} %collective-permute-done.9.low_ref, ...), custom_call_target="tpu_custom_call" | custom-call | flops 1358954496 | bytes 2359296 | tf_op jit(solution)/shard_map/attention/pallas_call | solution.py:77
  46.3 0.0 collective-permute-done.2.low_ref
  46.3 2.2 %collective-permute-start.15 = (bf16[1152,128]{1,0:T(8,128)(2,1)S(1)}, bf16[1152,128]{1,0:T(8,128)(2,1)S(1)}, u32[]{:S(2)}, u32[]{:S(2)}) collective-permute-start(bf16[1152,128]{1,0:T(8,128)(2,1)S(1)} %attention.4.refs_2_), channel_id=1, source_target_pairs={{0,24},{4,28},{8,16},{12,20},{16,8},{20,12},{24,0},{28,4},{1,25},{... | collective-permute-start | bytes 884744 | tf_op jit(solution)/shard_map/ppermute | solution.py:231
  48.6 0.0 collective-permute-done.3.high_ref
  48.6 0.2 collective-permute-start.12
  48.8 0.0 copy-done.6
  48.8 0.1 constant_dynamic-slice_fusion.1
  48.9 0.0 copy-start.7
  48.9 5.5 %attention.3.refs_2_ = bf16[1152,128]{1,0:T(8,128)(2,1)S(1)} custom-call(s32[5]{0:T(128)S(1)} %pad_add_fusion.1.info_ref, bf16[1152,384]{1,0:T(8,128)(2,1)S(1)} %bitcast.24, bf16[1152,384]{1,0:T(8,128)(2,1)S(1)} %bitcast.15, bf16[1152,384]{1,0:T(8,128)(2,1)S(1)} %bitcast.21, bf16[2,1152,128]{2,1,0:T(8,128)(2,1)} %collective-permute-done.2.low_ref, ...), custom_call_target="tpu_custom_call" | custom-call | flops 1358954496 | bytes 2359296 | tf_op jit(solution)/shard_map/attention/pallas_call | solution.py:77
  54.5 0.0 collective-permute-done.refs_1_
  54.5 1.2 %collective-permute-start.14 = (bf16[1152,128]{1,0:T(8,128)(2,1)S(1)}, bf16[1152,128]{1,0:T(8,128)(2,1)S(1)}, u32[]{:S(2)}, u32[]{:S(2)}) collective-permute-start(bf16[1152,128]{1,0:T(8,128)(2,1)S(1)} %attention.5.refs_3_), channel_id=1, source_target_pairs={{0,16},{16,0},{1,17},{17,1},{2,18},{18,2},{3,19},{19,3},{4,20},{20... | collective-permute-start | bytes 884744 | tf_op jit(solution)/shard_map/ppermute | solution.py:227
  55.7 2.8 %collective-permute-done.11.refs_4_ = bf16[1152,128]{1,0:T(8,128)(2,1)S(1)} collective-permute-done((bf16[1152,128]{1,0:T(8,128)(2,1)S(1)}, bf16[1152,128]{1,0:T(8,128)(2,1)S(1)}, u32[]{:S(2)}, u32[]{:S(2)}) %collective-permute-start.11) | collective-permute-done | bytes 294944 | tf_op jit(solution)/shard_map/ppermute | solution.py:229
  58.5 1.2 %collective-permute-start.16 = (bf16[1152,128]{1,0:T(8,128)(2,1)S(1)}, bf16[1152,128]{1,0:T(8,128)(2,1)S(1)}, u32[]{:S(2)}, u32[]{:S(2)}) collective-permute-start(bf16[1152,128]{1,0:T(8,128)(2,1)S(1)} %attention.5.refs_3_), channel_id=1, source_target_pairs={{0,24},{4,28},{8,16},{12,20},{16,8},{20,12},{24,0},{28,4},{1,25},{... | collective-permute-start | bytes 884744 | tf_op jit(solution)/shard_map/ppermute | solution.py:231
  59.7 0.0 collective-permute-done.13.refs_6_
  59.7 0.2 collective-permute-start.4
  59.9 0.0 collective-permute-done.15.refs_8_
  59.9 1.2 %collective-permute-start.5 = (bf16[1152,128]{1,0:T(8,128)(2,1)S(1)}, bf16[1152,128]{1,0:T(8,128)(2,1)S(1)}, u32[]{:S(2)}, u32[]{:S(2)}) collective-permute-start(bf16[1152,128]{1,0:T(8,128)(2,1)S(1)} %attention.3.refs_2_), channel_id=1, source_target_pairs={{0,16},{16,0},{1,17},{17,1},{2,18},{18,2},{3,19},{19,3},{4,20},{20... | collective-permute-start | bytes 884744 | tf_op jit(solution)/shard_map/ppermute | solution.py:227
  61.1 6.8 %collective-permute-done.12.refs_5_ = bf16[1152,128]{1,0:T(8,128)(2,1)S(1)} collective-permute-done((bf16[1152,128]{1,0:T(8,128)(2,1)S(1)}, bf16[1152,128]{1,0:T(8,128)(2,1)S(1)}, u32[]{:S(2)}, u32[]{:S(2)}) %collective-permute-start.12) | collective-permute-done | bytes 294944 | tf_op jit(solution)/shard_map/ppermute | solution.py:229
  68.0 0.8 collective-permute-start.6
  68.7 0.1 pad_add_fusion.info_ref
  68.8 0.0 collective-permute-done.14.refs_7_
  68.8 0.0 collective-permute-done.16.refs_9_
  68.8 4.2 %partial_projection.2 = (f32[1152,384]{1,0:T(8,128)S(1)}, f32[1152,384]{1,0:T(8,128)S(1)}) custom-call(s32[19]{0:T(128)S(1)} %pad_add_fusion.info_ref, bf16[384,768]{1,0:T(8,128)(2,1)S(1)} %copy-done.3, bf16[384,768]{1,0:T(8,128)(2,1)S(1)} %collective-permute-done.refs_1_, bf16[1152,128]{1,0:T(8,128)(2,1)S(1)} %attention.4.refs_2_, ...), custom_call_target="tpu_custom_call" | custom-call | flops 1811939328 | bytes 7667712 | tf_op jit(solution)/shard_map/partial_projection/pallas_call | solution.py:132
  73.0 7.6 %collective-permute-done.4.refs_3_ = bf16[1152,128]{1,0:T(8,128)(2,1)S(1)} collective-permute-done((bf16[1152,128]{1,0:T(8,128)(2,1)S(1)}, bf16[1152,128]{1,0:T(8,128)(2,1)S(1)}, u32[]{:S(2)}, u32[]{:S(2)}) %collective-permute-start.4) | collective-permute-done | bytes 294944 | tf_op jit(solution)/shard_map/ppermute | solution.py:229
  80.6 0.0 collective-permute-done.5.refs_4_
  80.6 0.0 collective-permute-done.6.refs_5_
  80.6 2.3 %partial_projection.3 = (f32[1152,384]{1,0:T(8,128)S(1)}, bf16[1152,384]{1,0:T(8,128)(2,1)S(1)}) custom-call(s32[19]{0:T(128)S(1)} %pad_add_fusion.info_ref, bf16[384,768]{1,0:T(8,128)(2,1)S(1)} %copy-done.3, bf16[384,768]{1,0:T(8,128)(2,1)S(1)} %collective-permute-done.refs_1_, bf16[1152,128]{1,0:T(8,128)(2,1)S(1)} %attention.3.refs_2_, ...), custom_call_target="tpu_custom_call" | custom-call | flops 905969664 | bytes 6488064 | tf_op jit(solution)/shard_map/partial_projection/pallas_call | solution.py:132
  82.9 8.1 %collective-permute-start.17 = (bf16[1152,384]{1,0:T(8,128)(2,1)S(1)}, bf16[1152,384]{1,0:T(8,128)(2,1)S(1)}, u32[]{:S(2)}, u32[]{:S(2)}) collective-permute-start(bf16[1152,384]{1,0:T(8,128)(2,1)S(1)} %get-tuple-element.30), channel_id=1, source_target_pairs={{0,4},{4,0},{8,12},{12,8},{1,5},{5,1},{9,13},{13,9},{2,6},{6,2},{1... | collective-permute-start | bytes 2654216 | tf_op jit(solution)/shard_map/ppermute | solution.py:229
  91.0 2.1 %collective-permute-done.17 = bf16[1152,384]{1,0:T(8,128)(2,1)S(1)} collective-permute-done((bf16[1152,384]{1,0:T(8,128)(2,1)S(1)}, bf16[1152,384]{1,0:T(8,128)(2,1)S(1)}, u32[]{:S(2)}, u32[]{:S(2)}) %collective-permute-start.17) | collective-permute-done | bytes 884768 | tf_op jit(solution)/shard_map/ppermute | solution.py:229
  93.0 1.1 %add_convert_fusion = bf16[1152,384]{1,0:T(8,128)(2,1)} fusion(f32[1152,384]{1,0:T(8,128)S(1)} %get-tuple-element.29, bf16[1152,384]{1,0:T(8,128)(2,1)S(1)} %collective-permute-done.17), kind=kLoop, calls=%fused_computation | loop fusion | flops 1327104 | bytes 3538944 | tf_op jit(solution)/shard_map/convert_element_type | solution.py:285
  (8 shorter events, 0.0 us)
Async XLA Ops:
  0.0 22.5 %copy-start = (s32[3,4]{1,0:T(4,128)S(1)}, s32[3,4]{1,0:T(4,128)}, u32[]{:S(2)}) copy-start(s32[3,4]{1,0:T(4,128)} %param.14) | copy-start | bytes 148
  0.0 9.0 %copy-start.5 = (bf16[1,1152,2,384]{3,2,1,0:T(2,128)(2,1)S(1)}, bf16[1,1152,2,384]{3,2,1,0:T(2,128)(2,1)}, u32[]{:S(2)}) copy-start(bf16[1,1152,2,384]{3,2,1,0:T(2,128)(2,1)} %param.11) | copy-start | bytes 5308420
  2.9 19.8 %collective-permute-start.7 = (bf16[2,1152,128]{2,1,0:T(8,128)(2,1)}, bf16[2,1152,128]{2,1,0:T(8,128)(2,1)}, u32[]{:S(2)}, u32[]{:S(2)}) collective-permute-start(bf16[2,1152,128]{2,1,0:T(8,128)(2,1)} %pack_heads.3), channel_id=1, source_target_pairs={{0,1},{1,2},{2,3},{4,5},{5,6},{6,7},{8,9},{9,10},{10,11},{12,13},{... | collective-permute-start | bytes 1769480 | tf_op jit(solution)/shard_map/ppermute | solution.py:241
  6.1 19.9 %collective-permute-start.8 = (bf16[2,1152,128]{2,1,0:T(8,128)(2,1)}, bf16[2,1152,128]{2,1,0:T(8,128)(2,1)}, u32[]{:S(2)}, u32[]{:S(2)}) collective-permute-start(bf16[2,1152,128]{2,1,0:T(8,128)(2,1)} %pack_heads.3), channel_id=1, source_target_pairs={{1,0},{2,1},{3,2},{5,4},{6,5},{7,6},{9,8},{10,9},{11,10},{13,12},{... | collective-permute-start | bytes 1769480 | tf_op jit(solution)/shard_map/ppermute | solution.py:242
  10.4 23.1 %collective-permute-start.1 = (bf16[1152,384]{1,0:T(8,128)(2,1)}, bf16[1152,384]{1,0:T(8,128)(2,1)}, u32[]{:S(2)}, u32[]{:S(2)}) collective-permute-start(bf16[1152,384]{1,0:T(8,128)(2,1)} %get-tuple-element.32), channel_id=1, source_target_pairs={{0,16},{16,0},{1,17},{17,1},{2,18},{18,2},{3,19},{19,3},{4,20},{20... | collective-permute-start | bytes 2654216 | tf_op jit(solution)/shard_map/ppermute | solution.py:227
  14.3 25.9 %collective-permute-start.10 = (bf16[2,1152,128]{2,1,0:T(8,128)(2,1)}, bf16[2,1152,128]{2,1,0:T(8,128)(2,1)}, u32[]{:S(2)}, u32[]{:S(2)}) collective-permute-start(bf16[2,1152,128]{2,1,0:T(8,128)(2,1)} %pack_heads.5), channel_id=1, source_target_pairs={{1,0},{2,1},{3,2},{5,4},{6,5},{7,6},{9,8},{10,9},{11,10},{13,12},{... | collective-permute-start | bytes 1769480 | tf_op jit(solution)/shard_map/ppermute | solution.py:242
  16.2 24.3 %collective-permute-start.9 = (bf16[2,1152,128]{2,1,0:T(8,128)(2,1)}, bf16[2,1152,128]{2,1,0:T(8,128)(2,1)}, u32[]{:S(2)}, u32[]{:S(2)}) collective-permute-start(bf16[2,1152,128]{2,1,0:T(8,128)(2,1)} %pack_heads.5), channel_id=1, source_target_pairs={{0,1},{1,2},{2,3},{4,5},{5,6},{6,7},{8,9},{9,10},{10,11},{12,13},{... | collective-permute-start | bytes 1769480 | tf_op jit(solution)/shard_map/ppermute | solution.py:241
  19.6 15.1 %copy-start.4 = (bf16[1,1152,384]{2,1,0:T(8,128)(2,1)S(1)}, bf16[1,1152,384]{2,1,0:T(8,128)(2,1)}, u32[]{:S(2)}) copy-start(bf16[1,1152,384]{2,1,0:T(8,128)(2,1)} %param.8) | copy-start | bytes 2654212
  22.5 12.2 %copy-start.1 = (bf16[1,1152,384]{2,1,0:T(8,128)(2,1)S(1)}, bf16[1,1152,384]{2,1,0:T(8,128)(2,1)}, u32[]{:S(2)}) copy-start(bf16[1,1152,384]{2,1,0:T(8,128)(2,1)} %param.9) | copy-start | bytes 2654212
  22.5 12.2 %copy-start.2 = (bf16[1,1152,384]{2,1,0:T(8,128)(2,1)S(1)}, bf16[1,1152,384]{2,1,0:T(8,128)(2,1)}, u32[]{:S(2)}) copy-start(bf16[1,1152,384]{2,1,0:T(8,128)(2,1)} %param.10) | copy-start | bytes 2654212
  22.7 23.6 %collective-permute-start.2 = (bf16[2,1152,128]{2,1,0:T(8,128)(2,1)}, bf16[2,1152,128]{2,1,0:T(8,128)(2,1)}, u32[]{:S(2)}, u32[]{:S(2)}) collective-permute-start(bf16[2,1152,128]{2,1,0:T(8,128)(2,1)} %pack_heads.4), channel_id=1, source_target_pairs={{0,1},{1,2},{2,3},{4,5},{5,6},{6,7},{8,9},{9,10},{10,11},{12,13},{... | collective-permute-start | bytes 1769480 | tf_op jit(solution)/shard_map/ppermute | solution.py:241
  26.0 22.5 %collective-permute-start.3 = (bf16[2,1152,128]{2,1,0:T(8,128)(2,1)}, bf16[2,1152,128]{2,1,0:T(8,128)(2,1)}, u32[]{:S(2)}, u32[]{:S(2)}) collective-permute-start(bf16[2,1152,128]{2,1,0:T(8,128)(2,1)} %pack_heads.4), channel_id=1, source_target_pairs={{1,0},{2,1},{3,2},{5,4},{6,5},{7,6},{9,8},{10,9},{11,10},{13,12},{... | collective-permute-start | bytes 1769480 | tf_op jit(solution)/shard_map/ppermute | solution.py:242
  33.4 21.0 %collective-permute-start = (bf16[384,768]{1,0:T(8,128)(2,1)}, bf16[384,768]{1,0:T(8,128)(2,1)S(1)}, u32[]{:S(2)}, u32[]{:S(2)}) collective-permute-start(bf16[384,768]{1,0:T(8,128)(2,1)} %get-tuple-element.20), channel_id=1, source_target_pairs={{0,8},{4,12},{8,0},{12,4},{1,9},{5,13},{9,1},{13,5},{2,10},{6,14},... | collective-permute-start | bytes 1769480 | tf_op jit(solution)/shard_map/ppermute | solution.py:229
  40.2 8.6 %copy-start.6 = (bf16[2,2,1536]{2,1,0:T(2,128)(2,1)S(1)}, bf16[2,2,1536]{2,1,0:T(2,128)(2,1)}, u32[]{:S(2)}) copy-start(bf16[2,2,1536]{2,1,0:T(2,128)(2,1)} %param.12) | copy-start | bytes 36868
  40.2 18.2 %collective-permute-start.11 = (bf16[1152,128]{1,0:T(8,128)(2,1)S(1)}, bf16[1152,128]{1,0:T(8,128)(2,1)S(1)}, u32[]{:S(2)}, u32[]{:S(2)}) collective-permute-start(bf16[1152,128]{1,0:T(8,128)(2,1)S(1)} %attention.4.refs_2_), channel_id=1, source_target_pairs={{0,8},{4,12},{8,0},{12,4},{1,9},{5,13},{9,1},{13,5},{2,10},{6,14},... | collective-permute-start | bytes 884744 | tf_op jit(solution)/shard_map/ppermute | solution.py:229
  40.5 19.2 %collective-permute-start.13 = (bf16[1152,128]{1,0:T(8,128)(2,1)S(1)}, bf16[1152,128]{1,0:T(8,128)(2,1)S(1)}, u32[]{:S(2)}, u32[]{:S(2)}) collective-permute-start(bf16[1152,128]{1,0:T(8,128)(2,1)S(1)} %attention.4.refs_2_), channel_id=1, source_target_pairs={{0,16},{16,0},{1,17},{17,1},{2,18},{18,2},{3,19},{19,3},{4,20},{20... | collective-permute-start | bytes 884744 | tf_op jit(solution)/shard_map/ppermute | solution.py:227
  46.3 13.6 %collective-permute-start.15 = (bf16[1152,128]{1,0:T(8,128)(2,1)S(1)}, bf16[1152,128]{1,0:T(8,128)(2,1)S(1)}, u32[]{:S(2)}, u32[]{:S(2)}) collective-permute-start(bf16[1152,128]{1,0:T(8,128)(2,1)S(1)} %attention.4.refs_2_), channel_id=1, source_target_pairs={{0,24},{4,28},{8,16},{12,20},{16,8},{20,12},{24,0},{28,4},{1,25},{... | collective-permute-start | bytes 884744 | tf_op jit(solution)/shard_map/ppermute | solution.py:231
  48.6 19.4 %collective-permute-start.12 = (bf16[1152,128]{1,0:T(8,128)(2,1)S(1)}, bf16[1152,128]{1,0:T(8,128)(2,1)S(1)}, u32[]{:S(2)}, u32[]{:S(2)}) collective-permute-start(bf16[1152,128]{1,0:T(8,128)(2,1)S(1)} %attention.5.refs_3_), channel_id=1, source_target_pairs={{0,8},{4,12},{8,0},{12,4},{1,9},{5,13},{9,1},{13,5},{2,10},{6,14},... | collective-permute-start | bytes 884744 | tf_op jit(solution)/shard_map/ppermute | solution.py:229
  48.9 19.8 %copy-start.7 = (s32[18]{0:T(128)S(1)}, s32[18]{0:T(128)}, u32[]{:S(2)}) copy-start(s32[18]{0:T(128)} %param.15) | copy-start | bytes 220
  48.9 19.9 %copy-start.3 = (bf16[384,768]{1,0:T(8,128)(2,1)S(1)}, bf16[384,768]{1,0:T(8,128)(2,1)}, u32[]{:S(2)}) copy-start(bf16[384,768]{1,0:T(8,128)(2,1)} %get-tuple-element.19.refs_0_) | copy-start | bytes 1769476
  54.5 14.3 %collective-permute-start.14 = (bf16[1152,128]{1,0:T(8,128)(2,1)S(1)}, bf16[1152,128]{1,0:T(8,128)(2,1)S(1)}, u32[]{:S(2)}, u32[]{:S(2)}) collective-permute-start(bf16[1152,128]{1,0:T(8,128)(2,1)S(1)} %attention.5.refs_3_), channel_id=1, source_target_pairs={{0,16},{16,0},{1,17},{17,1},{2,18},{18,2},{3,19},{19,3},{4,20},{20... | collective-permute-start | bytes 884744 | tf_op jit(solution)/shard_map/ppermute | solution.py:227
  58.5 10.3 %collective-permute-start.16 = (bf16[1152,128]{1,0:T(8,128)(2,1)S(1)}, bf16[1152,128]{1,0:T(8,128)(2,1)S(1)}, u32[]{:S(2)}, u32[]{:S(2)}) collective-permute-start(bf16[1152,128]{1,0:T(8,128)(2,1)S(1)} %attention.5.refs_3_), channel_id=1, source_target_pairs={{0,24},{4,28},{8,16},{12,20},{16,8},{20,12},{24,0},{28,4},{1,25},{... | collective-permute-start | bytes 884744 | tf_op jit(solution)/shard_map/ppermute | solution.py:231
  59.7 20.9 %collective-permute-start.4 = (bf16[1152,128]{1,0:T(8,128)(2,1)S(1)}, bf16[1152,128]{1,0:T(8,128)(2,1)S(1)}, u32[]{:S(2)}, u32[]{:S(2)}) collective-permute-start(bf16[1152,128]{1,0:T(8,128)(2,1)S(1)} %attention.3.refs_2_), channel_id=1, source_target_pairs={{0,8},{4,12},{8,0},{12,4},{1,9},{5,13},{9,1},{13,5},{2,10},{6,14},... | collective-permute-start | bytes 884744 | tf_op jit(solution)/shard_map/ppermute | solution.py:229
  59.9 20.7 %collective-permute-start.5 = (bf16[1152,128]{1,0:T(8,128)(2,1)S(1)}, bf16[1152,128]{1,0:T(8,128)(2,1)S(1)}, u32[]{:S(2)}, u32[]{:S(2)}) collective-permute-start(bf16[1152,128]{1,0:T(8,128)(2,1)S(1)} %attention.3.refs_2_), channel_id=1, source_target_pairs={{0,16},{16,0},{1,17},{17,1},{2,18},{18,2},{3,19},{19,3},{4,20},{20... | collective-permute-start | bytes 884744 | tf_op jit(solution)/shard_map/ppermute | solution.py:227
  68.0 12.6 %collective-permute-start.6 = (bf16[1152,128]{1,0:T(8,128)(2,1)S(1)}, bf16[1152,128]{1,0:T(8,128)(2,1)S(1)}, u32[]{:S(2)}, u32[]{:S(2)}) collective-permute-start(bf16[1152,128]{1,0:T(8,128)(2,1)S(1)} %attention.3.refs_2_), channel_id=1, source_target_pairs={{0,24},{4,28},{8,16},{12,20},{16,8},{20,12},{24,0},{28,4},{1,25},{... | collective-permute-start | bytes 884744 | tf_op jit(solution)/shard_map/ppermute | solution.py:231
  82.9 10.1 %collective-permute-start.17 = (bf16[1152,384]{1,0:T(8,128)(2,1)S(1)}, bf16[1152,384]{1,0:T(8,128)(2,1)S(1)}, u32[]{:S(2)}, u32[]{:S(2)}) collective-permute-start(bf16[1152,384]{1,0:T(8,128)(2,1)S(1)} %get-tuple-element.30), channel_id=1, source_target_pairs={{0,4},{4,0},{8,12},{12,8},{1,5},{5,1},{9,13},{13,9},{2,6},{6,2},{1... | collective-permute-start | bytes 2654216 | tf_op jit(solution)/shard_map/ppermute | solution.py:229

commit v4 on v3

--- a/solution.py
+++ b/solution.py
@@ -13,9 +13,10 @@
 FAR = 1e30
 EXP2_SCALE = math.log2(math.e) / math.sqrt(HD)
 VMEM_LIMIT = 24 * 1024 * 1024
-
-
-def attention_kernel(info_ref, q_ref, k_ref, v_ref, low_ref, high_ref, out_ref):
+COPY_PARTS = 3
+
+
+def attention_kernel(info_ref, q_ref, k_ref, v_ref, side_a_ref, side_b_ref, out_ref):
     tiles_time = info_ref.shape[0] - 2
     tile = q_ref.shape[0] // tiles_time
     width_oks = (None, info_ref[tiles_time] == 1, info_ref[tiles_time + 1] == 1)
@@ -32,7 +33,7 @@
         blocks = []
         row_max = None
         for keys, width_ok in zip(
-            (k_ref[rows, :], low_ref[0, rows, :], high_ref[0, rows, :]), width_oks
+            (k_ref[rows, :], side_a_ref[0, rows, :], side_b_ref[0, rows, :]), width_oks
         ):
             scores = lax.dot_general(
                 query, keys, (((1,), (1,)), ((), ())), preferred_element_type=jnp.float32
@@ -54,7 +55,7 @@
             jnp.exp2(block * EXP2_SCALE - jnp.where(allowed, shift, FAR)).astype(jnp.bfloat16)
             for block, allowed in blocks
         ]
-        values = jnp.concatenate([v_ref[rows, :], low_ref[1, rows, :], high_ref[1, rows, :]], axis=0)
+        values = jnp.concatenate([v_ref[rows, :], side_a_ref[1, rows, :], side_b_ref[1, rows, :]], axis=0)
         total = jnp.dot(
             jnp.concatenate(weights, axis=1),
             jnp.concatenate([values, jnp.ones_like(values)], axis=1),
@@ -69,7 +70,7 @@
         ready = later
 
 
-def attention(info, queries, keys, values, low, high, head, tile):
+def attention(info, queries, keys, values, side_a, side_b, head, tile):
     count = queries.shape[0]
     side = pl.BlockSpec((2, count, HD), lambda i, info: (0, 0, 0))
     whole = pl.BlockSpec((count, HD), lambda i, info: (0, head))
@@ -88,16 +89,19 @@
             flops=4 * pairs * HD, bytes_accessed=8 * count * HD * 2, transcendentals=pairs
         ),
         name="attention",
-    )(info, queries, keys, values, low, high)
+    )(info, queries, keys, values, side_a, side_b)
 
 
 def partial_kernel(first, own_cols, info_ref, *refs):
-    near_ref, far_ref, *pieces, gate_ref, base_own_ref, base_other_ref, own_ref, other_ref = refs
+    w_refs, refs = refs[:4], refs[4:]
+    *pieces, gate_ref, base_own_ref, base_other_ref, own_ref, other_ref = refs
     tile = own_ref.shape[0]
     frames = tile // FRAME
     time_tile = pl.program_id(0)
     cond_first = info_ref[0] == 0
-    weights = jnp.concatenate([near_ref[...], far_ref[...]], axis=0)
+    weights = jnp.concatenate(
+        [jnp.concatenate([w[...] for w in w_refs[i : i + 2]], axis=1) for i in (0, 2)], axis=0
+    )
     half = len(pieces) // 2
     parts = []
     for which in range(2):
@@ -108,7 +112,7 @@
         parts.append(gate_ref[which] * projected)
     for frame in range(frames):
         rows = slice(frame * FRAME, (frame + 1) * FRAME)
-        guide = 1.0 + 0.5 * info_ref[1 + time_tile * frames + frame].astype(jnp.float32)
+        guide = 1.0 + 0.5 * info_ref[5 + time_tile * frames + frame].astype(jnp.float32)
         scales = (jnp.where(cond_first, guide, 1.0 - guide), jnp.where(cond_first, 1.0 - guide, guide))
         total = scales[0] * parts[0][rows] + scales[1] * parts[1][rows]
         own, other = total[:, :own_cols], total[:, own_cols:]
@@ -126,7 +130,10 @@
     count, width = base[0].shape
     first = group.start == 0
     depth = len(group) * HD
-    weight = pl.BlockSpec((depth, 2 * width), lambda t, info: (group.start // len(group), 0))
+    weight_specs = [
+        pl.BlockSpec((depth, width), lambda t, info, place=place: (group.start // len(group), info[place]))
+        for place in range(1, 5)
+    ]
     rows = pl.BlockSpec((tile, width), lambda t, info: (t, 0))
     piece = pl.BlockSpec((tile, HD), lambda t, info: (t, 0))
     return pl.pallas_call(
@@ -138,7 +145,7 @@
         grid_spec=pltpu.PrefetchScalarGridSpec(
             num_scalar_prefetch=1,
             grid=(count // tile,),
-            in_specs=[weight] * 2
+            in_specs=weight_specs
             + [piece] * len(pieces)
             + [pl.BlockSpec(gate.shape, lambda t, info: (0, 0, 0)), rows, rows],
             out_specs=[rows, rows],
@@ -150,59 +157,44 @@
             transcendentals=0,
         ),
         name="partial_projection",
-    )(info, *weights, *pieces, gate, *base)
-
-
-def pack_kernel(k_ref, v_ref, *out_refs):
-    for head, out_ref in enumerate(out_refs):
-        cols = slice(head * HD, (head + 1) * HD)
-        out_ref[0] = k_ref[:, cols]
-        out_ref[1] = v_ref[:, cols]
-
-
-def pack_heads(keys, values, first, heads, tile):
-    count = keys.shape[0]
-    rows = pl.BlockSpec((tile, heads * HD), lambda t: (t, first // heads))
+    )(info, *[w for w in weights for _ in range(2)], *pieces, gate, *base)
+
+
+def copy_kernel(plan, info_ref, *refs):
+    *arrays, sems = refs
+    copies = []
+    for source, cols, width, target, place in plan:
+        src, dst = arrays[source], arrays[target]
+        first = cols if cols is not None else pl.multiple_of(info_ref[0] * width, width)
+        for part in range(COPY_PARTS):
+            size = src.shape[0] // COPY_PARTS
+            rows = pl.ds(part * size, size)
+            to = dst.at[rows, :] if place is None else dst.at[place, rows, :]
+            copies.append((src.at[rows, pl.ds(first, width)], to))
+    copies = [
+        pltpu.make_async_copy(src, to, sems.at[index]) for index, (src, to) in enumerate(copies)
+    ]
+    for copy in copies:
+        copy.start()
+    for copy in copies:
+        copy.wait()
+
+
+def copy_columns(info, sources, plan, targets):
+    moved = sum(2 * 2 * sources[source].shape[0] * width for source, _, width, _, _ in plan)
     return pl.pallas_call(
-        pack_kernel,
-        out_shape=[jax.ShapeDtypeStruct((2, count, HD), jnp.bfloat16)] * heads,
-        grid=(count // tile,),
-        in_specs=[rows, rows],
-        out_specs=[pl.BlockSpec((2, tile, HD), lambda t: (0, t, 0))] * heads,
-        cost_estimate=pl.CostEstimate(
-            flops=0, bytes_accessed=8 * count * heads * HD, transcendentals=0
-        ),
-        name="pack_heads",
-    )(keys, values)
-
-
-def split_kernel(info_ref, w_ref, near_ref, far_ref):
-    cols = near_ref.shape[1]
-    for index, out_ref in enumerate((near_ref, far_ref)):
-        for side in range(2):
-
-            @pl.when(pl.program_id(0) == 2 * index + side)
-            def _():
-                out_ref[:, side * (cols // 2) : (side + 1) * (cols // 2)] = w_ref[...]
-
-
-def split_weight(info, weight, width):
-    rows = weight.shape[0]
-    whole = pl.BlockSpec((rows, 2 * width), lambda i, info: (0, 0))
-    return pl.pallas_call(
-        split_kernel,
-        out_shape=[jax.ShapeDtypeStruct((rows, 2 * width), jnp.bfloat16)] * 2,
+        functools.partial(copy_kernel, plan),
+        out_shape=[jax.ShapeDtypeStruct(shape, jnp.bfloat16) for shape in targets],
         grid_spec=pltpu.PrefetchScalarGridSpec(
             num_scalar_prefetch=1,
-            grid=(4,),
-            in_specs=[pl.BlockSpec((rows, width), lambda i, info: (0, info[i]))],
-            out_specs=[whole, whole],
-        ),
-        cost_estimate=pl.CostEstimate(
-            flops=0, bytes_accessed=16 * rows * width, transcendentals=0
-        ),
-        name="split_weight",
-    )(info, weight)
+            grid=(1,),
+            in_specs=[pl.BlockSpec(memory_space=pl.ANY)] * len(sources),
+            out_specs=[pl.BlockSpec(memory_space=pl.ANY)] * len(targets),
+            scratch_shapes=[pltpu.SemaphoreType.DMA((COPY_PARTS * len(plan),))],
+        ),
+        cost_estimate=pl.CostEstimate(flops=0, bytes_accessed=moved, transcendentals=0),
+        name="copy_columns",
+    )(info, *sources)
 
 
 def local(queries, keys, values, residual, gate, out_weight, time_offsets, guidance_index):
@@ -217,8 +209,11 @@
     width_pos = lax.axis_index("tokens")
     width = gate.shape[2] // head_count
 
-    up = [(i, i + 1) for i in range(columns - 1)]
-    down = [(i + 1, i) for i in range(columns - 1)]
+    rounds = [
+        [pair for i in range(first, columns - 1, 2) for pair in ((i, i + 1), (i + 1, i))]
+        for first in range(2)
+    ]
+    near_pos = (width_pos ^ 1, ((width_pos + 1) ^ 1) - 1)
 
     def swap(value, branch_bit, head_bits):
         if not branch_bit and not head_bits:
@@ -232,14 +227,30 @@
             value, ("branch", "head"), [(i, i ^ flip) for i in range(2 * head_count)]
         )
 
-    packed = pack_heads(keys[0], values[0], 0, 1, tile)
-    (packed, late_keys, late_values, residual, out_weight) = lax.optimization_barrier(
-        (packed, keys[0], values[0], residual, out_weight)
-    )
-    for head in range(1, heads):
-        packed += pack_heads(late_keys, late_values, head, 1, tile)
-    low = [lax.ppermute(key_value, "tokens", up) for key_value in packed]
-    high = [lax.ppermute(key_value, "tokens", down) for key_value in packed]
+    branch_pair = branch_pos * (head_count // 2)
+    copy_info = jnp.stack([branch_pair + ((head_pos ^ 2) >> 1)])
+    key_value = (2, count, HD)
+    packed = copy_columns(
+        copy_info, (keys[0], values[0]), ((0, 0, HD, 2, 0), (1, 0, HD, 2, 1)), (key_value,)
+    )
+    (packed, late_keys, late_values, late_weight) = lax.optimization_barrier(
+        (packed, keys[0], values[0], out_weight)
+    )
+    *late, far = copy_columns(
+        copy_info,
+        (late_keys, late_values, late_weight),
+        [(array, head * HD, HD, 2 + head, array) for head in range(1, heads) for array in range(2)]
+        + [(2, None, 2 * width, 2 + heads, None)],
+        [key_value] * (heads - 1) + [(features, 2 * width)],
+    )
+    late, far, residual = lax.optimization_barrier((late, far, residual))
+    packed = list(packed) + late
+
+    def halo(part):
+        return [lax.ppermute(part, "tokens", pairs) for pairs in rounds]
+
+    sides = [halo(part) for part in packed[:2]]
+    far = swap(far, 0, 2)
 
     first_half, second_half = residual[0, :, 0], residual[0, :, 1]
     mine = jnp.where(branch_pos == 0, first_half, second_half)
@@ -253,34 +264,42 @@
     ).astype(jnp.float32)
     gate_block = jnp.where(branch_pos == 0, gate_block, gate_block[::-1])
 
-    distances = jnp.arange(4, dtype=jnp.int32)
-    near, far = split_weight(
-        branch_pos * head_count + (head_pos ^ distances), out_weight, width
-    )
-    far = swap(far, 0, 2)
-
     offsets = lax.dynamic_index_in_dim(time_offsets, width_pos, 1, keepdims=False)
-    edges = jnp.stack([width_pos > 0, width_pos < tiles_wide - 1]).astype(jnp.int32)
+    edges = jnp.stack([(pos >= 0) & (pos < tiles_wide) for pos in near_pos]).astype(jnp.int32)
     attention_info = jnp.concatenate([offsets, edges])
-    projection_info = jnp.concatenate([branch_pos[None].astype(jnp.int32), guidance_index])
+    places = [branch_pos * head_count + head_pos, branch_pos * head_count + (head_pos ^ 1)]
+    places += [head_pos & 1, (head_pos & 1) ^ 1]
+    projection_info = jnp.concatenate([jnp.stack([branch_pos] + places), guidance_index])
 
     pieces = {}
     head_queries = queries[0]
     for head in range(heads):
         if head == 1:
             head_queries, other = lax.optimization_barrier((head_queries, other))
+        if head == 2:
+            head_queries, far, pieces[1, 0, 0], pieces[1, 0, 1] = lax.optimization_barrier(
+                (head_queries, far, pieces[1, 0, 0], pieces[1, 0, 1])
+            )
+            pieces[1, 2, 0] = swap(pieces[1, 0, 0], 0, 2)
         own = attention(
-            attention_info, head_queries, keys[0], values[0], low[head], high[head], head, tile
-        )
-        for branch_bit in range(2):
-            for bits in (0, 2):
-                pieces[branch_bit, bits, head] = swap(own, branch_bit, bits)
+            attention_info, head_queries, keys[0], values[0], *sides[head], head, tile
+        )
+        if head + 2 < heads:
+            own, part = lax.optimization_barrier((own, packed[head + 2]))
+            sides.append(halo(part))
+        pieces[0, 0, head] = own
+        pieces[1, 0, head] = swap(own, 1, 0)
+        pieces[0, 2, head] = swap(own, 0, 2)
+        if head == 1:
+            pieces[1, 2, head] = swap(pieces[0, 2, head], 1, 0)
+        elif head:
+            pieces[1, 2, head] = swap(pieces[1, 0, head], 0, 2)
 
     base = (mine, other)
     for group in (range(heads - 1), range(heads - 1, heads)):
         ordered = [pieces[bit, bits, head] for bit in range(2) for bits in (0, 2) for head in group]
         base = partial_projection(
-            projection_info, (near, far), ordered, gate_block, base, tile, group
+            projection_info, (out_weight, far), ordered, gate_block, base, tile, group
         )
     return (base[0] + swap(base[1], 0, 1).astype(jnp.float32)).astype(jnp.bfloat16)
 

time: 94.8 us -> 164 us (1.73)
  Pallas kernels: 35.3 us -> 96.8 us
  starting transfers between devices: 35.7 us -> 27 us
  local copies, waits for them, and re-layouts: 0.54 us -> 9.24 us
  waiting for transfers between devices: 19.3 us -> 26 us
    pallas_call x4 -> x2, Pallas kernels: 12.3 us -> 73.9 us  [copy_columns(): pl.pallas_call(functools.partial(copy_kernel, plan), out_shape=[jax.Shape...]
    ppermute x9 -> x6, starting transfers between devices: 21.8 us -> 10.4 us  [halo(): return [lax.ppermute(part, 'tokens', pairs) for pairs in rounds]]
    ppermute x9 -> x6, waiting for transfers between devices: 0.02 us -> 10.1 us  [halo(): return [lax.ppermute(part, 'tokens', pairs) for pairs in rounds]]
    ppermute x5 -> x7, waiting for transfers between devices: 19.3 us -> 11 us  [swap(): lax.ppermute(value, 'head', [(i, i ^ head_bits) for i in range(head_count)])]
    unnamed x16 -> x40, local copies, waits for them, and re-layouts: 0.04 us -> 6.69 us
    ppermute x4 -> x5, waiting for transfers between devices: 0.01 us -> 4.97 us  [swap(): return lax.ppermute(value, 'branch', [(0, 1), (1, 0)])]
    ppermute x5 -> x7, starting transfers between devices: 10.1 us -> 13.2 us  [swap(): lax.ppermute(value, 'head', [(i, i ^ head_bits) for i in range(head_count)])]
    select_n x1, other arithmetic: 1.08 us -> 2.97 us  [local(): mine = jnp.where(branch_pos == 0, first_half, second_half)]
  transfers between devices with their start and end apart: 18 -> 18, of which waited for: 4 -> 9; matrix products, arithmetic and copies ran while one was open for 2% -> 1% of each run, Pallas kernels for 32% -> 13%
where the time goes in v4:
time: 164 us
  Pallas kernels  96.8 us (59%)
  starting transfers between devices  27 us (16%)
  waiting for transfers between devices  26 us (16%)
  local copies, waits for them, and re-layouts  9.24 us (6%)
  other arithmetic  4.25 us (3%)
    pallas_call x2, Pallas kernels, copy_columns(): pl.pallas_call(functools.partial(copy_kernel, plan), out_shape=[jax.Shape...  73.9 us
    pallas_call x3, Pallas kernels, attention(): pl.pallas_call(attention_kernel, out_shape=jax.ShapeDtypeStruct((count, H...  16.2 us
    ppermute x7, starting transfers between devices, swap(): lax.ppermute(value, 'head', [(i, i ^ head_bits) for i in range(head_count)])  13.2 us
    ppermute x7, waiting for transfers between devices, swap(): lax.ppermute(value, 'head', [(i, i ^ head_bits) for i in range(head_count)])  11 us
    ppermute x6, starting transfers between devices, halo(): return [lax.ppermute(part, 'tokens', pairs) for pairs in rounds]  10.4 us
    ppermute x6, waiting for transfers between devices, halo(): return [lax.ppermute(part, 'tokens', pairs) for pairs in rounds]  10.1 us
    pallas_call x2, Pallas kernels, partial_projection(): pl.pallas_call(functools.partial(partial_kernel, first, width), out_shape...  6.79 us
    unnamed x40, local copies, waits for them, and re-layouts  6.69 us
  transfers between devices with their start and end apart: 18, of which 9 were waited for; matrix products, arithmetic and copies ran while one was open for 1% of the time, Pallas kernels for 13%

profile of v4, /device:TPU:9, one launch (start us, length us, event | category | flops | bytes accessed | tf_op | source)
XLA Modules:
  0.0 163.6 jit_solution(6905921026915861880)
XLA Ops:
  0.0 19.0 %copy_columns.2 = bf16[2,1152,128]{2,1,0:T(8,128)(2,1)} custom-call(s32[1]{0:T(128)} %bitcast.6.info_ref, bf16[1152,384]{1,0:T(8,128)(2,1)} %bitcast.15, bf16[1152,384]{1,0:T(8,128)(2,1)} %bitcast.20), custom_call_target="tpu_custom_call" | custom-call | bytes 1179648 | tf_op jit(solution)/shard_map/copy_columns/pallas_call | solution.py:185
  19.0 0.0 copy-start.17
  19.0 54.8 %copy_columns.3 = (bf16[2,1152,128]{2,1,0:T(8,128)(2,1)}, bf16[2,1152,128]{2,1,0:T(8,128)(2,1)}, bf16[384,768]{1,0:T(8,128)(2,1)}) custom-call(s32[1]{0:T(128)} %bitcast.6.info_ref, bf16[1152,384]{1,0:T(8,128)(2,1)} %bitcast.16, bf16[1152,384]{1,0:T(8,128)(2,1)} %bitcast.21, bf16[384,3072]{1,0:T(8,128)(2,1)} %refs_1_.3), custom_call_target="tpu_custom_call" | custom-call | bytes 3538944 | tf_op jit(solution)/shard_map/copy_columns/pallas_call | solution.py:185
  73.9 1.5 copy.9
  75.4 3.0 %select_bitcast_fusion = (bf16[1152,384]{1,0:T(8,128)(2,1)}, bf16[1152,384]{1,0:T(8,128)(2,1)}) fusion(pred[]{:T(512)S(6)} %eq.2, bf16[1,1152,2,384]{3,1,2,0:T(8,128)(2,1)} %copy.9), kind=kLoop, calls=%fused_computation.1 | loop fusion | flops 884736 | bytes 3538945 | tf_op jit(solution)/shard_map/jit(_where)/select_n | solution.py:256
  78.4 1.2 collective-permute-start
  79.6 0.2 collective-permute-start.2
  79.8 4.3 %collective-permute-start.3 = (bf16[2,1152,128]{2,1,0:T(8,128)(2,1)}, bf16[2,1152,128]{2,1,0:T(8,128)(2,1)}, u32[]{:S(2)}, u32[]{:S(2)}) collective-permute-start(bf16[2,1152,128]{2,1,0:T(8,128)(2,1)} %copy_columns.2), channel_id=1, source_target_pairs={{1,2},{2,1},{5,6},{6,5},{9,10},{10,9},{13,14},{14,13},{17,18},{18,... | collective-permute-start | bytes 1769480 | tf_op jit(solution)/shard_map/ppermute | solution.py:250
  84.1 0.1 collective-permute-start.5
  84.2 1.9 %collective-permute-start.6 = (bf16[2,1152,128]{2,1,0:T(8,128)(2,1)}, bf16[2,1152,128]{2,1,0:T(8,128)(2,1)}, u32[]{:S(2)}, u32[]{:S(2)}) collective-permute-start(bf16[2,1152,128]{2,1,0:T(8,128)(2,1)} %get-tuple-element.40), channel_id=1, source_target_pairs={{1,2},{2,1},{5,6},{6,5},{9,10},{10,9},{13,14},{14,13},{17,18},{18,... | collective-permute-start | bytes 1769480 | tf_op jit(solution)/shard_map/ppermute | solution.py:250
  86.1 0.2 dynamic-slice_reduce_fusion
  86.3 0.1 add_convert_fusion.1
  86.4 0.1 pad_add_fusion.info_ref
  86.5 7.3 %collective-permute-done.2.side_a_ref = bf16[2,1152,128]{2,1,0:T(8,128)(2,1)S(1)} collective-permute-done((bf16[2,1152,128]{2,1,0:T(8,128)(2,1)}, bf16[2,1152,128]{2,1,0:T(8,128)(2,1)S(1)}, u32[]{:S(2)}, u32[]{:S(2)}) %collective-permute-start.2) | collective-permute-done | bytes 589856 | tf_op jit(solution)/shard_map/ppermute | solution.py:250
  93.8 0.8 copy-done.15
  94.6 1.2 collective-permute-start.1
  95.8 1.0 collective-permute-done.3.side_b_ref
  96.8 0.0 copy-done.4
  96.8 1.1 copy-done.16
  97.9 5.5 %attention.3.refs_4_ = bf16[1152,128]{1,0:T(8,128)(2,1)S(1)} custom-call(s32[5]{0:T(128)S(1)} %pad_add_fusion.info_ref, bf16[1152,384]{1,0:T(8,128)(2,1)S(1)} %bitcast.25, bf16[1152,384]{1,0:T(8,128)(2,1)S(1)} %bitcast.17, bf16[1152,384]{1,0:T(8,128)(2,1)S(1)} %bitcast.22, bf16[2,1152,128]{2,1,0:T(8,128)(2,1)S(1)} %copy-done.16, ...), custom_call_target="tpu_custom_call" | custom-call | flops 1358954496 | bytes 2359296 | tf_op jit(solution)/shard_map/attention/pallas_call | solution.py:78
  103.3 0.0 copy-done.19
  103.4 0.0 copy-start.3
  103.4 0.0 copy-start.5
  103.4 0.0 copy-start.14
  103.4 0.1 collective-permute-start.8
  103.5 0.0 collective-permute-done.refs_14_
  103.5 3.8 %collective-permute-start.9 = (bf16[2,1152,128]{2,1,0:T(8,128)(2,1)S(1)}, bf16[2,1152,128]{2,1,0:T(8,128)(2,1)S(1)}, u32[]{:S(2)}, u32[]{:S(2)}) collective-permute-start(bf16[2,1152,128]{2,1,0:T(8,128)(2,1)S(1)} %copy-done.19), channel_id=1, source_target_pairs={{1,2},{2,1},{5,6},{6,5},{9,10},{10,9},{13,14},{14,13},{17,18},{18,... | collective-permute-start | bytes 1769480 | tf_op jit(solution)/shard_map/ppermute | solution.py:250
  107.3 0.0 collective-permute-done.5.side_a_ref
  107.3 0.3 collective-permute-start.4
  107.6 1.8 %collective-permute-done.6.side_b_ref = bf16[2,1152,128]{2,1,0:T(8,128)(2,1)} collective-permute-done((bf16[2,1152,128]{2,1,0:T(8,128)(2,1)}, bf16[2,1152,128]{2,1,0:T(8,128)(2,1)}, u32[]{:S(2)}, u32[]{:S(2)}) %collective-permute-start.6) | collective-permute-done | bytes 589856 | tf_op jit(solution)/shard_map/ppermute | solution.py:250
  109.4 6.4 %attention.4.refs_5_ = bf16[1152,128]{1,0:T(8,128)(2,1)} custom-call(s32[5]{0:T(128)S(1)} %pad_add_fusion.info_ref, bf16[1152,384]{1,0:T(8,128)(2,1)S(1)} %bitcast.26, bf16[1152,384]{1,0:T(8,128)(2,1)S(1)} %bitcast.18, bf16[1152,384]{1,0:T(8,128)(2,1)S(1)} %bitcast.23, bf16[2,1152,128]{2,1,0:T(8,128)(2,1)} %collective-permute-done.5.side_a_ref, ...), custom_call_target="tpu_custom_call" | custom-call | flops 1358954496 | bytes 2359296 | tf_op jit(solution)/shard_map/attention/pallas_call | solution.py:78
  115.8 0.3 collective-permute-start.7
  116.1 0.0 collective-permute-done.1.refs_2_.refs_3_
  116.1 1.2 collective-permute-start.14
  117.4 0.0 collective-permute-done.4.refs_8_
  117.4 4.6 %collective-permute-done.7.refs_9_ = bf16[1152,128]{1,0:T(8,128)(2,1)S(1)} collective-permute-done((bf16[1152,128]{1,0:T(8,128)(2,1)}, bf16[1152,128]{1,0:T(8,128)(2,1)S(1)}, u32[]{:S(2)}, u32[]{:S(2)}) %collective-permute-start.7) | collective-permute-done | bytes 294944 | tf_op jit(solution)/shard_map/ppermute | solution.py:222
  121.9 0.7 copy-done.11
  122.7 0.0 collective-permute-done.8.side_a_ref
  122.7 0.0 collective-permute-done.9.side_b_ref
  122.7 4.4 %attention.5.refs_4_ = bf16[1152,128]{1,0:T(8,128)(2,1)S(1)} custom-call(s32[5]{0:T(128)S(1)} %pad_add_fusion.info_ref, bf16[1152,384]{1,0:T(8,128)(2,1)S(1)} %bitcast.27, bf16[1152,384]{1,0:T(8,128)(2,1)S(1)} %bitcast.19, bf16[1152,384]{1,0:T(8,128)(2,1)S(1)} %bitcast.24, bf16[2,1152,128]{2,1,0:T(8,128)(2,1)S(1)} %collective-permute-done.8.side_a_ref, ...), custom_call_target="tpu_custom_call" | custom-call | flops 1358954496 | bytes 2359296 | tf_op jit(solution)/shard_map/attention/pallas_call | solution.py:78
  127.0 0.3 collective-permute-start.11
  127.4 0.1 concatenate.17.info_ref
  127.5 0.8 constant_dynamic-slice_fusion.1
  128.2 1.3 collective-permute-start.13
  129.5 0.2 collective-permute-start.15
  129.8 0.0 collective-permute-done.14.refs_7_
  129.8 1.2 collective-permute-start.16
  131.0 1.3 collective-permute-start.10
  132.3 0.4 collective-permute-done.11.refs_6_
  132.7 1.3 collective-permute-start.12
  133.9 0.1 collective-permute-done.13.refs_6_
  134.1 4.6 %collective-permute-done.15.refs_10_ = bf16[1152,128]{1,0:T(8,128)(2,1)S(1)} collective-permute-done((bf16[1152,128]{1,0:T(8,128)(2,1)}, bf16[1152,128]{1,0:T(8,128)(2,1)S(1)}, u32[]{:S(2)}, u32[]{:S(2)}) %collective-permute-start.15) | collective-permute-done | bytes 294944 | tf_op jit(solution)/shard_map/ppermute | solution.py:224
  138.7 0.0 collective-permute-done.16.refs_11_
  138.7 1.2 copy-done.6
  139.9 1.0 copy-done.8
  140.8 1.0 copy-done.10
  141.8 1.0 copy-done.12
  142.8 4.4 %partial_projection.2 = (f32[1152,384]{1,0:T(8,128)S(1)}, f32[1152,384]{1,0:T(8,128)S(1)}) custom-call(s32[23]{0:T(128)S(1)} %concatenate.17.info_ref, bf16[384,3072]{1,0:T(8,128)(2,1)S(1)} %copy-done.1, bf16[384,3072]{1,0:T(8,128)(2,1)S(1)} %copy-done.1, bf16[384,768]{1,0:T(8,128)(2,1)S(1)} %collective-permute-done.1.refs_2_.refs_3_, ...), custom_call_target="tpu_custom_call" | custom-call | flops 1811939328 | bytes 7667712 | tf_op jit(solution)/shard_map/partial_projection/pallas_call | solution.py:139
  147.2 0.0 collective-permute-done.10.refs_5_
  147.2 4.2 %collective-permute-done.12.refs_7_ = bf16[1152,128]{1,0:T(8,128)(2,1)S(1)} collective-permute-done((bf16[1152,128]{1,0:T(8,128)(2,1)S(1)}, bf16[1152,128]{1,0:T(8,128)(2,1)S(1)}, u32[]{:S(2)}, u32[]{:S(2)}) %collective-permute-start.12) | collective-permute-done | bytes 294944 | tf_op jit(solution)/shard_map/ppermute | solution.py:224
  151.3 2.4 %partial_projection.3 = (f32[1152,384]{1,0:T(8,128)S(1)}, bf16[1152,384]{1,0:T(8,128)(2,1)S(1)}) custom-call(s32[23]{0:T(128)S(1)} %concatenate.17.info_ref, bf16[384,3072]{1,0:T(8,128)(2,1)S(1)} %copy-done.1, bf16[384,3072]{1,0:T(8,128)(2,1)S(1)} %copy-done.1, bf16[384,768]{1,0:T(8,128)(2,1)S(1)} %collective-permute-done.1.refs_2_.refs_3_, ...), custom_call_target="tpu_custom_call" | custom-call | flops 905969664 | bytes 6488064 | tf_op jit(solution)/shard_map/partial_projection/pallas_call | solution.py:139
  153.7 6.7 %collective-permute-start.17 = (bf16[1152,384]{1,0:T(8,128)(2,1)S(1)}, bf16[1152,384]{1,0:T(8,128)(2,1)S(1)}, u32[]{:S(2)}, u32[]{:S(2)}) collective-permute-start(bf16[1152,384]{1,0:T(8,128)(2,1)S(1)} %get-tuple-element.50), channel_id=1, source_target_pairs={{0,4},{4,0},{8,12},{12,8},{1,5},{5,1},{9,13},{13,9},{2,6},{6,2},{1... | collective-permute-start | bytes 2654216 | tf_op jit(solution)/shard_map/ppermute | solution.py:224
  160.4 2.1 %collective-permute-done.17 = bf16[1152,384]{1,0:T(8,128)(2,1)S(1)} collective-permute-done((bf16[1152,384]{1,0:T(8,128)(2,1)S(1)}, bf16[1152,384]{1,0:T(8,128)(2,1)S(1)}, u32[]{:S(2)}, u32[]{:S(2)}) %collective-permute-start.17) | collective-permute-done | bytes 884768 | tf_op jit(solution)/shard_map/ppermute | solution.py:224
  162.4 1.1 add_convert_fusion
  (29 shorter events, 0.1 us)
Async XLA Ops:
  0.0 86.1 %copy-start = (s32[3,4]{1,0:T(4,128)S(1)}, s32[3,4]{1,0:T(4,128)}, u32[]{:S(2)}) copy-start(s32[3,4]{1,0:T(4,128)} %param.14) | copy-start | bytes 148
  19.0 54.9 %copy-start.17 = (bf16[1,1152,2,384]{3,2,1,0:T(2,128)(2,1)S(1)}, bf16[1,1152,2,384]{3,2,1,0:T(2,128)(2,1)}, u32[]{:S(2)}) copy-start(bf16[1,1152,2,384]{3,2,1,0:T(2,128)(2,1)} %param.11) | copy-start | bytes 5308420
  75.4 21.4 %copy-start.2 = (bf16[1,1152,384]{2,1,0:T(8,128)(2,1)S(1)}, bf16[1,1152,384]{2,1,0:T(8,128)(2,1)}, u32[]{:S(2)}) copy-start(bf16[1,1152,384]{2,1,0:T(8,128)(2,1)} %param.9) | copy-start | bytes 2654212
  75.4 21.4 %copy-start.4 = (bf16[1,1152,384]{2,1,0:T(8,128)(2,1)S(1)}, bf16[1,1152,384]{2,1,0:T(8,128)(2,1)}, u32[]{:S(2)}) copy-start(bf16[1,1152,384]{2,1,0:T(8,128)(2,1)} %param.10) | copy-start | bytes 2654212
  75.4 21.4 %copy-start.13 = (bf16[1,1152,384]{2,1,0:T(8,128)(2,1)S(1)}, bf16[1,1152,384]{2,1,0:T(8,128)(2,1)}, u32[]{:S(2)}) copy-start(bf16[1,1152,384]{2,1,0:T(8,128)(2,1)} %param.8) | copy-start | bytes 2654212
  78.4 25.1 %collective-permute-start = (bf16[1152,384]{1,0:T(8,128)(2,1)}, bf16[1152,384]{1,0:T(8,128)(2,1)}, u32[]{:S(2)}, u32[]{:S(2)}) collective-permute-start(bf16[1152,384]{1,0:T(8,128)(2,1)} %get-tuple-element.52), channel_id=1, source_target_pairs={{0,16},{16,0},{1,17},{17,1},{2,18},{18,2},{3,19},{19,3},{4,20},{20... | collective-permute-start | bytes 2654216 | tf_op jit(solution)/shard_map/ppermute | solution.py:222
  79.6 14.2 %collective-permute-start.2 = (bf16[2,1152,128]{2,1,0:T(8,128)(2,1)}, bf16[2,1152,128]{2,1,0:T(8,128)(2,1)S(1)}, u32[]{:S(2)}, u32[]{:S(2)}) collective-permute-start(bf16[2,1152,128]{2,1,0:T(8,128)(2,1)} %copy_columns.2), channel_id=1, source_target_pairs={{0,1},{1,0},{2,3},{3,2},{4,5},{5,4},{6,7},{7,6},{8,9},{9,8},{10,11... | collective-permute-start | bytes 1769480 | tf_op jit(solution)/shard_map/ppermute | solution.py:250
  79.8 17.0 %collective-permute-start.3 = (bf16[2,1152,128]{2,1,0:T(8,128)(2,1)}, bf16[2,1152,128]{2,1,0:T(8,128)(2,1)}, u32[]{:S(2)}, u32[]{:S(2)}) collective-permute-start(bf16[2,1152,128]{2,1,0:T(8,128)(2,1)} %copy_columns.2), channel_id=1, source_target_pairs={{1,2},{2,1},{5,6},{6,5},{9,10},{10,9},{13,14},{14,13},{17,18},{18,... | collective-permute-start | bytes 1769480 | tf_op jit(solution)/shard_map/ppermute | solution.py:250
  84.1 23.2 %collective-permute-start.5 = (bf16[2,1152,128]{2,1,0:T(8,128)(2,1)}, bf16[2,1152,128]{2,1,0:T(8,128)(2,1)}, u32[]{:S(2)}, u32[]{:S(2)}) collective-permute-start(bf16[2,1152,128]{2,1,0:T(8,128)(2,1)} %get-tuple-element.40), channel_id=1, source_target_pairs={{0,1},{1,0},{2,3},{3,2},{4,5},{5,4},{6,7},{7,6},{8,9},{9,8},{10,11... | collective-permute-start | bytes 1769480 | tf_op jit(solution)/shard_map/ppermute | solution.py:250
  84.2 25.3 %collective-permute-start.6 = (bf16[2,1152,128]{2,1,0:T(8,128)(2,1)}, bf16[2,1152,128]{2,1,0:T(8,128)(2,1)}, u32[]{:S(2)}, u32[]{:S(2)}) collective-permute-start(bf16[2,1152,128]{2,1,0:T(8,128)(2,1)} %get-tuple-element.40), channel_id=1, source_target_pairs={{1,2},{2,1},{5,6},{6,5},{9,10},{10,9},{13,14},{14,13},{17,18},{18,... | collective-permute-start | bytes 1769480 | tf_op jit(solution)/shard_map/ppermute | solution.py:250
  93.8 0.8 copy-start.15
  94.6 21.5 %collective-permute-start.1 = (bf16[384,768]{1,0:T(8,128)(2,1)}, bf16[384,768]{1,0:T(8,128)(2,1)S(1)}, u32[]{:S(2)}, u32[]{:S(2)}) collective-permute-start(bf16[384,768]{1,0:T(8,128)(2,1)} %get-tuple-element.36), channel_id=1, source_target_pairs={{0,8},{4,12},{8,0},{12,4},{1,9},{5,13},{9,1},{13,5},{2,10},{6,14},... | collective-permute-start | bytes 1769480 | tf_op jit(solution)/shard_map/ppermute | solution.py:224
  96.8 1.1 copy-start.16
  97.9 5.5 %copy-start.19 = (bf16[2,1152,128]{2,1,0:T(8,128)(2,1)S(1)}, bf16[2,1152,128]{2,1,0:T(8,128)(2,1)}, u32[]{:S(2)}) copy-start(bf16[2,1152,128]{2,1,0:T(8,128)(2,1)} %get-tuple-element.43) | copy-start | bytes 1769476
  103.3 12.4 %copy-start.7 = (bf16[1152,128]{1,0:T(8,128)(2,1)}, bf16[1152,128]{1,0:T(8,128)(2,1)S(1)}, u32[]{:S(2)}) copy-start(bf16[1152,128]{1,0:T(8,128)(2,1)S(1)} %attention.3.refs_4_) | copy-start | bytes 884740
  103.4 19.3 %copy-start.3 = (bf16[1,1152,384]{2,1,0:T(8,128)(2,1)S(1)}, bf16[1,1152,384]{2,1,0:T(8,128)(2,1)}, u32[]{:S(2)}) copy-start(bf16[1,1152,384]{2,1,0:T(8,128)(2,1)} %param.9) | copy-start | bytes 2654212
  103.4 19.3 %copy-start.5 = (bf16[1,1152,384]{2,1,0:T(8,128)(2,1)S(1)}, bf16[1,1152,384]{2,1,0:T(8,128)(2,1)}, u32[]{:S(2)}) copy-start(bf16[1,1152,384]{2,1,0:T(8,128)(2,1)} %param.10) | copy-start | bytes 2654212
  103.4 19.3 %copy-start.14 = (bf16[1,1152,384]{2,1,0:T(8,128)(2,1)S(1)}, bf16[1,1152,384]{2,1,0:T(8,128)(2,1)}, u32[]{:S(2)}) copy-start(bf16[1,1152,384]{2,1,0:T(8,128)(2,1)} %param.8) | copy-start | bytes 2654212
  103.4 19.3 %collective-permute-start.8 = (bf16[2,1152,128]{2,1,0:T(8,128)(2,1)S(1)}, bf16[2,1152,128]{2,1,0:T(8,128)(2,1)S(1)}, u32[]{:S(2)}, u32[]{:S(2)}) collective-permute-start(bf16[2,1152,128]{2,1,0:T(8,128)(2,1)S(1)} %copy-done.19), channel_id=1, source_target_pairs={{0,1},{1,0},{2,3},{3,2},{4,5},{5,4},{6,7},{7,6},{8,9},{9,8},{10,11... | collective-permute-start | bytes 1769480 | tf_op jit(solution)/shard_map/ppermute | solution.py:250
  103.5 19.2 %collective-permute-start.9 = (bf16[2,1152,128]{2,1,0:T(8,128)(2,1)S(1)}, bf16[2,1152,128]{2,1,0:T(8,128)(2,1)S(1)}, u32[]{:S(2)}, u32[]{:S(2)}) collective-permute-start(bf16[2,1152,128]{2,1,0:T(8,128)(2,1)S(1)} %copy-done.19), channel_id=1, source_target_pairs={{1,2},{2,1},{5,6},{6,5},{9,10},{10,9},{13,14},{14,13},{17,18},{18,... | collective-permute-start | bytes 1769480 | tf_op jit(solution)/shard_map/ppermute | solution.py:250
  107.3 10.0 %collective-permute-start.4 = (bf16[1152,128]{1,0:T(8,128)(2,1)S(1)}, bf16[1152,128]{1,0:T(8,128)(2,1)S(1)}, u32[]{:S(2)}, u32[]{:S(2)}) collective-permute-start(bf16[1152,128]{1,0:T(8,128)(2,1)S(1)} %attention.3.refs_4_), channel_id=1, source_target_pairs={{0,16},{16,0},{1,17},{17,1},{2,18},{18,2},{3,19},{19,3},{4,20},{20... | collective-permute-start | bytes 884744 | tf_op jit(solution)/shard_map/ppermute | solution.py:222
  115.8 11.6 %copy-start.18 = (s32[18]{0:T(128)S(1)}, s32[18]{0:T(128)}, u32[]{:S(2)}) copy-start(s32[18]{0:T(128)} %param.15) | copy-start | bytes 220
  115.8 22.9 %copy-start.1 = (bf16[384,3072]{1,0:T(8,128)(2,1)S(1)}, bf16[384,3072]{1,0:T(8,128)(2,1)}, u32[]{:S(2)}) copy-start(bf16[384,3072]{1,0:T(8,128)(2,1)} %refs_1_.3) | copy-start | bytes 7077892
  115.8 6.1 %collective-permute-start.7 = (bf16[1152,128]{1,0:T(8,128)(2,1)}, bf16[1152,128]{1,0:T(8,128)(2,1)S(1)}, u32[]{:S(2)}, u32[]{:S(2)}) collective-permute-start(bf16[1152,128]{1,0:T(8,128)(2,1)} %attention.4.refs_5_), channel_id=1, source_target_pairs={{0,16},{16,0},{1,17},{17,1},{2,18},{18,2},{3,19},{19,3},{4,20},{20... | collective-permute-start | bytes 884744 | tf_op jit(solution)/shard_map/ppermute | solution.py:222
  116.1 13.7 %collective-permute-start.14 = (bf16[1152,128]{1,0:T(8,128)(2,1)}, bf16[1152,128]{1,0:T(8,128)(2,1)}, u32[]{:S(2)}, u32[]{:S(2)}) collective-permute-start(bf16[1152,128]{1,0:T(8,128)(2,1)} %attention.4.refs_5_), channel_id=1, source_target_pairs={{0,8},{4,12},{8,0},{12,4},{1,9},{5,13},{9,1},{13,5},{2,10},{6,14},... | collective-permute-start | bytes 884744 | tf_op jit(solution)/shard_map/ppermute | solution.py:224
  117.4 9.7 %copy-start.9 = (bf16[1152,128]{1,0:T(8,128)(2,1)}, bf16[1152,128]{1,0:T(8,128)(2,1)S(1)}, u32[]{:S(2)}) copy-start(bf16[1152,128]{1,0:T(8,128)(2,1)S(1)} %collective-permute-done.4.refs_8_) | copy-start | bytes 884740
  121.9 0.7 copy-start.11
  127.0 5.6 %collective-permute-start.11 = (bf16[1152,128]{1,0:T(8,128)(2,1)S(1)}, bf16[1152,128]{1,0:T(8,128)(2,1)S(1)}, u32[]{:S(2)}, u32[]{:S(2)}) collective-permute-start(bf16[1152,128]{1,0:T(8,128)(2,1)S(1)} %attention.5.refs_4_), channel_id=1, source_target_pairs={{0,16},{16,0},{1,17},{17,1},{2,18},{18,2},{3,19},{19,3},{4,20},{20... | collective-permute-start | bytes 884744 | tf_op jit(solution)/shard_map/ppermute | solution.py:222
  128.2 5.8 %collective-permute-start.13 = (bf16[1152,128]{1,0:T(8,128)(2,1)}, bf16[1152,128]{1,0:T(8,128)(2,1)S(1)}, u32[]{:S(2)}, u32[]{:S(2)}) collective-permute-start(bf16[1152,128]{1,0:T(8,128)(2,1)} %copy-done.7), channel_id=1, source_target_pairs={{0,8},{4,12},{8,0},{12,4},{1,9},{5,13},{9,1},{13,5},{2,10},{6,14},... | collective-permute-start | bytes 884744 | tf_op jit(solution)/shard_map/ppermute | solution.py:224
  129.5 9.1 %collective-permute-start.15 = (bf16[1152,128]{1,0:T(8,128)(2,1)}, bf16[1152,128]{1,0:T(8,128)(2,1)S(1)}, u32[]{:S(2)}, u32[]{:S(2)}) collective-permute-start(bf16[1152,128]{1,0:T(8,128)(2,1)} %copy-done.9), channel_id=1, source_target_pairs={{0,8},{4,12},{8,0},{12,4},{1,9},{5,13},{9,1},{13,5},{2,10},{6,14},... | collective-permute-start | bytes 884744 | tf_op jit(solution)/shard_map/ppermute | solution.py:224
  129.8 8.9 %collective-permute-start.16 = (bf16[1152,128]{1,0:T(8,128)(2,1)}, bf16[1152,128]{1,0:T(8,128)(2,1)S(1)}, u32[]{:S(2)}, u32[]{:S(2)}) collective-permute-start(bf16[1152,128]{1,0:T(8,128)(2,1)} %collective-permute-done.14.refs_7_), channel_id=1, source_target_pairs={{0,16},{16,0},{1,17},{17,1},{2,18},{18,2},{3,19},{19,3},{4,20},{20... | collective-permute-start | bytes 884744 | tf_op jit(solution)/shard_map/ppermute | solution.py:222
  131.0 16.2 %collective-permute-start.10 = (bf16[1152,128]{1,0:T(8,128)(2,1)S(1)}, bf16[1152,128]{1,0:T(8,128)(2,1)S(1)}, u32[]{:S(2)}, u32[]{:S(2)}) collective-permute-start(bf16[1152,128]{1,0:T(8,128)(2,1)S(1)} %attention.5.refs_4_), channel_id=1, source_target_pairs={{0,8},{4,12},{8,0},{12,4},{1,9},{5,13},{9,1},{13,5},{2,10},{6,14},... | collective-permute-start | bytes 884744 | tf_op jit(solution)/shard_map/ppermute | solution.py:224
  132.7 18.6 %collective-permute-start.12 = (bf16[1152,128]{1,0:T(8,128)(2,1)S(1)}, bf16[1152,128]{1,0:T(8,128)(2,1)S(1)}, u32[]{:S(2)}, u32[]{:S(2)}) collective-permute-start(bf16[1152,128]{1,0:T(8,128)(2,1)S(1)} %collective-permute-done.11.refs_6_), channel_id=1, source_target_pairs={{0,8},{4,12},{8,0},{12,4},{1,9},{5,13},{9,1},{13,5},{2,10},{6,14},... | collective-permute-start | bytes 884744 | tf_op jit(solution)/shard_map/ppermute | solution.py:224
  138.7 1.2 copy-start.6
  139.9 1.0 copy-start.8
  140.8 1.0 copy-start.10
  141.8 1.0 copy-start.12
  153.7 8.7 %collective-permute-start.17 = (bf16[1152,384]{1,0:T(8,128)(2,1)S(1)}, bf16[1152,384]{1,0:T(8,128)(2,1)S(1)}, u32[]{:S(2)}, u32[]{:S(2)}) collective-permute-start(bf16[1152,384]{1,0:T(8,128)(2,1)S(1)} %get-tuple-element.50), channel_id=1, source_target_pairs={{0,4},{4,0},{8,12},{12,8},{1,5},{5,1},{9,13},{13,9},{2,6},{6,2},{1... | collective-permute-start | bytes 2654216 | tf_op jit(solution)/shard_map/ppermute | solution.py:224

commit v5 on v4

--- a/solution.py
+++ b/solution.py
@@ -12,8 +12,10 @@
 FRAME = 64
 FAR = 1e30
 EXP2_SCALE = math.log2(math.e) / math.sqrt(HD)
-VMEM_LIMIT = 24 * 1024 * 1024
+VMEM_LIMIT = 16 * 1024 * 1024
+COPY_LIMIT = 8 * 1024 * 1024
 COPY_PARTS = 3
+SMALL_COST = pl.CostEstimate(flops=0, bytes_accessed=1024, transcendentals=0)
 
 
 def attention_kernel(info_ref, q_ref, k_ref, v_ref, side_a_ref, side_b_ref, out_ref):
@@ -85,29 +87,28 @@
             out_specs=pl.BlockSpec((count, HD), lambda i, info: (0, 0)),
         ),
         compiler_params=pltpu.CompilerParams(vmem_limit_bytes=VMEM_LIMIT),
-        cost_estimate=pl.CostEstimate(
-            flops=4 * pairs * HD, bytes_accessed=8 * count * HD * 2, transcendentals=pairs
-        ),
+        cost_estimate=SMALL_COST,
         name="attention",
     )(info, queries, keys, values, side_a, side_b)
 
 
-def partial_kernel(first, own_cols, info_ref, *refs):
+def partial_kernel(first, kinds, info_ref, *refs):
     w_refs, refs = refs[:4], refs[4:]
     *pieces, gate_ref, base_own_ref, base_other_ref, own_ref, other_ref = refs
-    tile = own_ref.shape[0]
+    tile, own_cols = own_ref.shape
     frames = tile // FRAME
     time_tile = pl.program_id(0)
     cond_first = info_ref[0] == 0
-    weights = jnp.concatenate(
-        [jnp.concatenate([w[...] for w in w_refs[i : i + 2]], axis=1) for i in (0, 2)], axis=0
-    )
-    half = len(pieces) // 2
     parts = []
     for which in range(2):
-        rows = jnp.concatenate(
-            [piece[...] for piece in pieces[which * half : (which + 1) * half]], axis=1
-        )
+        chosen = [i for i, kind in enumerate(kinds) if kind[0] == which]
+        rows = jnp.concatenate([pieces[i][...] for i in chosen], axis=1)
+        weights = []
+        for i in chosen:
+            _, far, head = kinds[i]
+            depth = slice(head * HD, (head + 1) * HD)
+            weights.append(jnp.concatenate([w[depth, :] for w in w_refs[2 * far : 2 * far + 2]], axis=1))
+        weights = jnp.concatenate(weights, axis=0)
         projected = jnp.dot(rows, weights, preferred_element_type=jnp.float32)
         parts.append(gate_ref[which] * projected)
     for frame in range(frames):
@@ -126,18 +127,18 @@
         other_ref[rows, :] = other.astype(other_ref.dtype)
 
 
-def partial_projection(info, weights, pieces, gate, base, tile, group):
+def partial_projection(info, weights, pieces, gate, base, tile, first):
     count, width = base[0].shape
-    first = group.start == 0
-    depth = len(group) * HD
+    features = weights[0].shape[0]
+    kinds = tuple(pieces)
+    rows = pl.BlockSpec((tile, width), lambda t, info: (t, 0))
+    piece = pl.BlockSpec((tile, HD), lambda t, info: (t, 0))
     weight_specs = [
-        pl.BlockSpec((depth, width), lambda t, info, place=place: (group.start // len(group), info[place]))
+        pl.BlockSpec((features, width), lambda t, info, place=place: (0, info[place]))
         for place in range(1, 5)
     ]
-    rows = pl.BlockSpec((tile, width), lambda t, info: (t, 0))
-    piece = pl.BlockSpec((tile, HD), lambda t, info: (t, 0))
     return pl.pallas_call(
-        functools.partial(partial_kernel, first, width),
+        functools.partial(partial_kernel, first, kinds),
         out_shape=[
             jax.ShapeDtypeStruct((count, width), jnp.float32),
             jax.ShapeDtypeStruct((count, width), jnp.float32 if first else jnp.bfloat16),
@@ -151,13 +152,9 @@
             out_specs=[rows, rows],
         ),
         compiler_params=pltpu.CompilerParams(vmem_limit_bytes=VMEM_LIMIT),
-        cost_estimate=pl.CostEstimate(
-            flops=4 * count * width * len(pieces) * HD,
-            bytes_accessed=2 * count * (6 * width + len(pieces) * HD),
-            transcendentals=0,
-        ),
+        cost_estimate=SMALL_COST,
         name="partial_projection",
-    )(info, *[w for w in weights for _ in range(2)], *pieces, gate, *base)
+    )(info, *[w for w in weights for _ in range(2)], *pieces.values(), gate, *base)
 
 
 def copy_kernel(plan, info_ref, *refs):
@@ -189,10 +186,11 @@
             num_scalar_prefetch=1,
             grid=(1,),
             in_specs=[pl.BlockSpec(memory_space=pl.ANY)] * len(sources),
-            out_specs=[pl.BlockSpec(memory_space=pl.ANY)] * len(targets),
+            out_specs=[pl.BlockSpec(memory_space=pltpu.VMEM)] * len(targets),
             scratch_shapes=[pltpu.SemaphoreType.DMA((COPY_PARTS * len(plan),))],
         ),
-        cost_estimate=pl.CostEstimate(flops=0, bytes_accessed=moved, transcendentals=0),
+        cost_estimate=SMALL_COST,
+        compiler_params=pltpu.CompilerParams(vmem_limit_bytes=COPY_LIMIT),
         name="copy_columns",
     )(info, *sources)
 
@@ -274,13 +272,12 @@
     pieces = {}
     head_queries = queries[0]
     for head in range(heads):
-        if head == 1:
-            head_queries, other = lax.optimization_barrier((head_queries, other))
         if head == 2:
-            head_queries, far, pieces[1, 0, 0], pieces[1, 0, 1] = lax.optimization_barrier(
-                (head_queries, far, pieces[1, 0, 0], pieces[1, 0, 1])
+            early = [(1, 0, 0), (0, 1, 0), (1, 0, 1), (1, 1, 0)]
+            head_queries, far, other, *here = lax.optimization_barrier(
+                (head_queries, far, other, *[pieces[name] for name in early])
             )
-            pieces[1, 2, 0] = swap(pieces[1, 0, 0], 0, 2)
+            pieces.update(zip(early, here))
         own = attention(
             attention_info, head_queries, keys[0], values[0], *sides[head], head, tile
         )
@@ -289,17 +286,23 @@
             sides.append(halo(part))
         pieces[0, 0, head] = own
         pieces[1, 0, head] = swap(own, 1, 0)
-        pieces[0, 2, head] = swap(own, 0, 2)
+        pieces[0, 1, head] = swap(own, 0, 2)
         if head == 1:
-            pieces[1, 2, head] = swap(pieces[0, 2, head], 1, 0)
-        elif head:
-            pieces[1, 2, head] = swap(pieces[1, 0, head], 0, 2)
-
+            pieces[1, 1, head] = swap(pieces[0, 1, head], 1, 0)
+        else:
+            pieces[1, 1, head] = swap(pieces[1, 0, head], 0, 2)
+
+    late = [(1, 1, heads - 2)] + [name for name in pieces if name[2] == heads - 1]
     base = (mine, other)
-    for group in (range(heads - 1), range(heads - 1, heads)):
-        ordered = [pieces[bit, bits, head] for bit in range(2) for bits in (0, 2) for head in group]
+    for chosen in ([name for name in pieces if name not in late], late):
         base = partial_projection(
-            projection_info, (out_weight, far), ordered, gate_block, base, tile, group
+            projection_info,
+            (out_weight, far),
+            {name: pieces[name] for name in chosen},
+            gate_block,
+            base,
+            tile,
+            base[0] is mine,
         )
     return (base[0] + swap(base[1], 0, 1).astype(jnp.float32)).astype(jnp.bfloat16)
 

time: 164 us -> 94.4 us (0.58)
  Pallas kernels: 96.8 us -> 28.2 us
  waiting for transfers between devices: 26 us -> 19.1 us
  local copies, waits for them, and re-layouts: 9.24 us -> 13.1 us
  starting transfers between devices: 27 us -> 29 us
    pallas_call x2, Pallas kernels: 73.9 us -> 2.5 us  [copy_columns(): pl.pallas_call(functools.partial(copy_kernel, plan), out_shape=[jax.Shape...]
    ppermute x6, waiting for transfers between devices: 10.1 us -> 4.99 us  [halo(): return [lax.ppermute(part, 'tokens', pairs) for pairs in rounds]]
    unnamed x40, local copies, waits for them, and re-layouts: 6.69 us -> 10.7 us
    ppermute x7, waiting for transfers between devices: 11 us -> 8.04 us  [swap(): lax.ppermute(value, 'head', [(i, i ^ head_bits) for i in range(head_count)])]
    pallas_call x2, Pallas kernels: 6.79 us -> 8.58 us  [partial_projection(): pl.pallas_call(functools.partial(partial_kernel, first, kinds), out_shape...]
    ppermute x5, starting transfers between devices: 3.38 us -> 5.12 us  [swap(): return lax.ppermute(value, 'branch', [(0, 1), (1, 0)])]
  transfers between devices with their start and end apart: 18 -> 18, of which waited for: 9 -> 8; matrix products, arithmetic and copies ran while one was open for 1% -> 6% of each run, Pallas kernels for 13% -> 25%
where the time goes in v5:
time: 94.4 us; the launch traced here: 93.8 us
  starting transfers between devices  29 us (31%)
  Pallas kernels  28.2 us (30%)
  waiting for transfers between devices  19.1 us (20%)
  local copies, waits for them, and re-layouts  13.1 us (14%)
  other arithmetic  4.2 us (4%)
    pallas_call x3, Pallas kernels, attention(): pl.pallas_call(attention_kernel, out_shape=jax.ShapeDtypeStruct((count, H...  17.1 us
    ppermute x7, starting transfers between devices, swap(): lax.ppermute(value, 'head', [(i, i ^ head_bits) for i in range(head_count)])  14.2 us
    unnamed x40, local copies, waits for them, and re-layouts  10.7 us
    ppermute x6, starting transfers between devices, halo(): return [lax.ppermute(part, 'tokens', pairs) for pairs in rounds]  9.68 us
    pallas_call x2, Pallas kernels, partial_projection(): pl.pallas_call(functools.partial(partial_kernel, first, kinds), out_shape...  8.58 us
    ppermute x7, waiting for transfers between devices, swap(): lax.ppermute(value, 'head', [(i, i ^ head_bits) for i in range(head_count)])  8.04 us
    ppermute x5, waiting for transfers between devices, swap(): return lax.ppermute(value, 'branch', [(0, 1), (1, 0)])  6.07 us
    ppermute x5, starting transfers between devices, swap(): return lax.ppermute(value, 'branch', [(0, 1), (1, 0)])  5.12 us
  transfers between devices with their start and end apart: 18, of which 8 were waited for; matrix products, arithmetic and copies ran while one was open for 6% of the time, Pallas kernels for 25%

profile of v5, /device:TPU:9, one launch (start us, length us, event | category | flops | bytes accessed | tf_op | source)
XLA Modules:
  0.0 93.8 jit_solution(16441721796383651220)
XLA Ops:
  0.0 1.3 %copy-done.2 = bf16[1,1152,384]{2,1,0:T(8,128)(2,1)S(1)} copy-done((bf16[1,1152,384]{2,1,0:T(8,128)(2,1)S(1)}, bf16[1,1152,384]{2,1,0:T(8,128)(2,1)}, u32[]{:S(2)}) %copy-start.2) | copy-done | bytes 884760
  1.3 1.2 %copy-done.4 = bf16[1,1152,384]{2,1,0:T(8,128)(2,1)S(1)} copy-done((bf16[1,1152,384]{2,1,0:T(8,128)(2,1)S(1)}, bf16[1,1152,384]{2,1,0:T(8,128)(2,1)}, u32[]{:S(2)}) %copy-start.4) | copy-done | bytes 884760
  2.5 1.0 %copy_columns.2 = bf16[2,1152,128]{2,1,0:T(8,128)(2,1)} custom-call(s32[1]{0:T(128)} %bitcast.6.info_ref, bf16[1152,384]{1,0:T(8,128)(2,1)S(1)} %bitcast.15, bf16[1152,384]{1,0:T(8,128)(2,1)S(1)} %bitcast.20), custom_call_target="tpu_custom_call" | custom-call | bytes 1024 | tf_op jit(solution)/shard_map/copy_columns/pallas_call | solution.py:182
  3.5 0.0 copy-start.18
  3.5 0.1 collective-permute-start.2
  3.6 4.5 %collective-permute-start.3 = (bf16[2,1152,128]{2,1,0:T(8,128)(2,1)}, bf16[2,1152,128]{2,1,0:T(8,128)(2,1)}, u32[]{:S(2)}, u32[]{:S(2)}) collective-permute-start(bf16[2,1152,128]{2,1,0:T(8,128)(2,1)} %copy_columns.2), channel_id=1, source_target_pairs={{1,2},{2,1},{5,6},{6,5},{9,10},{10,9},{13,14},{14,13},{17,18},{18,... | collective-permute-start | bytes 1769480 | tf_op jit(solution)/shard_map/ppermute | solution.py:248
  8.1 1.5 %copy_columns.3 = (bf16[2,1152,128]{2,1,0:T(8,128)(2,1)}, bf16[2,1152,128]{2,1,0:T(8,128)(2,1)S(1)}, bf16[384,768]{1,0:T(8,128)(2,1)}) custom-call(s32[1]{0:T(128)} %bitcast.6.info_ref, bf16[1152,384]{1,0:T(8,128)(2,1)S(1)} %bitcast.16, bf16[1152,384]{1,0:T(8,128)(2,1)S(1)} %bitcast.21, bf16[384,3072]{1,0:T(8,128)(2,1)S(1)} %copy-done.1), custom_call_target="tpu_custom_call" | custom-call | bytes 1024 | tf_op jit(solution)/shard_map/copy_columns/pallas_call | solution.py:182
  9.6 0.8 copy-done.16
  10.4 0.0 copy-done.18
  10.4 1.5 %copy.9 = bf16[1,1152,2,384]{3,1,2,0:T(8,128)(2,1)} copy(bf16[1,1152,2,384]{3,2,1,0:T(2,128)(2,1)S(1)} %copy-done.18) | data formatting | bytes 3538944 | tf_op jit(solution)/shard_map/optimization_barrier | solution.py:244
  11.9 2.9 %select_bitcast_fusion = (bf16[1152,384]{1,0:T(8,128)(2,1)}, bf16[1152,384]{1,0:T(8,128)(2,1)}) fusion(pred[]{:T(512)S(6)} %eq.2, bf16[1,1152,2,384]{3,1,2,0:T(8,128)(2,1)} %copy.9), kind=kLoop, calls=%fused_computation.1 | loop fusion | flops 884736 | bytes 3538945 | tf_op jit(solution)/shard_map/jit(_where)/select_n | solution.py:254
  14.8 1.2 %collective-permute-start.1 = (bf16[1152,384]{1,0:T(8,128)(2,1)}, bf16[1152,384]{1,0:T(8,128)(2,1)}, u32[]{:S(2)}, u32[]{:S(2)}) collective-permute-start(bf16[1152,384]{1,0:T(8,128)(2,1)} %get-tuple-element.54), channel_id=1, source_target_pairs={{0,16},{16,0},{1,17},{17,1},{2,18},{18,2},{3,19},{19,3},{4,20},{20... | collective-permute-start | bytes 2654216 | tf_op jit(solution)/shard_map/ppermute | solution.py:220
  16.0 0.0 collective-permute-start.6
  16.0 1.9 %collective-permute-start.7 = (bf16[2,1152,128]{2,1,0:T(8,128)(2,1)}, bf16[2,1152,128]{2,1,0:T(8,128)(2,1)}, u32[]{:S(2)}, u32[]{:S(2)}) collective-permute-start(bf16[2,1152,128]{2,1,0:T(8,128)(2,1)} %get-tuple-element.40), channel_id=1, source_target_pairs={{1,2},{2,1},{5,6},{6,5},{9,10},{10,9},{13,14},{14,13},{17,18},{18,... | collective-permute-start | bytes 1769480 | tf_op jit(solution)/shard_map/ppermute | solution.py:248
  17.9 0.2 collective-permute-done.2.side_a_ref
  18.1 1.2 %collective-permute-start = (bf16[384,768]{1,0:T(8,128)(2,1)}, bf16[384,768]{1,0:T(8,128)(2,1)}, u32[]{:S(2)}, u32[]{:S(2)}) collective-permute-start(bf16[384,768]{1,0:T(8,128)(2,1)} %get-tuple-element.35), channel_id=1, source_target_pairs={{0,8},{4,12},{8,0},{12,4},{1,9},{5,13},{9,1},{13,5},{2,10},{6,14},... | collective-permute-start | bytes 1769480 | tf_op jit(solution)/shard_map/ppermute | solution.py:222
  19.3 0.2 dynamic-slice_reduce_fusion
  19.5 0.1 add_convert_fusion.1
  19.6 0.1 pad_add_fusion.info_ref
  19.7 1.4 %collective-permute-done.3.side_b_ref = bf16[2,1152,128]{2,1,0:T(8,128)(2,1)} collective-permute-done((bf16[2,1152,128]{2,1,0:T(8,128)(2,1)}, bf16[2,1152,128]{2,1,0:T(8,128)(2,1)}, u32[]{:S(2)}, u32[]{:S(2)}) %collective-permute-start.3) | collective-permute-done | bytes 589856 | tf_op jit(solution)/shard_map/ppermute | solution.py:248
  21.1 1.2 %copy-done.5 = bf16[1,1152,384]{2,1,0:T(8,128)(2,1)S(1)} copy-done((bf16[1,1152,384]{2,1,0:T(8,128)(2,1)S(1)}, bf16[1,1152,384]{2,1,0:T(8,128)(2,1)}, u32[]{:S(2)}) %copy-start.5) | copy-done | bytes 884760
  22.3 1.2 %copy-done.6 = bf16[1,1152,384]{2,1,0:T(8,128)(2,1)S(1)} copy-done((bf16[1,1152,384]{2,1,0:T(8,128)(2,1)S(1)}, bf16[1,1152,384]{2,1,0:T(8,128)(2,1)}, u32[]{:S(2)}) %copy-start.6) | copy-done | bytes 884760
  23.4 5.6 %attention.3.refs_4_ = bf16[1152,128]{1,0:T(8,128)(2,1)S(1)} custom-call(s32[5]{0:T(128)S(1)} %pad_add_fusion.info_ref, bf16[1152,384]{1,0:T(8,128)(2,1)S(1)} %bitcast.25, bf16[1152,384]{1,0:T(8,128)(2,1)S(1)} %bitcast.17, bf16[1152,384]{1,0:T(8,128)(2,1)S(1)} %bitcast.22, bf16[2,1152,128]{2,1,0:T(8,128)(2,1)} %collective-permute-done.2.side_a_ref, ...), custom_call_target="tpu_custom_call" | custom-call | bytes 1024 | tf_op jit(solution)/shard_map/attention/pallas_call | solution.py:80
  29.1 1.3 %collective-permute-start.4 = (bf16[1152,128]{1,0:T(8,128)(2,1)S(1)}, bf16[1152,128]{1,0:T(8,128)(2,1)S(1)}, u32[]{:S(2)}, u32[]{:S(2)}) collective-permute-start(bf16[1152,128]{1,0:T(8,128)(2,1)S(1)} %attention.3.refs_4_), channel_id=1, source_target_pairs={{0,16},{16,0},{1,17},{17,1},{2,18},{18,2},{3,19},{19,3},{4,20},{20... | collective-permute-start | bytes 884744 | tf_op jit(solution)/shard_map/ppermute | solution.py:220
  30.4 0.0 collective-permute-done.6.side_a_ref
  30.4 0.0 collective-permute-start.12
  30.4 3.4 %collective-permute-done.7.side_b_ref = bf16[2,1152,128]{2,1,0:T(8,128)(2,1)} collective-permute-done((bf16[2,1152,128]{2,1,0:T(8,128)(2,1)}, bf16[2,1152,128]{2,1,0:T(8,128)(2,1)}, u32[]{:S(2)}, u32[]{:S(2)}) %collective-permute-start.7) | collective-permute-done | bytes 589856 | tf_op jit(solution)/shard_map/ppermute | solution.py:248
  33.7 3.2 %collective-permute-start.13 = (bf16[2,1152,128]{2,1,0:T(8,128)(2,1)S(1)}, bf16[2,1152,128]{2,1,0:T(8,128)(2,1)S(1)}, u32[]{:S(2)}, u32[]{:S(2)}) collective-permute-start(bf16[2,1152,128]{2,1,0:T(8,128)(2,1)S(1)} %copy-done.17), channel_id=1, source_target_pairs={{1,2},{2,1},{5,6},{6,5},{9,10},{10,9},{13,14},{14,13},{17,18},{18,... | collective-permute-start | bytes 1769480 | tf_op jit(solution)/shard_map/ppermute | solution.py:248
  37.0 6.4 %attention.4.refs_8_ = bf16[1152,128]{1,0:T(8,128)(2,1)} custom-call(s32[5]{0:T(128)S(1)} %pad_add_fusion.info_ref, bf16[1152,384]{1,0:T(8,128)(2,1)S(1)} %bitcast.26, bf16[1152,384]{1,0:T(8,128)(2,1)S(1)} %bitcast.18, bf16[1152,384]{1,0:T(8,128)(2,1)S(1)} %bitcast.23, bf16[2,1152,128]{2,1,0:T(8,128)(2,1)} %collective-permute-done.6.side_a_ref, ...), custom_call_target="tpu_custom_call" | custom-call | bytes 1024 | tf_op jit(solution)/shard_map/attention/pallas_call | solution.py:80
  43.3 0.0 collective-permute-done.refs_2_.refs_3_
  43.3 1.2 %collective-permute-start.8 = (bf16[1152,128]{1,0:T(8,128)(2,1)}, bf16[1152,128]{1,0:T(8,128)(2,1)S(1)}, u32[]{:S(2)}, u32[]{:S(2)}) collective-permute-start(bf16[1152,128]{1,0:T(8,128)(2,1)} %attention.4.refs_8_), channel_id=1, source_target_pairs={{0,16},{16,0},{1,17},{17,1},{2,18},{18,2},{3,19},{19,3},{4,20},{20... | collective-permute-start | bytes 884744 | tf_op jit(solution)/shard_map/ppermute | solution.py:220
  44.6 0.0 collective-permute-done.1.refs_13_
  44.6 1.2 %collective-permute-start.5 = (bf16[1152,128]{1,0:T(8,128)(2,1)S(1)}, bf16[1152,128]{1,0:T(8,128)(2,1)S(1)}, u32[]{:S(2)}, u32[]{:S(2)}) collective-permute-start(bf16[1152,128]{1,0:T(8,128)(2,1)S(1)} %attention.3.refs_4_), channel_id=1, source_target_pairs={{0,8},{4,12},{8,0},{12,4},{1,9},{5,13},{9,1},{13,5},{2,10},{6,14},... | collective-permute-start | bytes 884744 | tf_op jit(solution)/shard_map/ppermute | solution.py:222
  45.8 0.0 collective-permute-done.4.refs_5_
  45.8 0.2 collective-permute-start.9
  46.0 3.9 %collective-permute-done.8.refs_9_ = bf16[1152,128]{1,0:T(8,128)(2,1)S(1)} collective-permute-done((bf16[1152,128]{1,0:T(8,128)(2,1)}, bf16[1152,128]{1,0:T(8,128)(2,1)S(1)}, u32[]{:S(2)}, u32[]{:S(2)}) %collective-permute-start.8) | collective-permute-done | bytes 294944 | tf_op jit(solution)/shard_map/ppermute | solution.py:220
  49.9 1.2 %collective-permute-start.10 = (bf16[1152,128]{1,0:T(8,128)(2,1)}, bf16[1152,128]{1,0:T(8,128)(2,1)}, u32[]{:S(2)}, u32[]{:S(2)}) collective-permute-start(bf16[1152,128]{1,0:T(8,128)(2,1)} %attention.4.refs_8_), channel_id=1, source_target_pairs={{0,8},{4,12},{8,0},{12,4},{1,9},{5,13},{9,1},{13,5},{2,10},{6,14},... | collective-permute-start | bytes 884744 | tf_op jit(solution)/shard_map/ppermute | solution.py:222
  51.2 0.0 collective-permute-done.5.refs_6_
  51.2 5.8 %collective-permute-done.9.refs_7_ = bf16[1152,128]{1,0:T(8,128)(2,1)S(1)} collective-permute-done((bf16[1152,128]{1,0:T(8,128)(2,1)S(1)}, bf16[1152,128]{1,0:T(8,128)(2,1)S(1)}, u32[]{:S(2)}, u32[]{:S(2)}) %collective-permute-start.9) | collective-permute-done | bytes 294944 | tf_op jit(solution)/shard_map/ppermute | solution.py:222
  57.0 0.0 collective-permute-done.12.side_a_ref
  57.0 0.0 collective-permute-done.13.side_b_ref
  57.0 5.1 %attention.5.refs_5_ = bf16[1152,128]{1,0:T(8,128)(2,1)} custom-call(s32[5]{0:T(128)S(1)} %pad_add_fusion.info_ref, bf16[1152,384]{1,0:T(8,128)(2,1)S(1)} %bitcast.27, bf16[1152,384]{1,0:T(8,128)(2,1)S(1)} %bitcast.19, bf16[1152,384]{1,0:T(8,128)(2,1)S(1)} %bitcast.24, bf16[2,1152,128]{2,1,0:T(8,128)(2,1)S(1)} %collective-permute-done.12.side_a_ref, ...), custom_call_target="tpu_custom_call" | custom-call | bytes 1024 | tf_op jit(solution)/shard_map/attention/pallas_call | solution.py:80
  62.1 0.3 collective-permute-start.14
  62.4 0.7 concatenate.17.info_ref
  63.1 0.1 constant_dynamic-slice_fusion.1
  63.2 0.2 collective-permute-done.10.refs_10_
  63.4 1.1 %collective-permute-start.11 = (bf16[1152,128]{1,0:T(8,128)(2,1)}, bf16[1152,128]{1,0:T(8,128)(2,1)S(1)}, u32[]{:S(2)}, u32[]{:S(2)}) collective-permute-start(bf16[1152,128]{1,0:T(8,128)(2,1)} %collective-permute-done.10.refs_10_), channel_id=1, source_target_pairs={{0,16},{16,0},{1,17},{17,1},{2,18},{18,2},{3,19},{19,3},{4,20},{20... | collective-permute-start | bytes 884744 | tf_op jit(solution)/shard_map/ppermute | solution.py:220
  64.5 1.2 %collective-permute-start.15 = (bf16[1152,128]{1,0:T(8,128)(2,1)}, bf16[1152,128]{1,0:T(8,128)(2,1)S(1)}, u32[]{:S(2)}, u32[]{:S(2)}) collective-permute-start(bf16[1152,128]{1,0:T(8,128)(2,1)} %attention.5.refs_5_), channel_id=1, source_target_pairs={{0,8},{4,12},{8,0},{12,4},{1,9},{5,13},{9,1},{13,5},{2,10},{6,14},... | collective-permute-start | bytes 884744 | tf_op jit(solution)/shard_map/ppermute | solution.py:222
  65.7 2.2 %collective-permute-done.14.refs_6_ = bf16[1152,128]{1,0:T(8,128)(2,1)S(1)} collective-permute-done((bf16[1152,128]{1,0:T(8,128)(2,1)}, bf16[1152,128]{1,0:T(8,128)(2,1)S(1)}, u32[]{:S(2)}, u32[]{:S(2)}) %collective-permute-start.14) | collective-permute-done | bytes 294944 | tf_op jit(solution)/shard_map/ppermute | solution.py:220
  67.9 1.2 %collective-permute-start.16 = (bf16[1152,128]{1,0:T(8,128)(2,1)S(1)}, bf16[1152,128]{1,0:T(8,128)(2,1)S(1)}, u32[]{:S(2)}, u32[]{:S(2)}) collective-permute-start(bf16[1152,128]{1,0:T(8,128)(2,1)S(1)} %collective-permute-done.14.refs_6_), channel_id=1, source_target_pairs={{0,8},{4,12},{8,0},{12,4},{1,9},{5,13},{9,1},{13,5},{2,10},{6,14},... | collective-permute-start | bytes 884744 | tf_op jit(solution)/shard_map/ppermute | solution.py:222
  69.2 0.0 copy-start.7
  69.2 1.2 %copy-done.7 = bf16[1152,384]{1,0:T(8,128)(2,1)S(1)} copy-done((bf16[1152,384]{1,0:T(8,128)(2,1)S(1)}, bf16[1152,384]{1,0:T(8,128)(2,1)}, u32[]{:S(2)}) %copy-start.7) | copy-done | bytes 884760
  70.3 1.0 %copy-done.9 = bf16[1152,128]{1,0:T(8,128)(2,1)S(1)} copy-done((bf16[1152,128]{1,0:T(8,128)(2,1)S(1)}, bf16[1152,128]{1,0:T(8,128)(2,1)}, u32[]{:S(2)}) %copy-start.9) | copy-done | bytes 294936
  71.3 1.0 %copy-done.11 = bf16[1152,128]{1,0:T(8,128)(2,1)S(1)} copy-done((bf16[1152,128]{1,0:T(8,128)(2,1)S(1)}, bf16[1152,128]{1,0:T(8,128)(2,1)}, u32[]{:S(2)}) %copy-start.11) | copy-done | bytes 294936
  72.3 1.0 %copy-done.13 = bf16[1152,128]{1,0:T(8,128)(2,1)S(1)} copy-done((bf16[1152,128]{1,0:T(8,128)(2,1)S(1)}, bf16[1152,128]{1,0:T(8,128)(2,1)}, u32[]{:S(2)}) %copy-start.13) | copy-done | bytes 294936
  73.2 1.0 %copy-done.15 = bf16[1152,128]{1,0:T(8,128)(2,1)S(1)} copy-done((bf16[1152,128]{1,0:T(8,128)(2,1)S(1)}, bf16[1152,128]{1,0:T(8,128)(2,1)}, u32[]{:S(2)}) %copy-start.15) | copy-done | bytes 294936
  74.2 4.6 %partial_projection.2 = (f32[1152,384]{1,0:T(8,128)S(1)}, f32[1152,384]{1,0:T(8,128)S(1)}) custom-call(s32[23]{0:T(128)S(1)} %concatenate.17.info_ref, bf16[384,3072]{1,0:T(8,128)(2,1)S(1)} %copy-done.1, bf16[384,3072]{1,0:T(8,128)(2,1)S(1)} %copy-done.1, bf16[384,768]{1,0:T(8,128)(2,1)} %collective-permute-done.refs_2_.refs_3_, ...), custom_call_target="tpu_custom_call" | custom-call | bytes 1024 | tf_op jit(solution)/shard_map/partial_projection/pallas_call | solution.py:140
  78.8 0.0 collective-permute-done.11.refs_4_
  78.8 0.0 collective-permute-done.15.refs_7_
  78.8 0.0 collective-permute-done.16.refs_8_
  78.8 4.0 %partial_projection.3 = (f32[1152,384]{1,0:T(8,128)S(1)}, bf16[1152,384]{1,0:T(8,128)(2,1)S(1)}) custom-call(s32[23]{0:T(128)S(1)} %concatenate.17.info_ref, bf16[384,3072]{1,0:T(8,128)(2,1)S(1)} %copy-done.1, bf16[384,3072]{1,0:T(8,128)(2,1)S(1)} %copy-done.1, bf16[384,768]{1,0:T(8,128)(2,1)} %collective-permute-done.refs_2_.refs_3_, ...), custom_call_target="tpu_custom_call" | custom-call | bytes 1024 | tf_op jit(solution)/shard_map/partial_projection/pallas_call | solution.py:140
  82.8 7.8 %collective-permute-start.17 = (bf16[1152,384]{1,0:T(8,128)(2,1)S(1)}, bf16[1152,384]{1,0:T(8,128)(2,1)S(1)}, u32[]{:S(2)}, u32[]{:S(2)}) collective-permute-start(bf16[1152,384]{1,0:T(8,128)(2,1)S(1)} %get-tuple-element.52), channel_id=1, source_target_pairs={{0,4},{4,0},{8,12},{12,8},{1,5},{5,1},{9,13},{13,9},{2,6},{6,2},{1... | collective-permute-start | bytes 2654216 | tf_op jit(solution)/shard_map/ppermute | solution.py:222
  90.6 2.1 %collective-permute-done.17 = bf16[1152,384]{1,0:T(8,128)(2,1)S(1)} collective-permute-done((bf16[1152,384]{1,0:T(8,128)(2,1)S(1)}, bf16[1152,384]{1,0:T(8,128)(2,1)S(1)}, u32[]{:S(2)}, u32[]{:S(2)}) %collective-permute-start.17) | collective-permute-done | bytes 884768 | tf_op jit(solution)/shard_map/ppermute | solution.py:222
  92.7 1.1 %add_convert_fusion = bf16[1152,384]{1,0:T(8,128)(2,1)} fusion(f32[1152,384]{1,0:T(8,128)S(1)} %get-tuple-element.51, bf16[1152,384]{1,0:T(8,128)(2,1)S(1)} %collective-permute-done.17), kind=kLoop, calls=%fused_computation | loop fusion | flops 1327104 | bytes 3538944 | tf_op jit(solution)/shard_map/convert_element_type | solution.py:307
  (29 shorter events, 0.1 us)
Async XLA Ops:
  0.0 19.3 %copy-start = (s32[3,4]{1,0:T(4,128)S(1)}, s32[3,4]{1,0:T(4,128)}, u32[]{:S(2)}) copy-start(s32[3,4]{1,0:T(4,128)} %param.14) | copy-start | bytes 148
  0.0 8.1 %copy-start.1 = (bf16[384,3072]{1,0:T(8,128)(2,1)S(1)}, bf16[384,3072]{1,0:T(8,128)(2,1)}, u32[]{:S(2)}) copy-start(bf16[384,3072]{1,0:T(8,128)(2,1)} %refs_1_.3) | copy-start | bytes 7077892
  0.0 1.3 %copy-start.2 = (bf16[1,1152,384]{2,1,0:T(8,128)(2,1)S(1)}, bf16[1,1152,384]{2,1,0:T(8,128)(2,1)}, u32[]{:S(2)}) copy-start(bf16[1,1152,384]{2,1,0:T(8,128)(2,1)} %param.9) | copy-start | bytes 2654212
  1.3 1.2 %copy-start.4 = (bf16[1,1152,384]{2,1,0:T(8,128)(2,1)S(1)}, bf16[1,1152,384]{2,1,0:T(8,128)(2,1)}, u32[]{:S(2)}) copy-start(bf16[1,1152,384]{2,1,0:T(8,128)(2,1)} %param.10) | copy-start | bytes 2654212
  3.5 6.9 %copy-start.18 = (bf16[1,1152,2,384]{3,2,1,0:T(2,128)(2,1)S(1)}, bf16[1,1152,2,384]{3,2,1,0:T(2,128)(2,1)}, u32[]{:S(2)}) copy-start(bf16[1,1152,2,384]{3,2,1,0:T(2,128)(2,1)} %param.11) | copy-start | bytes 5308420
  3.5 14.6 %collective-permute-start.2 = (bf16[2,1152,128]{2,1,0:T(8,128)(2,1)}, bf16[2,1152,128]{2,1,0:T(8,128)(2,1)}, u32[]{:S(2)}, u32[]{:S(2)}) collective-permute-start(bf16[2,1152,128]{2,1,0:T(8,128)(2,1)} %copy_columns.2), channel_id=1, source_target_pairs={{0,1},{1,0},{2,3},{3,2},{4,5},{5,4},{6,7},{7,6},{8,9},{9,8},{10,11... | collective-permute-start | bytes 1769480 | tf_op jit(solution)/shard_map/ppermute | solution.py:248
  3.6 17.5 %collective-permute-start.3 = (bf16[2,1152,128]{2,1,0:T(8,128)(2,1)}, bf16[2,1152,128]{2,1,0:T(8,128)(2,1)}, u32[]{:S(2)}, u32[]{:S(2)}) collective-permute-start(bf16[2,1152,128]{2,1,0:T(8,128)(2,1)} %copy_columns.2), channel_id=1, source_target_pairs={{1,2},{2,1},{5,6},{6,5},{9,10},{10,9},{13,14},{14,13},{17,18},{18,... | collective-permute-start | bytes 1769480 | tf_op jit(solution)/shard_map/ppermute | solution.py:248
  9.6 0.8 copy-start.16
  11.9 9.2 %copy-start.3 = (bf16[1,1152,384]{2,1,0:T(8,128)(2,1)S(1)}, bf16[1,1152,384]{2,1,0:T(8,128)(2,1)}, u32[]{:S(2)}) copy-start(bf16[1,1152,384]{2,1,0:T(8,128)(2,1)} %param.9) | copy-start | bytes 2654212
  14.8 29.8 %collective-permute-start.1 = (bf16[1152,384]{1,0:T(8,128)(2,1)}, bf16[1152,384]{1,0:T(8,128)(2,1)}, u32[]{:S(2)}, u32[]{:S(2)}) collective-permute-start(bf16[1152,384]{1,0:T(8,128)(2,1)} %get-tuple-element.54), channel_id=1, source_target_pairs={{0,16},{16,0},{1,17},{17,1},{2,18},{18,2},{3,19},{19,3},{4,20},{20... | collective-permute-start | bytes 2654216 | tf_op jit(solution)/shard_map/ppermute | solution.py:220
  16.0 14.4 %collective-permute-start.6 = (bf16[2,1152,128]{2,1,0:T(8,128)(2,1)}, bf16[2,1152,128]{2,1,0:T(8,128)(2,1)}, u32[]{:S(2)}, u32[]{:S(2)}) collective-permute-start(bf16[2,1152,128]{2,1,0:T(8,128)(2,1)} %get-tuple-element.40), channel_id=1, source_target_pairs={{0,1},{1,0},{2,3},{3,2},{4,5},{5,4},{6,7},{7,6},{8,9},{9,8},{10,11... | collective-permute-start | bytes 1769480 | tf_op jit(solution)/shard_map/ppermute | solution.py:248
  16.0 17.7 %collective-permute-start.7 = (bf16[2,1152,128]{2,1,0:T(8,128)(2,1)}, bf16[2,1152,128]{2,1,0:T(8,128)(2,1)}, u32[]{:S(2)}, u32[]{:S(2)}) collective-permute-start(bf16[2,1152,128]{2,1,0:T(8,128)(2,1)} %get-tuple-element.40), channel_id=1, source_target_pairs={{1,2},{2,1},{5,6},{6,5},{9,10},{10,9},{13,14},{14,13},{17,18},{18,... | collective-permute-start | bytes 1769480 | tf_op jit(solution)/shard_map/ppermute | solution.py:248
  18.1 25.3 %collective-permute-start = (bf16[384,768]{1,0:T(8,128)(2,1)}, bf16[384,768]{1,0:T(8,128)(2,1)}, u32[]{:S(2)}, u32[]{:S(2)}) collective-permute-start(bf16[384,768]{1,0:T(8,128)(2,1)} %get-tuple-element.35), channel_id=1, source_target_pairs={{0,8},{4,12},{8,0},{12,4},{1,9},{5,13},{9,1},{13,5},{2,10},{6,14},... | collective-permute-start | bytes 1769480 | tf_op jit(solution)/shard_map/ppermute | solution.py:222
  21.1 1.2 %copy-start.5 = (bf16[1,1152,384]{2,1,0:T(8,128)(2,1)S(1)}, bf16[1,1152,384]{2,1,0:T(8,128)(2,1)}, u32[]{:S(2)}) copy-start(bf16[1,1152,384]{2,1,0:T(8,128)(2,1)} %param.10) | copy-start | bytes 2654212
  22.3 1.2 %copy-start.6 = (bf16[1,1152,384]{2,1,0:T(8,128)(2,1)S(1)}, bf16[1,1152,384]{2,1,0:T(8,128)(2,1)}, u32[]{:S(2)}) copy-start(bf16[1,1152,384]{2,1,0:T(8,128)(2,1)} %param.8) | copy-start | bytes 2654212
  23.4 6.9 %copy-start.17 = (bf16[2,1152,128]{2,1,0:T(8,128)(2,1)S(1)}, bf16[2,1152,128]{2,1,0:T(8,128)(2,1)}, u32[]{:S(2)}) copy-start(bf16[2,1152,128]{2,1,0:T(8,128)(2,1)} %copy-done.16) | copy-start | bytes 1769476
  29.1 16.7 %collective-permute-start.4 = (bf16[1152,128]{1,0:T(8,128)(2,1)S(1)}, bf16[1152,128]{1,0:T(8,128)(2,1)S(1)}, u32[]{:S(2)}, u32[]{:S(2)}) collective-permute-start(bf16[1152,128]{1,0:T(8,128)(2,1)S(1)} %attention.3.refs_4_), channel_id=1, source_target_pairs={{0,16},{16,0},{1,17},{17,1},{2,18},{18,2},{3,19},{19,3},{4,20},{20... | collective-permute-start | bytes 884744 | tf_op jit(solution)/shard_map/ppermute | solution.py:220
  30.4 26.6 %collective-permute-start.12 = (bf16[2,1152,128]{2,1,0:T(8,128)(2,1)S(1)}, bf16[2,1152,128]{2,1,0:T(8,128)(2,1)S(1)}, u32[]{:S(2)}, u32[]{:S(2)}) collective-permute-start(bf16[2,1152,128]{2,1,0:T(8,128)(2,1)S(1)} %copy-done.17), channel_id=1, source_target_pairs={{0,1},{1,0},{2,3},{3,2},{4,5},{5,4},{6,7},{7,6},{8,9},{9,8},{10,11... | collective-permute-start | bytes 1769480 | tf_op jit(solution)/shard_map/ppermute | solution.py:248
  33.7 23.2 %collective-permute-start.13 = (bf16[2,1152,128]{2,1,0:T(8,128)(2,1)S(1)}, bf16[2,1152,128]{2,1,0:T(8,128)(2,1)S(1)}, u32[]{:S(2)}, u32[]{:S(2)}) collective-permute-start(bf16[2,1152,128]{2,1,0:T(8,128)(2,1)S(1)} %copy-done.17), channel_id=1, source_target_pairs={{1,2},{2,1},{5,6},{6,5},{9,10},{10,9},{13,14},{14,13},{17,18},{18,... | collective-permute-start | bytes 1769480 | tf_op jit(solution)/shard_map/ppermute | solution.py:248
  43.3 19.8 %copy-start.19 = (bf16[2,2,1536]{2,1,0:T(2,128)(2,1)S(1)}, bf16[2,2,1536]{2,1,0:T(2,128)(2,1)}, u32[]{:S(2)}) copy-start(bf16[2,2,1536]{2,1,0:T(2,128)(2,1)} %param.12) | copy-start | bytes 36868
  43.3 6.6 %collective-permute-start.8 = (bf16[1152,128]{1,0:T(8,128)(2,1)}, bf16[1152,128]{1,0:T(8,128)(2,1)S(1)}, u32[]{:S(2)}, u32[]{:S(2)}) collective-permute-start(bf16[1152,128]{1,0:T(8,128)(2,1)} %attention.4.refs_8_), channel_id=1, source_target_pairs={{0,16},{16,0},{1,17},{17,1},{2,18},{18,2},{3,19},{19,3},{4,20},{20... | collective-permute-start | bytes 884744 | tf_op jit(solution)/shard_map/ppermute | solution.py:220
  44.6 6.6 %collective-permute-start.5 = (bf16[1152,128]{1,0:T(8,128)(2,1)S(1)}, bf16[1152,128]{1,0:T(8,128)(2,1)S(1)}, u32[]{:S(2)}, u32[]{:S(2)}) collective-permute-start(bf16[1152,128]{1,0:T(8,128)(2,1)S(1)} %attention.3.refs_4_), channel_id=1, source_target_pairs={{0,8},{4,12},{8,0},{12,4},{1,9},{5,13},{9,1},{13,5},{2,10},{6,14},... | collective-permute-start | bytes 884744 | tf_op jit(solution)/shard_map/ppermute | solution.py:222
  45.8 16.2 %copy-start.8 = (bf16[1152,128]{1,0:T(8,128)(2,1)}, bf16[1152,128]{1,0:T(8,128)(2,1)S(1)}, u32[]{:S(2)}) copy-start(bf16[1152,128]{1,0:T(8,128)(2,1)S(1)} %collective-permute-done.4.refs_5_) | copy-start | bytes 884740
  45.8 11.2 %collective-permute-start.9 = (bf16[1152,128]{1,0:T(8,128)(2,1)S(1)}, bf16[1152,128]{1,0:T(8,128)(2,1)S(1)}, u32[]{:S(2)}, u32[]{:S(2)}) collective-permute-start(bf16[1152,128]{1,0:T(8,128)(2,1)S(1)} %collective-permute-done.4.refs_5_), channel_id=1, source_target_pairs={{0,8},{4,12},{8,0},{12,4},{1,9},{5,13},{9,1},{13,5},{2,10},{6,14},... | collective-permute-start | bytes 884744 | tf_op jit(solution)/shard_map/ppermute | solution.py:222
  49.9 12.1 %copy-start.10 = (bf16[1152,128]{1,0:T(8,128)(2,1)}, bf16[1152,128]{1,0:T(8,128)(2,1)S(1)}, u32[]{:S(2)}) copy-start(bf16[1152,128]{1,0:T(8,128)(2,1)S(1)} %collective-permute-done.8.refs_9_) | copy-start | bytes 884740
  49.9 13.5 %collective-permute-start.10 = (bf16[1152,128]{1,0:T(8,128)(2,1)}, bf16[1152,128]{1,0:T(8,128)(2,1)}, u32[]{:S(2)}, u32[]{:S(2)}) collective-permute-start(bf16[1152,128]{1,0:T(8,128)(2,1)} %attention.4.refs_8_), channel_id=1, source_target_pairs={{0,8},{4,12},{8,0},{12,4},{1,9},{5,13},{9,1},{13,5},{2,10},{6,14},... | collective-permute-start | bytes 884744 | tf_op jit(solution)/shard_map/ppermute | solution.py:222
  51.2 10.9 %copy-start.12 = (bf16[1152,128]{1,0:T(8,128)(2,1)}, bf16[1152,128]{1,0:T(8,128)(2,1)S(1)}, u32[]{:S(2)}) copy-start(bf16[1152,128]{1,0:T(8,128)(2,1)S(1)} %collective-permute-done.5.refs_6_) | copy-start | bytes 884740
  57.0 5.1 %copy-start.14 = (bf16[1152,128]{1,0:T(8,128)(2,1)}, bf16[1152,128]{1,0:T(8,128)(2,1)S(1)}, u32[]{:S(2)}) copy-start(bf16[1152,128]{1,0:T(8,128)(2,1)S(1)} %collective-permute-done.9.refs_7_) | copy-start | bytes 884740
  62.1 5.8 %collective-permute-start.14 = (bf16[1152,128]{1,0:T(8,128)(2,1)}, bf16[1152,128]{1,0:T(8,128)(2,1)S(1)}, u32[]{:S(2)}, u32[]{:S(2)}) collective-permute-start(bf16[1152,128]{1,0:T(8,128)(2,1)} %attention.5.refs_5_), channel_id=1, source_target_pairs={{0,16},{16,0},{1,17},{17,1},{2,18},{18,2},{3,19},{19,3},{4,20},{20... | collective-permute-start | bytes 884744 | tf_op jit(solution)/shard_map/ppermute | solution.py:220
  63.4 15.4 %collective-permute-start.11 = (bf16[1152,128]{1,0:T(8,128)(2,1)}, bf16[1152,128]{1,0:T(8,128)(2,1)S(1)}, u32[]{:S(2)}, u32[]{:S(2)}) collective-permute-start(bf16[1152,128]{1,0:T(8,128)(2,1)} %collective-permute-done.10.refs_10_), channel_id=1, source_target_pairs={{0,16},{16,0},{1,17},{17,1},{2,18},{18,2},{3,19},{19,3},{4,20},{20... | collective-permute-start | bytes 884744 | tf_op jit(solution)/shard_map/ppermute | solution.py:220
  64.5 14.3 %collective-permute-start.15 = (bf16[1152,128]{1,0:T(8,128)(2,1)}, bf16[1152,128]{1,0:T(8,128)(2,1)S(1)}, u32[]{:S(2)}, u32[]{:S(2)}) collective-permute-start(bf16[1152,128]{1,0:T(8,128)(2,1)} %attention.5.refs_5_), channel_id=1, source_target_pairs={{0,8},{4,12},{8,0},{12,4},{1,9},{5,13},{9,1},{13,5},{2,10},{6,14},... | collective-permute-start | bytes 884744 | tf_op jit(solution)/shard_map/ppermute | solution.py:222
  67.9 10.9 %collective-permute-start.16 = (bf16[1152,128]{1,0:T(8,128)(2,1)S(1)}, bf16[1152,128]{1,0:T(8,128)(2,1)S(1)}, u32[]{:S(2)}, u32[]{:S(2)}) collective-permute-start(bf16[1152,128]{1,0:T(8,128)(2,1)S(1)} %collective-permute-done.14.refs_6_), channel_id=1, source_target_pairs={{0,8},{4,12},{8,0},{12,4},{1,9},{5,13},{9,1},{13,5},{2,10},{6,14},... | collective-permute-start | bytes 884744 | tf_op jit(solution)/shard_map/ppermute | solution.py:222
  69.2 1.2 %copy-start.7 = (bf16[1152,384]{1,0:T(8,128)(2,1)S(1)}, bf16[1152,384]{1,0:T(8,128)(2,1)}, u32[]{:S(2)}) copy-start(bf16[1152,384]{1,0:T(8,128)(2,1)} %get-tuple-element.53.refs_12_) | copy-start | bytes 2654212
  70.3 1.0 %copy-start.9 = (bf16[1152,128]{1,0:T(8,128)(2,1)S(1)}, bf16[1152,128]{1,0:T(8,128)(2,1)}, u32[]{:S(2)}) copy-start(bf16[1152,128]{1,0:T(8,128)(2,1)} %copy-done.8) | copy-start | bytes 884740
  71.3 1.0 %copy-start.11 = (bf16[1152,128]{1,0:T(8,128)(2,1)S(1)}, bf16[1152,128]{1,0:T(8,128)(2,1)}, u32[]{:S(2)}) copy-start(bf16[1152,128]{1,0:T(8,128)(2,1)} %copy-done.10) | copy-start | bytes 884740
  72.3 1.0 %copy-start.13 = (bf16[1152,128]{1,0:T(8,128)(2,1)S(1)}, bf16[1152,128]{1,0:T(8,128)(2,1)}, u32[]{:S(2)}) copy-start(bf16[1152,128]{1,0:T(8,128)(2,1)} %copy-done.12) | copy-start | bytes 884740
  73.2 1.0 %copy-start.15 = (bf16[1152,128]{1,0:T(8,128)(2,1)S(1)}, bf16[1152,128]{1,0:T(8,128)(2,1)}, u32[]{:S(2)}) copy-start(bf16[1152,128]{1,0:T(8,128)(2,1)} %copy-done.14) | copy-start | bytes 884740
  82.8 9.8 %collective-permute-start.17 = (bf16[1152,384]{1,0:T(8,128)(2,1)S(1)}, bf16[1152,384]{1,0:T(8,128)(2,1)S(1)}, u32[]{:S(2)}, u32[]{:S(2)}) collective-permute-start(bf16[1152,384]{1,0:T(8,128)(2,1)S(1)} %get-tuple-element.52), channel_id=1, source_target_pairs={{0,4},{4,0},{8,12},{12,8},{1,5},{5,1},{9,13},{13,9},{2,6},{6,2},{1... | collective-permute-start | bytes 2654216 | tf_op jit(solution)/shard_map/ppermute | solution.py:222

commit v6 on v5

v6 whole, which is shorter than its diff:
```python
import functools
import math

import jax
import jax.numpy as jnp
from jax import lax
from jax.experimental import pallas as pl
from jax.experimental.pallas import tpu as pltpu
from jax.sharding import PartitionSpec as P

HD = 128
FRAME = 64
FAR = 1e30
EXP2_SCALE = math.log2(math.e) / math.sqrt(HD)
VMEM_LIMIT = 16 * 1024 * 1024
COPY_LIMIT = 8 * 1024 * 1024
COPY_PARTS = 3
SCALARS = pl.BlockSpec(memory_space=pltpu.SMEM)
IN_VMEM = pl.BlockSpec(memory_space=pltpu.VMEM)
SMALL_COST = pl.CostEstimate(flops=0, bytes_accessed=1024, transcendentals=0)


def attention_kernel(info_ref, q_ref, own_ref, side_a_ref, side_b_ref, out_ref):
    tiles_time = info_ref.shape[0] - 2
    tile = q_ref.shape[0] // tiles_time
    width_oks = (None, info_ref[tiles_time] == 1, info_ref[tiles_time + 1] == 1)

    def window(t):
        first = t - info_ref[t]
        base = jnp.clip(first, 0, tiles_time - 2)
        inside = [(base + step >= first) & (base + step <= first + 1) for step in range(2)]
        return pl.ds(pl.multiple_of(base * tile, tile), 2 * tile), inside

    def score(t):
        rows, inside = window(t)
        query = q_ref[t * tile : (t + 1) * tile, :]
        blocks = []
        row_max = None
        for ref, width_ok in zip((own_ref, side_a_ref, side_b_ref), width_oks):
            scores = lax.dot_general(
                query, ref[0, rows, :], (((1,), (1,)), ((), ())), preferred_element_type=jnp.float32
            )
            for step in range(2):
                allowed = inside[step] if width_ok is None else inside[step] & width_ok
                block = scores[:, step * tile : (step + 1) * tile]
                lanes = block[:, :HD]
                for first in range(HD, tile, HD):
                    lanes = jnp.maximum(lanes, block[:, first : first + HD])
                lanes = jnp.where(allowed, lanes, -FAR)
                row_max = lanes if row_max is None else jnp.maximum(row_max, lanes)
                blocks.append((block, allowed))
        return blocks, jnp.max(row_max, axis=1, keepdims=True) * EXP2_SCALE

    def blend(t, blocks, shift):
        rows, _ = window(t)
        weights = [
            jnp.exp2(block * EXP2_SCALE - jnp.where(allowed, shift, FAR)).astype(jnp.bfloat16)
            for block, allowed in blocks
        ]
        values = jnp.concatenate(
            [ref[1, rows, :] for ref in (own_ref, side_a_ref, side_b_ref)], axis=0
        )
        total = jnp.dot(
            jnp.concatenate(weights, axis=1),
            jnp.concatenate([values, jnp.ones_like(values)], axis=1),
            preferred_element_type=jnp.float32,
        )
        out_ref[t * tile : (t + 1) * tile, :] = (total[:, :HD] / total[:, HD:]).astype(jnp.bfloat16)

    ready = score(0)
    for t in range(tiles_time):
        later = score(t + 1) if t + 1 < tiles_time else None
        blend(t, *ready)
        ready = later


def attention(info, *operands):
    return pl.pallas_call(
        attention_kernel,
        out_shape=jax.ShapeDtypeStruct(operands[0].shape, jnp.bfloat16),
        in_specs=[SCALARS] + [IN_VMEM] * len(operands),
        out_specs=IN_VMEM,
        compiler_params=pltpu.CompilerParams(vmem_limit_bytes=VMEM_LIMIT),
        cost_estimate=SMALL_COST,
        name="attention",
    )(info, *operands)


def partial_kernel(first, kinds, tile, info_ref, *refs):
    w_refs, refs = refs[:2], refs[2:]
    *pieces, gate_ref, base_own_ref, base_other_ref, own_ref, other_ref = refs
    own_cols = own_ref.shape[1]
    frames = tile // FRAME
    cond_first = info_ref[0] == 0
    places = [pl.ds(pl.multiple_of(info_ref[i] * own_cols, own_cols), own_cols) for i in (1, 2)]
    chosen = [[i for i, kind in enumerate(kinds) if kind[0] == which] for which in range(2)]
    weights = []
    for names in chosen:
        blocks = []
        for _, far, head in [kinds[i] for i in names]:
            depth = slice(head * HD, (head + 1) * HD)
            blocks.append(jnp.concatenate([w_refs[far][depth, place] for place in places], axis=1))
        weights.append(jnp.concatenate(blocks, axis=0))
    for time_tile in range(own_ref.shape[0] // tile):
        token_rows = slice(time_tile * tile, (time_tile + 1) * tile)
        parts = []
        for which in range(2):
            attended = jnp.concatenate([pieces[i][token_rows, :] for i in chosen[which]], axis=1)
            projected = jnp.dot(attended, weights[which], preferred_element_type=jnp.float32)
            parts.append(gate_ref[which] * projected)
        for frame in range(frames):
            rows = slice(frame * FRAME, (frame + 1) * FRAME)
            out_rows = slice(time_tile * tile + rows.start, time_tile * tile + rows.stop)
            guide = 1.0 + 0.5 * info_ref[3 + time_tile * frames + frame].astype(jnp.float32)
            scales = (
                jnp.where(cond_first, guide, 1.0 - guide),
                jnp.where(cond_first, 1.0 - guide, guide),
            )
            total = scales[0] * parts[0][rows] + scales[1] * parts[1][rows]
            own, other = total[:, :own_cols], total[:, own_cols:]
            if first:
                own += scales[0] * base_own_ref[out_rows, :].astype(jnp.float32)
                own += scales[1] * base_other_ref[out_rows, :].astype(jnp.float32)
            else:
                own += base_own_ref[out_rows, :]
                other += base_other_ref[out_rows, :]
            own_ref[out_rows, :] = own
            other_ref[out_rows, :] = other.astype(other_ref.dtype)


def partial_projection(info, weights, pieces, gate, base, tile, first):
    shape = base[0].shape
    return pl.pallas_call(
        functools.partial(partial_kernel, first, tuple(pieces), tile),
        out_shape=[
            jax.ShapeDtypeStruct(shape, jnp.float32),
            jax.ShapeDtypeStruct(shape, jnp.float32 if first else jnp.bfloat16),
        ],
        in_specs=[SCALARS] + [IN_VMEM] * (len(weights) + len(pieces) + 3),
        out_specs=[IN_VMEM] * 2,
        compiler_params=pltpu.CompilerParams(vmem_limit_bytes=VMEM_LIMIT),
        cost_estimate=SMALL_COST,
        name="partial_projection",
    )(info, *weights, *pieces.values(), gate, *base)


def copy_kernel(plan, info_ref, *refs):
    *arrays, sems = refs
    copies = []
    for source, block, width, target, place in plan:
        src, dst = arrays[source], arrays[target]
        first = block * width
        if block < 0:
            first = pl.multiple_of(info_ref[block + info_ref.shape[0]] * width, width)
        for part in range(COPY_PARTS):
            size = src.shape[0] // COPY_PARTS
            rows = pl.ds(part * size, size)
            to = dst.at[rows, :] if place is None else dst.at[place, rows, :]
            copies.append((src.at[rows, pl.ds(first, width)], to))
    copies = [
        pltpu.make_async_copy(src, to, sems.at[index]) for index, (src, to) in enumerate(copies)
    ]
    for copy in copies:
        copy.start()
    for copy in copies:
        copy.wait()


def copy_columns(info, sources, plan, targets):
    return pl.pallas_call(
        functools.partial(copy_kernel, plan),
        out_shape=[jax.ShapeDtypeStruct(shape, jnp.bfloat16) for shape in targets],
        in_specs=[SCALARS] + [pl.BlockSpec(memory_space=pltpu.HBM)] * len(sources),
        out_specs=[IN_VMEM] * len(targets),
        scratch_shapes=[pltpu.SemaphoreType.DMA((COPY_PARTS * len(plan),))],
        compiler_params=pltpu.CompilerParams(vmem_limit_bytes=COPY_LIMIT),
        cost_estimate=SMALL_COST,
        name="copy_columns",
    )(info, *[pltpu.with_memory_space_constraint(source, pltpu.HBM) for source in sources])


def local(queries, keys, values, residual, gate, out_weight, time_offsets, guidance_index):
    tiles_time, tiles_wide = time_offsets.shape
    count, features = queries.shape[1:]
    tile = count // tiles_time
    heads = features // HD
    head_count = lax.axis_size("head")
    columns = lax.axis_size("tokens")
    branch_pos = lax.axis_index("branch")
    head_pos = lax.axis_index("head")
    width_pos = lax.axis_index("tokens")
    width = gate.shape[2] // head_count

    rounds = [
        [pair for i in range(first, columns - 1, 2) for pair in ((i, i + 1), (i + 1, i))]
        for first in range(2)
    ]
    near_pos = (width_pos ^ 1, ((width_pos + 1) ^ 1) - 1)

    def swap(value, branch_bit, head_bits):
        if not branch_bit and not head_bits:
            return value
        if not head_bits:
            return lax.ppermute(value, "branch", [(0, 1), (1, 0)])
        if not branch_bit:
            return lax.ppermute(value, "head", [(i, i ^ head_bits) for i in range(head_count)])
        flip = head_count + head_bits
        return lax.ppermute(
            value, ("branch", "head"), [(i, i ^ flip) for i in range(2 * head_count)]
        )

    pair = head_pos >> 1
    branch_pair = branch_pos * (head_count // 2)
    copy_info = jnp.stack([branch_pair + pair, branch_pair + (pair ^ 1)])
    query, key_value, pair_weight = (count, HD), (2, count, HD), (features, 2 * width)
    packed = copy_columns(
        copy_info, (keys[0], values[0]), [(0, 0, HD, 2, 0), (1, 0, HD, 2, 1)], [key_value]
    )
    packed, late_sources = lax.optimization_barrier(
        (packed, (queries[0], keys[0], values[0], out_weight))
    )
    plan, targets = [], []

    def plan_copies(sources, block, width, places, target):
        for source, place in zip(sources, places):
            plan.append((source, block, width, len(late_sources) + len(targets), place))
        targets.append(target)

    for head in range(1, heads):
        plan_copies((1, 2), head, HD, (0, 1), key_value)
    for head in range(heads):
        plan_copies((0,), head, HD, (None,), query)
    for block in (-2, -1):
        plan_copies((3,), block, 2 * width, (None,), pair_weight)
    late = copy_columns(copy_info, late_sources, plan, targets)
    packed, head_queries, (near, far) = list(packed) + list(late)[: heads - 1], list(late[heads - 1 : -2]), late[-2:]

    def halo(part):
        return [lax.ppermute(part, "tokens", pairs) for pairs in rounds]

    sides = [halo(part) for part in packed[:2]]
    far = swap(far, 0, 2)

    sides[0], residual = lax.optimization_barrier((sides[0], residual))
    first_half, second_half = residual[0, :, 0], residual[0, :, 1]
    mine = jnp.where(branch_pos == 0, first_half, second_half)
    other = swap(jnp.where(branch_pos == 0, second_half, first_half), 1, 0)
    gate_block = jnp.concatenate(
        [
            lax.dynamic_slice(gate, (0, branch_pos, place * width), (2, 1, width))
            for place in (head_pos, head_pos ^ 1)
        ],
        axis=2,
    ).astype(jnp.float32)
    gate_block = jnp.where(branch_pos == 0, gate_block, gate_block[::-1])

    offsets = lax.dynamic_index_in_dim(time_offsets, width_pos, 1, keepdims=False)
    edges = jnp.stack([(pos >= 0) & (pos < tiles_wide) for pos in near_pos]).astype(jnp.int32)
    attention_info = jnp.concatenate([offsets, edges])
    place = head_pos & 1
    projection_info = jnp.concatenate([jnp.stack([branch_pos, place, place ^ 1]), guidance_index])

    pieces = {}

    def await_pieces(head, *names, more=()):
        head_queries[head], here, more = lax.optimization_barrier(
            (head_queries[head], [pieces[name] for name in names], more)
        )
        pieces.update(zip(names, here))
        return more

    for head in range(heads):
        if head == 0:
            head_queries[0], far, projection_info, gate_block = lax.optimization_barrier(
                (head_queries[0], far, projection_info, gate_block)
            )
        elif head == 1:
            await_pieces(head, (0, 1, 0))
        else:
            other = await_pieces(head, (1, 0, 0), (1, 0, 1), (1, 1, 0), more=other)
        own = attention(attention_info, head_queries[head], packed[head], *sides[head])
        if head + 2 < heads:
            own, part = lax.optimization_barrier((own, packed[head + 2]))
            sides.append(halo(part))
        pieces[0, 0, head] = own
        pieces[1, 0, head] = swap(own, 1, 0)
        pieces[0, 1, head] = swap(own, 0, 2)
        if head == 1:
            pieces[1, 1, head] = swap(pieces[0, 1, head], 1, 0)
        else:
            pieces[1, 1, head] = swap(pieces[1, 0, head], 0, 2)

    late = [(1, 1, heads - 2)] + [name for name in pieces if name[2] == heads - 1]
    base = (mine, other)
    for chosen in ([name for name in pieces if name not in late], late):
        base = partial_projection(
            projection_info,
            (near, far),
            {name: pieces[name] for name in chosen},
            gate_block,
            base,
            tile,
            base[0] is mine,
        )
    return (base[0] + swap(base[1], 0, 1).astype(jnp.float32)).astype(jnp.bfloat16)


def solution(mesh):
    return jax.shard_map(
        local,
        mesh=mesh,
        in_specs=(
            P("branch", "tokens", "head"),
            P("branch", "tokens", "head"),
            P("branch", "tokens", "head"),
            P("branch", "tokens", None, "head"),
            P(),
            P("head", None),
            P(),
            P(),
        ),
        out_specs=P("tokens", ("branch", "head")),
        check_vma=False,
    )
```

time: 94.4 us -> 96.1 us (1.018)
  the two profiles are of different devices: /device:TPU:9 before, /device:TPU:0 now
where the time goes in v6:
time: 96.1 us; the launch traced here: 95.7 us
  waiting for transfers between devices  38.7 us (40%)
  starting transfers between devices  25.9 us (27%)
  Pallas kernels  24.5 us (25%)
  local copies, waits for them, and re-layouts  4.83 us (5%)
  other arithmetic  1.66 us (2%)
    ppermute x7, waiting for transfers between devices, swap(): lax.ppermute(value, 'head', [(i, i ^ head_bits) for i in range(head_count)])  24.7 us
    pallas_call x3, Pallas kernels, attention(): pl.pallas_call(attention_kernel, out_shape=jax.ShapeDtypeStruct(operands[...  14.1 us
    ppermute x5, waiting for transfers between devices, swap(): return lax.ppermute(value, 'branch', [(0, 1), (1, 0)])  13.9 us
    ppermute x6, starting transfers between devices, halo(): return [lax.ppermute(part, 'tokens', pairs) for pairs in rounds]  11.3 us
    ppermute x7, starting transfers between devices, swap(): lax.ppermute(value, 'head', [(i, i ^ head_bits) for i in range(head_count)])  9.26 us
    ppermute x5, starting transfers between devices, swap(): return lax.ppermute(value, 'branch', [(0, 1), (1, 0)])  5.37 us
    pallas_call x2, Pallas kernels, copy_columns(): pl.pallas_call(functools.partial(copy_kernel, plan), out_shape=[jax.Shape...  5.28 us
    pallas_call x2, Pallas kernels, partial_projection(): pl.pallas_call(functools.partial(partial_kernel, first, tuple(pieces), ti...  5.1 us
  transfers between devices with their start and end apart: 18, of which 8 were waited for; matrix products, arithmetic and copies ran while one was open for 3% of the time, Pallas kernels for 21%

profile of v6, /device:TPU:0, one launch (start us, length us, event | category | flops | bytes accessed | tf_op | source)
XLA Modules:
  0.0 95.7 jit_solution(17314390009072220469)
XLA Ops:
  0.0 0.0 copy-start
  0.0 0.1 pad_add_fusion.info_ref
  0.1 1.7 %copy_columns.2.own_ref = bf16[2,1152,128]{2,1,0:T(8,128)(2,1)S(1)} custom-call(s32[2]{0:T(128)S(1)} %pad_add_fusion.info_ref, bf16[1152,384]{1,0:T(8,128)(2,1)} %bitcast.14, bf16[1152,384]{1,0:T(8,128)(2,1)} %bitcast.16), custom_call_target="tpu_custom_call" | custom-call | bytes 1024 | tf_op jit(solution)/shard_map/copy_columns/pallas_call | solution.py:170
  1.8 0.0 copy-start.7
  1.8 3.1 %collective-permute-start.1 = (bf16[2,1152,128]{2,1,0:T(8,128)(2,1)S(1)}, bf16[2,1152,128]{2,1,0:T(8,128)(2,1)}, u32[]{:S(2)}, u32[]{:S(2)}) collective-permute-start(bf16[2,1152,128]{2,1,0:T(8,128)(2,1)S(1)} %copy_columns.2.own_ref), channel_id=1, source_target_pairs={{0,1},{1,0},{2,3},{3,2},{4,5},{5,4},{6,7},{7,6},{8,9},{9,8},{10,11... | collective-permute-start | bytes 1769480 | tf_op jit(solution)/shard_map/ppermute | solution.py:239
  4.9 1.5 %collective-permute-start.2 = (bf16[2,1152,128]{2,1,0:T(8,128)(2,1)S(1)}, bf16[2,1152,128]{2,1,0:T(8,128)(2,1)}, u32[]{:S(2)}, u32[]{:S(2)}) collective-permute-start(bf16[2,1152,128]{2,1,0:T(8,128)(2,1)S(1)} %copy_columns.2.own_ref), channel_id=1, source_target_pairs={{1,2},{2,1},{5,6},{6,5},{9,10},{10,9},{13,14},{14,13},{17,18},{18,... | collective-permute-start | bytes 1769480 | tf_op jit(solution)/shard_map/ppermute | solution.py:239
  6.4 3.6 %copy_columns.3 = (bf16[2,1152,128]{2,1,0:T(8,128)(2,1)S(1)}, bf16[2,1152,128]{2,1,0:T(8,128)(2,1)S(1)}, bf16[1152,128]{1,0:T(8,128)(2,1)S(1)}, bf16[1152,128]{1...) custom-call(s32[2]{0:T(128)S(1)} %pad_add_fusion.info_ref, ...), custom_call_target="tpu_custom_call" | custom-call | bytes 1024 | tf_op jit(solution)/shard_map/copy_columns/pallas_call | solution.py:170
  10.0 0.0 copy-start.1
  10.0 0.7 copy-done.1
  10.7 0.7 copy-done.3
  11.4 0.7 copy-done.5
  12.1 3.6 %collective-permute-start.4 = (bf16[2,1152,128]{2,1,0:T(8,128)(2,1)S(1)}, bf16[2,1152,128]{2,1,0:T(8,128)(2,1)S(1)}, u32[]{:S(2)}, u32[]{:S(2)}) collective-permute-start(bf16[2,1152,128]{2,1,0:T(8,128)(2,1)S(1)} %get-tuple-element.54.own_ref), channel_id=1, source_target_pairs={{0,1},{1,0},{2,3},{3,2},{4,5},{5,4},{6,7},{7,6},{8,9},{9,8},{10,11... | collective-permute-start | bytes 1769480 | tf_op jit(solution)/shard_map/ppermute | solution.py:239
  15.7 1.5 %collective-permute-start.5 = (bf16[2,1152,128]{2,1,0:T(8,128)(2,1)S(1)}, bf16[2,1152,128]{2,1,0:T(8,128)(2,1)}, u32[]{:S(2)}, u32[]{:S(2)}) collective-permute-start(bf16[2,1152,128]{2,1,0:T(8,128)(2,1)S(1)} %get-tuple-element.54.own_ref), channel_id=1, source_target_pairs={{1,2},{2,1},{5,6},{6,5},{9,10},{10,9},{13,14},{14,13},{17,18},{18,... | collective-permute-start | bytes 1769480 | tf_op jit(solution)/shard_map/ppermute | solution.py:239
  17.2 1.5 %collective-permute-start = (bf16[384,768]{1,0:T(8,128)(2,1)}, bf16[384,768]{1,0:T(8,128)(2,1)S(1)}, u32[]{:S(2)}, u32[]{:S(2)}) collective-permute-start(bf16[384,768]{1,0:T(8,128)(2,1)} %get-tuple-element.42), channel_id=1, source_target_pairs={{0,8},{4,12},{8,0},{12,4},{1,9},{5,13},{9,1},{13,5},{2,10},{6,14},... | collective-permute-start | bytes 1769480 | tf_op jit(solution)/shard_map/ppermute | solution.py:206
  18.7 0.1 add_convert_fusion.1
  18.7 0.0 copy-done
  18.8 0.2 dynamic-slice_reduce_fusion
  18.9 0.1 pad_add_fusion.2.info_ref
  19.0 0.0 copy-done.7
  19.0 0.1 pad_add_fusion.1.info_ref
  19.1 0.8 constant_dynamic-slice_fusion.1
  19.9 11.7 %collective-permute-done.refs_1_ = bf16[384,768]{1,0:T(8,128)(2,1)S(1)} collective-permute-done((bf16[384,768]{1,0:T(8,128)(2,1)}, bf16[384,768]{1,0:T(8,128)(2,1)S(1)}, u32[]{:S(2)}, u32[]{:S(2)}) %collective-permute-start) | collective-permute-done | bytes 589856 | tf_op jit(solution)/shard_map/ppermute | solution.py:206
  31.6 0.0 collective-permute-done.1.side_a_ref
  31.6 0.0 collective-permute-done.2.side_b_ref
  31.6 1.7 %copy.9 = bf16[1,1152,2,384]{3,1,2,0:T(8,128)(2,1)S(1)} copy(bf16[1,1152,2,384]{3,2,1,0:T(2,128)(2,1)} %param.11) | data formatting | bytes 3538944 | tf_op jit(solution)/shard_map/optimization_barrier | solution.py:244
  33.3 0.0 copy-start.6
  33.3 0.2 select_bitcast_fusion
  33.5 0.0 copy-start.4
  33.5 1.6 %collective-permute-start.11 = (bf16[1152,384]{1,0:T(8,128)(2,1)S(1)}, bf16[1152,384]{1,0:T(8,128)(2,1)S(1)}, u32[]{:S(2)}, u32[]{:S(2)}) collective-permute-start(bf16[1152,384]{1,0:T(8,128)(2,1)S(1)} %get-tuple-element.70), channel_id=1, source_target_pairs={{0,16},{16,0},{1,17},{17,1},{2,18},{18,2},{3,19},{19,3},{4,20},{20... | collective-permute-start | bytes 2654216 | tf_op jit(solution)/shard_map/ppermute | solution.py:204
  35.1 0.0 copy-done.6
  35.1 5.0 %attention.3.refs_2_ = bf16[1152,128]{1,0:T(8,128)(2,1)S(1)} custom-call(s32[5]{0:T(128)S(1)} %pad_add_fusion.2.info_ref, bf16[1152,128]{1,0:T(8,128)(2,1)S(1)} %copy-done.6, bf16[2,1152,128]{2,1,0:T(8,128)(2,1)S(1)} %copy_columns.2.own_ref, bf16[2,1152,128]{2,1,0:T(8,128)(2,1)} %collective-permute-done.1.side_a_ref, ...), custom_call_target="tpu_custom_call" | custom-call | bytes 1024 | tf_op jit(solution)/shard_map/attention/pallas_call | solution.py:78
  40.0 0.0 copy-start.2
  40.0 1.6 %collective-permute-start.3 = (bf16[1152,128]{1,0:T(8,128)(2,1)S(1)}, bf16[1152,128]{1,0:T(8,128)(2,1)S(1)}, u32[]{:S(2)}, u32[]{:S(2)}) collective-permute-start(bf16[1152,128]{1,0:T(8,128)(2,1)S(1)} %attention.3.refs_2_), channel_id=1, source_target_pairs={{0,8},{4,12},{8,0},{12,4},{1,9},{5,13},{9,1},{13,5},{2,10},{6,14},... | collective-permute-start | bytes 884744 | tf_op jit(solution)/shard_map/ppermute | solution.py:206
  41.6 0.7 collective-permute-start.8
  42.3 0.0 collective-permute-done.4.side_a_ref
  42.3 0.8 collective-permute-start.12
  43.1 3.7 %collective-permute-done.3.refs_4_ = bf16[1152,128]{1,0:T(8,128)(2,1)S(1)} collective-permute-done((bf16[1152,128]{1,0:T(8,128)(2,1)S(1)}, bf16[1152,128]{1,0:T(8,128)(2,1)S(1)}, u32[]{:S(2)}, u32[]{:S(2)}) %collective-permute-start.3) | collective-permute-done | bytes 294944 | tf_op jit(solution)/shard_map/ppermute | solution.py:206
  46.8 0.9 collective-permute-start.13
  47.7 0.0 collective-permute-done.5.side_b_ref
  47.7 4.8 %attention.4.refs_6_ = bf16[1152,128]{1,0:T(8,128)(2,1)S(1)} custom-call(s32[5]{0:T(128)S(1)} %pad_add_fusion.2.info_ref, bf16[1152,128]{1,0:T(8,128)(2,1)S(1)} %copy-done.4, bf16[2,1152,128]{2,1,0:T(8,128)(2,1)S(1)} %get-tuple-element.54.own_ref, bf16[2,1152,128]{2,1,0:T(8,128)(2,1)S(1)} %collective-permute-done.4.side_a_ref, ...), custom_call_target="tpu_custom_call" | custom-call | bytes 1024 | tf_op jit(solution)/shard_map/attention/pallas_call | solution.py:78
  52.6 1.0 %collective-permute-start.9 = (bf16[1152,128]{1,0:T(8,128)(2,1)S(1)}, bf16[1152,128]{1,0:T(8,128)(2,1)S(1)}, u32[]{:S(2)}, u32[]{:S(2)}) collective-permute-start(bf16[1152,128]{1,0:T(8,128)(2,1)S(1)} %attention.4.refs_6_), channel_id=1, source_target_pairs={{0,16},{16,0},{1,17},{17,1},{2,18},{18,2},{3,19},{19,3},{4,20},{20... | collective-permute-start | bytes 884744 | tf_op jit(solution)/shard_map/ppermute | solution.py:204
  53.6 8.9 %collective-permute-done.8.refs_3_ = bf16[1152,128]{1,0:T(8,128)(2,1)S(1)} collective-permute-done((bf16[1152,128]{1,0:T(8,128)(2,1)S(1)}, bf16[1152,128]{1,0:T(8,128)(2,1)S(1)}, u32[]{:S(2)}, u32[]{:S(2)}) %collective-permute-start.8) | collective-permute-done | bytes 294944 | tf_op jit(solution)/shard_map/ppermute | solution.py:204
  62.5 1.5 %collective-permute-start.10 = (bf16[1152,128]{1,0:T(8,128)(2,1)S(1)}, bf16[1152,128]{1,0:T(8,128)(2,1)S(1)}, u32[]{:S(2)}, u32[]{:S(2)}) collective-permute-start(bf16[1152,128]{1,0:T(8,128)(2,1)S(1)} %collective-permute-done.8.refs_3_), channel_id=1, source_target_pairs={{0,8},{4,12},{8,0},{12,4},{1,9},{5,13},{9,1},{13,5},{2,10},{6,14},... | collective-permute-start | bytes 884744 | tf_op jit(solution)/shard_map/ppermute | solution.py:206
  64.0 1.8 %collective-permute-done.9.refs_7_ = bf16[1152,128]{1,0:T(8,128)(2,1)S(1)} collective-permute-done((bf16[1152,128]{1,0:T(8,128)(2,1)S(1)}, bf16[1152,128]{1,0:T(8,128)(2,1)S(1)}, u32[]{:S(2)}, u32[]{:S(2)}) %collective-permute-start.9) | collective-permute-done | bytes 294944 | tf_op jit(solution)/shard_map/ppermute | solution.py:204
  65.8 1.5 %collective-permute-start.6 = (bf16[1152,128]{1,0:T(8,128)(2,1)S(1)}, bf16[1152,128]{1,0:T(8,128)(2,1)S(1)}, u32[]{:S(2)}, u32[]{:S(2)}) collective-permute-start(bf16[1152,128]{1,0:T(8,128)(2,1)S(1)} %attention.4.refs_6_), channel_id=1, source_target_pairs={{0,8},{4,12},{8,0},{12,4},{1,9},{5,13},{9,1},{13,5},{2,10},{6,14},... | collective-permute-start | bytes 884744 | tf_op jit(solution)/shard_map/ppermute | solution.py:206
  67.4 4.5 %collective-permute-done.10.refs_5_ = bf16[1152,128]{1,0:T(8,128)(2,1)S(1)} collective-permute-done((bf16[1152,128]{1,0:T(8,128)(2,1)S(1)}, bf16[1152,128]{1,0:T(8,128)(2,1)S(1)}, u32[]{:S(2)}, u32[]{:S(2)}) %collective-permute-start.10) | collective-permute-done | bytes 294944 | tf_op jit(solution)/shard_map/ppermute | solution.py:206
  71.9 0.0 collective-permute-done.11.refs_11_
  71.9 0.0 collective-permute-done.12.side_a_ref
  71.9 0.0 collective-permute-done.13.side_b_ref
  71.9 4.3 %attention.5.refs_3_ = bf16[1152,128]{1,0:T(8,128)(2,1)S(1)} custom-call(s32[5]{0:T(128)S(1)} %pad_add_fusion.2.info_ref, bf16[1152,128]{1,0:T(8,128)(2,1)S(1)} %copy-done.2, bf16[2,1152,128]{2,1,0:T(8,128)(2,1)S(1)} %get-tuple-element.58.own_ref, bf16[2,1152,128]{2,1,0:T(8,128)(2,1)S(1)} %collective-permute-done.12.side_a_ref, ...), custom_call_target="tpu_custom_call" | custom-call | bytes 1024 | tf_op jit(solution)/shard_map/attention/pallas_call | solution.py:78
  76.2 1.6 %collective-permute-start.14 = (bf16[1152,128]{1,0:T(8,128)(2,1)S(1)}, bf16[1152,128]{1,0:T(8,128)(2,1)S(1)}, u32[]{:S(2)}, u32[]{:S(2)}) collective-permute-start(bf16[1152,128]{1,0:T(8,128)(2,1)S(1)} %attention.5.refs_3_), channel_id=1, source_target_pairs={{0,16},{16,0},{1,17},{17,1},{2,18},{18,2},{3,19},{19,3},{4,20},{20... | collective-permute-start | bytes 884744 | tf_op jit(solution)/shard_map/ppermute | solution.py:204
  77.8 0.0 collective-permute-done.6.refs_8_
  77.8 0.5 collective-permute-start.7
  78.3 1.5 %collective-permute-start.15 = (bf16[1152,128]{1,0:T(8,128)(2,1)S(1)}, bf16[1152,128]{1,0:T(8,128)(2,1)S(1)}, u32[]{:S(2)}, u32[]{:S(2)}) collective-permute-start(bf16[1152,128]{1,0:T(8,128)(2,1)S(1)} %attention.5.refs_3_), channel_id=1, source_target_pairs={{0,8},{4,12},{8,0},{12,4},{1,9},{5,13},{9,1},{13,5},{2,10},{6,14},... | collective-permute-start | bytes 884744 | tf_op jit(solution)/shard_map/ppermute | solution.py:206
  79.8 3.2 %collective-permute-done.14.refs_4_ = bf16[1152,128]{1,0:T(8,128)(2,1)S(1)} collective-permute-done((bf16[1152,128]{1,0:T(8,128)(2,1)S(1)}, bf16[1152,128]{1,0:T(8,128)(2,1)S(1)}, u32[]{:S(2)}, u32[]{:S(2)}) %collective-permute-start.14) | collective-permute-done | bytes 294944 | tf_op jit(solution)/shard_map/ppermute | solution.py:204
  83.0 1.5 %collective-permute-start.16 = (bf16[1152,128]{1,0:T(8,128)(2,1)S(1)}, bf16[1152,128]{1,0:T(8,128)(2,1)S(1)}, u32[]{:S(2)}, u32[]{:S(2)}) collective-permute-start(bf16[1152,128]{1,0:T(8,128)(2,1)S(1)} %collective-permute-done.14.refs_4_), channel_id=1, source_target_pairs={{0,8},{4,12},{8,0},{12,4},{1,9},{5,13},{9,1},{13,5},{2,10},{6,14},... | collective-permute-start | bytes 884744 | tf_op jit(solution)/shard_map/ppermute | solution.py:206
  84.5 2.8 %partial_projection.2 = (f32[1152,384]{1,0:T(8,128)S(1)}, f32[1152,384]{1,0:T(8,128)S(1)}) custom-call(s32[21]{0:T(128)S(1)} %pad_add_fusion.1.info_ref, bf16[384,768]{1,0:T(8,128)(2,1)S(1)} %get-tuple-element.44.refs_0_, bf16[384,768]{1,0:T(8,128)(2,1)S(1)} %collective-permute-done.refs_1_, bf16[1152,128]{1,0:T(8,128)(2,1)S(1)} %attention.3.refs_2_, ...), custom_call_target="tpu_custom_call" | custom-call | bytes 1024 | tf_op jit(solution)/shard_map/partial_projection/pallas_call | solution.py:133
  87.3 0.0 collective-permute-done.7.refs_2_
  87.3 0.0 collective-permute-done.15.refs_5_
  87.3 2.4 %collective-permute-done.16.refs_6_ = bf16[1152,128]{1,0:T(8,128)(2,1)S(1)} collective-permute-done((bf16[1152,128]{1,0:T(8,128)(2,1)S(1)}, bf16[1152,128]{1,0:T(8,128)(2,1)S(1)}, u32[]{:S(2)}, u32[]{:S(2)}) %collective-permute-start.16) | collective-permute-done | bytes 294944 | tf_op jit(solution)/shard_map/ppermute | solution.py:206
  89.7 2.3 %partial_projection.3 = (f32[1152,384]{1,0:T(8,128)S(1)}, bf16[1152,384]{1,0:T(8,128)(2,1)S(1)}) custom-call(s32[21]{0:T(128)S(1)} %pad_add_fusion.1.info_ref, bf16[384,768]{1,0:T(8,128)(2,1)S(1)} %get-tuple-element.44.refs_0_, bf16[384,768]{1,0:T(8,128)(2,1)S(1)} %collective-permute-done.refs_1_, bf16[1152,128]{1,0:T(8,128)(2,1)S(1)} %collective-permute-done.7.refs_2_, ...), custom_call_target="tpu_custom_call" | custom-call | bytes 1024 | tf_op jit(solution)/shard_map/partial_projection/pallas_call | solution.py:133
  92.1 0.1 collective-permute-start.17
  92.1 2.4 %collective-permute-done.17 = bf16[1152,384]{1,0:T(8,128)(2,1)S(1)} collective-permute-done((bf16[1152,384]{1,0:T(8,128)(2,1)S(1)}, bf16[1152,384]{1,0:T(8,128)(2,1)S(1)}, u32[]{:S(2)}, u32[]{:S(2)}) %collective-permute-start.17) | collective-permute-done | bytes 884768 | tf_op jit(solution)/shard_map/ppermute | solution.py:206
  94.6 1.2 %add_convert_fusion = bf16[1152,384]{1,0:T(8,128)(2,1)} fusion(f32[1152,384]{1,0:T(8,128)S(1)} %get-tuple-element.67, bf16[1152,384]{1,0:T(8,128)(2,1)S(1)} %collective-permute-done.17), kind=kLoop, calls=%fused_computation | loop fusion | flops 1327104 | bytes 3538944 | tf_op jit(solution)/shard_map/convert_element_type | solution.py:305
  (6 shorter events, 0.0 us)
Async XLA Ops:
  0.0 18.8 %copy-start = (s32[3,4]{1,0:T(4,128)S(1)}, s32[3,4]{1,0:T(4,128)}, u32[]{:S(2)}) copy-start(s32[3,4]{1,0:T(4,128)} %param.14) | copy-start | bytes 148
  1.8 17.2 %copy-start.7 = (s32[18]{0:T(128)S(1)}, s32[18]{0:T(128)}, u32[]{:S(2)}) copy-start(s32[18]{0:T(128)} %param.15) | copy-start | bytes 220
  1.8 29.8 %collective-permute-start.1 = (bf16[2,1152,128]{2,1,0:T(8,128)(2,1)S(1)}, bf16[2,1152,128]{2,1,0:T(8,128)(2,1)}, u32[]{:S(2)}, u32[]{:S(2)}) collective-permute-start(bf16[2,1152,128]{2,1,0:T(8,128)(2,1)S(1)} %copy_columns.2.own_ref), channel_id=1, source_target_pairs={{0,1},{1,0},{2,3},{3,2},{4,5},{5,4},{6,7},{7,6},{8,9},{9,8},{10,11... | collective-permute-start | bytes 1769480 | tf_op jit(solution)/shard_map/ppermute | solution.py:239
  4.9 26.7 %collective-permute-start.2 = (bf16[2,1152,128]{2,1,0:T(8,128)(2,1)S(1)}, bf16[2,1152,128]{2,1,0:T(8,128)(2,1)}, u32[]{:S(2)}, u32[]{:S(2)}) collective-permute-start(bf16[2,1152,128]{2,1,0:T(8,128)(2,1)S(1)} %copy_columns.2.own_ref), channel_id=1, source_target_pairs={{1,2},{2,1},{5,6},{6,5},{9,10},{10,9},{13,14},{14,13},{17,18},{18,... | collective-permute-start | bytes 1769480 | tf_op jit(solution)/shard_map/ppermute | solution.py:239
  10.0 0.7 copy-start.1
  10.7 0.7 copy-start.3
  11.4 0.7 copy-start.5
  12.1 30.2 %collective-permute-start.4 = (bf16[2,1152,128]{2,1,0:T(8,128)(2,1)S(1)}, bf16[2,1152,128]{2,1,0:T(8,128)(2,1)S(1)}, u32[]{:S(2)}, u32[]{:S(2)}) collective-permute-start(bf16[2,1152,128]{2,1,0:T(8,128)(2,1)S(1)} %get-tuple-element.54.own_ref), channel_id=1, source_target_pairs={{0,1},{1,0},{2,3},{3,2},{4,5},{5,4},{6,7},{7,6},{8,9},{9,8},{10,11... | collective-permute-start | bytes 1769480 | tf_op jit(solution)/shard_map/ppermute | solution.py:239
  15.7 32.0 %collective-permute-start.5 = (bf16[2,1152,128]{2,1,0:T(8,128)(2,1)S(1)}, bf16[2,1152,128]{2,1,0:T(8,128)(2,1)}, u32[]{:S(2)}, u32[]{:S(2)}) collective-permute-start(bf16[2,1152,128]{2,1,0:T(8,128)(2,1)S(1)} %get-tuple-element.54.own_ref), channel_id=1, source_target_pairs={{1,2},{2,1},{5,6},{6,5},{9,10},{10,9},{13,14},{14,13},{17,18},{18,... | collective-permute-start | bytes 1769480 | tf_op jit(solution)/shard_map/ppermute | solution.py:239
  17.2 14.4 %collective-permute-start = (bf16[384,768]{1,0:T(8,128)(2,1)}, bf16[384,768]{1,0:T(8,128)(2,1)S(1)}, u32[]{:S(2)}, u32[]{:S(2)}) collective-permute-start(bf16[384,768]{1,0:T(8,128)(2,1)} %get-tuple-element.42), channel_id=1, source_target_pairs={{0,8},{4,12},{8,0},{12,4},{1,9},{5,13},{9,1},{13,5},{2,10},{6,14},... | collective-permute-start | bytes 1769480 | tf_op jit(solution)/shard_map/ppermute | solution.py:206
  33.3 1.8 %copy-start.6 = (bf16[1152,128]{1,0:T(8,128)(2,1)S(1)}, bf16[1152,128]{1,0:T(8,128)(2,1)}, u32[]{:S(2)}) copy-start(bf16[1152,128]{1,0:T(8,128)(2,1)} %copy-done.5) | copy-start | bytes 884740
  33.5 14.2 %copy-start.4 = (bf16[1152,128]{1,0:T(8,128)(2,1)S(1)}, bf16[1152,128]{1,0:T(8,128)(2,1)}, u32[]{:S(2)}) copy-start(bf16[1152,128]{1,0:T(8,128)(2,1)} %copy-done.3) | copy-start | bytes 884740
  33.5 38.4 %collective-permute-start.11 = (bf16[1152,384]{1,0:T(8,128)(2,1)S(1)}, bf16[1152,384]{1,0:T(8,128)(2,1)S(1)}, u32[]{:S(2)}, u32[]{:S(2)}) collective-permute-start(bf16[1152,384]{1,0:T(8,128)(2,1)S(1)} %get-tuple-element.70), channel_id=1, source_target_pairs={{0,16},{16,0},{1,17},{17,1},{2,18},{18,2},{3,19},{19,3},{4,20},{20... | collective-permute-start | bytes 2654216 | tf_op jit(solution)/shard_map/ppermute | solution.py:204
  40.0 31.9 %copy-start.2 = (bf16[1152,128]{1,0:T(8,128)(2,1)S(1)}, bf16[1152,128]{1,0:T(8,128)(2,1)}, u32[]{:S(2)}) copy-start(bf16[1152,128]{1,0:T(8,128)(2,1)} %copy-done.1) | copy-start | bytes 884740
  40.0 6.8 %collective-permute-start.3 = (bf16[1152,128]{1,0:T(8,128)(2,1)S(1)}, bf16[1152,128]{1,0:T(8,128)(2,1)S(1)}, u32[]{:S(2)}, u32[]{:S(2)}) collective-permute-start(bf16[1152,128]{1,0:T(8,128)(2,1)S(1)} %attention.3.refs_2_), channel_id=1, source_target_pairs={{0,8},{4,12},{8,0},{12,4},{1,9},{5,13},{9,1},{13,5},{2,10},{6,14},... | collective-permute-start | bytes 884744 | tf_op jit(solution)/shard_map/ppermute | solution.py:206
  41.6 20.9 %collective-permute-start.8 = (bf16[1152,128]{1,0:T(8,128)(2,1)S(1)}, bf16[1152,128]{1,0:T(8,128)(2,1)S(1)}, u32[]{:S(2)}, u32[]{:S(2)}) collective-permute-start(bf16[1152,128]{1,0:T(8,128)(2,1)S(1)} %attention.3.refs_2_), channel_id=1, source_target_pairs={{0,16},{16,0},{1,17},{17,1},{2,18},{18,2},{3,19},{19,3},{4,20},{20... | collective-permute-start | bytes 884744 | tf_op jit(solution)/shard_map/ppermute | solution.py:204
  42.3 29.6 %collective-permute-start.12 = (bf16[2,1152,128]{2,1,0:T(8,128)(2,1)S(1)}, bf16[2,1152,128]{2,1,0:T(8,128)(2,1)S(1)}, u32[]{:S(2)}, u32[]{:S(2)}) collective-permute-start(bf16[2,1152,128]{2,1,0:T(8,128)(2,1)S(1)} %get-tuple-element.58.own_ref), channel_id=1, source_target_pairs={{0,1},{1,0},{2,3},{3,2},{4,5},{5,4},{6,7},{7,6},{8,9},{9,8},{10,11... | collective-permute-start | bytes 1769480 | tf_op jit(solution)/shard_map/ppermute | solution.py:239
  46.8 25.1 %collective-permute-start.13 = (bf16[2,1152,128]{2,1,0:T(8,128)(2,1)S(1)}, bf16[2,1152,128]{2,1,0:T(8,128)(2,1)S(1)}, u32[]{:S(2)}, u32[]{:S(2)}) collective-permute-start(bf16[2,1152,128]{2,1,0:T(8,128)(2,1)S(1)} %get-tuple-element.58.own_ref), channel_id=1, source_target_pairs={{1,2},{2,1},{5,6},{6,5},{9,10},{10,9},{13,14},{14,13},{17,18},{18,... | collective-permute-start | bytes 1769480 | tf_op jit(solution)/shard_map/ppermute | solution.py:239
  52.6 13.3 %collective-permute-start.9 = (bf16[1152,128]{1,0:T(8,128)(2,1)S(1)}, bf16[1152,128]{1,0:T(8,128)(2,1)S(1)}, u32[]{:S(2)}, u32[]{:S(2)}) collective-permute-start(bf16[1152,128]{1,0:T(8,128)(2,1)S(1)} %attention.4.refs_6_), channel_id=1, source_target_pairs={{0,16},{16,0},{1,17},{17,1},{2,18},{18,2},{3,19},{19,3},{4,20},{20... | collective-permute-start | bytes 884744 | tf_op jit(solution)/shard_map/ppermute | solution.py:204
  62.5 9.4 %collective-permute-start.10 = (bf16[1152,128]{1,0:T(8,128)(2,1)S(1)}, bf16[1152,128]{1,0:T(8,128)(2,1)S(1)}, u32[]{:S(2)}, u32[]{:S(2)}) collective-permute-start(bf16[1152,128]{1,0:T(8,128)(2,1)S(1)} %collective-permute-done.8.refs_3_), channel_id=1, source_target_pairs={{0,8},{4,12},{8,0},{12,4},{1,9},{5,13},{9,1},{13,5},{2,10},{6,14},... | collective-permute-start | bytes 884744 | tf_op jit(solution)/shard_map/ppermute | solution.py:206
  65.8 12.0 %collective-permute-start.6 = (bf16[1152,128]{1,0:T(8,128)(2,1)S(1)}, bf16[1152,128]{1,0:T(8,128)(2,1)S(1)}, u32[]{:S(2)}, u32[]{:S(2)}) collective-permute-start(bf16[1152,128]{1,0:T(8,128)(2,1)S(1)} %attention.4.refs_6_), channel_id=1, source_target_pairs={{0,8},{4,12},{8,0},{12,4},{1,9},{5,13},{9,1},{13,5},{2,10},{6,14},... | collective-permute-start | bytes 884744 | tf_op jit(solution)/shard_map/ppermute | solution.py:206
  76.2 6.8 %collective-permute-start.14 = (bf16[1152,128]{1,0:T(8,128)(2,1)S(1)}, bf16[1152,128]{1,0:T(8,128)(2,1)S(1)}, u32[]{:S(2)}, u32[]{:S(2)}) collective-permute-start(bf16[1152,128]{1,0:T(8,128)(2,1)S(1)} %attention.5.refs_3_), channel_id=1, source_target_pairs={{0,16},{16,0},{1,17},{17,1},{2,18},{18,2},{3,19},{19,3},{4,20},{20... | collective-permute-start | bytes 884744 | tf_op jit(solution)/shard_map/ppermute | solution.py:204
  77.8 9.5 %collective-permute-start.7 = (bf16[1152,128]{1,0:T(8,128)(2,1)S(1)}, bf16[1152,128]{1,0:T(8,128)(2,1)S(1)}, u32[]{:S(2)}, u32[]{:S(2)}) collective-permute-start(bf16[1152,128]{1,0:T(8,128)(2,1)S(1)} %collective-permute-done.6.refs_8_), channel_id=1, source_target_pairs={{0,16},{16,0},{1,17},{17,1},{2,18},{18,2},{3,19},{19,3},{4,20},{20... | collective-permute-start | bytes 884744 | tf_op jit(solution)/shard_map/ppermute | solution.py:204
  78.3 9.0 %collective-permute-start.15 = (bf16[1152,128]{1,0:T(8,128)(2,1)S(1)}, bf16[1152,128]{1,0:T(8,128)(2,1)S(1)}, u32[]{:S(2)}, u32[]{:S(2)}) collective-permute-start(bf16[1152,128]{1,0:T(8,128)(2,1)S(1)} %attention.5.refs_3_), channel_id=1, source_target_pairs={{0,8},{4,12},{8,0},{12,4},{1,9},{5,13},{9,1},{13,5},{2,10},{6,14},... | collective-permute-start | bytes 884744 | tf_op jit(solution)/shard_map/ppermute | solution.py:206
  83.0 6.7 %collective-permute-start.16 = (bf16[1152,128]{1,0:T(8,128)(2,1)S(1)}, bf16[1152,128]{1,0:T(8,128)(2,1)S(1)}, u32[]{:S(2)}, u32[]{:S(2)}) collective-permute-start(bf16[1152,128]{1,0:T(8,128)(2,1)S(1)} %collective-permute-done.14.refs_4_), channel_id=1, source_target_pairs={{0,8},{4,12},{8,0},{12,4},{1,9},{5,13},{9,1},{13,5},{2,10},{6,14},... | collective-permute-start | bytes 884744 | tf_op jit(solution)/shard_map/ppermute | solution.py:206
  92.1 2.5 %collective-permute-start.17 = (bf16[1152,384]{1,0:T(8,128)(2,1)S(1)}, bf16[1152,384]{1,0:T(8,128)(2,1)S(1)}, u32[]{:S(2)}, u32[]{:S(2)}) collective-permute-start(bf16[1152,384]{1,0:T(8,128)(2,1)S(1)} %get-tuple-element.68), channel_id=1, source_target_pairs={{0,4},{4,0},{8,12},{12,8},{1,5},{5,1},{9,13},{13,9},{2,6},{6,2},{1... | collective-permute-start | bytes 2654216 | tf_op jit(solution)/shard_map/ppermute | solution.py:206

commit v7 on v6

--- a/solution.py
+++ b/solution.py
@@ -15,12 +15,22 @@
 VMEM_LIMIT = 16 * 1024 * 1024
 COPY_LIMIT = 8 * 1024 * 1024
 COPY_PARTS = 3
+LATE_PACK = True
+RESIDUAL_FIRST = True
+SPLIT = 2
+BEFORE_X = {1: (), 2: ((1, 1, 0),)}
+BEFORE_Y = {1: (), 2: ()}
+RESIDUAL_AFTER = 0
+AWAITED = {0: (), 1: ('far', (0, 1, 0)), 2: ('far', 'other', (1, 0, 0), (0, 1, 0)), 3: ((1, 0, 1),)}
+RELAY = ('y', 'x', 'y')
+LATE = ((1, 1, 1),)
 SCALARS = pl.BlockSpec(memory_space=pltpu.SMEM)
 IN_VMEM = pl.BlockSpec(memory_space=pltpu.VMEM)
 SMALL_COST = pl.CostEstimate(flops=0, bytes_accessed=1024, transcendentals=0)
 
 
-def attention_kernel(info_ref, q_ref, own_ref, side_a_ref, side_b_ref, out_ref):
+def attention_kernel(first, last, info_ref, q_ref, own_ref, side_a_ref, side_b_ref, *refs):
+    *earlier, out_ref = refs
     tiles_time = info_ref.shape[0] - 2
     tile = q_ref.shape[0] // tiles_time
     width_oks = (None, info_ref[tiles_time] == 1, info_ref[tiles_time + 1] == 1)
@@ -67,16 +77,18 @@
         )
         out_ref[t * tile : (t + 1) * tile, :] = (total[:, :HD] / total[:, HD:]).astype(jnp.bfloat16)
 
-    ready = score(0)
-    for t in range(tiles_time):
-        later = score(t + 1) if t + 1 < tiles_time else None
+    ready = score(first)
+    for ref in earlier:
+        out_ref[: first * tile, :] = ref[: first * tile, :]
+    for t in range(first, last):
+        later = score(t + 1) if t + 1 < last else None
         blend(t, *ready)
         ready = later
 
 
-def attention(info, *operands):
+def attention(info, tiles, *operands):
     return pl.pallas_call(
-        attention_kernel,
+        functools.partial(attention_kernel, *tiles),
         out_shape=jax.ShapeDtypeStruct(operands[0].shape, jnp.bfloat16),
         in_specs=[SCALARS] + [IN_VMEM] * len(operands),
         out_specs=IN_VMEM,
@@ -212,39 +224,51 @@
     pair = head_pos >> 1
     branch_pair = branch_pos * (head_count // 2)
     copy_info = jnp.stack([branch_pair + pair, branch_pair + (pair ^ 1)])
-    query, key_value, pair_weight = (count, HD), (2, count, HD), (features, 2 * width)
-    packed = copy_columns(
-        copy_info, (keys[0], values[0]), [(0, 0, HD, 2, 0), (1, 0, HD, 2, 1)], [key_value]
-    )
-    packed, late_sources = lax.optimization_barrier(
-        (packed, (queries[0], keys[0], values[0], out_weight))
-    )
-    plan, targets = [], []
-
-    def plan_copies(sources, block, width, places, target):
-        for source, place in zip(sources, places):
-            plan.append((source, block, width, len(late_sources) + len(targets), place))
-        targets.append(target)
-
-    for head in range(1, heads):
-        plan_copies((1, 2), head, HD, (0, 1), key_value)
-    for head in range(heads):
-        plan_copies((0,), head, HD, (None,), query)
-    for block in (-2, -1):
-        plan_copies((3,), block, 2 * width, (None,), pair_weight)
-    late = copy_columns(copy_info, late_sources, plan, targets)
-    packed, head_queries, (near, far) = list(packed) + list(late)[: heads - 1], list(late[heads - 1 : -2]), late[-2:]
+    sources = (queries[0], keys[0], values[0], out_weight)
+    key_value = [((1, 2), head, HD, (0, 1), (2, count, HD)) for head in range(heads)]
+    query = [((0,), head, HD, (None,), (count, HD)) for head in range(heads)]
+    pair_weight = [((3,), block, 2 * width, (None,), (features, 2 * width)) for block in (-2, -1)]
+
+    def pack(parts, after=None):
+        here = sources
+        if after is not None:
+            _, here = lax.optimization_barrier((after, sources))
+        used = sorted({index for part in parts for index in part[0]})
+        plan = [
+            (used.index(source), block, cols, len(used) + target, place)
+            for target, (froms, block, cols, places, _) in enumerate(parts)
+            for source, place in zip(froms, places)
+        ]
+        return copy_columns(
+            copy_info, [here[index] for index in used], plan, [part[-1] for part in parts]
+        )
+
+    def split_residual(residual):
+        first_half, second_half = residual[0, :, 0], residual[0, :, 1]
+        mine = jnp.where(branch_pos == 0, first_half, second_half)
+        return mine, jnp.where(branch_pos == 0, second_half, first_half)
+
+    packed = pack(key_value[:1])
+    after = packed
+    if RESIDUAL_AFTER == 0:
+        _, residual = lax.optimization_barrier((packed, residual))
+        mine, other = split_residual(residual)
+        after = (packed, other) if RESIDUAL_FIRST else packed
+    late_key_value, far = pack([key_value[1], pair_weight[1]], after)
+    packed = list(packed) + [late_key_value]
 
     def halo(part):
         return [lax.ppermute(part, "tokens", pairs) for pairs in rounds]
 
-    sides = [halo(part) for part in packed[:2]]
-    far = swap(far, 0, 2)
-
-    sides[0], residual = lax.optimization_barrier((sides[0], residual))
-    first_half, second_half = residual[0, :, 0], residual[0, :, 1]
-    mine = jnp.where(branch_pos == 0, first_half, second_half)
-    other = swap(jnp.where(branch_pos == 0, second_half, first_half), 1, 0)
+    sides = [halo(part) for part in packed]
+    near, *late = pack(pair_weight[:1] + query + key_value[2:], sides[0] if LATE_PACK else packed)
+    head_queries, packed = late[:heads], packed + late[heads:]
+    store = {"far": swap(far, 0, 2)}
+
+    if RESIDUAL_AFTER:
+        _, residual = lax.optimization_barrier(((packed[1], sides[0])[RESIDUAL_AFTER - 1], residual))
+        mine, other = split_residual(residual)
+    store["other"] = swap(other, 1, 0)
     gate_block = jnp.concatenate(
         [
             lax.dynamic_slice(gate, (0, branch_pos, place * width), (2, 1, width))
@@ -260,43 +284,41 @@
     place = head_pos & 1
     projection_info = jnp.concatenate([jnp.stack([branch_pos, place, place ^ 1]), guidance_index])
 
-    pieces = {}
-
-    def await_pieces(head, *names, more=()):
-        head_queries[head], here, more = lax.optimization_barrier(
-            (head_queries[head], [pieces[name] for name in names], more)
-        )
-        pieces.update(zip(names, here))
-        return more
+    def await_names(names, value):
+        value, awaited = lax.optimization_barrier((value, [store[name] for name in names]))
+        store.update(zip(names, awaited))
+        return value
 
     for head in range(heads):
-        if head == 0:
-            head_queries[0], far, projection_info, gate_block = lax.optimization_barrier(
-                (head_queries[0], far, projection_info, gate_block)
-            )
-        elif head == 1:
-            await_pieces(head, (0, 1, 0))
+        head_queries[head] = await_names(AWAITED.get(head, ()), head_queries[head])
+        operands = [head_queries[head], packed[head], *sides[head]]
+        if head == heads - 1 and SPLIT:
+            own = attention(attention_info, (0, SPLIT), *operands)
+            own = await_names(AWAITED.get(heads, ()), own)
+            own = attention(attention_info, (SPLIT, tiles_time), *operands, own)
         else:
-            other = await_pieces(head, (1, 0, 0), (1, 0, 1), (1, 1, 0), more=other)
-        own = attention(attention_info, head_queries[head], packed[head], *sides[head])
+            own = attention(attention_info, (0, tiles_time), *operands)
         if head + 2 < heads:
             own, part = lax.optimization_barrier((own, packed[head + 2]))
             sides.append(halo(part))
-        pieces[0, 0, head] = own
-        pieces[1, 0, head] = swap(own, 1, 0)
-        pieces[0, 1, head] = swap(own, 0, 2)
-        if head == 1:
-            pieces[1, 1, head] = swap(pieces[0, 1, head], 1, 0)
+        store[0, 0, head] = own
+        store[1, 0, head] = swap(await_names(BEFORE_X.get(head, ()), own), 1, 0)
+        store[0, 1, head] = swap(await_names(BEFORE_Y.get(head, ()), own), 0, 2)
+        if RELAY[head] == "x":
+            store[1, 1, head] = swap(store[0, 1, head], 1, 0)
+        elif RELAY[head] == "y":
+            store[1, 1, head] = swap(store[1, 0, head], 0, 2)
         else:
-            pieces[1, 1, head] = swap(pieces[1, 0, head], 0, 2)
-
-    late = [(1, 1, heads - 2)] + [name for name in pieces if name[2] == heads - 1]
-    base = (mine, other)
-    for chosen in ([name for name in pieces if name not in late], late):
+            store[1, 1, head] = swap(own, 1, 2)
+
+    names = [name for name in store if isinstance(name, tuple)]
+    late = [name for name in names if name[2] == heads - 1 or name in LATE]
+    base = (mine, store["other"])
+    for chosen in ([name for name in names if name not in late], late):
         base = partial_projection(
             projection_info,
-            (near, far),
-            {name: pieces[name] for name in chosen},
+            (near, store["far"]),
+            {name: store[name] for name in chosen},
             gate_block,
             base,
             tile,

time: 96.1 us -> 79.8 us (0.83)
  the two profiles are of different devices: /device:TPU:0 before, /device:TPU:9 now
where the time goes in v7:
time: 79.8 us; the launch traced here: 79.2 us
  starting transfers between devices  30.3 us (38%)
  Pallas kernels  28.3 us (35%)
  waiting for transfers between devices  8.9 us (11%)
  local copies, waits for them, and re-layouts  6.85 us (9%)
  other arithmetic  4.59 us (6%)
    pallas_call x4, Pallas kernels, attention(): pl.pallas_call(functools.partial(attention_kernel, *tiles), out_shape=jax...  15.2 us
    ppermute x7, starting transfers between devices, swap(): lax.ppermute(value, 'head', [(i, i ^ head_bits) for i in range(head_count)])  14.2 us
    ppermute x6, starting transfers between devices, halo(): return [lax.ppermute(part, 'tokens', pairs) for pairs in rounds]  11.3 us
    pallas_call x3, Pallas kernels, copy_columns(): pl.pallas_call(functools.partial(copy_kernel, plan), out_shape=[jax.Shape...  6.81 us
    pallas_call x2, Pallas kernels, partial_projection(): pl.pallas_call(functools.partial(partial_kernel, first, tuple(pieces), ti...  6.31 us
    unnamed x26, local copies, waits for them, and re-layouts  5.14 us
    ppermute x5, starting transfers between devices, swap(): return lax.ppermute(value, 'branch', [(0, 1), (1, 0)])  4.68 us
    ppermute x7, waiting for transfers between devices, swap(): lax.ppermute(value, 'head', [(i, i ^ head_bits) for i in range(head_count)])  3.64 us
  transfers between devices with their start and end apart: 18, of which 6 were waited for; matrix products, arithmetic and copies ran while one was open for 6% of the time, Pallas kernels for 30%

profile of v7, /device:TPU:9, one launch (start us, length us, event | category | flops | bytes accessed | tf_op | source)
XLA Modules:
  0.0 79.2 jit_solution(12364848935566945572)
XLA Ops:
  0.0 0.0 copy-start
  0.0 0.1 pad_add_fusion.1.info_ref
  0.1 1.7 %copy_columns.3.own_ref = bf16[2,1152,128]{2,1,0:T(8,128)(2,1)S(1)} custom-call(s32[2]{0:T(128)S(1)} %pad_add_fusion.1.info_ref, bf16[1152,384]{1,0:T(8,128)(2,1)} %bitcast.14, bf16[1152,384]{1,0:T(8,128)(2,1)} %bitcast.17), custom_call_target="tpu_custom_call" | custom-call | bytes 1024 | tf_op jit(solution)/shard_map/copy_columns/pallas_call | solution.py:182
  1.8 0.1 collective-permute-start
  1.9 4.5 %collective-permute-start.1 = (bf16[2,1152,128]{2,1,0:T(8,128)(2,1)S(1)}, bf16[2,1152,128]{2,1,0:T(8,128)(2,1)}, u32[]{:S(2)}, u32[]{:S(2)}) collective-permute-start(bf16[2,1152,128]{2,1,0:T(8,128)(2,1)S(1)} %copy_columns.3.own_ref), channel_id=1, source_target_pairs={{1,2},{2,1},{5,6},{6,5},{9,10},{10,9},{13,14},{14,13},{17,18},{18,... | collective-permute-start | bytes 1769480 | tf_op jit(solution)/shard_map/ppermute | solution.py:261
  6.4 1.4 %copy.9 = bf16[1,1152,2,384]{3,1,2,0:T(8,128)(2,1)} copy(bf16[1,1152,2,384]{3,2,1,0:T(2,128)(2,1)S(1)} %copy-done.11) | data formatting | bytes 3538944 | tf_op jit(solution)/shard_map/optimization_barrier | solution.py:254
  7.8 2.5 %select_bitcast_fusion = (bf16[1152,384]{1,0:T(8,128)(2,1)S(1)}, bf16[1152,384]{1,0:T(8,128)(2,1)}) fusion(pred[]{:T(512)S(6)} %eq.2, bf16[1,1152,2,384]{3,1,2,0:T(8,128)(2,1)} %copy.9), kind=kLoop, calls=%fused_computation.1 | loop fusion | flops 884736 | bytes 3538945 | tf_op jit(solution)/shard_map/jit(_where)/select_n | solution.py:248
  10.3 2.8 %copy_columns.5 = (bf16[2,1152,128]{2,1,0:T(8,128)(2,1)S(1)}, bf16[384,768]{1,0:T(8,128)(2,1)}) custom-call(s32[2]{0:T(128)S(1)} %pad_add_fusion.1.info_ref, bf16[1152,384]{1,0:T(8,128)(2,1)} %bitcast.15, bf16[1152,384]{1,0:T(8,128)(2,1)} %bitcast.18, bf16[384,3072]{1,0:T(8,128)(2,1)} %refs_2_), custom_call_target="tpu_custom_call" | custom-call | bytes 1024 | tf_op jit(solution)/shard_map/copy_columns/pallas_call | solution.py:182
  13.1 1.3 %collective-permute-start.2 = (bf16[384,768]{1,0:T(8,128)(2,1)}, bf16[384,768]{1,0:T(8,128)(2,1)S(1)}, u32[]{:S(2)}, u32[]{:S(2)}) collective-permute-start(bf16[384,768]{1,0:T(8,128)(2,1)} %get-tuple-element.49), channel_id=1, source_target_pairs={{0,8},{4,12},{8,0},{12,4},{1,9},{5,13},{9,1},{13,5},{2,10},{6,14},... | collective-permute-start | bytes 1769480 | tf_op jit(solution)/shard_map/ppermute | solution.py:218
  14.4 0.0 collective-permute-start.6
  14.4 1.2 %collective-permute-start.4 = (bf16[1152,384]{1,0:T(8,128)(2,1)}, bf16[1152,384]{1,0:T(8,128)(2,1)}, u32[]{:S(2)}, u32[]{:S(2)}) collective-permute-start(bf16[1152,384]{1,0:T(8,128)(2,1)} %get-tuple-element.72), channel_id=1, source_target_pairs={{0,16},{16,0},{1,17},{17,1},{2,18},{18,2},{3,19},{19,3},{4,20},{20... | collective-permute-start | bytes 2654216 | tf_op jit(solution)/shard_map/ppermute | solution.py:216
  15.6 0.2 dynamic-slice_reduce_fusion
  15.8 0.1 add_convert_fusion.1
  15.9 0.1 pad_add_fusion.2.info_ref
  16.0 0.2 collective-permute-done.side_a_ref
  16.2 0.8 %copy-done.1 = bf16[2,1152,128]{2,1,0:T(8,128)(2,1)} copy-done((bf16[2,1152,128]{2,1,0:T(8,128)(2,1)}, bf16[2,1152,128]{2,1,0:T(8,128)(2,1)S(1)}, u32[]{:S(2)}) %copy-start.1) | copy-done | bytes 589848
  17.0 3.2 %collective-permute-start.7 = (bf16[2,1152,128]{2,1,0:T(8,128)(2,1)S(1)}, bf16[2,1152,128]{2,1,0:T(8,128)(2,1)S(1)}, u32[]{:S(2)}, u32[]{:S(2)}) collective-permute-start(bf16[2,1152,128]{2,1,0:T(8,128)(2,1)S(1)} %get-tuple-element.57.own_ref), channel_id=1, source_target_pairs={{1,2},{2,1},{5,6},{6,5},{9,10},{10,9},{13,14},{14,13},{17,18},{18,... | collective-permute-start | bytes 1769480 | tf_op jit(solution)/shard_map/ppermute | solution.py:261
  20.2 0.0 copy-start.2
  20.2 0.0 collective-permute-done.1.side_b_ref
  20.2 2.3 %copy_columns.4 = (bf16[384,768]{1,0:T(8,128)(2,1)S(1)}, bf16[1152,128]{1,0:T(8,128)(2,1)S(1)}, bf16[1152,128]{1,0:T(8,128)(2,1)S(1)}, bf16[1152,128]{1,0:T(8,128)(2,1)S(1)}, bf16[2,1152,128]{2,1,0:T(8,128)(2,1)S(1)}) custom-call(s32[2]{0:T(128)S(1)} %pad_add_fusion.1.info_ref, bf16[1152,384]{1,0:T(8,128)(2,1)} %bitcast.20, bf16[1152,384]{1,0:T(8,128)(2,1)} %bitcast.16, ...), custom_call_target="tpu_custom_call" | custom-call | bytes 1024 | tf_op jit(solution)/shard_map/copy_columns/pallas_call | solution.py:182
  22.5 4.7 %attention.4.refs_2_ = bf16[1152,128]{1,0:T(8,128)(2,1)S(1)} custom-call(s32[5]{0:T(128)S(1)} %pad_add_fusion.2.info_ref, bf16[1152,128]{1,0:T(8,128)(2,1)S(1)} %get-tuple-element.50.q_ref, bf16[2,1152,128]{2,1,0:T(8,128)(2,1)S(1)} %copy_columns.3.own_ref, bf16[2,1152,128]{2,1,0:T(8,128)(2,1)S(1)} %copy-done.2, ...), custom_call_target="tpu_custom_call" | custom-call | bytes 1024 | tf_op jit(solution)/shard_map/attention/pallas_call | solution.py:90
  27.3 1.3 %collective-permute-start.3 = (bf16[1152,128]{1,0:T(8,128)(2,1)S(1)}, bf16[1152,128]{1,0:T(8,128)(2,1)S(1)}, u32[]{:S(2)}, u32[]{:S(2)}) collective-permute-start(bf16[1152,128]{1,0:T(8,128)(2,1)S(1)} %attention.4.refs_2_), channel_id=1, source_target_pairs={{0,8},{4,12},{8,0},{12,4},{1,9},{5,13},{9,1},{13,5},{2,10},{6,14},... | collective-permute-start | bytes 884744 | tf_op jit(solution)/shard_map/ppermute | solution.py:218
  28.6 0.0 collective-permute-done.2.refs_1_
  28.6 0.0 collective-permute-start.10
  28.6 0.0 collective-permute-done.6.side_a_ref
  28.6 3.6 %collective-permute-start.11 = (bf16[2,1152,128]{2,1,0:T(8,128)(2,1)S(1)}, bf16[2,1152,128]{2,1,0:T(8,128)(2,1)S(1)}, u32[]{:S(2)}, u32[]{:S(2)}) collective-permute-start(bf16[2,1152,128]{2,1,0:T(8,128)(2,1)S(1)} %get-tuple-element.59.own_ref), channel_id=1, source_target_pairs={{1,2},{2,1},{5,6},{6,5},{9,10},{10,9},{13,14},{14,13},{17,18},{18,... | collective-permute-start | bytes 1769480 | tf_op jit(solution)/shard_map/ppermute | solution.py:261
  32.2 1.1 %collective-permute-done.3.refs_4_ = bf16[1152,128]{1,0:T(8,128)(2,1)S(1)} collective-permute-done((bf16[1152,128]{1,0:T(8,128)(2,1)S(1)}, bf16[1152,128]{1,0:T(8,128)(2,1)S(1)}, u32[]{:S(2)}, u32[]{:S(2)}) %collective-permute-start.3) | collective-permute-done | bytes 294944 | tf_op jit(solution)/shard_map/ppermute | solution.py:218
  33.3 0.7 copy-done.3
  34.0 1.2 %collective-permute-start.5 = (bf16[1152,128]{1,0:T(8,128)(2,1)S(1)}, bf16[1152,128]{1,0:T(8,128)(2,1)S(1)}, u32[]{:S(2)}, u32[]{:S(2)}) collective-permute-start(bf16[1152,128]{1,0:T(8,128)(2,1)S(1)} %attention.4.refs_2_), channel_id=1, source_target_pairs={{0,16},{16,0},{1,17},{17,1},{2,18},{18,2},{3,19},{19,3},{4,20},{20... | collective-permute-start | bytes 884744 | tf_op jit(solution)/shard_map/ppermute | solution.py:216
  35.3 0.0 collective-permute-done.7.side_b_ref
  35.3 4.7 %attention.5.refs_6_ = bf16[1152,128]{1,0:T(8,128)(2,1)S(1)} custom-call(s32[5]{0:T(128)S(1)} %pad_add_fusion.2.info_ref, bf16[1152,128]{1,0:T(8,128)(2,1)S(1)} %get-tuple-element.56.q_ref, bf16[2,1152,128]{2,1,0:T(8,128)(2,1)S(1)} %get-tuple-element.57.own_ref, bf16[2,1152,128]{2,1,0:T(8,128)(2,1)} %collective-permute-done.6.side_a_ref, ...), custom_call_target="tpu_custom_call" | custom-call | bytes 1024 | tf_op jit(solution)/shard_map/attention/pallas_call | solution.py:90
  40.0 0.3 collective-permute-start.12
  40.3 0.0 collective-permute-done.5.refs_3_
  40.3 1.2 %collective-permute-start.13 = (bf16[1152,128]{1,0:T(8,128)(2,1)S(1)}, bf16[1152,128]{1,0:T(8,128)(2,1)S(1)}, u32[]{:S(2)}, u32[]{:S(2)}) collective-permute-start(bf16[1152,128]{1,0:T(8,128)(2,1)S(1)} %collective-permute-done.5.refs_3_), channel_id=1, source_target_pairs={{0,8},{4,12},{8,0},{12,4},{1,9},{5,13},{9,1},{13,5},{2,10},{6,14},... | collective-permute-start | bytes 884744 | tf_op jit(solution)/shard_map/ppermute | solution.py:218
  41.6 0.0 collective-permute-done.4.refs_11_
  41.6 0.2 collective-permute-start.8
  41.8 0.0 collective-permute-done.10.side_a_ref
  41.8 2.7 %collective-permute-done.11.side_b_ref = bf16[2,1152,128]{2,1,0:T(8,128)(2,1)S(1)} collective-permute-done((bf16[2,1152,128]{2,1,0:T(8,128)(2,1)S(1)}, bf16[2,1152,128]{2,1,0:T(8,128)(2,1)S(1)}, u32[]{:S(2)}, u32[]{:S(2)}) %collective-permute-start.11) | collective-permute-done | bytes 589856 | tf_op jit(solution)/shard_map/ppermute | solution.py:261
  44.5 3.0 %attention.6.refs_0_ = bf16[1152,128]{1,0:T(8,128)(2,1)S(1)} custom-call(s32[5]{0:T(128)S(1)} %pad_add_fusion.2.info_ref, bf16[1152,128]{1,0:T(8,128)(2,1)S(1)} %get-tuple-element.58.q_ref, bf16[2,1152,128]{2,1,0:T(8,128)(2,1)S(1)} %get-tuple-element.59.own_ref, bf16[2,1152,128]{2,1,0:T(8,128)(2,1)S(1)} %collective-permute-done.10.side_a_ref, ...), custom_call_target="tpu_custom_call" | custom-call | bytes 1024 | tf_op jit(solution)/shard_map/attention/pallas_call | solution.py:90
  47.5 0.0 copy-start.12
  47.6 0.0 collective-permute-done.12.refs_7_
  47.6 2.7 %attention.7.refs_3_ = bf16[1152,128]{1,0:T(8,128)(2,1)S(1)} custom-call(s32[5]{0:T(128)S(1)} %pad_add_fusion.2.info_ref, bf16[1152,128]{1,0:T(8,128)(2,1)S(1)} %get-tuple-element.58.q_ref, bf16[2,1152,128]{2,1,0:T(8,128)(2,1)S(1)} %get-tuple-element.59.own_ref, bf16[2,1152,128]{2,1,0:T(8,128)(2,1)S(1)} %collective-permute-done.10.side_a_ref, ...), custom_call_target="tpu_custom_call" | custom-call | bytes 1024 | tf_op jit(solution)/shard_map/attention/pallas_call | solution.py:90
  50.3 0.0 collective-permute-done.13.refs_5_
  50.3 0.0 copy-start.9
  50.4 0.7 copy-done.9
  51.1 1.7 %collective-permute-start.14 = (bf16[1152,128]{1,0:T(8,128)(2,1)S(1)}, bf16[1152,128]{1,0:T(8,128)(2,1)}, u32[]{:S(2)}, u32[]{:S(2)}) collective-permute-start(bf16[1152,128]{1,0:T(8,128)(2,1)S(1)} %attention.7.refs_3_), channel_id=1, source_target_pairs={{0,16},{16,0},{1,17},{17,1},{2,18},{18,2},{3,19},{19,3},{4,20},{20... | collective-permute-start | bytes 884744 | tf_op jit(solution)/shard_map/ppermute | solution.py:216
  52.8 0.1 constant_dynamic-slice_fusion.1
  52.9 1.5 %collective-permute-start.15 = (bf16[1152,128]{1,0:T(8,128)(2,1)S(1)}, bf16[1152,128]{1,0:T(8,128)(2,1)S(1)}, u32[]{:S(2)}, u32[]{:S(2)}) collective-permute-start(bf16[1152,128]{1,0:T(8,128)(2,1)S(1)} %attention.7.refs_3_), channel_id=1, source_target_pairs={{0,8},{4,12},{8,0},{12,4},{1,9},{5,13},{9,1},{13,5},{2,10},{6,14},... | collective-permute-start | bytes 884744 | tf_op jit(solution)/shard_map/ppermute | solution.py:218
  54.4 0.0 collective-permute-done.8.refs_8_
  54.4 0.2 collective-permute-start.9
  54.6 2.3 %collective-permute-done.14.refs_4_ = bf16[1152,128]{1,0:T(8,128)(2,1)} collective-permute-done((bf16[1152,128]{1,0:T(8,128)(2,1)S(1)}, bf16[1152,128]{1,0:T(8,128)(2,1)}, u32[]{:S(2)}, u32[]{:S(2)}) %collective-permute-start.14) | collective-permute-done | bytes 294944 | tf_op jit(solution)/shard_map/ppermute | solution.py:216
  57.0 1.7 %collective-permute-start.16 = (bf16[1152,128]{1,0:T(8,128)(2,1)}, bf16[1152,128]{1,0:T(8,128)(2,1)S(1)}, u32[]{:S(2)}, u32[]{:S(2)}) collective-permute-start(bf16[1152,128]{1,0:T(8,128)(2,1)} %collective-permute-done.14.refs_4_), channel_id=1, source_target_pairs={{0,8},{4,12},{8,0},{12,4},{1,9},{5,13},{9,1},{13,5},{2,10},{6,14},... | collective-permute-start | bytes 884744 | tf_op jit(solution)/shard_map/ppermute | solution.py:218
  58.7 0.7 pad_add_fusion.info_ref
  59.4 1.0 %copy-done.6 = bf16[1152,128]{1,0:T(8,128)(2,1)S(1)} copy-done((bf16[1152,128]{1,0:T(8,128)(2,1)S(1)}, bf16[1152,128]{1,0:T(8,128)(2,1)}, u32[]{:S(2)}) %copy-start.6) | copy-done | bytes 294936
  60.4 1.0 %copy-done.8 = bf16[1152,128]{1,0:T(8,128)(2,1)S(1)} copy-done((bf16[1152,128]{1,0:T(8,128)(2,1)S(1)}, bf16[1152,128]{1,0:T(8,128)(2,1)}, u32[]{:S(2)}) %copy-start.8) | copy-done | bytes 294936
  61.3 1.0 %copy-done.10 = bf16[1152,128]{1,0:T(8,128)(2,1)S(1)} copy-done((bf16[1152,128]{1,0:T(8,128)(2,1)S(1)}, bf16[1152,128]{1,0:T(8,128)(2,1)}, u32[]{:S(2)}) %copy-start.10) | copy-done | bytes 294936
  62.3 3.5 %partial_projection.2 = (f32[1152,384]{1,0:T(8,128)S(1)}, f32[1152,384]{1,0:T(8,128)S(1)}) custom-call(s32[21]{0:T(128)S(1)} %pad_add_fusion.info_ref, bf16[384,768]{1,0:T(8,128)(2,1)S(1)} %get-tuple-element.42.refs_0_, bf16[384,768]{1,0:T(8,128)(2,1)S(1)} %collective-permute-done.2.refs_1_, bf16[1152,128]{1,0:T(8,128)(2,1)S(1)} %attention.4.refs_2_, ...), custom_call_target="tpu_custom_call" | custom-call | bytes 1024 | tf_op jit(solution)/shard_map/partial_projection/pallas_call | solution.py:145
  65.8 0.0 collective-permute-done.15.refs_5_
  65.8 0.0 collective-permute-done.9.refs_2_
  65.9 0.4 collective-permute-done.16.refs_6_
  66.3 2.8 %partial_projection.3 = (f32[1152,384]{1,0:T(8,128)S(1)}, bf16[1152,384]{1,0:T(8,128)(2,1)S(1)}) custom-call(s32[21]{0:T(128)S(1)} %pad_add_fusion.info_ref, bf16[384,768]{1,0:T(8,128)(2,1)S(1)} %get-tuple-element.42.refs_0_, bf16[384,768]{1,0:T(8,128)(2,1)S(1)} %collective-permute-done.2.refs_1_, bf16[1152,128]{1,0:T(8,128)(2,1)S(1)} %collective-permute-done.9.refs_2_, ...), custom_call_target="tpu_custom_call" | custom-call | bytes 1024 | tf_op jit(solution)/shard_map/partial_projection/pallas_call | solution.py:145
  69.1 6.9 %collective-permute-start.17 = (bf16[1152,384]{1,0:T(8,128)(2,1)S(1)}, bf16[1152,384]{1,0:T(8,128)(2,1)S(1)}, u32[]{:S(2)}, u32[]{:S(2)}) collective-permute-start(bf16[1152,384]{1,0:T(8,128)(2,1)S(1)} %get-tuple-element.70), channel_id=1, source_target_pairs={{0,4},{4,0},{8,12},{12,8},{1,5},{5,1},{9,13},{13,9},{2,6},{6,2},{1... | collective-permute-start | bytes 2654216 | tf_op jit(solution)/shard_map/ppermute | solution.py:218
  76.0 2.1 %collective-permute-done.17 = bf16[1152,384]{1,0:T(8,128)(2,1)S(1)} collective-permute-done((bf16[1152,384]{1,0:T(8,128)(2,1)S(1)}, bf16[1152,384]{1,0:T(8,128)(2,1)S(1)}, u32[]{:S(2)}, u32[]{:S(2)}) %collective-permute-start.17) | collective-permute-done | bytes 884768 | tf_op jit(solution)/shard_map/ppermute | solution.py:218
  78.1 1.1 %add_convert_fusion = bf16[1152,384]{1,0:T(8,128)(2,1)} fusion(f32[1152,384]{1,0:T(8,128)S(1)} %get-tuple-element.69, bf16[1152,384]{1,0:T(8,128)(2,1)S(1)} %collective-permute-done.17), kind=kLoop, calls=%fused_computation | loop fusion | flops 1327104 | bytes 3538944 | tf_op jit(solution)/shard_map/convert_element_type | solution.py:327
  (18 shorter events, 0.0 us)
Async XLA Ops:
  0.0 15.6 %copy-start = (s32[3,4]{1,0:T(4,128)S(1)}, s32[3,4]{1,0:T(4,128)}, u32[]{:S(2)}) copy-start(s32[3,4]{1,0:T(4,128)} %param.14) | copy-start | bytes 148
  0.0 6.4 %copy-start.11 = (bf16[1,1152,2,384]{3,2,1,0:T(2,128)(2,1)S(1)}, bf16[1,1152,2,384]{3,2,1,0:T(2,128)(2,1)}, u32[]{:S(2)}) copy-start(bf16[1,1152,2,384]{3,2,1,0:T(2,128)(2,1)} %param.11) | copy-start | bytes 5308420
  1.8 14.4 %collective-permute-start = (bf16[2,1152,128]{2,1,0:T(8,128)(2,1)S(1)}, bf16[2,1152,128]{2,1,0:T(8,128)(2,1)S(1)}, u32[]{:S(2)}, u32[]{:S(2)}) collective-permute-start(bf16[2,1152,128]{2,1,0:T(8,128)(2,1)S(1)} %copy_columns.3.own_ref), channel_id=1, source_target_pairs={{0,1},{1,0},{2,3},{3,2},{4,5},{5,4},{6,7},{7,6},{8,9},{9,8},{10,11... | collective-permute-start | bytes 1769480 | tf_op jit(solution)/shard_map/ppermute | solution.py:261
  1.9 18.3 %collective-permute-start.1 = (bf16[2,1152,128]{2,1,0:T(8,128)(2,1)S(1)}, bf16[2,1152,128]{2,1,0:T(8,128)(2,1)}, u32[]{:S(2)}, u32[]{:S(2)}) collective-permute-start(bf16[2,1152,128]{2,1,0:T(8,128)(2,1)S(1)} %copy_columns.3.own_ref), channel_id=1, source_target_pairs={{1,2},{2,1},{5,6},{6,5},{9,10},{10,9},{13,14},{14,13},{17,18},{18,... | collective-permute-start | bytes 1769480 | tf_op jit(solution)/shard_map/ppermute | solution.py:261
  13.1 15.5 %collective-permute-start.2 = (bf16[384,768]{1,0:T(8,128)(2,1)}, bf16[384,768]{1,0:T(8,128)(2,1)S(1)}, u32[]{:S(2)}, u32[]{:S(2)}) collective-permute-start(bf16[384,768]{1,0:T(8,128)(2,1)} %get-tuple-element.49), channel_id=1, source_target_pairs={{0,8},{4,12},{8,0},{12,4},{1,9},{5,13},{9,1},{13,5},{2,10},{6,14},... | collective-permute-start | bytes 1769480 | tf_op jit(solution)/shard_map/ppermute | solution.py:218
  14.4 14.2 %collective-permute-start.6 = (bf16[2,1152,128]{2,1,0:T(8,128)(2,1)S(1)}, bf16[2,1152,128]{2,1,0:T(8,128)(2,1)}, u32[]{:S(2)}, u32[]{:S(2)}) collective-permute-start(bf16[2,1152,128]{2,1,0:T(8,128)(2,1)S(1)} %get-tuple-element.57.own_ref), channel_id=1, source_target_pairs={{0,1},{1,0},{2,3},{3,2},{4,5},{5,4},{6,7},{7,6},{8,9},{9,8},{10,11... | collective-permute-start | bytes 1769480 | tf_op jit(solution)/shard_map/ppermute | solution.py:261
  14.4 27.1 %collective-permute-start.4 = (bf16[1152,384]{1,0:T(8,128)(2,1)}, bf16[1152,384]{1,0:T(8,128)(2,1)}, u32[]{:S(2)}, u32[]{:S(2)}) collective-permute-start(bf16[1152,384]{1,0:T(8,128)(2,1)} %get-tuple-element.72), channel_id=1, source_target_pairs={{0,16},{16,0},{1,17},{17,1},{2,18},{18,2},{3,19},{19,3},{4,20},{20... | collective-permute-start | bytes 2654216 | tf_op jit(solution)/shard_map/ppermute | solution.py:216
  16.2 0.8 %copy-start.1 = (bf16[2,1152,128]{2,1,0:T(8,128)(2,1)}, bf16[2,1152,128]{2,1,0:T(8,128)(2,1)S(1)}, u32[]{:S(2)}) copy-start(bf16[2,1152,128]{2,1,0:T(8,128)(2,1)S(1)} %collective-permute-done.side_a_ref) | copy-start | bytes 1769476
  17.0 18.3 %collective-permute-start.7 = (bf16[2,1152,128]{2,1,0:T(8,128)(2,1)S(1)}, bf16[2,1152,128]{2,1,0:T(8,128)(2,1)S(1)}, u32[]{:S(2)}, u32[]{:S(2)}) collective-permute-start(bf16[2,1152,128]{2,1,0:T(8,128)(2,1)S(1)} %get-tuple-element.57.own_ref), channel_id=1, source_target_pairs={{1,2},{2,1},{5,6},{6,5},{9,10},{10,9},{13,14},{14,13},{17,18},{18,... | collective-permute-start | bytes 1769480 | tf_op jit(solution)/shard_map/ppermute | solution.py:261
  20.2 2.3 %copy-start.2 = (bf16[2,1152,128]{2,1,0:T(8,128)(2,1)S(1)}, bf16[2,1152,128]{2,1,0:T(8,128)(2,1)}, u32[]{:S(2)}) copy-start(bf16[2,1152,128]{2,1,0:T(8,128)(2,1)} %copy-done.1) | copy-start | bytes 1769476
  27.3 6.0 %collective-permute-start.3 = (bf16[1152,128]{1,0:T(8,128)(2,1)S(1)}, bf16[1152,128]{1,0:T(8,128)(2,1)S(1)}, u32[]{:S(2)}, u32[]{:S(2)}) collective-permute-start(bf16[1152,128]{1,0:T(8,128)(2,1)S(1)} %attention.4.refs_2_), channel_id=1, source_target_pairs={{0,8},{4,12},{8,0},{12,4},{1,9},{5,13},{9,1},{13,5},{2,10},{6,14},... | collective-permute-start | bytes 884744 | tf_op jit(solution)/shard_map/ppermute | solution.py:218
  28.6 13.2 %collective-permute-start.10 = (bf16[2,1152,128]{2,1,0:T(8,128)(2,1)S(1)}, bf16[2,1152,128]{2,1,0:T(8,128)(2,1)S(1)}, u32[]{:S(2)}, u32[]{:S(2)}) collective-permute-start(bf16[2,1152,128]{2,1,0:T(8,128)(2,1)S(1)} %get-tuple-element.59.own_ref), channel_id=1, source_target_pairs={{0,1},{1,0},{2,3},{3,2},{4,5},{5,4},{6,7},{7,6},{8,9},{9,8},{10,11... | collective-permute-start | bytes 1769480 | tf_op jit(solution)/shard_map/ppermute | solution.py:261
  28.6 15.9 %collective-permute-start.11 = (bf16[2,1152,128]{2,1,0:T(8,128)(2,1)S(1)}, bf16[2,1152,128]{2,1,0:T(8,128)(2,1)S(1)}, u32[]{:S(2)}, u32[]{:S(2)}) collective-permute-start(bf16[2,1152,128]{2,1,0:T(8,128)(2,1)S(1)} %get-tuple-element.59.own_ref), channel_id=1, source_target_pairs={{1,2},{2,1},{5,6},{6,5},{9,10},{10,9},{13,14},{14,13},{17,18},{18,... | collective-permute-start | bytes 1769480 | tf_op jit(solution)/shard_map/ppermute | solution.py:261
  33.3 0.7 copy-start.3
  34.0 6.3 %collective-permute-start.5 = (bf16[1152,128]{1,0:T(8,128)(2,1)S(1)}, bf16[1152,128]{1,0:T(8,128)(2,1)S(1)}, u32[]{:S(2)}, u32[]{:S(2)}) collective-permute-start(bf16[1152,128]{1,0:T(8,128)(2,1)S(1)} %attention.4.refs_2_), channel_id=1, source_target_pairs={{0,16},{16,0},{1,17},{17,1},{2,18},{18,2},{3,19},{19,3},{4,20},{20... | collective-permute-start | bytes 884744 | tf_op jit(solution)/shard_map/ppermute | solution.py:216
  40.0 7.5 %collective-permute-start.12 = (bf16[1152,128]{1,0:T(8,128)(2,1)S(1)}, bf16[1152,128]{1,0:T(8,128)(2,1)S(1)}, u32[]{:S(2)}, u32[]{:S(2)}) collective-permute-start(bf16[1152,128]{1,0:T(8,128)(2,1)S(1)} %attention.5.refs_6_), channel_id=1, source_target_pairs={{0,16},{16,0},{1,17},{17,1},{2,18},{18,2},{3,19},{19,3},{4,20},{20... | collective-permute-start | bytes 884744 | tf_op jit(solution)/shard_map/ppermute | solution.py:216
  40.3 10.0 %copy-start.5 = (bf16[1152,128]{1,0:T(8,128)(2,1)}, bf16[1152,128]{1,0:T(8,128)(2,1)S(1)}, u32[]{:S(2)}) copy-start(bf16[1152,128]{1,0:T(8,128)(2,1)S(1)} %collective-permute-done.5.refs_3_) | copy-start | bytes 884740
  40.3 10.0 %collective-permute-start.13 = (bf16[1152,128]{1,0:T(8,128)(2,1)S(1)}, bf16[1152,128]{1,0:T(8,128)(2,1)S(1)}, u32[]{:S(2)}, u32[]{:S(2)}) collective-permute-start(bf16[1152,128]{1,0:T(8,128)(2,1)S(1)} %collective-permute-done.5.refs_3_), channel_id=1, source_target_pairs={{0,8},{4,12},{8,0},{12,4},{1,9},{5,13},{9,1},{13,5},{2,10},{6,14},... | collective-permute-start | bytes 884744 | tf_op jit(solution)/shard_map/ppermute | solution.py:218
  41.6 12.8 %collective-permute-start.8 = (bf16[1152,128]{1,0:T(8,128)(2,1)S(1)}, bf16[1152,128]{1,0:T(8,128)(2,1)}, u32[]{:S(2)}, u32[]{:S(2)}) collective-permute-start(bf16[1152,128]{1,0:T(8,128)(2,1)S(1)} %attention.5.refs_6_), channel_id=1, source_target_pairs={{0,8},{4,12},{8,0},{12,4},{1,9},{5,13},{9,1},{13,5},{2,10},{6,14},... | collective-permute-start | bytes 884744 | tf_op jit(solution)/shard_map/ppermute | solution.py:218
  47.5 5.2 %copy-start.12 = (bf16[2,2,1536]{2,1,0:T(2,128)(2,1)S(1)}, bf16[2,2,1536]{2,1,0:T(2,128)(2,1)}, u32[]{:S(2)}) copy-start(bf16[2,2,1536]{2,1,0:T(2,128)(2,1)} %param.12) | copy-start | bytes 36868
  47.5 11.9 %copy-start.4 = (bf16[1152,128]{1,0:T(8,128)(2,1)S(1)}, bf16[1152,128]{1,0:T(8,128)(2,1)}, u32[]{:S(2)}) copy-start(bf16[1152,128]{1,0:T(8,128)(2,1)} %copy-done.3) | copy-start | bytes 884740
  47.6 2.8 %copy-start.7 = (bf16[1152,128]{1,0:T(8,128)(2,1)}, bf16[1152,128]{1,0:T(8,128)(2,1)S(1)}, u32[]{:S(2)}) copy-start(bf16[1152,128]{1,0:T(8,128)(2,1)S(1)} %collective-permute-done.12.refs_7_) | copy-start | bytes 884740
  50.3 0.7 copy-start.9
  51.1 5.9 %collective-permute-start.14 = (bf16[1152,128]{1,0:T(8,128)(2,1)S(1)}, bf16[1152,128]{1,0:T(8,128)(2,1)}, u32[]{:S(2)}, u32[]{:S(2)}) collective-permute-start(bf16[1152,128]{1,0:T(8,128)(2,1)S(1)} %attention.7.refs_3_), channel_id=1, source_target_pairs={{0,16},{16,0},{1,17},{17,1},{2,18},{18,2},{3,19},{19,3},{4,20},{20... | collective-permute-start | bytes 884744 | tf_op jit(solution)/shard_map/ppermute | solution.py:216
  52.9 13.0 %collective-permute-start.15 = (bf16[1152,128]{1,0:T(8,128)(2,1)S(1)}, bf16[1152,128]{1,0:T(8,128)(2,1)S(1)}, u32[]{:S(2)}, u32[]{:S(2)}) collective-permute-start(bf16[1152,128]{1,0:T(8,128)(2,1)S(1)} %attention.7.refs_3_), channel_id=1, source_target_pairs={{0,8},{4,12},{8,0},{12,4},{1,9},{5,13},{9,1},{13,5},{2,10},{6,14},... | collective-permute-start | bytes 884744 | tf_op jit(solution)/shard_map/ppermute | solution.py:218
  54.4 11.5 %collective-permute-start.9 = (bf16[1152,128]{1,0:T(8,128)(2,1)}, bf16[1152,128]{1,0:T(8,128)(2,1)S(1)}, u32[]{:S(2)}, u32[]{:S(2)}) collective-permute-start(bf16[1152,128]{1,0:T(8,128)(2,1)} %collective-permute-done.8.refs_8_), channel_id=1, source_target_pairs={{0,16},{16,0},{1,17},{17,1},{2,18},{18,2},{3,19},{19,3},{4,20},{20... | collective-permute-start | bytes 884744 | tf_op jit(solution)/shard_map/ppermute | solution.py:216
  57.0 9.3 %collective-permute-start.16 = (bf16[1152,128]{1,0:T(8,128)(2,1)}, bf16[1152,128]{1,0:T(8,128)(2,1)S(1)}, u32[]{:S(2)}, u32[]{:S(2)}) collective-permute-start(bf16[1152,128]{1,0:T(8,128)(2,1)} %collective-permute-done.14.refs_4_), channel_id=1, source_target_pairs={{0,8},{4,12},{8,0},{12,4},{1,9},{5,13},{9,1},{13,5},{2,10},{6,14},... | collective-permute-start | bytes 884744 | tf_op jit(solution)/shard_map/ppermute | solution.py:218
  59.4 1.0 %copy-start.6 = (bf16[1152,128]{1,0:T(8,128)(2,1)S(1)}, bf16[1152,128]{1,0:T(8,128)(2,1)}, u32[]{:S(2)}) copy-start(bf16[1152,128]{1,0:T(8,128)(2,1)} %copy-done.5) | copy-start | bytes 884740
  60.4 1.0 %copy-start.8 = (bf16[1152,128]{1,0:T(8,128)(2,1)S(1)}, bf16[1152,128]{1,0:T(8,128)(2,1)}, u32[]{:S(2)}) copy-start(bf16[1152,128]{1,0:T(8,128)(2,1)} %copy-done.7) | copy-start | bytes 884740
  61.3 1.0 %copy-start.10 = (bf16[1152,128]{1,0:T(8,128)(2,1)S(1)}, bf16[1152,128]{1,0:T(8,128)(2,1)}, u32[]{:S(2)}) copy-start(bf16[1152,128]{1,0:T(8,128)(2,1)} %copy-done.9) | copy-start | bytes 884740
  69.1 9.0 %collective-permute-start.17 = (bf16[1152,384]{1,0:T(8,128)(2,1)S(1)}, bf16[1152,384]{1,0:T(8,128)(2,1)S(1)}, u32[]{:S(2)}, u32[]{:S(2)}) collective-permute-start(bf16[1152,384]{1,0:T(8,128)(2,1)S(1)} %get-tuple-element.70), channel_id=1, source_target_pairs={{0,4},{4,0},{8,12},{12,8},{1,5},{5,1},{9,13},{13,9},{2,6},{6,2},{1... | collective-permute-start | bytes 2654216 | tf_op jit(solution)/shard_map/ppermute | solution.py:218

commit v8 on v7

--- a/solution.py
+++ b/solution.py
@@ -12,16 +12,17 @@
 FRAME = 64
 FAR = 1e30
 EXP2_SCALE = math.log2(math.e) / math.sqrt(HD)
-VMEM_LIMIT = 16 * 1024 * 1024
+VMEM_LIMIT = 14 * 1024 * 1024
 COPY_LIMIT = 8 * 1024 * 1024
 COPY_PARTS = 3
 LATE_PACK = True
 RESIDUAL_FIRST = True
-SPLIT = 2
-BEFORE_X = {1: (), 2: ((1, 1, 0),)}
+SPLIT = 0
+TIE_PARTIAL = True
+BEFORE_X = {1: (), 2: ()}
 BEFORE_Y = {1: (), 2: ()}
 RESIDUAL_AFTER = 0
-AWAITED = {0: (), 1: ('far', (0, 1, 0)), 2: ('far', 'other', (1, 0, 0), (0, 1, 0)), 3: ((1, 0, 1),)}
+AWAITED = {0: (), 1: ('far', 'other'), 2: ('far', 'other', (1, 0, 0), (0, 1, 0)), 3: ((1, 0, 1),)}
 RELAY = ('y', 'x', 'y')
 LATE = ((1, 1, 1),)
 SCALARS = pl.BlockSpec(memory_space=pltpu.SMEM)
@@ -41,49 +42,59 @@
         inside = [(base + step >= first) & (base + step <= first + 1) for step in range(2)]
         return pl.ds(pl.multiple_of(base * tile, tile), 2 * tile), inside
 
-    def score(t):
+    refs = (own_ref, side_a_ref, side_b_ref)
+
+    def score(t, side):
         rows, inside = window(t)
-        query = q_ref[t * tile : (t + 1) * tile, :]
-        blocks = []
-        row_max = None
-        for ref, width_ok in zip((own_ref, side_a_ref, side_b_ref), width_oks):
-            scores = lax.dot_general(
-                query, ref[0, rows, :], (((1,), (1,)), ((), ())), preferred_element_type=jnp.float32
-            )
-            for step in range(2):
-                allowed = inside[step] if width_ok is None else inside[step] & width_ok
-                block = scores[:, step * tile : (step + 1) * tile]
-                lanes = block[:, :HD]
-                for first in range(HD, tile, HD):
-                    lanes = jnp.maximum(lanes, block[:, first : first + HD])
-                lanes = jnp.where(allowed, lanes, -FAR)
-                row_max = lanes if row_max is None else jnp.maximum(row_max, lanes)
-                blocks.append((block, allowed))
-        return blocks, jnp.max(row_max, axis=1, keepdims=True) * EXP2_SCALE
-
-    def blend(t, blocks, shift):
+        scores = lax.dot_general(
+            q_ref[t * tile : (t + 1) * tile, :],
+            refs[side][0, rows, :],
+            (((1,), (1,)), ((), ())),
+            preferred_element_type=jnp.float32,
+        )
+        blocks, largest = [], None
+        for step in range(2):
+            allowed = inside[step] if side == 0 else inside[step] & width_oks[side]
+            block = scores[:, step * tile : (step + 1) * tile]
+            lanes = block[:, :HD]
+            for start in range(HD, tile, HD):
+                lanes = jnp.maximum(lanes, block[:, start : start + HD])
+            lanes = jnp.where(allowed, lanes, -FAR)
+            largest = lanes if largest is None else jnp.maximum(largest, lanes)
+            blocks.append((block, allowed))
+        return blocks, largest
+
+    def blend(t, side, blocks, shift):
         rows, _ = window(t)
         weights = [
             jnp.exp2(block * EXP2_SCALE - jnp.where(allowed, shift, FAR)).astype(jnp.bfloat16)
             for block, allowed in blocks
         ]
-        values = jnp.concatenate(
-            [ref[1, rows, :] for ref in (own_ref, side_a_ref, side_b_ref)], axis=0
-        )
-        total = jnp.dot(
+        values = refs[side][1, rows, :]
+        return jnp.dot(
             jnp.concatenate(weights, axis=1),
             jnp.concatenate([values, jnp.ones_like(values)], axis=1),
             preferred_element_type=jnp.float32,
         )
-        out_ref[t * tile : (t + 1) * tile, :] = (total[:, :HD] / total[:, HD:]).astype(jnp.bfloat16)
-
-    ready = score(first)
+
+    ready = [score(first, side) for side in range(3)]
     for ref in earlier:
         out_ref[: first * tile, :] = ref[: first * tile, :]
     for t in range(first, last):
-        later = score(t + 1) if t + 1 < last else None
-        blend(t, *ready)
+        row_max = jnp.maximum(jnp.maximum(ready[0][1], ready[1][1]), ready[2][1])
+        shift = jnp.max(row_max, axis=1, keepdims=True) * EXP2_SCALE
+        later, total = [], None
+        for side in range(3):
+            if t + 1 < last:
+                later.append(score(t + 1, side))
+            part = blend(t, side, ready[side][0], shift)
+            total = part if total is None else total + part
+        out_ref[t * tile : (t + 1) * tile, :] = (total[:, :HD] / total[:, HD:]).astype(jnp.bfloat16)
         ready = later
+
+
+def pinned(operands):
+    return [pltpu.with_memory_space_constraint(operand, pltpu.VMEM) for operand in operands]
 
 
 def attention(info, tiles, *operands):
@@ -95,7 +106,7 @@
         compiler_params=pltpu.CompilerParams(vmem_limit_bytes=VMEM_LIMIT),
         cost_estimate=SMALL_COST,
         name="attention",
-    )(info, *operands)
+    )(info, *pinned(operands))
 
 
 def partial_kernel(first, kinds, tile, info_ref, *refs):
@@ -153,7 +164,7 @@
         compiler_params=pltpu.CompilerParams(vmem_limit_bytes=VMEM_LIMIT),
         cost_estimate=SMALL_COST,
         name="partial_projection",
-    )(info, *weights, *pieces.values(), gate, *base)
+    )(info, *pinned([*weights, *pieces.values()]), gate, *pinned(base))
 
 
 def copy_kernel(plan, info_ref, *refs):
@@ -191,6 +202,30 @@
     )(info, *[pltpu.with_memory_space_constraint(source, pltpu.HBM) for source in sources])
 
 
+def halves_kernel(info_ref, both_ref, mine_ref, other_ref, sems):
+    copies = [
+        pltpu.make_async_copy(both_ref.at[half], to, sems.at[index])
+        for index, (half, to) in enumerate(((info_ref[0], mine_ref), (1 - info_ref[0], other_ref)))
+    ]
+    for copy in copies:
+        copy.start()
+    for copy in copies:
+        copy.wait()
+
+
+def split_halves(info, both):
+    return pl.pallas_call(
+        halves_kernel,
+        out_shape=[jax.ShapeDtypeStruct(both.shape[1:], both.dtype)] * 2,
+        in_specs=[SCALARS, pl.BlockSpec(memory_space=pl.ANY)],
+        out_specs=[IN_VMEM] * 2,
+        scratch_shapes=[pltpu.SemaphoreType.DMA((2,))],
+        compiler_params=pltpu.CompilerParams(vmem_limit_bytes=COPY_LIMIT),
+        cost_estimate=SMALL_COST,
+        name="split_halves",
+    )(info, both)
+
+
 def local(queries, keys, values, residual, gate, out_weight, time_offsets, guidance_index):
     tiles_time, tiles_wide = time_offsets.shape
     count, features = queries.shape[1:]
@@ -244,9 +279,7 @@
         )
 
     def split_residual(residual):
-        first_half, second_half = residual[0, :, 0], residual[0, :, 1]
-        mine = jnp.where(branch_pos == 0, first_half, second_half)
-        return mine, jnp.where(branch_pos == 0, second_half, first_half)
+        return split_halves(branch_pos[None], jnp.transpose(residual[0], (1, 0, 2)))
 
     packed = pack(key_value[:1])
     after = packed
@@ -283,6 +316,14 @@
     attention_info = jnp.concatenate([offsets, edges])
     place = head_pos & 1
     projection_info = jnp.concatenate([jnp.stack([branch_pos, place, place ^ 1]), guidance_index])
+
+    def relay(head):
+        if RELAY[head] == "x":
+            store[1, 1, head] = swap(store[0, 1, head], 1, 0)
+        elif RELAY[head] == "y":
+            store[1, 1, head] = swap(store[1, 0, head], 0, 2)
+        else:
+            store[1, 1, head] = swap(store[0, 0, head], 1, 2)
 
     def await_names(names, value):
         value, awaited = lax.optimization_barrier((value, [store[name] for name in names]))
@@ -304,26 +345,30 @@
         store[0, 0, head] = own
         store[1, 0, head] = swap(await_names(BEFORE_X.get(head, ()), own), 1, 0)
         store[0, 1, head] = swap(await_names(BEFORE_Y.get(head, ()), own), 0, 2)
-        if RELAY[head] == "x":
-            store[1, 1, head] = swap(store[0, 1, head], 1, 0)
-        elif RELAY[head] == "y":
-            store[1, 1, head] = swap(store[1, 0, head], 0, 2)
-        else:
-            store[1, 1, head] = swap(own, 1, 2)
+        if head < heads - 1:
+            relay(head)
 
     names = [name for name in store if isinstance(name, tuple)]
     late = [name for name in names if name[2] == heads - 1 or name in LATE]
     base = (mine, store["other"])
-    for chosen in ([name for name in names if name not in late], late):
-        base = partial_projection(
+
+    def partial(names, base):
+        return partial_projection(
             projection_info,
             (near, store["far"]),
-            {name: store[name] for name in chosen},
+            {name: store[name] for name in names},
             gate_block,
             base,
             tile,
             base[0] is mine,
         )
+
+    base = partial([name for name in names if name not in late], base)
+    if TIE_PARTIAL:
+        name = (1, 0, heads - 1) if RELAY[-1] == "y" else (0, 1, heads - 1)
+        base, store[name] = lax.optimization_barrier((base, store[name]))
+    relay(heads - 1)
+    base = partial(late + [(1, 1, heads - 1)], base)
     return (base[0] + swap(base[1], 0, 1).astype(jnp.float32)).astype(jnp.bfloat16)
 
 

time: 79.8 us -> 79.2 us (level)
  waiting for transfers between devices: 8.9 us -> 15 us
  other arithmetic: 4.59 us -> 1.43 us
  starting transfers between devices: 30.3 us -> 27.2 us
  local copies, waits for them, and re-layouts: 6.85 us -> 4.5 us
  Pallas kernels: 28.3 us -> 29.6 us
    ppermute x7, waiting for transfers between devices: 3.64 us -> 8.15 us  [swap(): lax.ppermute(value, 'head', [(i, i ^ head_bits) for i in range(head_count)])]
    select_n x1 -> x0, other arithmetic: 2.51 us -> none  [split_residual(): mine = jnp.where(branch_pos == 0, first_half, second_half)]
    ppermute x7, starting transfers between devices: 14.2 us -> 12.1 us  [swap(): lax.ppermute(value, 'head', [(i, i ^ head_bits) for i in range(head_count)])]
    unnamed x26 -> x18, local copies, waits for them, and re-layouts: 5.14 us -> 3.26 us
    ppermute x5, waiting for transfers between devices: 2.35 us -> 4.14 us  [swap(): return lax.ppermute(value, 'branch', [(0, 1), (1, 0)])]
    pallas_call x0 -> x1, Pallas kernels: none -> 1.3 us  [split_halves(): pl.pallas_call(halves_kernel, out_shape=[jax.ShapeDtypeStruct(both.shape[...]
    optimization_barrier x1, local copies, waits for them, and re-layouts: 1.44 us -> 0.23 us  [local(): _, residual = lax.optimization_barrier((packed, residual))]
    pallas_call x4 -> x3, Pallas kernels: 15.2 us -> 14.8 us  [attention(): pl.pallas_call(functools.partial(attention_kernel, *tiles), out_shape=jax...]
  transfers between devices with their start and end apart: 18 -> 18, of which waited for: 6 -> 6; matrix products, arithmetic and copies ran while one was open for 6% -> 2% of each run, Pallas kernels for 30% -> 33%
where the time goes in v8:
time: 79.2 us; the launch traced here: 77.9 us
  Pallas kernels  29.6 us (37%)
  starting transfers between devices  27.2 us (34%)
  waiting for transfers between devices  15 us (19%)
  local copies, waits for them, and re-layouts  4.5 us (6%)
  other arithmetic  1.43 us (2%)
    pallas_call x3, Pallas kernels, attention(): pl.pallas_call(functools.partial(attention_kernel, *tiles), out_shape=jax...  14.8 us
    ppermute x7, starting transfers between devices, swap(): lax.ppermute(value, 'head', [(i, i ^ head_bits) for i in range(head_count)])  12.1 us
    ppermute x6, starting transfers between devices, halo(): return [lax.ppermute(part, 'tokens', pairs) for pairs in rounds]  10.7 us
    ppermute x7, waiting for transfers between devices, swap(): lax.ppermute(value, 'head', [(i, i ^ head_bits) for i in range(head_count)])  8.15 us
    pallas_call x3, Pallas kernels, copy_columns(): pl.pallas_call(functools.partial(copy_kernel, plan), out_shape=[jax.Shape...  7.6 us
    pallas_call x2, Pallas kernels, partial_projection(): pl.pallas_call(functools.partial(partial_kernel, first, tuple(pieces), ti...  5.94 us
    ppermute x5, starting transfers between devices, swap(): return lax.ppermute(value, 'branch', [(0, 1), (1, 0)])  4.34 us
    ppermute x5, waiting for transfers between devices, swap(): return lax.ppermute(value, 'branch', [(0, 1), (1, 0)])  4.14 us
  transfers between devices with their start and end apart: 18, of which 6 were waited for; matrix products, arithmetic and copies ran while one was open for 2% of the time, Pallas kernels for 33%

profile of v8, /device:TPU:9, one launch (start us, length us, event | category | flops | bytes accessed | tf_op | source)
XLA Modules:
  0.0 77.9 jit_solution(14900158682165732446)
XLA Ops:
  0.0 0.0 copy-start
  0.0 0.1 pad_add_fusion.1.info_ref
  0.1 1.7 %copy_columns.3.own_ref = bf16[2,1152,128]{2,1,0:T(8,128)(2,1)S(1)} custom-call(s32[2]{0:T(128)S(1)} %pad_add_fusion.1.info_ref, bf16[1152,384]{1,0:T(8,128)(2,1)} %bitcast.16, bf16[1152,384]{1,0:T(8,128)(2,1)} %bitcast.19), custom_call_target="tpu_custom_call" | custom-call | bytes 1024 | tf_op jit(solution)/shard_map/copy_columns/pallas_call | solution.py:193
  1.8 0.1 collective-permute-start
  1.9 4.5 %collective-permute-start.1 = (bf16[2,1152,128]{2,1,0:T(8,128)(2,1)S(1)}, bf16[2,1152,128]{2,1,0:T(8,128)(2,1)}, u32[]{:S(2)}, u32[]{:S(2)}) collective-permute-start(bf16[2,1152,128]{2,1,0:T(8,128)(2,1)S(1)} %copy_columns.3.own_ref), channel_id=1, source_target_pairs={{1,2},{2,1},{5,6},{6,5},{9,10},{10,9},{13,14},{14,13},{17,18},{18,... | collective-permute-start | bytes 1769480 | tf_op jit(solution)/shard_map/ppermute | solution.py:294
  6.4 0.0 copy-done.7
  6.4 0.2 copy.11
  6.6 1.3 %split_halves.1 = (bf16[1152,384]{1,0:T(8,128)(2,1)S(1)}, bf16[1152,384]{1,0:T(8,128)(2,1)}) custom-call(s32[1]{0:T(128)} %bitcast.info_ref, bf16[2,1152,384]{2,1,0:T(8,128)(2,1)S(1)} %bitcast.15), custom_call_target="tpu_custom_call" | custom-call | bytes 1024 | tf_op jit(solution)/shard_map/split_halves/pallas_call | solution.py:217
  7.9 1.3 %collective-permute-start.3 = (bf16[1152,384]{1,0:T(8,128)(2,1)}, bf16[1152,384]{1,0:T(8,128)(2,1)}, u32[]{:S(2)}, u32[]{:S(2)}) collective-permute-start(bf16[1152,384]{1,0:T(8,128)(2,1)} %get-tuple-element.47), channel_id=1, source_target_pairs={{0,16},{16,0},{1,17},{17,1},{2,18},{18,2},{3,19},{19,3},{4,20},{20... | collective-permute-start | bytes 2654216 | tf_op jit(solution)/shard_map/ppermute | solution.py:251
  9.2 2.8 %copy_columns.5 = (bf16[2,1152,128]{2,1,0:T(8,128)(2,1)S(1)}, bf16[384,768]{1,0:T(8,128)(2,1)}) custom-call(s32[2]{0:T(128)S(1)} %pad_add_fusion.1.info_ref, bf16[1152,384]{1,0:T(8,128)(2,1)} %bitcast.17, bf16[1152,384]{1,0:T(8,128)(2,1)} %bitcast.20, bf16[384,3072]{1,0:T(8,128)(2,1)} %refs_2_), custom_call_target="tpu_custom_call" | custom-call | bytes 1024 | tf_op jit(solution)/shard_map/copy_columns/pallas_call | solution.py:193
  12.0 1.3 %collective-permute-start.2 = (bf16[384,768]{1,0:T(8,128)(2,1)}, bf16[384,768]{1,0:T(8,128)(2,1)S(1)}, u32[]{:S(2)}, u32[]{:S(2)}) collective-permute-start(bf16[384,768]{1,0:T(8,128)(2,1)} %get-tuple-element.51), channel_id=1, source_target_pairs={{0,8},{4,12},{8,0},{12,4},{1,9},{5,13},{9,1},{13,5},{2,10},{6,14},... | collective-permute-start | bytes 1769480 | tf_op jit(solution)/shard_map/ppermute | solution.py:253
  13.3 0.0 collective-permute-start.6
  13.3 0.0 copy-done
  13.3 0.2 dynamic-slice_reduce_fusion
  13.5 0.1 add_convert_fusion.1
  13.5 0.1 pad_add_fusion.2.info_ref
  13.6 2.6 %collective-permute-done.side_a_ref = bf16[2,1152,128]{2,1,0:T(8,128)(2,1)S(1)} collective-permute-done((bf16[2,1152,128]{2,1,0:T(8,128)(2,1)S(1)}, bf16[2,1152,128]{2,1,0:T(8,128)(2,1)S(1)}, u32[]{:S(2)}, u32[]{:S(2)}) %collective-permute-start) | collective-permute-done | bytes 589856 | tf_op jit(solution)/shard_map/ppermute | solution.py:294
  16.2 0.8 %copy-done.1 = bf16[2,1152,128]{2,1,0:T(8,128)(2,1)} copy-done((bf16[2,1152,128]{2,1,0:T(8,128)(2,1)}, bf16[2,1152,128]{2,1,0:T(8,128)(2,1)S(1)}, u32[]{:S(2)}) %copy-start.1) | copy-done | bytes 589848
  17.0 3.2 %collective-permute-start.7 = (bf16[2,1152,128]{2,1,0:T(8,128)(2,1)S(1)}, bf16[2,1152,128]{2,1,0:T(8,128)(2,1)}, u32[]{:S(2)}, u32[]{:S(2)}) collective-permute-start(bf16[2,1152,128]{2,1,0:T(8,128)(2,1)S(1)} %get-tuple-element.59.own_ref), channel_id=1, source_target_pairs={{1,2},{2,1},{5,6},{6,5},{9,10},{10,9},{13,14},{14,13},{17,18},{18,... | collective-permute-start | bytes 1769480 | tf_op jit(solution)/shard_map/ppermute | solution.py:294
  20.2 0.0 copy-start.2
  20.2 0.0 collective-permute-done.1.side_b_ref
  20.2 3.1 %copy_columns.4 = (bf16[384,768]{1,0:T(8,128)(2,1)S(1)}, bf16[1152,128]{1,0:T(8,128)(2,1)S(1)}, bf16[1152,128]{1,0:T(8,128)(2,1)S(1)}, bf16[1152,128]{1,0:T(8,128)(2,1)S(1)}, bf16[2,1152,128]{2,1,0:T(8,128)(2,1)}) custom-call(s32[2]{0:T(128)S(1)} %pad_add_fusion.1.info_ref, bf16[1152,384]{1,0:T(8,128)(2,1)} %bitcast.22, bf16[1152,384]{1,0:T(8,128)(2,1)} %bitcast.18, ...), custom_call_target="tpu_custom_call" | custom-call | bytes 1024 | tf_op jit(solution)/shard_map/copy_columns/pallas_call | solution.py:193
  23.3 0.0 copy-start.3
  23.3 0.7 copy-done.3
  24.1 0.7 copy-done.5
  24.8 0.0 copy-done.2
  24.8 4.8 %attention.3.refs_2_ = bf16[1152,128]{1,0:T(8,128)(2,1)S(1)} custom-call(s32[5]{0:T(128)S(1)} %pad_add_fusion.2.info_ref, bf16[1152,128]{1,0:T(8,128)(2,1)S(1)} %get-tuple-element.54.q_ref, bf16[2,1152,128]{2,1,0:T(8,128)(2,1)S(1)} %copy_columns.3.own_ref, bf16[2,1152,128]{2,1,0:T(8,128)(2,1)S(1)} %copy-done.2, ...), custom_call_target="tpu_custom_call" | custom-call | bytes 1024 | tf_op jit(solution)/shard_map/attention/pallas_call | solution.py:101
  29.6 0.1 collective-permute-start.10
  29.7 0.0 collective-permute-done.2.refs_1_
  29.7 2.9 %collective-permute-start.11 = (bf16[2,1152,128]{2,1,0:T(8,128)(2,1)}, bf16[2,1152,128]{2,1,0:T(8,128)(2,1)}, u32[]{:S(2)}, u32[]{:S(2)}) collective-permute-start(bf16[2,1152,128]{2,1,0:T(8,128)(2,1)} %get-tuple-element.61.own_ref), channel_id=1, source_target_pairs={{1,2},{2,1},{5,6},{6,5},{9,10},{10,9},{13,14},{14,13},{17,18},{18,... | collective-permute-start | bytes 1769480 | tf_op jit(solution)/shard_map/ppermute | solution.py:294
  32.6 0.0 collective-permute-done.6.side_a_ref
  32.6 1.3 %collective-permute-start.4 = (bf16[1152,128]{1,0:T(8,128)(2,1)S(1)}, bf16[1152,128]{1,0:T(8,128)(2,1)}, u32[]{:S(2)}, u32[]{:S(2)}) collective-permute-start(bf16[1152,128]{1,0:T(8,128)(2,1)S(1)} %attention.3.refs_2_), channel_id=1, source_target_pairs={{0,16},{16,0},{1,17},{17,1},{2,18},{18,2},{3,19},{19,3},{4,20},{20... | collective-permute-start | bytes 884744 | tf_op jit(solution)/shard_map/ppermute | solution.py:251
  33.9 0.0 collective-permute-done.3.refs_11_
  33.9 1.2 %collective-permute-start.5 = (bf16[1152,128]{1,0:T(8,128)(2,1)S(1)}, bf16[1152,128]{1,0:T(8,128)(2,1)}, u32[]{:S(2)}, u32[]{:S(2)}) collective-permute-start(bf16[1152,128]{1,0:T(8,128)(2,1)S(1)} %attention.3.refs_2_), channel_id=1, source_target_pairs={{0,8},{4,12},{8,0},{12,4},{1,9},{5,13},{9,1},{13,5},{2,10},{6,14},... | collective-permute-start | bytes 884744 | tf_op jit(solution)/shard_map/ppermute | solution.py:253
  35.1 0.8 %constant_dynamic-slice_fusion.1 = (bf16[2,1,384]{2,1,0:T(2,128)(2,1)S(1)}, bf16[2,1,384]{2,1,0:T(2,128)(2,1)S(1)}) fusion(bf16[2,2,1536]{2,1,0:T(2,128)(2,1)} %param.12, s32[]{:T(128)S(6)} %select_n.24, s32[]{:T(128)S(6)} %select_n.25, s32[]{:T(128)S(6)} %select_n.26), kind=kLoop, calls=%fused_computation.7 | loop fusion | bytes 6156 | tf_op jit(solution)/shard_map/dynamic_slice | solution.py:307
  36.0 0.0 collective-permute-done.7.side_b_ref
  36.0 1.0 %copy-done.6 = bf16[1152,128]{1,0:T(8,128)(2,1)S(1)} copy-done((bf16[1152,128]{1,0:T(8,128)(2,1)S(1)}, bf16[1152,128]{1,0:T(8,128)(2,1)}, u32[]{:S(2)}) %copy-start.6) | copy-done | bytes 294936
  37.0 5.0 %attention.4.refs_6_ = bf16[1152,128]{1,0:T(8,128)(2,1)S(1)} custom-call(s32[5]{0:T(128)S(1)} %pad_add_fusion.2.info_ref, bf16[1152,128]{1,0:T(8,128)(2,1)S(1)} %copy-done.6, bf16[2,1152,128]{2,1,0:T(8,128)(2,1)S(1)} %get-tuple-element.59.own_ref, bf16[2,1152,128]{2,1,0:T(8,128)(2,1)} %collective-permute-done.6.side_a_ref, ...), custom_call_target="tpu_custom_call" | custom-call | bytes 1024 | tf_op jit(solution)/shard_map/attention/pallas_call | solution.py:101
  42.0 0.0 copy-start.8
  42.0 0.3 collective-permute-start.8
  42.3 0.0 collective-permute-done.4.refs_3_
  42.3 0.3 collective-permute-start.13
  42.5 0.0 collective-permute-done.5.refs_4_
  42.5 1.2 %collective-permute-start.12 = (bf16[1152,128]{1,0:T(8,128)(2,1)}, bf16[1152,128]{1,0:T(8,128)(2,1)S(1)}, u32[]{:S(2)}, u32[]{:S(2)}) collective-permute-start(bf16[1152,128]{1,0:T(8,128)(2,1)} %collective-permute-done.4.refs_3_), channel_id=1, source_target_pairs={{0,8},{4,12},{8,0},{12,4},{1,9},{5,13},{9,1},{13,5},{2,10},{6,14},... | collective-permute-start | bytes 884744 | tf_op jit(solution)/shard_map/ppermute | solution.py:253
  43.8 0.0 collective-permute-done.10.side_a_ref
  43.8 0.1 collective-permute-done.11.side_b_ref
  43.9 5.0 %attention.5.refs_3_ = bf16[1152,128]{1,0:T(8,128)(2,1)S(1)} custom-call(s32[5]{0:T(128)S(1)} %pad_add_fusion.2.info_ref, bf16[1152,128]{1,0:T(8,128)(2,1)S(1)} %copy-done.4, bf16[2,1152,128]{2,1,0:T(8,128)(2,1)} %get-tuple-element.61.own_ref, bf16[2,1152,128]{2,1,0:T(8,128)(2,1)S(1)} %collective-permute-done.10.side_a_ref, ...), custom_call_target="tpu_custom_call" | custom-call | bytes 1024 | tf_op jit(solution)/shard_map/attention/pallas_call | solution.py:101
  48.9 1.3 %collective-permute-start.14 = (bf16[1152,128]{1,0:T(8,128)(2,1)S(1)}, bf16[1152,128]{1,0:T(8,128)(2,1)S(1)}, u32[]{:S(2)}, u32[]{:S(2)}) collective-permute-start(bf16[1152,128]{1,0:T(8,128)(2,1)S(1)} %attention.5.refs_3_), channel_id=1, source_target_pairs={{0,16},{16,0},{1,17},{17,1},{2,18},{18,2},{3,19},{19,3},{4,20},{20... | collective-permute-start | bytes 884744 | tf_op jit(solution)/shard_map/ppermute | solution.py:251
  50.1 0.1 pad_add_fusion.info_ref
  50.2 1.3 %collective-permute-start.15 = (bf16[1152,128]{1,0:T(8,128)(2,1)S(1)}, bf16[1152,128]{1,0:T(8,128)(2,1)S(1)}, u32[]{:S(2)}, u32[]{:S(2)}) collective-permute-start(bf16[1152,128]{1,0:T(8,128)(2,1)S(1)} %attention.5.refs_3_), channel_id=1, source_target_pairs={{0,8},{4,12},{8,0},{12,4},{1,9},{5,13},{9,1},{13,5},{2,10},{6,14},... | collective-permute-start | bytes 884744 | tf_op jit(solution)/shard_map/ppermute | solution.py:253
  51.5 0.0 collective-permute-done.8.refs_8_
  51.5 0.3 collective-permute-start.9
  51.8 1.4 %collective-permute-done.12.refs_5_ = bf16[1152,128]{1,0:T(8,128)(2,1)S(1)} collective-permute-done((bf16[1152,128]{1,0:T(8,128)(2,1)}, bf16[1152,128]{1,0:T(8,128)(2,1)S(1)}, u32[]{:S(2)}, u32[]{:S(2)}) %collective-permute-start.12) | collective-permute-done | bytes 294944 | tf_op jit(solution)/shard_map/ppermute | solution.py:253
  53.2 0.0 collective-permute-done.13.refs_7_
  53.2 3.6 %partial_projection.2 = (f32[1152,384]{1,0:T(8,128)S(1)}, f32[1152,384]{1,0:T(8,128)S(1)}) custom-call(s32[21]{0:T(128)S(1)} %pad_add_fusion.info_ref, bf16[384,768]{1,0:T(8,128)(2,1)S(1)} %get-tuple-element.43.refs_0_, bf16[384,768]{1,0:T(8,128)(2,1)S(1)} %collective-permute-done.2.refs_1_, bf16[1152,128]{1,0:T(8,128)(2,1)S(1)} %attention.3.refs_2_, ...), custom_call_target="tpu_custom_call" | custom-call | bytes 1024 | tf_op jit(solution)/shard_map/partial_projection/pallas_call | solution.py:156
  56.8 0.0 collective-permute-done.14.refs_4_
  56.8 0.3 collective-permute-start.16
  57.1 4.1 %collective-permute-done.9.refs_2_ = bf16[1152,128]{1,0:T(8,128)(2,1)S(1)} collective-permute-done((bf16[1152,128]{1,0:T(8,128)(2,1)S(1)}, bf16[1152,128]{1,0:T(8,128)(2,1)S(1)}, u32[]{:S(2)}, u32[]{:S(2)}) %collective-permute-start.9) | collective-permute-done | bytes 294944 | tf_op jit(solution)/shard_map/ppermute | solution.py:251
  61.2 0.0 collective-permute-done.15.refs_5_
  61.2 4.7 %collective-permute-done.16.refs_6_ = bf16[1152,128]{1,0:T(8,128)(2,1)S(1)} collective-permute-done((bf16[1152,128]{1,0:T(8,128)(2,1)S(1)}, bf16[1152,128]{1,0:T(8,128)(2,1)S(1)}, u32[]{:S(2)}, u32[]{:S(2)}) %collective-permute-start.16) | collective-permute-done | bytes 294944 | tf_op jit(solution)/shard_map/ppermute | solution.py:253
  65.9 2.3 %partial_projection.3 = (f32[1152,384]{1,0:T(8,128)S(1)}, bf16[1152,384]{1,0:T(8,128)(2,1)S(1)}) custom-call(s32[21]{0:T(128)S(1)} %pad_add_fusion.info_ref, bf16[384,768]{1,0:T(8,128)(2,1)S(1)} %get-tuple-element.43.refs_0_, bf16[384,768]{1,0:T(8,128)(2,1)S(1)} %collective-permute-done.2.refs_1_, bf16[1152,128]{1,0:T(8,128)(2,1)S(1)} %collective-permute-done.9.refs_2_, ...), custom_call_target="tpu_custom_call" | custom-call | bytes 1024 | tf_op jit(solution)/shard_map/partial_projection/pallas_call | solution.py:156
  68.3 6.5 %collective-permute-start.17 = (bf16[1152,384]{1,0:T(8,128)(2,1)S(1)}, bf16[1152,384]{1,0:T(8,128)(2,1)S(1)}, u32[]{:S(2)}, u32[]{:S(2)}) collective-permute-start(bf16[1152,384]{1,0:T(8,128)(2,1)S(1)} %get-tuple-element.72), channel_id=1, source_target_pairs={{0,4},{4,0},{8,12},{12,8},{1,5},{5,1},{9,13},{13,9},{2,6},{6,2},{1... | collective-permute-start | bytes 2654216 | tf_op jit(solution)/shard_map/ppermute | solution.py:253
  74.7 2.1 %collective-permute-done.17 = bf16[1152,384]{1,0:T(8,128)(2,1)S(1)} collective-permute-done((bf16[1152,384]{1,0:T(8,128)(2,1)S(1)}, bf16[1152,384]{1,0:T(8,128)(2,1)S(1)}, u32[]{:S(2)}, u32[]{:S(2)}) %collective-permute-start.17) | collective-permute-done | bytes 884768 | tf_op jit(solution)/shard_map/ppermute | solution.py:253
  76.8 1.1 %add_convert_fusion = bf16[1152,384]{1,0:T(8,128)(2,1)} fusion(f32[1152,384]{1,0:T(8,128)S(1)} %get-tuple-element.71, bf16[1152,384]{1,0:T(8,128)(2,1)S(1)} %collective-permute-done.17), kind=kLoop, calls=%fused_computation.1 | loop fusion | flops 1327104 | bytes 3538944 | tf_op jit(solution)/shard_map/convert_element_type | solution.py:372
  (9 shorter events, 0.0 us)
Async XLA Ops:
  0.0 13.3 %copy-start = (s32[3,4]{1,0:T(4,128)S(1)}, s32[3,4]{1,0:T(4,128)}, u32[]{:S(2)}) copy-start(s32[3,4]{1,0:T(4,128)} %param.14) | copy-start | bytes 148
  0.0 6.4 %copy-start.7 = (bf16[1,1152,2,384]{3,2,1,0:T(2,128)(2,1)S(1)}, bf16[1,1152,2,384]{3,2,1,0:T(2,128)(2,1)}, u32[]{:S(2)}) copy-start(bf16[1,1152,2,384]{3,2,1,0:T(2,128)(2,1)} %param.11) | copy-start | bytes 5308420
  1.8 14.4 %collective-permute-start = (bf16[2,1152,128]{2,1,0:T(8,128)(2,1)S(1)}, bf16[2,1152,128]{2,1,0:T(8,128)(2,1)S(1)}, u32[]{:S(2)}, u32[]{:S(2)}) collective-permute-start(bf16[2,1152,128]{2,1,0:T(8,128)(2,1)S(1)} %copy_columns.3.own_ref), channel_id=1, source_target_pairs={{0,1},{1,0},{2,3},{3,2},{4,5},{5,4},{6,7},{7,6},{8,9},{9,8},{10,11... | collective-permute-start | bytes 1769480 | tf_op jit(solution)/shard_map/ppermute | solution.py:294
  1.9 18.3 %collective-permute-start.1 = (bf16[2,1152,128]{2,1,0:T(8,128)(2,1)S(1)}, bf16[2,1152,128]{2,1,0:T(8,128)(2,1)}, u32[]{:S(2)}, u32[]{:S(2)}) collective-permute-start(bf16[2,1152,128]{2,1,0:T(8,128)(2,1)S(1)} %copy_columns.3.own_ref), channel_id=1, source_target_pairs={{1,2},{2,1},{5,6},{6,5},{9,10},{10,9},{13,14},{14,13},{17,18},{18,... | collective-permute-start | bytes 1769480 | tf_op jit(solution)/shard_map/ppermute | solution.py:294
  7.9 26.0 %collective-permute-start.3 = (bf16[1152,384]{1,0:T(8,128)(2,1)}, bf16[1152,384]{1,0:T(8,128)(2,1)}, u32[]{:S(2)}, u32[]{:S(2)}) collective-permute-start(bf16[1152,384]{1,0:T(8,128)(2,1)} %get-tuple-element.47), channel_id=1, source_target_pairs={{0,16},{16,0},{1,17},{17,1},{2,18},{18,2},{3,19},{19,3},{4,20},{20... | collective-permute-start | bytes 2654216 | tf_op jit(solution)/shard_map/ppermute | solution.py:251
  12.0 17.7 %collective-permute-start.2 = (bf16[384,768]{1,0:T(8,128)(2,1)}, bf16[384,768]{1,0:T(8,128)(2,1)S(1)}, u32[]{:S(2)}, u32[]{:S(2)}) collective-permute-start(bf16[384,768]{1,0:T(8,128)(2,1)} %get-tuple-element.51), channel_id=1, source_target_pairs={{0,8},{4,12},{8,0},{12,4},{1,9},{5,13},{9,1},{13,5},{2,10},{6,14},... | collective-permute-start | bytes 1769480 | tf_op jit(solution)/shard_map/ppermute | solution.py:253
  13.3 19.3 %collective-permute-start.6 = (bf16[2,1152,128]{2,1,0:T(8,128)(2,1)S(1)}, bf16[2,1152,128]{2,1,0:T(8,128)(2,1)}, u32[]{:S(2)}, u32[]{:S(2)}) collective-permute-start(bf16[2,1152,128]{2,1,0:T(8,128)(2,1)S(1)} %get-tuple-element.59.own_ref), channel_id=1, source_target_pairs={{0,1},{1,0},{2,3},{3,2},{4,5},{5,4},{6,7},{7,6},{8,9},{9,8},{10,11... | collective-permute-start | bytes 1769480 | tf_op jit(solution)/shard_map/ppermute | solution.py:294
  16.2 0.8 %copy-start.1 = (bf16[2,1152,128]{2,1,0:T(8,128)(2,1)}, bf16[2,1152,128]{2,1,0:T(8,128)(2,1)S(1)}, u32[]{:S(2)}) copy-start(bf16[2,1152,128]{2,1,0:T(8,128)(2,1)S(1)} %collective-permute-done.side_a_ref) | copy-start | bytes 1769476
  17.0 19.0 %collective-permute-start.7 = (bf16[2,1152,128]{2,1,0:T(8,128)(2,1)S(1)}, bf16[2,1152,128]{2,1,0:T(8,128)(2,1)}, u32[]{:S(2)}, u32[]{:S(2)}) collective-permute-start(bf16[2,1152,128]{2,1,0:T(8,128)(2,1)S(1)} %get-tuple-element.59.own_ref), channel_id=1, source_target_pairs={{1,2},{2,1},{5,6},{6,5},{9,10},{10,9},{13,14},{14,13},{17,18},{18,... | collective-permute-start | bytes 1769480 | tf_op jit(solution)/shard_map/ppermute | solution.py:294
  20.2 4.6 %copy-start.2 = (bf16[2,1152,128]{2,1,0:T(8,128)(2,1)S(1)}, bf16[2,1152,128]{2,1,0:T(8,128)(2,1)}, u32[]{:S(2)}) copy-start(bf16[2,1152,128]{2,1,0:T(8,128)(2,1)} %copy-done.1) | copy-start | bytes 1769476
  23.3 0.7 copy-start.3
  24.1 0.7 copy-start.5
  29.6 14.2 %collective-permute-start.10 = (bf16[2,1152,128]{2,1,0:T(8,128)(2,1)}, bf16[2,1152,128]{2,1,0:T(8,128)(2,1)S(1)}, u32[]{:S(2)}, u32[]{:S(2)}) collective-permute-start(bf16[2,1152,128]{2,1,0:T(8,128)(2,1)} %get-tuple-element.61.own_ref), channel_id=1, source_target_pairs={{0,1},{1,0},{2,3},{3,2},{4,5},{5,4},{6,7},{7,6},{8,9},{9,8},{10,11... | collective-permute-start | bytes 1769480 | tf_op jit(solution)/shard_map/ppermute | solution.py:294
  29.7 14.2 %collective-permute-start.11 = (bf16[2,1152,128]{2,1,0:T(8,128)(2,1)}, bf16[2,1152,128]{2,1,0:T(8,128)(2,1)}, u32[]{:S(2)}, u32[]{:S(2)}) collective-permute-start(bf16[2,1152,128]{2,1,0:T(8,128)(2,1)} %get-tuple-element.61.own_ref), channel_id=1, source_target_pairs={{1,2},{2,1},{5,6},{6,5},{9,10},{10,9},{13,14},{14,13},{17,18},{18,... | collective-permute-start | bytes 1769480 | tf_op jit(solution)/shard_map/ppermute | solution.py:294
  32.6 9.6 %collective-permute-start.4 = (bf16[1152,128]{1,0:T(8,128)(2,1)S(1)}, bf16[1152,128]{1,0:T(8,128)(2,1)}, u32[]{:S(2)}, u32[]{:S(2)}) collective-permute-start(bf16[1152,128]{1,0:T(8,128)(2,1)S(1)} %attention.3.refs_2_), channel_id=1, source_target_pairs={{0,16},{16,0},{1,17},{17,1},{2,18},{18,2},{3,19},{19,3},{4,20},{20... | collective-permute-start | bytes 884744 | tf_op jit(solution)/shard_map/ppermute | solution.py:251
  33.9 8.6 %collective-permute-start.5 = (bf16[1152,128]{1,0:T(8,128)(2,1)S(1)}, bf16[1152,128]{1,0:T(8,128)(2,1)}, u32[]{:S(2)}, u32[]{:S(2)}) collective-permute-start(bf16[1152,128]{1,0:T(8,128)(2,1)S(1)} %attention.3.refs_2_), channel_id=1, source_target_pairs={{0,8},{4,12},{8,0},{12,4},{1,9},{5,13},{9,1},{13,5},{2,10},{6,14},... | collective-permute-start | bytes 884744 | tf_op jit(solution)/shard_map/ppermute | solution.py:253
  35.1 8.7 %copy-start.4 = (bf16[1152,128]{1,0:T(8,128)(2,1)S(1)}, bf16[1152,128]{1,0:T(8,128)(2,1)}, u32[]{:S(2)}) copy-start(bf16[1152,128]{1,0:T(8,128)(2,1)} %copy-done.3) | copy-start | bytes 884740
  36.0 1.0 %copy-start.6 = (bf16[1152,128]{1,0:T(8,128)(2,1)S(1)}, bf16[1152,128]{1,0:T(8,128)(2,1)}, u32[]{:S(2)}) copy-start(bf16[1152,128]{1,0:T(8,128)(2,1)} %copy-done.5) | copy-start | bytes 884740
  42.0 8.2 %copy-start.8 = (s32[18]{0:T(128)S(1)}, s32[18]{0:T(128)}, u32[]{:S(2)}) copy-start(s32[18]{0:T(128)} %param.15) | copy-start | bytes 220
  42.0 9.6 %collective-permute-start.8 = (bf16[1152,128]{1,0:T(8,128)(2,1)S(1)}, bf16[1152,128]{1,0:T(8,128)(2,1)S(1)}, u32[]{:S(2)}, u32[]{:S(2)}) collective-permute-start(bf16[1152,128]{1,0:T(8,128)(2,1)S(1)} %attention.4.refs_6_), channel_id=1, source_target_pairs={{0,8},{4,12},{8,0},{12,4},{1,9},{5,13},{9,1},{13,5},{2,10},{6,14},... | collective-permute-start | bytes 884744 | tf_op jit(solution)/shard_map/ppermute | solution.py:253
  42.3 10.9 %collective-permute-start.13 = (bf16[1152,128]{1,0:T(8,128)(2,1)S(1)}, bf16[1152,128]{1,0:T(8,128)(2,1)S(1)}, u32[]{:S(2)}, u32[]{:S(2)}) collective-permute-start(bf16[1152,128]{1,0:T(8,128)(2,1)S(1)} %attention.4.refs_6_), channel_id=1, source_target_pairs={{0,16},{16,0},{1,17},{17,1},{2,18},{18,2},{3,19},{19,3},{4,20},{20... | collective-permute-start | bytes 884744 | tf_op jit(solution)/shard_map/ppermute | solution.py:251
  42.5 10.6 %collective-permute-start.12 = (bf16[1152,128]{1,0:T(8,128)(2,1)}, bf16[1152,128]{1,0:T(8,128)(2,1)S(1)}, u32[]{:S(2)}, u32[]{:S(2)}) collective-permute-start(bf16[1152,128]{1,0:T(8,128)(2,1)} %collective-permute-done.4.refs_3_), channel_id=1, source_target_pairs={{0,8},{4,12},{8,0},{12,4},{1,9},{5,13},{9,1},{13,5},{2,10},{6,14},... | collective-permute-start | bytes 884744 | tf_op jit(solution)/shard_map/ppermute | solution.py:253
  48.9 7.9 %collective-permute-start.14 = (bf16[1152,128]{1,0:T(8,128)(2,1)S(1)}, bf16[1152,128]{1,0:T(8,128)(2,1)S(1)}, u32[]{:S(2)}, u32[]{:S(2)}) collective-permute-start(bf16[1152,128]{1,0:T(8,128)(2,1)S(1)} %attention.5.refs_3_), channel_id=1, source_target_pairs={{0,16},{16,0},{1,17},{17,1},{2,18},{18,2},{3,19},{19,3},{4,20},{20... | collective-permute-start | bytes 884744 | tf_op jit(solution)/shard_map/ppermute | solution.py:251
  50.2 11.0 %collective-permute-start.15 = (bf16[1152,128]{1,0:T(8,128)(2,1)S(1)}, bf16[1152,128]{1,0:T(8,128)(2,1)S(1)}, u32[]{:S(2)}, u32[]{:S(2)}) collective-permute-start(bf16[1152,128]{1,0:T(8,128)(2,1)S(1)} %attention.5.refs_3_), channel_id=1, source_target_pairs={{0,8},{4,12},{8,0},{12,4},{1,9},{5,13},{9,1},{13,5},{2,10},{6,14},... | collective-permute-start | bytes 884744 | tf_op jit(solution)/shard_map/ppermute | solution.py:253
  51.5 9.7 %collective-permute-start.9 = (bf16[1152,128]{1,0:T(8,128)(2,1)S(1)}, bf16[1152,128]{1,0:T(8,128)(2,1)S(1)}, u32[]{:S(2)}, u32[]{:S(2)}) collective-permute-start(bf16[1152,128]{1,0:T(8,128)(2,1)S(1)} %collective-permute-done.8.refs_8_), channel_id=1, source_target_pairs={{0,16},{16,0},{1,17},{17,1},{2,18},{18,2},{3,19},{19,3},{4,20},{20... | collective-permute-start | bytes 884744 | tf_op jit(solution)/shard_map/ppermute | solution.py:251
  56.8 9.2 %collective-permute-start.16 = (bf16[1152,128]{1,0:T(8,128)(2,1)S(1)}, bf16[1152,128]{1,0:T(8,128)(2,1)S(1)}, u32[]{:S(2)}, u32[]{:S(2)}) collective-permute-start(bf16[1152,128]{1,0:T(8,128)(2,1)S(1)} %collective-permute-done.14.refs_4_), channel_id=1, source_target_pairs={{0,8},{4,12},{8,0},{12,4},{1,9},{5,13},{9,1},{13,5},{2,10},{6,14},... | collective-permute-start | bytes 884744 | tf_op jit(solution)/shard_map/ppermute | solution.py:253
  68.3 8.5 %collective-permute-start.17 = (bf16[1152,384]{1,0:T(8,128)(2,1)S(1)}, bf16[1152,384]{1,0:T(8,128)(2,1)S(1)}, u32[]{:S(2)}, u32[]{:S(2)}) collective-permute-start(bf16[1152,384]{1,0:T(8,128)(2,1)S(1)} %get-tuple-element.72), channel_id=1, source_target_pairs={{0,4},{4,0},{8,12},{12,8},{1,5},{5,1},{9,13},{13,9},{2,6},{6,2},{1... | collective-permute-start | bytes 2654216 | tf_op jit(solution)/shard_map/ppermute | solution.py:253

commit v9 on v8

--- a/solution.py
+++ b/solution.py
@@ -13,17 +13,16 @@
 FAR = 1e30
 EXP2_SCALE = math.log2(math.e) / math.sqrt(HD)
 VMEM_LIMIT = 14 * 1024 * 1024
-COPY_LIMIT = 8 * 1024 * 1024
+COPY_LIMIT = 2 * 1024 * 1024
 COPY_PARTS = 3
-LATE_PACK = True
 RESIDUAL_FIRST = True
 SPLIT = 0
 TIE_PARTIAL = True
 BEFORE_X = {1: (), 2: ()}
-BEFORE_Y = {1: (), 2: ()}
+BEFORE_Y = {1: (), 2: ((1, 1, 0),)}
 RESIDUAL_AFTER = 0
-AWAITED = {0: (), 1: ('far', 'other'), 2: ('far', 'other', (1, 0, 0), (0, 1, 0)), 3: ((1, 0, 1),)}
-RELAY = ('y', 'x', 'y')
+AWAITED = {0: (), 1: ('far', 'other', (0, 1, 0)), 2: ('far', 'other', (1, 0, 0), (0, 1, 0)), 3: ((1, 0, 1),)}
+RELAY = ('x', 'y', 'x')
 LATE = ((1, 1, 1),)
 SCALARS = pl.BlockSpec(memory_space=pltpu.SMEM)
 IN_VMEM = pl.BlockSpec(memory_space=pltpu.VMEM)
@@ -93,6 +92,10 @@
         ready = later
 
 
+def in_hbm(operands):
+    return [pltpu.with_memory_space_constraint(operand, pltpu.HBM) for operand in operands]
+
+
 def pinned(operands):
     return [pltpu.with_memory_space_constraint(operand, pltpu.VMEM) for operand in operands]
 
@@ -109,6 +112,34 @@
     )(info, *pinned(operands))
 
 
+def attention_copies_kernel(last, plan, source_count, info_ref, copy_info_ref, *refs):
+    operands, sources = refs[:4], refs[4 : 4 + source_count]
+    out_ref, targets, sems = refs[4 + source_count], refs[5 + source_count : -1], refs[-1]
+    copies = planned_copies(plan, copy_info_ref, sources + targets, sems)
+    for copy in copies:
+        copy.start()
+    attention_kernel(0, last, info_ref, *operands, out_ref)
+    for copy in copies:
+        copy.wait()
+
+
+def attention_copies(info, last, operands, copy_info, sources, plan, targets):
+    return pl.pallas_call(
+        functools.partial(attention_copies_kernel, last, plan, len(sources)),
+        out_shape=[
+            jax.ShapeDtypeStruct(shape, jnp.bfloat16) for shape in [operands[0].shape] + targets
+        ],
+        in_specs=[SCALARS] * 2
+        + [IN_VMEM] * len(operands)
+        + [pl.BlockSpec(memory_space=pltpu.HBM)] * len(sources),
+        out_specs=[IN_VMEM] * (1 + len(targets)),
+        scratch_shapes=[pltpu.SemaphoreType.DMA((COPY_PARTS * len(plan),))],
+        compiler_params=pltpu.CompilerParams(vmem_limit_bytes=VMEM_LIMIT),
+        cost_estimate=SMALL_COST,
+        name="attention_copies",
+    )(info, copy_info, *pinned(operands), *in_hbm(sources))
+
+
 def partial_kernel(first, kinds, tile, info_ref, *refs):
     w_refs, refs = refs[:2], refs[2:]
     *pieces, gate_ref, base_own_ref, base_other_ref, own_ref, other_ref = refs
@@ -116,6 +147,15 @@
     frames = tile // FRAME
     cond_first = info_ref[0] == 0
     places = [pl.ds(pl.multiple_of(info_ref[i] * own_cols, own_cols), own_cols) for i in (1, 2)]
+    gates = []
+    for which in range(2):
+        branch = info_ref[0] if which == 0 else 1 - info_ref[0]
+        cols = []
+        for place in (info_ref[3], info_ref[3] ^ 1):
+            here = pl.ds(pl.multiple_of(place * own_cols, own_cols), own_cols)
+            both = gate_ref[branch, :, here].astype(jnp.float32)
+            cols.append(jnp.where(cond_first, both[0:1], both[1:2]))
+        gates.append(jnp.concatenate(cols, axis=1))
     chosen = [[i for i, kind in enumerate(kinds) if kind[0] == which] for which in range(2)]
     weights = []
     for names in chosen:
@@ -130,11 +170,11 @@
         for which in range(2):
             attended = jnp.concatenate([pieces[i][token_rows, :] for i in chosen[which]], axis=1)
             projected = jnp.dot(attended, weights[which], preferred_element_type=jnp.float32)
-            parts.append(gate_ref[which] * projected)
+            parts.append(gates[which] * projected)
         for frame in range(frames):
             rows = slice(frame * FRAME, (frame + 1) * FRAME)
             out_rows = slice(time_tile * tile + rows.start, time_tile * tile + rows.stop)
-            guide = 1.0 + 0.5 * info_ref[3 + time_tile * frames + frame].astype(jnp.float32)
+            guide = 1.0 + 0.5 * info_ref[4 + time_tile * frames + frame].astype(jnp.float32)
             scales = (
                 jnp.where(cond_first, guide, 1.0 - guide),
                 jnp.where(cond_first, 1.0 - guide, guide),
@@ -167,8 +207,7 @@
     )(info, *pinned([*weights, *pieces.values()]), gate, *pinned(base))
 
 
-def copy_kernel(plan, info_ref, *refs):
-    *arrays, sems = refs
+def planned_copies(plan, info_ref, arrays, sems):
     copies = []
     for source, block, width, target, place in plan:
         src, dst = arrays[source], arrays[target]
@@ -180,9 +219,11 @@
             rows = pl.ds(part * size, size)
             to = dst.at[rows, :] if place is None else dst.at[place, rows, :]
             copies.append((src.at[rows, pl.ds(first, width)], to))
-    copies = [
-        pltpu.make_async_copy(src, to, sems.at[index]) for index, (src, to) in enumerate(copies)
-    ]
+    return [pltpu.make_async_copy(src, to, sems.at[i]) for i, (src, to) in enumerate(copies)]
+
+
+def copy_kernel(plan, info_ref, *refs):
+    copies = planned_copies(plan, info_ref, refs[:-1], refs[-1])
     for copy in copies:
         copy.start()
     for copy in copies:
@@ -199,7 +240,7 @@
         compiler_params=pltpu.CompilerParams(vmem_limit_bytes=COPY_LIMIT),
         cost_estimate=SMALL_COST,
         name="copy_columns",
-    )(info, *[pltpu.with_memory_space_constraint(source, pltpu.HBM) for source in sources])
+    )(info, *in_hbm(sources))
 
 
 def halves_kernel(info_ref, both_ref, mine_ref, other_ref, sems):
@@ -264,19 +305,21 @@
     query = [((0,), head, HD, (None,), (count, HD)) for head in range(heads)]
     pair_weight = [((3,), block, 2 * width, (None,), (features, 2 * width)) for block in (-2, -1)]
 
-    def pack(parts, after=None):
-        here = sources
-        if after is not None:
-            _, here = lax.optimization_barrier((after, sources))
+    def plan_of(parts):
         used = sorted({index for part in parts for index in part[0]})
         plan = [
             (used.index(source), block, cols, len(used) + target, place)
             for target, (froms, block, cols, places, _) in enumerate(parts)
             for source, place in zip(froms, places)
         ]
-        return copy_columns(
-            copy_info, [here[index] for index in used], plan, [part[-1] for part in parts]
-        )
+        return used, plan, [part[-1] for part in parts]
+
+    def pack(parts, after=None):
+        here = sources
+        if after is not None:
+            _, here = lax.optimization_barrier((after, sources))
+        used, plan, targets = plan_of(parts)
+        return copy_columns(copy_info, [here[index] for index in used], plan, targets)
 
     def split_residual(residual):
         return split_halves(branch_pos[None], jnp.transpose(residual[0], (1, 0, 2)))
@@ -287,35 +330,25 @@
         _, residual = lax.optimization_barrier((packed, residual))
         mine, other = split_residual(residual)
         after = (packed, other) if RESIDUAL_FIRST else packed
-    late_key_value, far = pack([key_value[1], pair_weight[1]], after)
+    late_key_value, far, first_query = pack([key_value[1], pair_weight[1], query[0]], after)
     packed = list(packed) + [late_key_value]
+    head_queries = [first_query]
 
     def halo(part):
         return [lax.ppermute(part, "tokens", pairs) for pairs in rounds]
 
     sides = [halo(part) for part in packed]
-    near, *late = pack(pair_weight[:1] + query + key_value[2:], sides[0] if LATE_PACK else packed)
-    head_queries, packed = late[:heads], packed + late[heads:]
     store = {"far": swap(far, 0, 2)}
 
     if RESIDUAL_AFTER:
         _, residual = lax.optimization_barrier(((packed[1], sides[0])[RESIDUAL_AFTER - 1], residual))
         mine, other = split_residual(residual)
     store["other"] = swap(other, 1, 0)
-    gate_block = jnp.concatenate(
-        [
-            lax.dynamic_slice(gate, (0, branch_pos, place * width), (2, 1, width))
-            for place in (head_pos, head_pos ^ 1)
-        ],
-        axis=2,
-    ).astype(jnp.float32)
-    gate_block = jnp.where(branch_pos == 0, gate_block, gate_block[::-1])
-
     offsets = lax.dynamic_index_in_dim(time_offsets, width_pos, 1, keepdims=False)
     edges = jnp.stack([(pos >= 0) & (pos < tiles_wide) for pos in near_pos]).astype(jnp.int32)
     attention_info = jnp.concatenate([offsets, edges])
     place = head_pos & 1
-    projection_info = jnp.concatenate([jnp.stack([branch_pos, place, place ^ 1]), guidance_index])
+    projection_info = jnp.concatenate([jnp.stack([branch_pos, place, place ^ 1, head_pos]), guidance_index])
 
     def relay(head):
         if RELAY[head] == "x":
@@ -333,15 +366,26 @@
     for head in range(heads):
         head_queries[head] = await_names(AWAITED.get(head, ()), head_queries[head])
         operands = [head_queries[head], packed[head], *sides[head]]
-        if head == heads - 1 and SPLIT:
+        if head == 0:
+            used, plan, targets = plan_of(pair_weight[:1] + query[1:] + key_value[2:])
+            own, near, *late = attention_copies(
+                attention_info,
+                tiles_time,
+                operands,
+                copy_info,
+                [sources[index] for index in used],
+                plan,
+                targets,
+            )
+            head_queries, packed = head_queries + late[: heads - 1], packed + late[heads - 1 :]
+        elif head == heads - 1 and SPLIT:
             own = attention(attention_info, (0, SPLIT), *operands)
             own = await_names(AWAITED.get(heads, ()), own)
             own = attention(attention_info, (SPLIT, tiles_time), *operands, own)
         else:
             own = attention(attention_info, (0, tiles_time), *operands)
         if head + 2 < heads:
-            own, part = lax.optimization_barrier((own, packed[head + 2]))
-            sides.append(halo(part))
+            sides.append(halo(packed[head + 2]))
         store[0, 0, head] = own
         store[1, 0, head] = swap(await_names(BEFORE_X.get(head, ()), own), 1, 0)
         store[0, 1, head] = swap(await_names(BEFORE_Y.get(head, ()), own), 0, 2)
@@ -357,7 +401,7 @@
             projection_info,
             (near, store["far"]),
             {name: store[name] for name in names},
-            gate_block,
+            gate,
             base,
             tile,
             base[0] is mine,

time: 79.2 us -> 81.7 us (1.032)
  local copies, waits for them, and re-layouts: 4.5 us -> 11.1 us
  waiting for transfers between devices: 15 us -> 11.2 us
  starting transfers between devices: 27.2 us -> 29.5 us
  Pallas kernels: 29.6 us -> 27.7 us
    pallas_call x0 -> x1, Pallas kernels: none -> 6.21 us  [attention_copies(): pl.pallas_call(functools.partial(attention_copies_kernel, last, plan, len...]
    unnamed x18 -> x32, local copies, waits for them, and re-layouts: 3.26 us -> 9.45 us
    pallas_call x3 -> x2, Pallas kernels: 14.8 us -> 9.36 us  [attention(): pl.pallas_call(functools.partial(attention_kernel, *tiles), out_shape=jax...]
    ppermute x7 -> x6, waiting for transfers between devices: 8.15 us -> 4.26 us  [swap(): lax.ppermute(value, 'head', [(i, i ^ head_bits) for i in range(head_count)])]
    pallas_call x3 -> x2, Pallas kernels: 7.6 us -> 4.82 us  [copy_columns(): pl.pallas_call(functools.partial(copy_kernel, plan), out_shape=[jax.Shape...]
    ppermute x5 -> x6, starting transfers between devices: 4.34 us -> 5.93 us  [swap(): return lax.ppermute(value, 'branch', [(0, 1), (1, 0)])]
    ppermute x7 -> x6, starting transfers between devices: 12.1 us -> 13.4 us  [swap(): lax.ppermute(value, 'head', [(i, i ^ head_bits) for i in range(head_count)])]
    concatenate x0 -> x1, local copies, waits for them, and re-layouts: none -> 1.24 us  [local(): jnp.concatenate([jnp.stack([branch_pos, place, place ^ 1, head_pos]), gui...]
  transfers between devices with their start and end apart: 18 -> 18, of which waited for: 6 -> 4; matrix products, arithmetic and copies ran while one was open for 2% -> 2% of each run, Pallas kernels for 33% -> 29%
where the time goes in v9:
time: 81.7 us; the launch traced here: 81.1 us
  starting transfers between devices  29.5 us (36%)
  Pallas kernels  27.7 us (34%)
  waiting for transfers between devices  11.2 us (14%)
  local copies, waits for them, and re-layouts  11.1 us (14%)
  other arithmetic  1.38 us (2%)
    ppermute x6, starting transfers between devices, swap(): lax.ppermute(value, 'head', [(i, i ^ head_bits) for i in range(head_count)])  13.4 us
    ppermute x6, starting transfers between devices, halo(): return [lax.ppermute(part, 'tokens', pairs) for pairs in rounds]  10.2 us
    unnamed x32, local copies, waits for them, and re-layouts  9.45 us
    pallas_call x2, Pallas kernels, attention(): pl.pallas_call(functools.partial(attention_kernel, *tiles), out_shape=jax...  9.36 us
    pallas_call x1, Pallas kernels, attention_copies(): pl.pallas_call(functools.partial(attention_copies_kernel, last, plan, len...  6.21 us
    pallas_call x2, Pallas kernels, partial_projection(): pl.pallas_call(functools.partial(partial_kernel, first, tuple(pieces), ti...  5.98 us
    ppermute x6, starting transfers between devices, swap(): return lax.ppermute(value, 'branch', [(0, 1), (1, 0)])  5.93 us
    ppermute x6, waiting for transfers between devices, swap(): return lax.ppermute(value, 'branch', [(0, 1), (1, 0)])  5.28 us
  transfers between devices with their start and end apart: 18, of which 4 were waited for; matrix products, arithmetic and copies ran while one was open for 2% of the time, Pallas kernels for 29%

profile of v9, /device:TPU:9, one launch (start us, length us, event | category | flops | bytes accessed | tf_op | source)
XLA Modules:
  0.0 81.1 jit_solution(11007915955613472132)
XLA Ops:
  0.0 0.0 copy-start
  0.0 0.1 pad_add_fusion.1.info_ref.copy_info_ref
  0.1 1.7 %copy_columns.2.refs_1_ = bf16[2,1152,128]{2,1,0:T(8,128)(2,1)S(1)} custom-call(s32[2]{0:T(128)S(1)} %pad_add_fusion.1.info_ref.copy_info_ref, bf16[1152,384]{1,0:T(8,128)(2,1)} %bitcast.17, bf16[1152,384]{1,0:T(8,128)(2,1)} %bitcast.20), custom_call_target="tpu_custom_call" | custom-call | bytes 1024 | tf_op jit(solution)/shard_map/copy_columns/pallas_call | solution.py:234
  1.8 0.1 collective-permute-start
  1.9 4.5 %collective-permute-start.1 = (bf16[2,1152,128]{2,1,0:T(8,128)(2,1)S(1)}, bf16[2,1152,128]{2,1,0:T(8,128)(2,1)}, u32[]{:S(2)}, u32[]{:S(2)}) collective-permute-start(bf16[2,1152,128]{2,1,0:T(8,128)(2,1)S(1)} %copy_columns.2.refs_1_), channel_id=1, source_target_pairs={{1,2},{2,1},{5,6},{6,5},{9,10},{10,9},{13,14},{14,13},{17,18},{18,... | collective-permute-start | bytes 1769480 | tf_op jit(solution)/shard_map/ppermute | solution.py:338
  6.4 0.2 copy.11
  6.6 1.3 %split_halves.1 = (bf16[1152,384]{1,0:T(8,128)(2,1)S(1)}, bf16[1152,384]{1,0:T(8,128)(2,1)}) custom-call(s32[1]{0:T(128)} %bitcast.info_ref, bf16[2,1152,384]{2,1,0:T(8,128)(2,1)S(1)} %bitcast.16), custom_call_target="tpu_custom_call" | custom-call | bytes 1024 | tf_op jit(solution)/shard_map/split_halves/pallas_call | solution.py:258
  7.9 3.1 %copy_columns.3 = (bf16[2,1152,128]{2,1,0:T(8,128)(2,1)}, bf16[384,768]{1,0:T(8,128)(2,1)}, bf16[1152,128]{1,0:T(8,128)(2,1)S(1)}) custom-call(s32[2]{0:T(128)S(1)} %pad_add_fusion.1.info_ref.copy_info_ref, bf16[1152,384]{1,0:T(8,128)(2,1)} %bitcast.23, bf16[1152,384]{1,0:T(8,128)(2,1)} %bitcast.18, bf16[1152,384]{1,0:T(8,128)(2,1)} %bitcast.21, ...), custom_call_target="tpu_custom_call" | custom-call | bytes 1024 | tf_op jit(solution)/shard_map/copy_columns/pallas_call | solution.py:234
  11.0 0.7 copy-done.11
  11.7 1.2 %collective-permute-start.2 = (bf16[384,768]{1,0:T(8,128)(2,1)}, bf16[384,768]{1,0:T(8,128)(2,1)S(1)}, u32[]{:S(2)}, u32[]{:S(2)}) collective-permute-start(bf16[384,768]{1,0:T(8,128)(2,1)} %get-tuple-element.48), channel_id=1, source_target_pairs={{0,8},{4,12},{8,0},{12,4},{1,9},{5,13},{9,1},{13,5},{2,10},{6,14},... | collective-permute-start | bytes 1769480 | tf_op jit(solution)/shard_map/ppermute | solution.py:294
  13.0 0.0 collective-permute-start.6
  13.0 1.2 %collective-permute-start.3 = (bf16[1152,384]{1,0:T(8,128)(2,1)}, bf16[1152,384]{1,0:T(8,128)(2,1)S(1)}, u32[]{:S(2)}, u32[]{:S(2)}) collective-permute-start(bf16[1152,384]{1,0:T(8,128)(2,1)} %get-tuple-element.39), channel_id=1, source_target_pairs={{0,16},{16,0},{1,17},{17,1},{2,18},{18,2},{3,19},{19,3},{4,20},{20... | collective-permute-start | bytes 2654216 | tf_op jit(solution)/shard_map/ppermute | solution.py:292
  14.2 0.2 dynamic-slice_reduce_fusion
  14.4 0.1 add_convert_fusion.1
  14.5 0.1 pad_add_fusion.info_ref
  14.5 1.6 %collective-permute-done.refs_2_ = bf16[2,1152,128]{2,1,0:T(8,128)(2,1)S(1)} collective-permute-done((bf16[2,1152,128]{2,1,0:T(8,128)(2,1)S(1)}, bf16[2,1152,128]{2,1,0:T(8,128)(2,1)S(1)}, u32[]{:S(2)}, u32[]{:S(2)}) %collective-permute-start) | collective-permute-done | bytes 589856 | tf_op jit(solution)/shard_map/ppermute | solution.py:338
  16.2 0.8 %copy-done.1 = bf16[2,1152,128]{2,1,0:T(8,128)(2,1)} copy-done((bf16[2,1152,128]{2,1,0:T(8,128)(2,1)}, bf16[2,1152,128]{2,1,0:T(8,128)(2,1)S(1)}, u32[]{:S(2)}) %copy-start.1) | copy-done | bytes 589848
  17.0 3.2 %collective-permute-start.7 = (bf16[2,1152,128]{2,1,0:T(8,128)(2,1)}, bf16[2,1152,128]{2,1,0:T(8,128)(2,1)S(1)}, u32[]{:S(2)}, u32[]{:S(2)}) collective-permute-start(bf16[2,1152,128]{2,1,0:T(8,128)(2,1)} %get-tuple-element.55.own_ref), channel_id=1, source_target_pairs={{1,2},{2,1},{5,6},{6,5},{9,10},{10,9},{13,14},{14,13},{17,18},{18,... | collective-permute-start | bytes 1769480 | tf_op jit(solution)/shard_map/ppermute | solution.py:338
  20.2 0.0 collective-permute-done.1.refs_3_
  20.2 1.1 %copy-done.2 = bf16[2,1152,128]{2,1,0:T(8,128)(2,1)S(1)} copy-done((bf16[2,1152,128]{2,1,0:T(8,128)(2,1)S(1)}, bf16[2,1152,128]{2,1,0:T(8,128)(2,1)}, u32[]{:S(2)}) %copy-start.2) | copy-done | bytes 589848
  21.3 1.0 %copy-done.12 = bf16[1152,128]{1,0:T(8,128)(2,1)S(1)} copy-done((bf16[1152,128]{1,0:T(8,128)(2,1)S(1)}, bf16[1152,128]{1,0:T(8,128)(2,1)}, u32[]{:S(2)}) %copy-start.12) | copy-done | bytes 294936
  22.2 6.2 %attention_copies.1 = (bf16[1152,128]{1,0:T(8,128)(2,1)S(1)}, bf16[384,768]{1,0:T(8,128)(2,1)S(1)}, bf16[1152,128]{1,0:T(8,128)(2,1)S(1)}, bf16[1152,128]{1,0:T(8,128)(2,1)S(1)}, bf16[2,1152,128]{2,1,0:T(8,128)(2,1)S(1)}) custom-call(s32[5]{0:T(128)S(1)} %pad_add_fusion.info_ref, s32[2]{0:T(128)S(1)} %pad_add_fusion.1.info_ref.copy_info_ref, ...), custom_call_target="tpu_custom_call" | custom-call | bytes 1024 | tf_op jit(solution)/shard_map/attention_copies/pallas_call | solution.py:127
  28.5 1.3 %collective-permute-start.4 = (bf16[1152,128]{1,0:T(8,128)(2,1)S(1)}, bf16[1152,128]{1,0:T(8,128)(2,1)S(1)}, u32[]{:S(2)}, u32[]{:S(2)}) collective-permute-start(bf16[1152,128]{1,0:T(8,128)(2,1)S(1)} %get-tuple-element.49.refs_2_), channel_id=1, source_target_pairs={{0,8},{4,12},{8,0},{12,4},{1,9},{5,13},{9,1},{13,5},{2,10},{6,14},... | collective-permute-start | bytes 884744 | tf_op jit(solution)/shard_map/ppermute | solution.py:294
  29.8 0.0 collective-permute-done.2.refs_1_
  29.8 0.0 collective-permute-start.10
  29.8 0.0 collective-permute-done.6.side_a_ref
  29.8 2.4 %collective-permute-start.11 = (bf16[2,1152,128]{2,1,0:T(8,128)(2,1)S(1)}, bf16[2,1152,128]{2,1,0:T(8,128)(2,1)S(1)}, u32[]{:S(2)}, u32[]{:S(2)}) collective-permute-start(bf16[2,1152,128]{2,1,0:T(8,128)(2,1)S(1)} %get-tuple-element.57.own_ref), channel_id=1, source_target_pairs={{1,2},{2,1},{5,6},{6,5},{9,10},{10,9},{13,14},{14,13},{17,18},{18,... | collective-permute-start | bytes 1769480 | tf_op jit(solution)/shard_map/ppermute | solution.py:338
  32.2 2.2 %collective-permute-done.4.refs_4_ = bf16[1152,128]{1,0:T(8,128)(2,1)S(1)} collective-permute-done((bf16[1152,128]{1,0:T(8,128)(2,1)S(1)}, bf16[1152,128]{1,0:T(8,128)(2,1)S(1)}, u32[]{:S(2)}, u32[]{:S(2)}) %collective-permute-start.4) | collective-permute-done | bytes 294944 | tf_op jit(solution)/shard_map/ppermute | solution.py:294
  34.4 1.2 %collective-permute-start.5 = (bf16[1152,128]{1,0:T(8,128)(2,1)S(1)}, bf16[1152,128]{1,0:T(8,128)(2,1)S(1)}, u32[]{:S(2)}, u32[]{:S(2)}) collective-permute-start(bf16[1152,128]{1,0:T(8,128)(2,1)S(1)} %get-tuple-element.49.refs_2_), channel_id=1, source_target_pairs={{0,16},{16,0},{1,17},{17,1},{2,18},{18,2},{3,19},{19,3},{4,20},{20... | collective-permute-start | bytes 884744 | tf_op jit(solution)/shard_map/ppermute | solution.py:292
  35.6 0.0 collective-permute-done.3.refs_11_
  35.6 0.3 collective-permute-start.13
  35.9 0.0 collective-permute-done.7.side_b_ref
  35.9 5.0 %attention.2.refs_6_ = bf16[1152,128]{1,0:T(8,128)(2,1)S(1)} custom-call(s32[5]{0:T(128)S(1)} %pad_add_fusion.info_ref, bf16[1152,128]{1,0:T(8,128)(2,1)S(1)} %get-tuple-element.54.q_ref, bf16[2,1152,128]{2,1,0:T(8,128)(2,1)} %get-tuple-element.55.own_ref, bf16[2,1152,128]{2,1,0:T(8,128)(2,1)} %collective-permute-done.6.side_a_ref, ...), custom_call_target="tpu_custom_call" | custom-call | bytes 1024 | tf_op jit(solution)/shard_map/attention/pallas_call | solution.py:104
  40.9 0.0 copy-start.13
  40.9 1.3 %collective-permute-start.14 = (bf16[1152,128]{1,0:T(8,128)(2,1)S(1)}, bf16[1152,128]{1,0:T(8,128)(2,1)}, u32[]{:S(2)}, u32[]{:S(2)}) collective-permute-start(bf16[1152,128]{1,0:T(8,128)(2,1)S(1)} %attention.2.refs_6_), channel_id=1, source_target_pairs={{0,8},{4,12},{8,0},{12,4},{1,9},{5,13},{9,1},{13,5},{2,10},{6,14},... | collective-permute-start | bytes 884744 | tf_op jit(solution)/shard_map/ppermute | solution.py:294
  42.2 0.0 collective-permute-done.5.refs_3_
  42.2 0.7 copy-done.7
  42.9 1.2 %collective-permute-start.8 = (bf16[1152,128]{1,0:T(8,128)(2,1)S(1)}, bf16[1152,128]{1,0:T(8,128)(2,1)}, u32[]{:S(2)}, u32[]{:S(2)}) collective-permute-start(bf16[1152,128]{1,0:T(8,128)(2,1)S(1)} %attention.2.refs_6_), channel_id=1, source_target_pairs={{0,16},{16,0},{1,17},{17,1},{2,18},{18,2},{3,19},{19,3},{4,20},{20... | collective-permute-start | bytes 884744 | tf_op jit(solution)/shard_map/ppermute | solution.py:292
  44.1 0.0 collective-permute-done.10.side_a_ref
  44.1 0.0 collective-permute-done.11.side_b_ref
  44.1 4.4 %attention.3.refs_3_ = bf16[1152,128]{1,0:T(8,128)(2,1)S(1)} custom-call(s32[5]{0:T(128)S(1)} %pad_add_fusion.info_ref, bf16[1152,128]{1,0:T(8,128)(2,1)S(1)} %get-tuple-element.56.q_ref, bf16[2,1152,128]{2,1,0:T(8,128)(2,1)S(1)} %get-tuple-element.57.own_ref, bf16[2,1152,128]{2,1,0:T(8,128)(2,1)S(1)} %collective-permute-done.10.side_a_ref, ...), custom_call_target="tpu_custom_call" | custom-call | bytes 1024 | tf_op jit(solution)/shard_map/attention/pallas_call | solution.py:104
  48.5 0.0 collective-permute-done.13.refs_5_
  48.5 0.7 copy-done.9
  49.3 1.8 %collective-permute-start.15 = (bf16[1152,128]{1,0:T(8,128)(2,1)S(1)}, bf16[1152,128]{1,0:T(8,128)(2,1)}, u32[]{:S(2)}, u32[]{:S(2)}) collective-permute-start(bf16[1152,128]{1,0:T(8,128)(2,1)S(1)} %attention.3.refs_3_), channel_id=1, source_target_pairs={{0,8},{4,12},{8,0},{12,4},{1,9},{5,13},{9,1},{13,5},{2,10},{6,14},... | collective-permute-start | bytes 884744 | tf_op jit(solution)/shard_map/ppermute | solution.py:294
  51.0 1.2 %concatenate.6.info_ref = s32[22]{0:T(128)} concatenate(s32[1]{0:T(128)} %bitcast.info_ref, s32[1]{0:T(128)} %bitcast.1, s32[1]{0:T(128)} %bitcast.2, s32[1]{0:T(128)} %bitcast.3, s32[18]{0:T(128)} %param.15), dimensions={0} | concatenate | bytes 176 | tf_op jit(solution)/shard_map/concatenate | solution.py:351
  52.3 1.2 %collective-permute-start.12 = (bf16[1152,128]{1,0:T(8,128)(2,1)S(1)}, bf16[1152,128]{1,0:T(8,128)(2,1)S(1)}, u32[]{:S(2)}, u32[]{:S(2)}) collective-permute-start(bf16[1152,128]{1,0:T(8,128)(2,1)S(1)} %attention.3.refs_3_), channel_id=1, source_target_pairs={{0,16},{16,0},{1,17},{17,1},{2,18},{18,2},{3,19},{19,3},{4,20},{20... | collective-permute-start | bytes 884744 | tf_op jit(solution)/shard_map/ppermute | solution.py:292
  53.5 0.0 collective-permute-done.8.refs_7_
  53.5 0.0 collective-permute-start.9
  53.5 0.0 collective-permute-done.14.refs_8_
  53.5 1.0 %copy-done.4 = bf16[1152,128]{1,0:T(8,128)(2,1)S(1)} copy-done((bf16[1152,128]{1,0:T(8,128)(2,1)S(1)}, bf16[1152,128]{1,0:T(8,128)(2,1)}, u32[]{:S(2)}) %copy-start.4) | copy-done | bytes 294936
  54.5 1.0 %copy-done.6 = bf16[1152,128]{1,0:T(8,128)(2,1)S(1)} copy-done((bf16[1152,128]{1,0:T(8,128)(2,1)S(1)}, bf16[1152,128]{1,0:T(8,128)(2,1)}, u32[]{:S(2)}) %copy-start.6) | copy-done | bytes 294936
  55.5 1.0 %copy-done.8 = bf16[1152,128]{1,0:T(8,128)(2,1)S(1)} copy-done((bf16[1152,128]{1,0:T(8,128)(2,1)S(1)}, bf16[1152,128]{1,0:T(8,128)(2,1)}, u32[]{:S(2)}) %copy-start.8) | copy-done | bytes 294936
  56.4 1.0 %copy-done.10 = bf16[1152,128]{1,0:T(8,128)(2,1)S(1)} copy-done((bf16[1152,128]{1,0:T(8,128)(2,1)S(1)}, bf16[1152,128]{1,0:T(8,128)(2,1)}, u32[]{:S(2)}) %copy-start.10) | copy-done | bytes 294936
  57.4 0.6 copy-done.14
  58.0 3.3 %partial_projection.2 = (f32[1152,384]{1,0:T(8,128)S(1)}, f32[1152,384]{1,0:T(8,128)S(1)}) custom-call(s32[22]{0:T(128)S(1)} %copy-done.14, bf16[384,768]{1,0:T(8,128)(2,1)S(1)} %get-tuple-element.45.refs_0_, bf16[384,768]{1,0:T(8,128)(2,1)S(1)} %collective-permute-done.2.refs_1_, bf16[1152,128]{1,0:T(8,128)(2,1)S(1)} %copy-done.4, ...), custom_call_target="tpu_custom_call" | custom-call | bytes 1024 | tf_op jit(solution)/shard_map/partial_projection/pallas_call | solution.py:196
  61.3 0.0 collective-permute-done.15.refs_5_
  61.3 0.8 %collective-permute-start.16 = (bf16[1152,128]{1,0:T(8,128)(2,1)}, bf16[1152,128]{1,0:T(8,128)(2,1)S(1)}, u32[]{:S(2)}, u32[]{:S(2)}) collective-permute-start(bf16[1152,128]{1,0:T(8,128)(2,1)} %collective-permute-done.15.refs_5_), channel_id=1, source_target_pairs={{0,16},{16,0},{1,17},{17,1},{2,18},{18,2},{3,19},{19,3},{4,20},{20... | collective-permute-start | bytes 884744 | tf_op jit(solution)/shard_map/ppermute | solution.py:292
  62.1 0.0 collective-permute-done.12.refs_4_
  62.1 0.0 collective-permute-done.9.refs_2_
  62.1 5.3 %collective-permute-done.16.refs_6_ = bf16[1152,128]{1,0:T(8,128)(2,1)S(1)} collective-permute-done((bf16[1152,128]{1,0:T(8,128)(2,1)}, bf16[1152,128]{1,0:T(8,128)(2,1)S(1)}, u32[]{:S(2)}, u32[]{:S(2)}) %collective-permute-start.16) | collective-permute-done | bytes 294944 | tf_op jit(solution)/shard_map/ppermute | solution.py:292
  67.4 2.7 %partial_projection.3 = (f32[1152,384]{1,0:T(8,128)S(1)}, bf16[1152,384]{1,0:T(8,128)(2,1)S(1)}) custom-call(s32[22]{0:T(128)S(1)} %copy-done.14, bf16[384,768]{1,0:T(8,128)(2,1)S(1)} %get-tuple-element.45.refs_0_, bf16[384,768]{1,0:T(8,128)(2,1)S(1)} %collective-permute-done.2.refs_1_, bf16[1152,128]{1,0:T(8,128)(2,1)S(1)} %collective-permute-done.9.refs_2_, ...), custom_call_target="tpu_custom_call" | custom-call | bytes 1024 | tf_op jit(solution)/shard_map/partial_projection/pallas_call | solution.py:196
  70.1 7.8 %collective-permute-start.17 = (bf16[1152,384]{1,0:T(8,128)(2,1)S(1)}, bf16[1152,384]{1,0:T(8,128)(2,1)S(1)}, u32[]{:S(2)}, u32[]{:S(2)}) collective-permute-start(bf16[1152,384]{1,0:T(8,128)(2,1)S(1)} %get-tuple-element.70), channel_id=1, source_target_pairs={{0,4},{4,0},{8,12},{12,8},{1,5},{5,1},{9,13},{13,9},{2,6},{6,2},{1... | collective-permute-start | bytes 2654216 | tf_op jit(solution)/shard_map/ppermute | solution.py:294
  77.9 2.1 %collective-permute-done.17 = bf16[1152,384]{1,0:T(8,128)(2,1)S(1)} collective-permute-done((bf16[1152,384]{1,0:T(8,128)(2,1)S(1)}, bf16[1152,384]{1,0:T(8,128)(2,1)S(1)}, u32[]{:S(2)}, u32[]{:S(2)}) %collective-permute-start.17) | collective-permute-done | bytes 884768 | tf_op jit(solution)/shard_map/ppermute | solution.py:294
  79.9 1.2 %add_convert_fusion = bf16[1152,384]{1,0:T(8,128)(2,1)} fusion(f32[1152,384]{1,0:T(8,128)S(1)} %get-tuple-element.69, bf16[1152,384]{1,0:T(8,128)(2,1)S(1)} %collective-permute-done.17), kind=kLoop, calls=%fused_computation.1 | loop fusion | flops 1327104 | bytes 3538944 | tf_op jit(solution)/shard_map/convert_element_type | solution.py:416
  (19 shorter events, 0.0 us)
Async XLA Ops:
  0.0 14.2 %copy-start = (s32[3,4]{1,0:T(4,128)S(1)}, s32[3,4]{1,0:T(4,128)}, u32[]{:S(2)}) copy-start(s32[3,4]{1,0:T(4,128)} %param.14) | copy-start | bytes 148
  0.0 6.4 %copy-start.15 = (bf16[1,1152,2,384]{3,2,1,0:T(2,128)(2,1)S(1)}, bf16[1,1152,2,384]{3,2,1,0:T(2,128)(2,1)}, u32[]{:S(2)}) copy-start(bf16[1,1152,2,384]{3,2,1,0:T(2,128)(2,1)} %param.11) | copy-start | bytes 5308420
  1.8 14.4 %collective-permute-start = (bf16[2,1152,128]{2,1,0:T(8,128)(2,1)S(1)}, bf16[2,1152,128]{2,1,0:T(8,128)(2,1)S(1)}, u32[]{:S(2)}, u32[]{:S(2)}) collective-permute-start(bf16[2,1152,128]{2,1,0:T(8,128)(2,1)S(1)} %copy_columns.2.refs_1_), channel_id=1, source_target_pairs={{0,1},{1,0},{2,3},{3,2},{4,5},{5,4},{6,7},{7,6},{8,9},{9,8},{10,11... | collective-permute-start | bytes 1769480 | tf_op jit(solution)/shard_map/ppermute | solution.py:338
  1.9 18.3 %collective-permute-start.1 = (bf16[2,1152,128]{2,1,0:T(8,128)(2,1)S(1)}, bf16[2,1152,128]{2,1,0:T(8,128)(2,1)}, u32[]{:S(2)}, u32[]{:S(2)}) collective-permute-start(bf16[2,1152,128]{2,1,0:T(8,128)(2,1)S(1)} %copy_columns.2.refs_1_), channel_id=1, source_target_pairs={{1,2},{2,1},{5,6},{6,5},{9,10},{10,9},{13,14},{14,13},{17,18},{18,... | collective-permute-start | bytes 1769480 | tf_op jit(solution)/shard_map/ppermute | solution.py:338
  11.0 0.7 copy-start.11
  11.7 18.0 %collective-permute-start.2 = (bf16[384,768]{1,0:T(8,128)(2,1)}, bf16[384,768]{1,0:T(8,128)(2,1)S(1)}, u32[]{:S(2)}, u32[]{:S(2)}) collective-permute-start(bf16[384,768]{1,0:T(8,128)(2,1)} %get-tuple-element.48), channel_id=1, source_target_pairs={{0,8},{4,12},{8,0},{12,4},{1,9},{5,13},{9,1},{13,5},{2,10},{6,14},... | collective-permute-start | bytes 1769480 | tf_op jit(solution)/shard_map/ppermute | solution.py:294
  13.0 16.8 %collective-permute-start.6 = (bf16[2,1152,128]{2,1,0:T(8,128)(2,1)}, bf16[2,1152,128]{2,1,0:T(8,128)(2,1)}, u32[]{:S(2)}, u32[]{:S(2)}) collective-permute-start(bf16[2,1152,128]{2,1,0:T(8,128)(2,1)} %get-tuple-element.55.own_ref), channel_id=1, source_target_pairs={{0,1},{1,0},{2,3},{3,2},{4,5},{5,4},{6,7},{7,6},{8,9},{9,8},{10,11... | collective-permute-start | bytes 1769480 | tf_op jit(solution)/shard_map/ppermute | solution.py:338
  13.0 22.6 %collective-permute-start.3 = (bf16[1152,384]{1,0:T(8,128)(2,1)}, bf16[1152,384]{1,0:T(8,128)(2,1)S(1)}, u32[]{:S(2)}, u32[]{:S(2)}) collective-permute-start(bf16[1152,384]{1,0:T(8,128)(2,1)} %get-tuple-element.39), channel_id=1, source_target_pairs={{0,16},{16,0},{1,17},{17,1},{2,18},{18,2},{3,19},{19,3},{4,20},{20... | collective-permute-start | bytes 2654216 | tf_op jit(solution)/shard_map/ppermute | solution.py:292
  16.2 0.8 %copy-start.1 = (bf16[2,1152,128]{2,1,0:T(8,128)(2,1)}, bf16[2,1152,128]{2,1,0:T(8,128)(2,1)S(1)}, u32[]{:S(2)}) copy-start(bf16[2,1152,128]{2,1,0:T(8,128)(2,1)S(1)} %collective-permute-done.refs_2_) | copy-start | bytes 1769476
  17.0 18.9 %collective-permute-start.7 = (bf16[2,1152,128]{2,1,0:T(8,128)(2,1)}, bf16[2,1152,128]{2,1,0:T(8,128)(2,1)S(1)}, u32[]{:S(2)}, u32[]{:S(2)}) collective-permute-start(bf16[2,1152,128]{2,1,0:T(8,128)(2,1)} %get-tuple-element.55.own_ref), channel_id=1, source_target_pairs={{1,2},{2,1},{5,6},{6,5},{9,10},{10,9},{13,14},{14,13},{17,18},{18,... | collective-permute-start | bytes 1769480 | tf_op jit(solution)/shard_map/ppermute | solution.py:338
  20.2 1.1 %copy-start.2 = (bf16[2,1152,128]{2,1,0:T(8,128)(2,1)S(1)}, bf16[2,1152,128]{2,1,0:T(8,128)(2,1)}, u32[]{:S(2)}) copy-start(bf16[2,1152,128]{2,1,0:T(8,128)(2,1)} %copy-done.1) | copy-start | bytes 1769476
  21.3 1.0 %copy-start.12 = (bf16[1152,128]{1,0:T(8,128)(2,1)S(1)}, bf16[1152,128]{1,0:T(8,128)(2,1)}, u32[]{:S(2)}) copy-start(bf16[1152,128]{1,0:T(8,128)(2,1)} %copy-done.11) | copy-start | bytes 884740
  28.5 20.1 %copy-start.3 = (bf16[1152,128]{1,0:T(8,128)(2,1)}, bf16[1152,128]{1,0:T(8,128)(2,1)S(1)}, u32[]{:S(2)}) copy-start(bf16[1152,128]{1,0:T(8,128)(2,1)S(1)} %get-tuple-element.49.refs_2_) | copy-start | bytes 884740
  28.5 5.9 %collective-permute-start.4 = (bf16[1152,128]{1,0:T(8,128)(2,1)S(1)}, bf16[1152,128]{1,0:T(8,128)(2,1)S(1)}, u32[]{:S(2)}, u32[]{:S(2)}) collective-permute-start(bf16[1152,128]{1,0:T(8,128)(2,1)S(1)} %get-tuple-element.49.refs_2_), channel_id=1, source_target_pairs={{0,8},{4,12},{8,0},{12,4},{1,9},{5,13},{9,1},{13,5},{2,10},{6,14},... | collective-permute-start | bytes 884744 | tf_op jit(solution)/shard_map/ppermute | solution.py:294
  29.8 14.4 %collective-permute-start.10 = (bf16[2,1152,128]{2,1,0:T(8,128)(2,1)S(1)}, bf16[2,1152,128]{2,1,0:T(8,128)(2,1)S(1)}, u32[]{:S(2)}, u32[]{:S(2)}) collective-permute-start(bf16[2,1152,128]{2,1,0:T(8,128)(2,1)S(1)} %get-tuple-element.57.own_ref), channel_id=1, source_target_pairs={{0,1},{1,0},{2,3},{3,2},{4,5},{5,4},{6,7},{7,6},{8,9},{9,8},{10,11... | collective-permute-start | bytes 1769480 | tf_op jit(solution)/shard_map/ppermute | solution.py:338
  29.8 14.4 %collective-permute-start.11 = (bf16[2,1152,128]{2,1,0:T(8,128)(2,1)S(1)}, bf16[2,1152,128]{2,1,0:T(8,128)(2,1)S(1)}, u32[]{:S(2)}, u32[]{:S(2)}) collective-permute-start(bf16[2,1152,128]{2,1,0:T(8,128)(2,1)S(1)} %get-tuple-element.57.own_ref), channel_id=1, source_target_pairs={{1,2},{2,1},{5,6},{6,5},{9,10},{10,9},{13,14},{14,13},{17,18},{18,... | collective-permute-start | bytes 1769480 | tf_op jit(solution)/shard_map/ppermute | solution.py:338
  34.4 14.1 %copy-start.5 = (bf16[1152,128]{1,0:T(8,128)(2,1)}, bf16[1152,128]{1,0:T(8,128)(2,1)S(1)}, u32[]{:S(2)}) copy-start(bf16[1152,128]{1,0:T(8,128)(2,1)S(1)} %collective-permute-done.4.refs_4_) | copy-start | bytes 884740
  34.4 7.8 %collective-permute-start.5 = (bf16[1152,128]{1,0:T(8,128)(2,1)S(1)}, bf16[1152,128]{1,0:T(8,128)(2,1)S(1)}, u32[]{:S(2)}, u32[]{:S(2)}) collective-permute-start(bf16[1152,128]{1,0:T(8,128)(2,1)S(1)} %get-tuple-element.49.refs_2_), channel_id=1, source_target_pairs={{0,16},{16,0},{1,17},{17,1},{2,18},{18,2},{3,19},{19,3},{4,20},{20... | collective-permute-start | bytes 884744 | tf_op jit(solution)/shard_map/ppermute | solution.py:292
  35.6 12.9 %collective-permute-start.13 = (bf16[1152,128]{1,0:T(8,128)(2,1)S(1)}, bf16[1152,128]{1,0:T(8,128)(2,1)S(1)}, u32[]{:S(2)}, u32[]{:S(2)}) collective-permute-start(bf16[1152,128]{1,0:T(8,128)(2,1)S(1)} %collective-permute-done.4.refs_4_), channel_id=1, source_target_pairs={{0,16},{16,0},{1,17},{17,1},{2,18},{18,2},{3,19},{19,3},{4,20},{20... | collective-permute-start | bytes 884744 | tf_op jit(solution)/shard_map/ppermute | solution.py:292
  40.9 12.6 %copy-start.13 = (bf16[2,2,1536]{2,1,0:T(2,128)(2,1)S(1)}, bf16[2,2,1536]{2,1,0:T(2,128)(2,1)}, u32[]{:S(2)}) copy-start(bf16[2,2,1536]{2,1,0:T(2,128)(2,1)} %refs_7_.3) | copy-start | bytes 36868
  40.9 12.6 %collective-permute-start.14 = (bf16[1152,128]{1,0:T(8,128)(2,1)S(1)}, bf16[1152,128]{1,0:T(8,128)(2,1)}, u32[]{:S(2)}, u32[]{:S(2)}) collective-permute-start(bf16[1152,128]{1,0:T(8,128)(2,1)S(1)} %attention.2.refs_6_), channel_id=1, source_target_pairs={{0,8},{4,12},{8,0},{12,4},{1,9},{5,13},{9,1},{13,5},{2,10},{6,14},... | collective-permute-start | bytes 884744 | tf_op jit(solution)/shard_map/ppermute | solution.py:294
  42.2 0.7 copy-start.7
  42.9 10.6 %collective-permute-start.8 = (bf16[1152,128]{1,0:T(8,128)(2,1)S(1)}, bf16[1152,128]{1,0:T(8,128)(2,1)}, u32[]{:S(2)}, u32[]{:S(2)}) collective-permute-start(bf16[1152,128]{1,0:T(8,128)(2,1)S(1)} %attention.2.refs_6_), channel_id=1, source_target_pairs={{0,16},{16,0},{1,17},{17,1},{2,18},{18,2},{3,19},{19,3},{4,20},{20... | collective-permute-start | bytes 884744 | tf_op jit(solution)/shard_map/ppermute | solution.py:292
  48.5 0.7 copy-start.9
  49.3 12.0 %collective-permute-start.15 = (bf16[1152,128]{1,0:T(8,128)(2,1)S(1)}, bf16[1152,128]{1,0:T(8,128)(2,1)}, u32[]{:S(2)}, u32[]{:S(2)}) collective-permute-start(bf16[1152,128]{1,0:T(8,128)(2,1)S(1)} %attention.3.refs_3_), channel_id=1, source_target_pairs={{0,8},{4,12},{8,0},{12,4},{1,9},{5,13},{9,1},{13,5},{2,10},{6,14},... | collective-permute-start | bytes 884744 | tf_op jit(solution)/shard_map/ppermute | solution.py:294
  52.3 9.8 %collective-permute-start.12 = (bf16[1152,128]{1,0:T(8,128)(2,1)S(1)}, bf16[1152,128]{1,0:T(8,128)(2,1)S(1)}, u32[]{:S(2)}, u32[]{:S(2)}) collective-permute-start(bf16[1152,128]{1,0:T(8,128)(2,1)S(1)} %attention.3.refs_3_), channel_id=1, source_target_pairs={{0,16},{16,0},{1,17},{17,1},{2,18},{18,2},{3,19},{19,3},{4,20},{20... | collective-permute-start | bytes 884744 | tf_op jit(solution)/shard_map/ppermute | solution.py:292
  53.5 8.6 %collective-permute-start.9 = (bf16[1152,128]{1,0:T(8,128)(2,1)}, bf16[1152,128]{1,0:T(8,128)(2,1)S(1)}, u32[]{:S(2)}, u32[]{:S(2)}) collective-permute-start(bf16[1152,128]{1,0:T(8,128)(2,1)} %collective-permute-done.8.refs_7_), channel_id=1, source_target_pairs={{0,8},{4,12},{8,0},{12,4},{1,9},{5,13},{9,1},{13,5},{2,10},{6,14},... | collective-permute-start | bytes 884744 | tf_op jit(solution)/shard_map/ppermute | solution.py:294
  53.5 1.0 %copy-start.4 = (bf16[1152,128]{1,0:T(8,128)(2,1)S(1)}, bf16[1152,128]{1,0:T(8,128)(2,1)}, u32[]{:S(2)}) copy-start(bf16[1152,128]{1,0:T(8,128)(2,1)} %copy-done.3) | copy-start | bytes 884740
  54.5 1.0 %copy-start.6 = (bf16[1152,128]{1,0:T(8,128)(2,1)S(1)}, bf16[1152,128]{1,0:T(8,128)(2,1)}, u32[]{:S(2)}) copy-start(bf16[1152,128]{1,0:T(8,128)(2,1)} %copy-done.5) | copy-start | bytes 884740
  55.4 1.0 %copy-start.8 = (bf16[1152,128]{1,0:T(8,128)(2,1)S(1)}, bf16[1152,128]{1,0:T(8,128)(2,1)}, u32[]{:S(2)}) copy-start(bf16[1152,128]{1,0:T(8,128)(2,1)} %copy-done.7) | copy-start | bytes 884740
  56.4 1.0 %copy-start.10 = (bf16[1152,128]{1,0:T(8,128)(2,1)S(1)}, bf16[1152,128]{1,0:T(8,128)(2,1)}, u32[]{:S(2)}) copy-start(bf16[1152,128]{1,0:T(8,128)(2,1)} %copy-done.9) | copy-start | bytes 884740
  57.4 0.6 copy-start.14
  61.3 6.1 %collective-permute-start.16 = (bf16[1152,128]{1,0:T(8,128)(2,1)}, bf16[1152,128]{1,0:T(8,128)(2,1)S(1)}, u32[]{:S(2)}, u32[]{:S(2)}) collective-permute-start(bf16[1152,128]{1,0:T(8,128)(2,1)} %collective-permute-done.15.refs_5_), channel_id=1, source_target_pairs={{0,16},{16,0},{1,17},{17,1},{2,18},{18,2},{3,19},{19,3},{4,20},{20... | collective-permute-start | bytes 884744 | tf_op jit(solution)/shard_map/ppermute | solution.py:292
  70.1 9.9 %collective-permute-start.17 = (bf16[1152,384]{1,0:T(8,128)(2,1)S(1)}, bf16[1152,384]{1,0:T(8,128)(2,1)S(1)}, u32[]{:S(2)}, u32[]{:S(2)}) collective-permute-start(bf16[1152,384]{1,0:T(8,128)(2,1)S(1)} %get-tuple-element.70), channel_id=1, source_target_pairs={{0,4},{4,0},{8,12},{12,8},{1,5},{5,1},{9,13},{13,9},{2,6},{6,2},{1... | collective-permute-start | bytes 2654216 | tf_op jit(solution)/shard_map/ppermute | solution.py:294

commit v10 on v9

--- a/solution.py
+++ b/solution.py
@@ -12,11 +12,12 @@
 FRAME = 64
 FAR = 1e30
 EXP2_SCALE = math.log2(math.e) / math.sqrt(HD)
-VMEM_LIMIT = 14 * 1024 * 1024
+VMEM_LIMIT = 10 * 1024 * 1024
 COPY_LIMIT = 2 * 1024 * 1024
 COPY_PARTS = 3
 RESIDUAL_FIRST = True
 SPLIT = 0
+INFO_HEAD = 6
 TIE_PARTIAL = True
 BEFORE_X = {1: (), 2: ()}
 BEFORE_Y = {1: (), 2: ((1, 1, 0),)}
@@ -140,71 +141,138 @@
     )(info, copy_info, *pinned(operands), *in_hbm(sources))
 
 
-def partial_kernel(first, kinds, tile, info_ref, *refs):
-    w_refs, refs = refs[:2], refs[2:]
-    *pieces, gate_ref, base_own_ref, base_other_ref, own_ref, other_ref = refs
-    own_cols = own_ref.shape[1]
-    frames = tile // FRAME
+def guided_share(info_ref, gate_ref, cols, frames, time_tile, attended, weights):
     cond_first = info_ref[0] == 0
-    places = [pl.ds(pl.multiple_of(info_ref[i] * own_cols, own_cols), own_cols) for i in (1, 2)]
-    gates = []
+    parts = []
     for which in range(2):
         branch = info_ref[0] if which == 0 else 1 - info_ref[0]
-        cols = []
+        gates = []
         for place in (info_ref[3], info_ref[3] ^ 1):
-            here = pl.ds(pl.multiple_of(place * own_cols, own_cols), own_cols)
-            both = gate_ref[branch, :, here].astype(jnp.float32)
-            cols.append(jnp.where(cond_first, both[0:1], both[1:2]))
-        gates.append(jnp.concatenate(cols, axis=1))
-    chosen = [[i for i, kind in enumerate(kinds) if kind[0] == which] for which in range(2)]
-    weights = []
-    for names in chosen:
-        blocks = []
-        for _, far, head in [kinds[i] for i in names]:
-            depth = slice(head * HD, (head + 1) * HD)
-            blocks.append(jnp.concatenate([w_refs[far][depth, place] for place in places], axis=1))
-        weights.append(jnp.concatenate(blocks, axis=0))
+            both = gate_ref[branch, :, pl.ds(pl.multiple_of(place * cols, cols), cols)]
+            both = both.astype(jnp.float32)
+            gates.append(jnp.where(cond_first, both[0:1], both[1:2]))
+        projected = jnp.dot(attended[which], weights[which], preferred_element_type=jnp.float32)
+        parts.append(jnp.concatenate(gates, axis=1) * projected)
+    for frame in range(frames):
+        rows = slice(frame * FRAME, (frame + 1) * FRAME)
+        guide = 1.0 + 0.5 * info_ref[INFO_HEAD + time_tile * frames + frame].astype(jnp.float32)
+        scales = (jnp.where(cond_first, guide, 1.0 - guide), jnp.where(cond_first, 1.0 - guide, guide))
+        yield rows, scales, scales[0] * parts[0][rows] + scales[1] * parts[1][rows]
+
+
+def weight_rows(blocks, kinds):
+    return [blocks[far][head * HD : (head + 1) * HD] for _, far, head in kinds]
+
+
+def first_kernel(kinds, late, info_ref, near_own_ref, near_other_ref, far_ref, *refs):
+    *pieces, gate_ref, mine_ref, other_ref, own_ref, partner_ref, late_ref = refs
+    tile, cols = own_ref.shape
+    places = [pl.ds(pl.multiple_of(info_ref[i] * cols, cols), cols) for i in (1, 2)]
+    blocks = [
+        jnp.concatenate([near_own_ref[...], near_other_ref[...]], axis=1),
+        jnp.concatenate([far_ref[:, place] for place in places], axis=1),
+    ]
+
+    @pl.when(pl.program_id(0) == 0)
+    def _():
+        late_ref[...] = jnp.concatenate(weight_rows(blocks, late), axis=0)
+
+    attended, weights = [], []
+    for which in range(2):
+        chosen = [i for i, kind in enumerate(kinds) if kind[0] == which]
+        attended.append(jnp.concatenate([pieces[i][...] for i in chosen], axis=1))
+        weights.append(jnp.concatenate(weight_rows(blocks, [kinds[i] for i in chosen]), axis=0))
+    for rows, scales, total in guided_share(
+        info_ref, gate_ref, cols, tile // FRAME, pl.program_id(0), attended, weights
+    ):
+        own = total[:, :cols]
+        own += scales[0] * mine_ref[rows, :].astype(jnp.float32)
+        own += scales[1] * other_ref[rows, :].astype(jnp.float32)
+        own_ref[rows, :] = own
+        partner_ref[rows, :] = total[:, cols:]
+
+
+def first_share(info, weight, far, pieces, gate, halves, other, late, tile):
+    count, cols = other.shape
+    features = weight.shape[0]
+    piece = pl.BlockSpec((tile, HD), lambda t, info: (t, 0))
+    rows = pl.BlockSpec((tile, cols), lambda t, info: (t, 0))
+    near = [
+        pl.BlockSpec((features, cols), lambda t, info, place=place: (0, info[place]))
+        for place in (4, 5)
+    ]
+    late_shape = (len(late) * HD, 2 * cols)
+    operands = in_hbm([weight, weight]) + pinned([far, *pieces.values()])
+    operands += [gate, *in_hbm([halves]), *pinned([other])]
+    return pl.pallas_call(
+        functools.partial(first_kernel, tuple(pieces), late),
+        out_shape=[
+            pltpu.VMEM((count, cols), jnp.float32),
+            pltpu.VMEM((count, cols), jnp.float32),
+            pltpu.VMEM(late_shape, jnp.bfloat16),
+        ],
+        grid_spec=pltpu.PrefetchScalarGridSpec(
+            num_scalar_prefetch=1,
+            grid=(count // tile,),
+            in_specs=near
+            + [pl.BlockSpec(far.shape, lambda t, info: (0, 0))]
+            + [piece] * len(pieces)
+            + [
+                pl.BlockSpec(gate.shape, lambda t, info: (0, 0, 0)),
+                pl.BlockSpec((None, tile, cols), lambda t, info: (info[0], t, 0)),
+                rows,
+            ],
+            out_specs=[rows, rows, pl.BlockSpec(late_shape, lambda t, info: (0, 0))],
+        ),
+        compiler_params=pltpu.CompilerParams(vmem_limit_bytes=VMEM_LIMIT),
+        cost_estimate=SMALL_COST,
+        name="first_share",
+    )(info, *operands)
+
+
+def last_kernel(chosen, tile, info_ref, w_ref, *refs):
+    *pieces, gate_ref, base_own_ref, base_partner_ref, own_ref, partner_ref = refs
+    cols = own_ref.shape[1]
+    weights = [
+        jnp.concatenate([w_ref[at * HD : (at + 1) * HD, :] for _, at in names], axis=0)
+        for names in chosen
+    ]
     for time_tile in range(own_ref.shape[0] // tile):
-        token_rows = slice(time_tile * tile, (time_tile + 1) * tile)
-        parts = []
-        for which in range(2):
-            attended = jnp.concatenate([pieces[i][token_rows, :] for i in chosen[which]], axis=1)
-            projected = jnp.dot(attended, weights[which], preferred_element_type=jnp.float32)
-            parts.append(gates[which] * projected)
-        for frame in range(frames):
-            rows = slice(frame * FRAME, (frame + 1) * FRAME)
-            out_rows = slice(time_tile * tile + rows.start, time_tile * tile + rows.stop)
-            guide = 1.0 + 0.5 * info_ref[4 + time_tile * frames + frame].astype(jnp.float32)
-            scales = (
-                jnp.where(cond_first, guide, 1.0 - guide),
-                jnp.where(cond_first, 1.0 - guide, guide),
-            )
-            total = scales[0] * parts[0][rows] + scales[1] * parts[1][rows]
-            own, other = total[:, :own_cols], total[:, own_cols:]
-            if first:
-                own += scales[0] * base_own_ref[out_rows, :].astype(jnp.float32)
-                own += scales[1] * base_other_ref[out_rows, :].astype(jnp.float32)
-            else:
-                own += base_own_ref[out_rows, :]
-                other += base_other_ref[out_rows, :]
-            own_ref[out_rows, :] = own
-            other_ref[out_rows, :] = other.astype(other_ref.dtype)
-
-
-def partial_projection(info, weights, pieces, gate, base, tile, first):
+        first = time_tile * tile
+        attended = [
+            jnp.concatenate([pieces[i][first : first + tile, :] for i, _ in names], axis=1)
+            for names in chosen
+        ]
+        for rows, _, total in guided_share(
+            info_ref, gate_ref, cols, tile // FRAME, time_tile, attended, weights
+        ):
+            to = slice(first + rows.start, first + rows.stop)
+            own_ref[to, :] = base_own_ref[to, :] + total[:, :cols]
+            partner_ref[to, :] = (base_partner_ref[to, :] + total[:, cols:]).astype(jnp.bfloat16)
+
+
+def last_share(info, weights, pieces, gate, base, late, tile):
     shape = base[0].shape
+    chosen = [
+        [
+            (i, [kind[1:] for kind in late].index(kind[1:]))
+            for i, kind in enumerate(pieces)
+            if kind[0] == which
+        ]
+        for which in range(2)
+    ]
     return pl.pallas_call(
-        functools.partial(partial_kernel, first, tuple(pieces), tile),
+        functools.partial(last_kernel, chosen, tile),
         out_shape=[
             jax.ShapeDtypeStruct(shape, jnp.float32),
-            jax.ShapeDtypeStruct(shape, jnp.float32 if first else jnp.bfloat16),
+            jax.ShapeDtypeStruct(shape, jnp.bfloat16),
         ],
-        in_specs=[SCALARS] + [IN_VMEM] * (len(weights) + len(pieces) + 3),
+        in_specs=[SCALARS] + [IN_VMEM] * (len(pieces) + 4),
         out_specs=[IN_VMEM] * 2,
         compiler_params=pltpu.CompilerParams(vmem_limit_bytes=VMEM_LIMIT),
         cost_estimate=SMALL_COST,
-        name="partial_projection",
-    )(info, *pinned([*weights, *pieces.values()]), gate, *pinned(base))
+        name="last_share",
+    )(info, *pinned([weights, *pieces.values()]), gate, *pinned(base))
 
 
 def planned_copies(plan, info_ref, arrays, sems):
@@ -243,28 +311,23 @@
     )(info, *in_hbm(sources))
 
 
-def halves_kernel(info_ref, both_ref, mine_ref, other_ref, sems):
-    copies = [
-        pltpu.make_async_copy(both_ref.at[half], to, sems.at[index])
-        for index, (half, to) in enumerate(((info_ref[0], mine_ref), (1 - info_ref[0], other_ref)))
-    ]
-    for copy in copies:
-        copy.start()
-    for copy in copies:
-        copy.wait()
-
-
-def split_halves(info, both):
+def half_kernel(info_ref, both_ref, out_ref, sem):
+    copy = pltpu.make_async_copy(both_ref.at[1 - info_ref[0]], out_ref, sem.at[0])
+    copy.start()
+    copy.wait()
+
+
+def other_half(info, both):
     return pl.pallas_call(
-        halves_kernel,
-        out_shape=[jax.ShapeDtypeStruct(both.shape[1:], both.dtype)] * 2,
-        in_specs=[SCALARS, pl.BlockSpec(memory_space=pl.ANY)],
-        out_specs=[IN_VMEM] * 2,
-        scratch_shapes=[pltpu.SemaphoreType.DMA((2,))],
+        half_kernel,
+        out_shape=jax.ShapeDtypeStruct(both.shape[1:], both.dtype),
+        in_specs=[SCALARS, pl.BlockSpec(memory_space=pltpu.HBM)],
+        out_specs=IN_VMEM,
+        scratch_shapes=[pltpu.SemaphoreType.DMA((1,))],
         compiler_params=pltpu.CompilerParams(vmem_limit_bytes=COPY_LIMIT),
         cost_estimate=SMALL_COST,
-        name="split_halves",
-    )(info, both)
+        name="other_half",
+    )(info, *in_hbm([both]))
 
 
 def local(queries, keys, values, residual, gate, out_weight, time_offsets, guidance_index):
@@ -322,13 +385,14 @@
         return copy_columns(copy_info, [here[index] for index in used], plan, targets)
 
     def split_residual(residual):
-        return split_halves(branch_pos[None], jnp.transpose(residual[0], (1, 0, 2)))
+        both = jnp.transpose(residual[0], (1, 0, 2))
+        return both, other_half(branch_pos[None], both)
 
     packed = pack(key_value[:1])
     after = packed
     if RESIDUAL_AFTER == 0:
         _, residual = lax.optimization_barrier((packed, residual))
-        mine, other = split_residual(residual)
+        halves, other = split_residual(residual)
         after = (packed, other) if RESIDUAL_FIRST else packed
     late_key_value, far, first_query = pack([key_value[1], pair_weight[1], query[0]], after)
     packed = list(packed) + [late_key_value]
@@ -342,13 +406,15 @@
 
     if RESIDUAL_AFTER:
         _, residual = lax.optimization_barrier(((packed[1], sides[0])[RESIDUAL_AFTER - 1], residual))
-        mine, other = split_residual(residual)
+        halves, other = split_residual(residual)
     store["other"] = swap(other, 1, 0)
     offsets = lax.dynamic_index_in_dim(time_offsets, width_pos, 1, keepdims=False)
     edges = jnp.stack([(pos >= 0) & (pos < tiles_wide) for pos in near_pos]).astype(jnp.int32)
     attention_info = jnp.concatenate([offsets, edges])
     place = head_pos & 1
-    projection_info = jnp.concatenate([jnp.stack([branch_pos, place, place ^ 1, head_pos]), guidance_index])
+    block = branch_pos * head_count + head_pos
+    places = [branch_pos, place, place ^ 1, head_pos, block, block ^ 1]
+    projection_info = jnp.concatenate([jnp.stack(places), guidance_index])
 
     def relay(head):
         if RELAY[head] == "x":
@@ -367,8 +433,8 @@
         head_queries[head] = await_names(AWAITED.get(head, ()), head_queries[head])
         operands = [head_queries[head], packed[head], *sides[head]]
         if head == 0:
-            used, plan, targets = plan_of(pair_weight[:1] + query[1:] + key_value[2:])
-            own, near, *late = attention_copies(
+            used, plan, targets = plan_of(query[1:] + key_value[2:])
+            own, *late = attention_copies(
                 attention_info,
                 tiles_time,
                 operands,
@@ -394,25 +460,25 @@
 
     names = [name for name in store if isinstance(name, tuple)]
     late = [name for name in names if name[2] == heads - 1 or name in LATE]
-    base = (mine, store["other"])
-
-    def partial(names, base):
-        return partial_projection(
-            projection_info,
-            (near, store["far"]),
-            {name: store[name] for name in names},
-            gate,
-            base,
-            tile,
-            base[0] is mine,
-        )
-
-    base = partial([name for name in names if name not in late], base)
+    late_rows = [(0, 0, heads - 1), (0, 1, heads - 1)]
+    late_rows += [(0,) + name[1:] for name in LATE]
+    *base, late_weights = first_share(
+        projection_info,
+        out_weight,
+        store["far"],
+        {name: store[name] for name in names if name not in late},
+        gate,
+        halves,
+        store["other"],
+        tuple(late_rows),
+        tile,
+    )
     if TIE_PARTIAL:
         name = (1, 0, heads - 1) if RELAY[-1] == "y" else (0, 1, heads - 1)
         base, store[name] = lax.optimization_barrier((base, store[name]))
     relay(heads - 1)
-    base = partial(late + [(1, 1, heads - 1)], base)
+    pieces = {name: store[name] for name in late + [(1, 1, heads - 1)]}
+    base = last_share(projection_info, late_weights, pieces, gate, base, late_rows, tile)
     return (base[0] + swap(base[1], 0, 1).astype(jnp.float32)).astype(jnp.bfloat16)
 
 

time: 81.7 us -> 82 us (level)
  waiting for transfers between devices: 11.2 us -> 16.1 us
  local copies, waits for them, and re-layouts: 11.1 us -> 7.18 us
  starting transfers between devices: 29.5 us -> 28.5 us
    ppermute x6, waiting for transfers between devices: 1.65 us -> 9.43 us  [halo(): return [lax.ppermute(part, 'tokens', pairs) for pairs in rounds]]
    unnamed x32 -> x22, local copies, waits for them, and re-layouts: 9.45 us -> 4.93 us
    ppermute x6, waiting for transfers between devices: 4.26 us -> 2.07 us  [swap(): lax.ppermute(value, 'head', [(i, i ^ head_bits) for i in range(head_count)])]
    pallas_call x3, Pallas kernels: 7.28 us -> 8.63 us  [the longest x1 4.8 us: first_share(): pl.pallas_call(functools.partial(first_kernel, tuple(pieces), late), out_...]
    optimization_barrier x1, local copies, waits for them, and re-layouts: 0.23 us -> 1.46 us  [local(): _, residual = lax.optimization_barrier((packed, residual))]
    ppermute x6, starting transfers between devices: 13.4 us -> 12.3 us  [swap(): lax.ppermute(value, 'head', [(i, i ^ head_bits) for i in range(head_count)])]
    pallas_call x1, Pallas kernels: 6.21 us -> 5.35 us  [attention_copies(): pl.pallas_call(functools.partial(attention_copies_kernel, last, plan, len...]
  transfers between devices with their start and end apart: 18 -> 18, of which waited for: 4 -> 5; matrix products, arithmetic and copies ran while one was open for 2% -> 3% of each run, Pallas kernels for 29% -> 29%
where the time goes in v10:
time: 82 us; the launch traced here: 81.5 us
  starting transfers between devices  28.5 us (35%)
  Pallas kernels  28.1 us (34%)
  waiting for transfers between devices  16.1 us (20%)
  local copies, waits for them, and re-layouts  7.18 us (9%)
  other arithmetic  1.37 us (2%)
    ppermute x6, starting transfers between devices, swap(): lax.ppermute(value, 'head', [(i, i ^ head_bits) for i in range(head_count)])  12.3 us
    ppermute x6, starting transfers between devices, halo(): return [lax.ppermute(part, 'tokens', pairs) for pairs in rounds]  9.68 us
    ppermute x6, waiting for transfers between devices, halo(): return [lax.ppermute(part, 'tokens', pairs) for pairs in rounds]  9.43 us
    pallas_call x2, Pallas kernels, attention(): pl.pallas_call(functools.partial(attention_kernel, *tiles), out_shape=jax...  9.34 us
    ppermute x6, starting transfers between devices, swap(): return lax.ppermute(value, 'branch', [(0, 1), (1, 0)])  6.58 us
    pallas_call x1, Pallas kernels, attention_copies(): pl.pallas_call(functools.partial(attention_copies_kernel, last, plan, len...  5.35 us
    unnamed x22, local copies, waits for them, and re-layouts  4.93 us
    pallas_call x2, Pallas kernels, copy_columns(): pl.pallas_call(functools.partial(copy_kernel, plan), out_shape=[jax.Shape...  4.81 us
  transfers between devices with their start and end apart: 18, of which 5 were waited for; matrix products, arithmetic and copies ran while one was open for 3% of the time, Pallas kernels for 29%

profile of v10, /device:TPU:9, one launch (start us, length us, event | category | flops | bytes accessed | tf_op | source)
XLA Modules:
  0.0 81.5 jit_solution(16474558473201062760)
XLA Ops:
  0.0 0.0 copy-start
  0.0 0.1 pad_add_fusion.1.info_ref.copy_info_ref
  0.1 1.7 %copy_columns.2.refs_1_ = bf16[2,1152,128]{2,1,0:T(8,128)(2,1)S(1)} custom-call(s32[2]{0:T(128)S(1)} %pad_add_fusion.1.info_ref.copy_info_ref, bf16[1152,384]{1,0:T(8,128)(2,1)} %bitcast.20, bf16[1152,384]{1,0:T(8,128)(2,1)} %bitcast.23), custom_call_target="tpu_custom_call" | custom-call | bytes 1024 | tf_op jit(solution)/shard_map/copy_columns/pallas_call | solution.py:302
  1.8 0.1 collective-permute-start
  1.9 4.5 %collective-permute-start.1 = (bf16[2,1152,128]{2,1,0:T(8,128)(2,1)S(1)}, bf16[2,1152,128]{2,1,0:T(8,128)(2,1)S(1)}, u32[]{:S(2)}, u32[]{:S(2)}) collective-permute-start(bf16[2,1152,128]{2,1,0:T(8,128)(2,1)S(1)} %copy_columns.2.refs_1_), channel_id=1, source_target_pairs={{1,2},{2,1},{5,6},{6,5},{9,10},{10,9},{13,14},{14,13},{17,18},{18,... | collective-permute-start | bytes 1769480 | tf_op jit(solution)/shard_map/ppermute | solution.py:402
  6.4 0.0 copy-done.9
  6.4 1.5 %copy.11 = bf16[1,1152,2,384]{3,1,2,0:T(8,128)(2,1)} copy(bf16[1,1152,2,384]{3,2,1,0:T(2,128)(2,1)S(1)} %copy-done.9) | data formatting | bytes 3538944 | tf_op jit(solution)/shard_map/optimization_barrier | solution.py:394
  7.8 1.2 %other_half.1 = bf16[1152,384]{1,0:T(8,128)(2,1)S(1)} custom-call(s32[1]{0:T(128)} %bitcast.info_ref, bf16[2,1152,384]{2,1,0:T(8,128)(2,1)} %bitcast.18), custom_call_target="tpu_custom_call" | custom-call | bytes 1024 | tf_op jit(solution)/shard_map/other_half/pallas_call | solution.py:321
  9.0 3.1 %copy_columns.3 = (bf16[2,1152,128]{2,1,0:T(8,128)(2,1)}, bf16[384,768]{1,0:T(8,128)(2,1)}, bf16[1152,128]{1,0:T(8,128)(2,1)S(1)}) custom-call(s32[2]{0:T(128)S(1)} %pad_add_fusion.1.info_ref.copy_info_ref, bf16[1152,384]{1,0:T(8,128)(2,1)} %bitcast.26, bf16[1152,384]{1,0:T(8,128)(2,1)} %bitcast.21, bf16[1152,384]{1,0:T(8,128)(2,1)} %bitcast.24, ...), custom_call_target="tpu_custom_call" | custom-call | bytes 1024 | tf_op jit(solution)/shard_map/copy_columns/pallas_call | solution.py:302
  12.1 0.0 copy-start.3
  12.1 0.7 copy-done.3
  12.8 1.2 %collective-permute-start.2 = (bf16[384,768]{1,0:T(8,128)(2,1)}, bf16[384,768]{1,0:T(8,128)(2,1)}, u32[]{:S(2)}, u32[]{:S(2)}) collective-permute-start(bf16[384,768]{1,0:T(8,128)(2,1)} %get-tuple-element.44), channel_id=1, source_target_pairs={{0,8},{4,12},{8,0},{12,4},{1,9},{5,13},{9,1},{13,5},{2,10},{6,14},... | collective-permute-start | bytes 1769480 | tf_op jit(solution)/shard_map/ppermute | solution.py:357
  14.1 1.9 %collective-permute-start.10 = (bf16[2,1152,128]{2,1,0:T(8,128)(2,1)}, bf16[2,1152,128]{2,1,0:T(8,128)(2,1)}, u32[]{:S(2)}, u32[]{:S(2)}) collective-permute-start(bf16[2,1152,128]{2,1,0:T(8,128)(2,1)} %get-tuple-element.56.own_ref), channel_id=1, source_target_pairs={{1,2},{2,1},{5,6},{6,5},{9,10},{10,9},{13,14},{14,13},{17,18},{18,... | collective-permute-start | bytes 1769480 | tf_op jit(solution)/shard_map/ppermute | solution.py:402
  16.0 1.3 %collective-permute-start.3 = (bf16[1152,384]{1,0:T(8,128)(2,1)S(1)}, bf16[1152,384]{1,0:T(8,128)(2,1)S(1)}, u32[]{:S(2)}, u32[]{:S(2)}) collective-permute-start(bf16[1152,384]{1,0:T(8,128)(2,1)S(1)} %other_half.1), channel_id=1, source_target_pairs={{0,16},{16,0},{1,17},{17,1},{2,18},{18,2},{3,19},{19,3},{4,20},{20... | collective-permute-start | bytes 2654216 | tf_op jit(solution)/shard_map/ppermute | solution.py:355
  17.3 0.0 copy-done
  17.3 0.2 dynamic-slice_reduce_fusion
  17.4 0.1 add_convert_fusion.1
  17.5 0.1 pad_add_fusion.info_ref
  17.6 0.0 collective-permute-done.refs_2_
  17.6 0.0 collective-permute-start.9
  17.6 1.6 %collective-permute-done.1.refs_3_ = bf16[2,1152,128]{2,1,0:T(8,128)(2,1)S(1)} collective-permute-done((bf16[2,1152,128]{2,1,0:T(8,128)(2,1)S(1)}, bf16[2,1152,128]{2,1,0:T(8,128)(2,1)S(1)}, u32[]{:S(2)}, u32[]{:S(2)}) %collective-permute-start.1) | collective-permute-done | bytes 589856 | tf_op jit(solution)/shard_map/ppermute | solution.py:402
  19.2 1.0 %copy-done.4 = bf16[1152,128]{1,0:T(8,128)(2,1)S(1)} copy-done((bf16[1152,128]{1,0:T(8,128)(2,1)S(1)}, bf16[1152,128]{1,0:T(8,128)(2,1)}, u32[]{:S(2)}) %copy-start.4) | copy-done | bytes 294936
  20.2 5.3 %attention_copies.1 = (bf16[1152,128]{1,0:T(8,128)(2,1)S(1)}, bf16[1152,128]{1,0:T(8,128)(2,1)S(1)}, bf16[1152,128]{1,0:T(8,128)(2,1)S(1)}, bf16[2,1152,128]{2,1,0:T(8,128)(2,1)S(1)}) custom-call(s32[5]{0:T(128)S(1)} %pad_add_fusion.info_ref, s32[2]{0:T(128)S(1)} %pad_add_fusion.1.info_ref.copy_info_ref, bf16[1152,128]{1,0:T(8,128)(2,1)S(1)} %copy-done.4, ...), custom_call_target="tpu_custom_call" | custom-call | bytes 1024 | tf_op jit(solution)/shard_map/attention_copies/pallas_call | solution.py:128
  25.5 0.0 copy-start.1
  25.5 1.3 %collective-permute-start.4 = (bf16[1152,128]{1,0:T(8,128)(2,1)S(1)}, bf16[1152,128]{1,0:T(8,128)(2,1)S(1)}, u32[]{:S(2)}, u32[]{:S(2)}) collective-permute-start(bf16[1152,128]{1,0:T(8,128)(2,1)S(1)} %get-tuple-element.45.refs_0_), channel_id=1, source_target_pairs={{0,8},{4,12},{8,0},{12,4},{1,9},{5,13},{9,1},{13,5},{2,10},{6,14},... | collective-permute-start | bytes 884744 | tf_op jit(solution)/shard_map/ppermute | solution.py:357
  26.8 0.0 collective-permute-done.2.far_ref
  26.8 0.0 collective-permute-start.6
  26.8 5.0 %collective-permute-done.10.side_b_ref = bf16[2,1152,128]{2,1,0:T(8,128)(2,1)} collective-permute-done((bf16[2,1152,128]{2,1,0:T(8,128)(2,1)}, bf16[2,1152,128]{2,1,0:T(8,128)(2,1)}, u32[]{:S(2)}, u32[]{:S(2)}) %collective-permute-start.10) | collective-permute-done | bytes 589856 | tf_op jit(solution)/shard_map/ppermute | solution.py:402
  31.8 3.2 %collective-permute-start.7 = (bf16[2,1152,128]{2,1,0:T(8,128)(2,1)S(1)}, bf16[2,1152,128]{2,1,0:T(8,128)(2,1)S(1)}, u32[]{:S(2)}, u32[]{:S(2)}) collective-permute-start(bf16[2,1152,128]{2,1,0:T(8,128)(2,1)S(1)} %get-tuple-element.53.own_ref), channel_id=1, source_target_pairs={{1,2},{2,1},{5,6},{6,5},{9,10},{10,9},{13,14},{14,13},{17,18},{18,... | collective-permute-start | bytes 1769480 | tf_op jit(solution)/shard_map/ppermute | solution.py:402
  35.1 0.0 collective-permute-done.4.refs_2_
  35.1 1.3 %collective-permute-start.5 = (bf16[1152,128]{1,0:T(8,128)(2,1)S(1)}, bf16[1152,128]{1,0:T(8,128)(2,1)S(1)}, u32[]{:S(2)}, u32[]{:S(2)}) collective-permute-start(bf16[1152,128]{1,0:T(8,128)(2,1)S(1)} %get-tuple-element.45.refs_0_), channel_id=1, source_target_pairs={{0,16},{16,0},{1,17},{17,1},{2,18},{18,2},{3,19},{19,3},{4,20},{20... | collective-permute-start | bytes 884744 | tf_op jit(solution)/shard_map/ppermute | solution.py:355
  36.3 0.0 collective-permute-done.3.refs_9_
  36.3 0.5 collective-permute-start.8
  36.9 0.0 collective-permute-done.9.side_a_ref
  36.9 5.0 %attention.3.refs_4_ = bf16[1152,128]{1,0:T(8,128)(2,1)S(1)} custom-call(s32[5]{0:T(128)S(1)} %pad_add_fusion.info_ref, bf16[1152,128]{1,0:T(8,128)(2,1)S(1)} %get-tuple-element.55.q_ref, bf16[2,1152,128]{2,1,0:T(8,128)(2,1)} %get-tuple-element.56.own_ref, bf16[2,1152,128]{2,1,0:T(8,128)(2,1)S(1)} %collective-permute-done.9.side_a_ref, ...), custom_call_target="tpu_custom_call" | custom-call | bytes 1024 | tf_op jit(solution)/shard_map/attention/pallas_call | solution.py:105
  41.9 0.0 copy-start.10
  41.9 0.0 copy-start.7
  41.9 1.0 %collective-permute-start.11 = (bf16[1152,128]{1,0:T(8,128)(2,1)S(1)}, bf16[1152,128]{1,0:T(8,128)(2,1)S(1)}, u32[]{:S(2)}, u32[]{:S(2)}) collective-permute-start(bf16[1152,128]{1,0:T(8,128)(2,1)S(1)} %attention.3.refs_4_), channel_id=1, source_target_pairs={{0,16},{16,0},{1,17},{17,1},{2,18},{18,2},{3,19},{19,3},{4,20},{20... | collective-permute-start | bytes 884744 | tf_op jit(solution)/shard_map/ppermute | solution.py:355
  42.9 0.0 collective-permute-done.5.refs_1_
  42.9 1.2 %collective-permute-start.12 = (bf16[1152,128]{1,0:T(8,128)(2,1)S(1)}, bf16[1152,128]{1,0:T(8,128)(2,1)S(1)}, u32[]{:S(2)}, u32[]{:S(2)}) collective-permute-start(bf16[1152,128]{1,0:T(8,128)(2,1)S(1)} %attention.3.refs_4_), channel_id=1, source_target_pairs={{0,8},{4,12},{8,0},{12,4},{1,9},{5,13},{9,1},{13,5},{2,10},{6,14},... | collective-permute-start | bytes 884744 | tf_op jit(solution)/shard_map/ppermute | solution.py:357
  44.1 0.0 collective-permute-done.6.side_a_ref
  44.2 2.8 %collective-permute-done.7.side_b_ref = bf16[2,1152,128]{2,1,0:T(8,128)(2,1)S(1)} collective-permute-done((bf16[2,1152,128]{2,1,0:T(8,128)(2,1)S(1)}, bf16[2,1152,128]{2,1,0:T(8,128)(2,1)S(1)}, u32[]{:S(2)}, u32[]{:S(2)}) %collective-permute-start.7) | collective-permute-done | bytes 589856 | tf_op jit(solution)/shard_map/ppermute | solution.py:402
  47.0 4.4 %attention.2.refs_1_ = bf16[1152,128]{1,0:T(8,128)(2,1)S(1)} custom-call(s32[5]{0:T(128)S(1)} %pad_add_fusion.info_ref, bf16[1152,128]{1,0:T(8,128)(2,1)S(1)} %get-tuple-element.52.q_ref, bf16[2,1152,128]{2,1,0:T(8,128)(2,1)S(1)} %get-tuple-element.53.own_ref, bf16[2,1152,128]{2,1,0:T(8,128)(2,1)S(1)} %collective-permute-done.6.side_a_ref, ...), custom_call_target="tpu_custom_call" | custom-call | bytes 1024 | tf_op jit(solution)/shard_map/attention/pallas_call | solution.py:105
  51.4 0.0 collective-permute-done.8.refs_3_
  51.4 1.3 %collective-permute-start.15 = (bf16[1152,128]{1,0:T(8,128)(2,1)S(1)}, bf16[1152,128]{1,0:T(8,128)(2,1)}, u32[]{:S(2)}, u32[]{:S(2)}) collective-permute-start(bf16[1152,128]{1,0:T(8,128)(2,1)S(1)} %attention.2.refs_1_), channel_id=1, source_target_pairs={{0,8},{4,12},{8,0},{12,4},{1,9},{5,13},{9,1},{13,5},{2,10},{6,14},... | collective-permute-start | bytes 884744 | tf_op jit(solution)/shard_map/ppermute | solution.py:357
  52.7 0.6 concatenate.6.info_ref
  53.3 1.2 %collective-permute-start.14 = (bf16[1152,128]{1,0:T(8,128)(2,1)S(1)}, bf16[1152,128]{1,0:T(8,128)(2,1)S(1)}, u32[]{:S(2)}, u32[]{:S(2)}) collective-permute-start(bf16[1152,128]{1,0:T(8,128)(2,1)S(1)} %attention.2.refs_1_), channel_id=1, source_target_pairs={{0,16},{16,0},{1,17},{17,1},{2,18},{18,2},{3,19},{19,3},{4,20},{20... | collective-permute-start | bytes 884744 | tf_op jit(solution)/shard_map/ppermute | solution.py:355
  54.5 0.0 collective-permute-done.11.refs_5_
  54.5 0.9 %collective-permute-start.13 = (bf16[1152,128]{1,0:T(8,128)(2,1)S(1)}, bf16[1152,128]{1,0:T(8,128)(2,1)S(1)}, u32[]{:S(2)}, u32[]{:S(2)}) collective-permute-start(bf16[1152,128]{1,0:T(8,128)(2,1)S(1)} %collective-permute-done.11.refs_5_), channel_id=1, source_target_pairs={{0,8},{4,12},{8,0},{12,4},{1,9},{5,13},{9,1},{13,5},{2,10},{6,14},... | collective-permute-start | bytes 884744 | tf_op jit(solution)/shard_map/ppermute | solution.py:357
  55.4 0.0 collective-permute-done.12.refs_6_
  55.4 0.7 copy-done.5
  56.1 1.0 %copy-done.2 = bf16[1152,128]{1,0:T(8,128)(2,1)S(1)} copy-done((bf16[1152,128]{1,0:T(8,128)(2,1)S(1)}, bf16[1152,128]{1,0:T(8,128)(2,1)}, u32[]{:S(2)}) %copy-start.2) | copy-done | bytes 294936
  57.1 1.0 %copy-done.6 = bf16[1152,128]{1,0:T(8,128)(2,1)S(1)} copy-done((bf16[1152,128]{1,0:T(8,128)(2,1)S(1)}, bf16[1152,128]{1,0:T(8,128)(2,1)}, u32[]{:S(2)}) %copy-start.6) | copy-done | bytes 294936
  58.0 0.6 copy-done.8
  58.6 4.8 %first_share.1 = (f32[1152,384]{1,0:T(8,128)S(1)}, f32[1152,384]{1,0:T(8,128)S(1)}, bf16[384,768]{1,0:T(8,128)(2,1)S(1)}) custom-call(s32[24]{0:T(128)S(1)} %copy-done.8, bf16[384,3072]{1,0:T(8,128)(2,1)} %near_other_ref.1, bf16[384,3072]{1,0:T(8,128)(2,1)} %near_other_ref.1, bf16[384,768]{1,0:T(8,128)(2,1)} %collective-permute-done.2.far_ref, ...), custom_call_target="tpu_custom_call" | custom-call | bytes 1024 | tf_op jit(solution)/shard_map/first_share/pallas_call | solution.py:207
  63.4 0.0 collective-permute-done.15.refs_3_
  63.4 1.3 %collective-permute-start.16 = (bf16[1152,128]{1,0:T(8,128)(2,1)}, bf16[1152,128]{1,0:T(8,128)(2,1)S(1)}, u32[]{:S(2)}, u32[]{:S(2)}) collective-permute-start(bf16[1152,128]{1,0:T(8,128)(2,1)} %collective-permute-done.15.refs_3_), channel_id=1, source_target_pairs={{0,16},{16,0},{1,17},{17,1},{2,18},{18,2},{3,19},{19,3},{4,20},{20... | collective-permute-start | bytes 884744 | tf_op jit(solution)/shard_map/ppermute | solution.py:355
  64.7 0.0 collective-permute-done.13.refs_0_
  64.7 0.0 collective-permute-done.14.refs_2_
  64.7 4.6 %collective-permute-done.16.refs_4_ = bf16[1152,128]{1,0:T(8,128)(2,1)S(1)} collective-permute-done((bf16[1152,128]{1,0:T(8,128)(2,1)}, bf16[1152,128]{1,0:T(8,128)(2,1)S(1)}, u32[]{:S(2)}, u32[]{:S(2)}) %collective-permute-start.16) | collective-permute-done | bytes 294944 | tf_op jit(solution)/shard_map/ppermute | solution.py:355
  69.3 2.6 %last_share.1 = (f32[1152,384]{1,0:T(8,128)S(1)}, bf16[1152,384]{1,0:T(8,128)(2,1)S(1)}) custom-call(s32[24]{0:T(128)S(1)} %copy-done.8, bf16[384,768]{1,0:T(8,128)(2,1)S(1)} %get-tuple-element.58.w_ref, bf16[1152,128]{1,0:T(8,128)(2,1)S(1)} %collective-permute-done.13.refs_0_, bf16[1152,128]{1,0:T(8,128)(2,1)S(1)} %attention.2.refs_1_, ...), custom_call_target="tpu_custom_call" | custom-call | bytes 1024 | tf_op jit(solution)/shard_map/last_share/pallas_call | solution.py:264
  72.0 6.3 %collective-permute-start.17 = (bf16[1152,384]{1,0:T(8,128)(2,1)S(1)}, bf16[1152,384]{1,0:T(8,128)(2,1)S(1)}, u32[]{:S(2)}, u32[]{:S(2)}) collective-permute-start(bf16[1152,384]{1,0:T(8,128)(2,1)S(1)} %get-tuple-element.66), channel_id=1, source_target_pairs={{0,4},{4,0},{8,12},{12,8},{1,5},{5,1},{9,13},{13,9},{2,6},{6,2},{1... | collective-permute-start | bytes 2654216 | tf_op jit(solution)/shard_map/ppermute | solution.py:357
  78.3 2.1 %collective-permute-done.17 = bf16[1152,384]{1,0:T(8,128)(2,1)S(1)} collective-permute-done((bf16[1152,384]{1,0:T(8,128)(2,1)S(1)}, bf16[1152,384]{1,0:T(8,128)(2,1)S(1)}, u32[]{:S(2)}, u32[]{:S(2)}) %collective-permute-start.17) | collective-permute-done | bytes 884768 | tf_op jit(solution)/shard_map/ppermute | solution.py:357
  80.3 1.1 %add_convert_fusion = bf16[1152,384]{1,0:T(8,128)(2,1)} fusion(f32[1152,384]{1,0:T(8,128)S(1)} %get-tuple-element.65, bf16[1152,384]{1,0:T(8,128)(2,1)S(1)} %collective-permute-done.17), kind=kLoop, calls=%fused_computation.1 | loop fusion | flops 1327104 | bytes 3538944 | tf_op jit(solution)/shard_map/convert_element_type | solution.py:482
  (9 shorter events, 0.0 us)
Async XLA Ops:
  0.0 17.3 %copy-start = (s32[3,4]{1,0:T(4,128)S(1)}, s32[3,4]{1,0:T(4,128)}, u32[]{:S(2)}) copy-start(s32[3,4]{1,0:T(4,128)} %param.14) | copy-start | bytes 148
  0.0 6.4 %copy-start.9 = (bf16[1,1152,2,384]{3,2,1,0:T(2,128)(2,1)S(1)}, bf16[1,1152,2,384]{3,2,1,0:T(2,128)(2,1)}, u32[]{:S(2)}) copy-start(bf16[1,1152,2,384]{3,2,1,0:T(2,128)(2,1)} %param.11) | copy-start | bytes 5308420
  1.8 15.8 %collective-permute-start = (bf16[2,1152,128]{2,1,0:T(8,128)(2,1)S(1)}, bf16[2,1152,128]{2,1,0:T(8,128)(2,1)S(1)}, u32[]{:S(2)}, u32[]{:S(2)}) collective-permute-start(bf16[2,1152,128]{2,1,0:T(8,128)(2,1)S(1)} %copy_columns.2.refs_1_), channel_id=1, source_target_pairs={{0,1},{1,0},{2,3},{3,2},{4,5},{5,4},{6,7},{7,6},{8,9},{9,8},{10,11... | collective-permute-start | bytes 1769480 | tf_op jit(solution)/shard_map/ppermute | solution.py:402
  1.9 17.3 %collective-permute-start.1 = (bf16[2,1152,128]{2,1,0:T(8,128)(2,1)S(1)}, bf16[2,1152,128]{2,1,0:T(8,128)(2,1)S(1)}, u32[]{:S(2)}, u32[]{:S(2)}) collective-permute-start(bf16[2,1152,128]{2,1,0:T(8,128)(2,1)S(1)} %copy_columns.2.refs_1_), channel_id=1, source_target_pairs={{1,2},{2,1},{5,6},{6,5},{9,10},{10,9},{13,14},{14,13},{17,18},{18,... | collective-permute-start | bytes 1769480 | tf_op jit(solution)/shard_map/ppermute | solution.py:402
  12.1 0.7 copy-start.3
  12.8 14.0 %collective-permute-start.2 = (bf16[384,768]{1,0:T(8,128)(2,1)}, bf16[384,768]{1,0:T(8,128)(2,1)}, u32[]{:S(2)}, u32[]{:S(2)}) collective-permute-start(bf16[384,768]{1,0:T(8,128)(2,1)} %get-tuple-element.44), channel_id=1, source_target_pairs={{0,8},{4,12},{8,0},{12,4},{1,9},{5,13},{9,1},{13,5},{2,10},{6,14},... | collective-permute-start | bytes 1769480 | tf_op jit(solution)/shard_map/ppermute | solution.py:357
  14.1 17.8 %collective-permute-start.10 = (bf16[2,1152,128]{2,1,0:T(8,128)(2,1)}, bf16[2,1152,128]{2,1,0:T(8,128)(2,1)}, u32[]{:S(2)}, u32[]{:S(2)}) collective-permute-start(bf16[2,1152,128]{2,1,0:T(8,128)(2,1)} %get-tuple-element.56.own_ref), channel_id=1, source_target_pairs={{1,2},{2,1},{5,6},{6,5},{9,10},{10,9},{13,14},{14,13},{17,18},{18,... | collective-permute-start | bytes 1769480 | tf_op jit(solution)/shard_map/ppermute | solution.py:402
  16.0 20.4 %collective-permute-start.3 = (bf16[1152,384]{1,0:T(8,128)(2,1)S(1)}, bf16[1152,384]{1,0:T(8,128)(2,1)S(1)}, u32[]{:S(2)}, u32[]{:S(2)}) collective-permute-start(bf16[1152,384]{1,0:T(8,128)(2,1)S(1)} %other_half.1), channel_id=1, source_target_pairs={{0,16},{16,0},{1,17},{17,1},{2,18},{18,2},{3,19},{19,3},{4,20},{20... | collective-permute-start | bytes 2654216 | tf_op jit(solution)/shard_map/ppermute | solution.py:355
  17.6 19.3 %collective-permute-start.9 = (bf16[2,1152,128]{2,1,0:T(8,128)(2,1)}, bf16[2,1152,128]{2,1,0:T(8,128)(2,1)S(1)}, u32[]{:S(2)}, u32[]{:S(2)}) collective-permute-start(bf16[2,1152,128]{2,1,0:T(8,128)(2,1)} %get-tuple-element.56.own_ref), channel_id=1, source_target_pairs={{0,1},{1,0},{2,3},{3,2},{4,5},{5,4},{6,7},{7,6},{8,9},{9,8},{10,11... | collective-permute-start | bytes 1769480 | tf_op jit(solution)/shard_map/ppermute | solution.py:402
  19.2 1.0 %copy-start.4 = (bf16[1152,128]{1,0:T(8,128)(2,1)S(1)}, bf16[1152,128]{1,0:T(8,128)(2,1)}, u32[]{:S(2)}) copy-start(bf16[1152,128]{1,0:T(8,128)(2,1)} %copy-done.3) | copy-start | bytes 884740
  25.5 25.8 %copy-start.1 = (bf16[1152,128]{1,0:T(8,128)(2,1)}, bf16[1152,128]{1,0:T(8,128)(2,1)S(1)}, u32[]{:S(2)}) copy-start(bf16[1152,128]{1,0:T(8,128)(2,1)S(1)} %get-tuple-element.45.refs_0_) | copy-start | bytes 884740
  25.5 9.5 %collective-permute-start.4 = (bf16[1152,128]{1,0:T(8,128)(2,1)S(1)}, bf16[1152,128]{1,0:T(8,128)(2,1)S(1)}, u32[]{:S(2)}, u32[]{:S(2)}) collective-permute-start(bf16[1152,128]{1,0:T(8,128)(2,1)S(1)} %get-tuple-element.45.refs_0_), channel_id=1, source_target_pairs={{0,8},{4,12},{8,0},{12,4},{1,9},{5,13},{9,1},{13,5},{2,10},{6,14},... | collective-permute-start | bytes 884744 | tf_op jit(solution)/shard_map/ppermute | solution.py:357
  26.8 17.3 %collective-permute-start.6 = (bf16[2,1152,128]{2,1,0:T(8,128)(2,1)S(1)}, bf16[2,1152,128]{2,1,0:T(8,128)(2,1)S(1)}, u32[]{:S(2)}, u32[]{:S(2)}) collective-permute-start(bf16[2,1152,128]{2,1,0:T(8,128)(2,1)S(1)} %get-tuple-element.53.own_ref), channel_id=1, source_target_pairs={{0,1},{1,0},{2,3},{3,2},{4,5},{5,4},{6,7},{7,6},{8,9},{9,8},{10,11... | collective-permute-start | bytes 1769480 | tf_op jit(solution)/shard_map/ppermute | solution.py:402
  31.8 15.2 %collective-permute-start.7 = (bf16[2,1152,128]{2,1,0:T(8,128)(2,1)S(1)}, bf16[2,1152,128]{2,1,0:T(8,128)(2,1)S(1)}, u32[]{:S(2)}, u32[]{:S(2)}) collective-permute-start(bf16[2,1152,128]{2,1,0:T(8,128)(2,1)S(1)} %get-tuple-element.53.own_ref), channel_id=1, source_target_pairs={{1,2},{2,1},{5,6},{6,5},{9,10},{10,9},{13,14},{14,13},{17,18},{18,... | collective-permute-start | bytes 1769480 | tf_op jit(solution)/shard_map/ppermute | solution.py:402
  35.1 7.8 %collective-permute-start.5 = (bf16[1152,128]{1,0:T(8,128)(2,1)S(1)}, bf16[1152,128]{1,0:T(8,128)(2,1)S(1)}, u32[]{:S(2)}, u32[]{:S(2)}) collective-permute-start(bf16[1152,128]{1,0:T(8,128)(2,1)S(1)} %get-tuple-element.45.refs_0_), channel_id=1, source_target_pairs={{0,16},{16,0},{1,17},{17,1},{2,18},{18,2},{3,19},{19,3},{4,20},{20... | collective-permute-start | bytes 884744 | tf_op jit(solution)/shard_map/ppermute | solution.py:355
  36.3 15.0 %collective-permute-start.8 = (bf16[1152,128]{1,0:T(8,128)(2,1)S(1)}, bf16[1152,128]{1,0:T(8,128)(2,1)S(1)}, u32[]{:S(2)}, u32[]{:S(2)}) collective-permute-start(bf16[1152,128]{1,0:T(8,128)(2,1)S(1)} %collective-permute-done.4.refs_2_), channel_id=1, source_target_pairs={{0,16},{16,0},{1,17},{17,1},{2,18},{18,2},{3,19},{19,3},{4,20},{20... | collective-permute-start | bytes 884744 | tf_op jit(solution)/shard_map/ppermute | solution.py:355
  41.9 10.8 %copy-start.10 = (s32[18]{0:T(128)S(1)}, s32[18]{0:T(128)}, u32[]{:S(2)}) copy-start(s32[18]{0:T(128)} %param.15) | copy-start | bytes 220
  41.9 14.2 %copy-start.7 = (bf16[2,2,1536]{2,1,0:T(2,128)(2,1)S(1)}, bf16[2,2,1536]{2,1,0:T(2,128)(2,1)}, u32[]{:S(2)}) copy-start(bf16[2,2,1536]{2,1,0:T(2,128)(2,1)} %refs_5_.1) | copy-start | bytes 36868
  41.9 12.6 %collective-permute-start.11 = (bf16[1152,128]{1,0:T(8,128)(2,1)S(1)}, bf16[1152,128]{1,0:T(8,128)(2,1)S(1)}, u32[]{:S(2)}, u32[]{:S(2)}) collective-permute-start(bf16[1152,128]{1,0:T(8,128)(2,1)S(1)} %attention.3.refs_4_), channel_id=1, source_target_pairs={{0,16},{16,0},{1,17},{17,1},{2,18},{18,2},{3,19},{19,3},{4,20},{20... | collective-permute-start | bytes 884744 | tf_op jit(solution)/shard_map/ppermute | solution.py:355
  42.9 12.5 %collective-permute-start.12 = (bf16[1152,128]{1,0:T(8,128)(2,1)S(1)}, bf16[1152,128]{1,0:T(8,128)(2,1)S(1)}, u32[]{:S(2)}, u32[]{:S(2)}) collective-permute-start(bf16[1152,128]{1,0:T(8,128)(2,1)S(1)} %attention.3.refs_4_), channel_id=1, source_target_pairs={{0,8},{4,12},{8,0},{12,4},{1,9},{5,13},{9,1},{13,5},{2,10},{6,14},... | collective-permute-start | bytes 884744 | tf_op jit(solution)/shard_map/ppermute | solution.py:357
  51.4 12.1 %collective-permute-start.15 = (bf16[1152,128]{1,0:T(8,128)(2,1)S(1)}, bf16[1152,128]{1,0:T(8,128)(2,1)}, u32[]{:S(2)}, u32[]{:S(2)}) collective-permute-start(bf16[1152,128]{1,0:T(8,128)(2,1)S(1)} %attention.2.refs_1_), channel_id=1, source_target_pairs={{0,8},{4,12},{8,0},{12,4},{1,9},{5,13},{9,1},{13,5},{2,10},{6,14},... | collective-permute-start | bytes 884744 | tf_op jit(solution)/shard_map/ppermute | solution.py:357
  53.3 11.4 %collective-permute-start.14 = (bf16[1152,128]{1,0:T(8,128)(2,1)S(1)}, bf16[1152,128]{1,0:T(8,128)(2,1)S(1)}, u32[]{:S(2)}, u32[]{:S(2)}) collective-permute-start(bf16[1152,128]{1,0:T(8,128)(2,1)S(1)} %attention.2.refs_1_), channel_id=1, source_target_pairs={{0,16},{16,0},{1,17},{17,1},{2,18},{18,2},{3,19},{19,3},{4,20},{20... | collective-permute-start | bytes 884744 | tf_op jit(solution)/shard_map/ppermute | solution.py:355
  54.5 10.2 %collective-permute-start.13 = (bf16[1152,128]{1,0:T(8,128)(2,1)S(1)}, bf16[1152,128]{1,0:T(8,128)(2,1)S(1)}, u32[]{:S(2)}, u32[]{:S(2)}) collective-permute-start(bf16[1152,128]{1,0:T(8,128)(2,1)S(1)} %collective-permute-done.11.refs_5_), channel_id=1, source_target_pairs={{0,8},{4,12},{8,0},{12,4},{1,9},{5,13},{9,1},{13,5},{2,10},{6,14},... | collective-permute-start | bytes 884744 | tf_op jit(solution)/shard_map/ppermute | solution.py:357
  55.4 0.7 copy-start.5
  56.1 1.0 %copy-start.2 = (bf16[1152,128]{1,0:T(8,128)(2,1)S(1)}, bf16[1152,128]{1,0:T(8,128)(2,1)}, u32[]{:S(2)}) copy-start(bf16[1152,128]{1,0:T(8,128)(2,1)} %copy-done.1) | copy-start | bytes 884740
  57.1 1.0 %copy-start.6 = (bf16[1152,128]{1,0:T(8,128)(2,1)S(1)}, bf16[1152,128]{1,0:T(8,128)(2,1)}, u32[]{:S(2)}) copy-start(bf16[1152,128]{1,0:T(8,128)(2,1)} %copy-done.5) | copy-start | bytes 884740
  58.0 0.6 copy-start.8
  63.4 5.8 %collective-permute-start.16 = (bf16[1152,128]{1,0:T(8,128)(2,1)}, bf16[1152,128]{1,0:T(8,128)(2,1)S(1)}, u32[]{:S(2)}, u32[]{:S(2)}) collective-permute-start(bf16[1152,128]{1,0:T(8,128)(2,1)} %collective-permute-done.15.refs_3_), channel_id=1, source_target_pairs={{0,16},{16,0},{1,17},{17,1},{2,18},{18,2},{3,19},{19,3},{4,20},{20... | collective-permute-start | bytes 884744 | tf_op jit(solution)/shard_map/ppermute | solution.py:355
  72.0 8.4 %collective-permute-start.17 = (bf16[1152,384]{1,0:T(8,128)(2,1)S(1)}, bf16[1152,384]{1,0:T(8,128)(2,1)S(1)}, u32[]{:S(2)}, u32[]{:S(2)}) collective-permute-start(bf16[1152,384]{1,0:T(8,128)(2,1)S(1)} %get-tuple-element.66), channel_id=1, source_target_pairs={{0,4},{4,0},{8,12},{12,8},{1,5},{5,1},{9,13},{13,9},{2,6},{6,2},{1... | collective-permute-start | bytes 2654216 | tf_op jit(solution)/shard_map/ppermute | solution.py:357

commit v11 on v8

--- a/solution.py
+++ b/solution.py
@@ -31,7 +31,7 @@
 
 
 def attention_kernel(first, last, info_ref, q_ref, own_ref, side_a_ref, side_b_ref, *refs):
-    *earlier, out_ref = refs
+    *earlier, out_ref, turned_ref = refs
     tiles_time = info_ref.shape[0] - 2
     tile = q_ref.shape[0] // tiles_time
     width_oks = (None, info_ref[tiles_time] == 1, info_ref[tiles_time + 1] == 1)
@@ -43,13 +43,14 @@
         return pl.ds(pl.multiple_of(base * tile, tile), 2 * tile), inside
 
     refs = (own_ref, side_a_ref, side_b_ref)
+    for side, ref in enumerate(refs):
+        turned_ref[side] = ref[0].T
 
     def score(t, side):
         rows, inside = window(t)
-        scores = lax.dot_general(
+        scores = jnp.dot(
             q_ref[t * tile : (t + 1) * tile, :],
-            refs[side][0, rows, :],
-            (((1,), (1,)), ((), ())),
+            turned_ref[side, :, rows],
             preferred_element_type=jnp.float32,
         )
         blocks, largest = [], None
@@ -103,6 +104,7 @@
         out_shape=jax.ShapeDtypeStruct(operands[0].shape, jnp.bfloat16),
         in_specs=[SCALARS] + [IN_VMEM] * len(operands),
         out_specs=IN_VMEM,
+        scratch_shapes=[pltpu.VMEM((3,) + operands[0].shape[::-1], jnp.bfloat16)],
         compiler_params=pltpu.CompilerParams(vmem_limit_bytes=VMEM_LIMIT),
         cost_estimate=SMALL_COST,
         name="attention",
@@ -116,6 +118,15 @@
     frames = tile // FRAME
     cond_first = info_ref[0] == 0
     places = [pl.ds(pl.multiple_of(info_ref[i] * own_cols, own_cols), own_cols) for i in (1, 2)]
+    gates = []
+    for which in range(2):
+        branch = info_ref[0] if which == 0 else 1 - info_ref[0]
+        cols = []
+        for place in (info_ref[3], info_ref[3] ^ 1):
+            here = pl.ds(pl.multiple_of(place * own_cols, own_cols), own_cols)
+            both = gate_ref[branch, :, here].astype(jnp.float32)
+            cols.append(jnp.where(cond_first, both[0:1], both[1:2]))
+        gates.append(jnp.concatenate(cols, axis=1))
     chosen = [[i for i, kind in enumerate(kinds) if kind[0] == which] for which in range(2)]
     weights = []
     for names in chosen:
@@ -130,11 +141,11 @@
         for which in range(2):
             attended = jnp.concatenate([pieces[i][token_rows, :] for i in chosen[which]], axis=1)
             projected = jnp.dot(attended, weights[which], preferred_element_type=jnp.float32)
-            parts.append(gate_ref[which] * projected)
+            parts.append(gates[which] * projected)
         for frame in range(frames):
             rows = slice(frame * FRAME, (frame + 1) * FRAME)
             out_rows = slice(time_tile * tile + rows.start, time_tile * tile + rows.stop)
-            guide = 1.0 + 0.5 * info_ref[3 + time_tile * frames + frame].astype(jnp.float32)
+            guide = 1.0 + 0.5 * info_ref[4 + time_tile * frames + frame].astype(jnp.float32)
             scales = (
                 jnp.where(cond_first, guide, 1.0 - guide),
                 jnp.where(cond_first, 1.0 - guide, guide),
@@ -302,20 +313,11 @@
         _, residual = lax.optimization_barrier(((packed[1], sides[0])[RESIDUAL_AFTER - 1], residual))
         mine, other = split_residual(residual)
     store["other"] = swap(other, 1, 0)
-    gate_block = jnp.concatenate(
-        [
-            lax.dynamic_slice(gate, (0, branch_pos, place * width), (2, 1, width))
-            for place in (head_pos, head_pos ^ 1)
-        ],
-        axis=2,
-    ).astype(jnp.float32)
-    gate_block = jnp.where(branch_pos == 0, gate_block, gate_block[::-1])
-
     offsets = lax.dynamic_index_in_dim(time_offsets, width_pos, 1, keepdims=False)
     edges = jnp.stack([(pos >= 0) & (pos < tiles_wide) for pos in near_pos]).astype(jnp.int32)
     attention_info = jnp.concatenate([offsets, edges])
     place = head_pos & 1
-    projection_info = jnp.concatenate([jnp.stack([branch_pos, place, place ^ 1]), guidance_index])
+    projection_info = jnp.concatenate([jnp.stack([branch_pos, place, place ^ 1, head_pos]), guidance_index])
 
     def relay(head):
         if RELAY[head] == "x":
@@ -357,7 +359,7 @@
             projection_info,
             (near, store["far"]),
             {name: store[name] for name in names},
-            gate_block,
+            gate,
             base,
             tile,
             base[0] is mine,

time: 79.2 us -> 76.1 us (0.961)
  starting transfers between devices: 27.2 us -> 24.5 us
    ppermute x6, waiting for transfers between devices: 2.66 us -> 7.38 us  [halo(): return [lax.ppermute(part, 'tokens', pairs) for pairs in rounds]]
    ppermute x7, waiting for transfers between devices: 8.15 us -> 3.97 us  [swap(): lax.ppermute(value, 'head', [(i, i ^ head_bits) for i in range(head_count)])]
    ppermute x7, starting transfers between devices: 12.1 us -> 9.51 us  [swap(): lax.ppermute(value, 'head', [(i, i ^ head_bits) for i in range(head_count)])]
    concatenate x0 -> x1, local copies, waits for them, and re-layouts: none -> 1.26 us  [local(): jnp.concatenate([jnp.stack([branch_pos, place, place ^ 1, head_pos]), gui...]
    unnamed x18 -> x16, local copies, waits for them, and re-layouts: 3.26 us -> 2.15 us
    dynamic_slice x1 -> x0, local copies, waits for them, and re-layouts: 0.83 us -> none  [local(): lax.dynamic_slice(gate, (0, branch_pos, place * width), (2, 1, width))]
  transfers between devices with their start and end apart: 18 -> 18, of which waited for: 6 -> 5; matrix products, arithmetic and copies ran while one was open for 2% -> 2% of each run, Pallas kernels for 33% -> 33%
where the time goes in v11:
time: 76.1 us; the launch traced here: 74.7 us
  Pallas kernels  29.3 us (39%)
  starting transfers between devices  24.5 us (32%)
  waiting for transfers between devices  15.5 us (20%)
  local copies, waits for them, and re-layouts  3.82 us (5%)
  other arithmetic  1.38 us (2%)
    pallas_call x3, Pallas kernels, attention(): pl.pallas_call(functools.partial(attention_kernel, *tiles), out_shape=jax...  14.8 us
    ppermute x6, starting transfers between devices, halo(): return [lax.ppermute(part, 'tokens', pairs) for pairs in rounds]  10.1 us
    ppermute x7, starting transfers between devices, swap(): lax.ppermute(value, 'head', [(i, i ^ head_bits) for i in range(head_count)])  9.51 us
    ppermute x6, waiting for transfers between devices, halo(): return [lax.ppermute(part, 'tokens', pairs) for pairs in rounds]  7.38 us
    pallas_call x3, Pallas kernels, copy_columns(): pl.pallas_call(functools.partial(copy_kernel, plan), out_shape=[jax.Shape...  6.83 us
    pallas_call x2, Pallas kernels, partial_projection(): pl.pallas_call(functools.partial(partial_kernel, first, tuple(pieces), ti...  6.36 us
    ppermute x5, starting transfers between devices, swap(): return lax.ppermute(value, 'branch', [(0, 1), (1, 0)])  4.91 us
    ppermute x5, waiting for transfers between devices, swap(): return lax.ppermute(value, 'branch', [(0, 1), (1, 0)])  4.2 us
  transfers between devices with their start and end apart: 18, of which 5 were waited for; matrix products, arithmetic and copies ran while one was open for 2% of the time, Pallas kernels for 33%

profile of v11, /device:TPU:9, one launch (start us, length us, event | category | flops | bytes accessed | tf_op | source)
XLA Modules:
  0.0 74.7 jit_solution(16167394139151151791)
XLA Ops:
  0.0 0.0 copy-start
  0.0 0.1 pad_add_fusion.info_ref
  0.1 1.7 %copy_columns.3.own_ref = bf16[2,1152,128]{2,1,0:T(8,128)(2,1)S(1)} custom-call(s32[2]{0:T(128)S(1)} %pad_add_fusion.info_ref, bf16[1152,384]{1,0:T(8,128)(2,1)} %bitcast.17, bf16[1152,384]{1,0:T(8,128)(2,1)} %bitcast.20), custom_call_target="tpu_custom_call" | custom-call | bytes 1024 | tf_op jit(solution)/shard_map/copy_columns/pallas_call | solution.py:204
  1.8 0.1 collective-permute-start
  1.9 4.5 %collective-permute-start.1 = (bf16[2,1152,128]{2,1,0:T(8,128)(2,1)S(1)}, bf16[2,1152,128]{2,1,0:T(8,128)(2,1)}, u32[]{:S(2)}, u32[]{:S(2)}) collective-permute-start(bf16[2,1152,128]{2,1,0:T(8,128)(2,1)S(1)} %copy_columns.3.own_ref), channel_id=1, source_target_pairs={{1,2},{2,1},{5,6},{6,5},{9,10},{10,9},{13,14},{14,13},{17,18},{18,... | collective-permute-start | bytes 1769480 | tf_op jit(solution)/shard_map/ppermute | solution.py:305
  6.4 0.0 copy-done.7
  6.4 0.2 copy.11
  6.6 1.3 %split_halves.1 = (bf16[1152,384]{1,0:T(8,128)(2,1)S(1)}, bf16[1152,384]{1,0:T(8,128)(2,1)}) custom-call(s32[1]{0:T(128)} %bitcast.info_ref, bf16[2,1152,384]{2,1,0:T(8,128)(2,1)S(1)} %bitcast.16), custom_call_target="tpu_custom_call" | custom-call | bytes 1024 | tf_op jit(solution)/shard_map/split_halves/pallas_call | solution.py:228
  7.9 1.3 %collective-permute-start.3 = (bf16[1152,384]{1,0:T(8,128)(2,1)}, bf16[1152,384]{1,0:T(8,128)(2,1)}, u32[]{:S(2)}, u32[]{:S(2)}) collective-permute-start(bf16[1152,384]{1,0:T(8,128)(2,1)} %get-tuple-element.47), channel_id=1, source_target_pairs={{0,16},{16,0},{1,17},{17,1},{2,18},{18,2},{3,19},{19,3},{4,20},{20... | collective-permute-start | bytes 2654216 | tf_op jit(solution)/shard_map/ppermute | solution.py:262
  9.2 2.8 %copy_columns.5 = (bf16[2,1152,128]{2,1,0:T(8,128)(2,1)S(1)}, bf16[384,768]{1,0:T(8,128)(2,1)}) custom-call(s32[2]{0:T(128)S(1)} %pad_add_fusion.info_ref, bf16[1152,384]{1,0:T(8,128)(2,1)} %bitcast.18, bf16[1152,384]{1,0:T(8,128)(2,1)} %bitcast.21, bf16[384,3072]{1,0:T(8,128)(2,1)} %refs_2_), custom_call_target="tpu_custom_call" | custom-call | bytes 1024 | tf_op jit(solution)/shard_map/copy_columns/pallas_call | solution.py:204
  12.0 1.3 %collective-permute-start.2 = (bf16[384,768]{1,0:T(8,128)(2,1)}, bf16[384,768]{1,0:T(8,128)(2,1)S(1)}, u32[]{:S(2)}, u32[]{:S(2)}) collective-permute-start(bf16[384,768]{1,0:T(8,128)(2,1)} %get-tuple-element.51), channel_id=1, source_target_pairs={{0,8},{4,12},{8,0},{12,4},{1,9},{5,13},{9,1},{13,5},{2,10},{6,14},... | collective-permute-start | bytes 1769480 | tf_op jit(solution)/shard_map/ppermute | solution.py:264
  13.3 0.0 collective-permute-start.6
  13.3 0.0 copy-done
  13.3 0.2 dynamic-slice_reduce_fusion
  13.5 0.1 add_convert_fusion.1
  13.6 0.1 pad_add_fusion.1.info_ref
  13.7 2.5 %collective-permute-done.side_a_ref = bf16[2,1152,128]{2,1,0:T(8,128)(2,1)S(1)} collective-permute-done((bf16[2,1152,128]{2,1,0:T(8,128)(2,1)S(1)}, bf16[2,1152,128]{2,1,0:T(8,128)(2,1)S(1)}, u32[]{:S(2)}, u32[]{:S(2)}) %collective-permute-start) | collective-permute-done | bytes 589856 | tf_op jit(solution)/shard_map/ppermute | solution.py:305
  16.2 0.8 %copy-done.1 = bf16[2,1152,128]{2,1,0:T(8,128)(2,1)} copy-done((bf16[2,1152,128]{2,1,0:T(8,128)(2,1)}, bf16[2,1152,128]{2,1,0:T(8,128)(2,1)S(1)}, u32[]{:S(2)}) %copy-start.1) | copy-done | bytes 589848
  17.0 3.2 %collective-permute-start.7 = (bf16[2,1152,128]{2,1,0:T(8,128)(2,1)S(1)}, bf16[2,1152,128]{2,1,0:T(8,128)(2,1)S(1)}, u32[]{:S(2)}, u32[]{:S(2)}) collective-permute-start(bf16[2,1152,128]{2,1,0:T(8,128)(2,1)S(1)} %get-tuple-element.59.own_ref), channel_id=1, source_target_pairs={{1,2},{2,1},{5,6},{6,5},{9,10},{10,9},{13,14},{14,13},{17,18},{18,... | collective-permute-start | bytes 1769480 | tf_op jit(solution)/shard_map/ppermute | solution.py:305
  20.2 0.0 copy-start.2
  20.2 0.0 collective-permute-done.1.side_b_ref
  20.2 2.3 %copy_columns.4 = (bf16[384,768]{1,0:T(8,128)(2,1)S(1)}, bf16[1152,128]{1,0:T(8,128)(2,1)S(1)}, bf16[1152,128]{1,0:T(8,128)(2,1)S(1)}, bf16[1152,128]{1,0:T(8,128)(2,1)S(1)}, bf16[2,1152,128]{2,1,0:T(8,128)(2,1)S(1)}) custom-call(s32[2]{0:T(128)S(1)} %pad_add_fusion.info_ref, bf16[1152,384]{1,0:T(8,128)(2,1)} %bitcast.23, bf16[1152,384]{1,0:T(8,128)(2,1)} %bitcast.19, ...), custom_call_target="tpu_custom_call" | custom-call | bytes 1024 | tf_op jit(solution)/shard_map/copy_columns/pallas_call | solution.py:204
  22.5 0.0 copy-done.2
  22.5 5.1 %attention.3.refs_2_ = bf16[1152,128]{1,0:T(8,128)(2,1)S(1)} custom-call(s32[5]{0:T(128)S(1)} %pad_add_fusion.1.info_ref, bf16[1152,128]{1,0:T(8,128)(2,1)S(1)} %get-tuple-element.54.q_ref, bf16[2,1152,128]{2,1,0:T(8,128)(2,1)S(1)} %copy_columns.3.own_ref, bf16[2,1152,128]{2,1,0:T(8,128)(2,1)S(1)} %copy-done.2, ...), custom_call_target="tpu_custom_call" | custom-call | bytes 1024 | tf_op jit(solution)/shard_map/attention/pallas_call | solution.py:102
  27.6 0.1 collective-permute-start.10
  27.7 0.0 collective-permute-done.2.refs_1_
  27.7 2.2 %collective-permute-start.11 = (bf16[2,1152,128]{2,1,0:T(8,128)(2,1)S(1)}, bf16[2,1152,128]{2,1,0:T(8,128)(2,1)S(1)}, u32[]{:S(2)}, u32[]{:S(2)}) collective-permute-start(bf16[2,1152,128]{2,1,0:T(8,128)(2,1)S(1)} %get-tuple-element.61.own_ref), channel_id=1, source_target_pairs={{1,2},{2,1},{5,6},{6,5},{9,10},{10,9},{13,14},{14,13},{17,18},{18,... | collective-permute-start | bytes 1769480 | tf_op jit(solution)/shard_map/ppermute | solution.py:305
  30.0 0.0 collective-permute-done.6.side_a_ref
  30.0 1.3 %collective-permute-start.4 = (bf16[1152,128]{1,0:T(8,128)(2,1)S(1)}, bf16[1152,128]{1,0:T(8,128)(2,1)}, u32[]{:S(2)}, u32[]{:S(2)}) collective-permute-start(bf16[1152,128]{1,0:T(8,128)(2,1)S(1)} %attention.3.refs_2_), channel_id=1, source_target_pairs={{0,16},{16,0},{1,17},{17,1},{2,18},{18,2},{3,19},{19,3},{4,20},{20... | collective-permute-start | bytes 884744 | tf_op jit(solution)/shard_map/ppermute | solution.py:262
  31.3 0.0 collective-permute-done.3.refs_11_
  31.3 1.2 %collective-permute-start.5 = (bf16[1152,128]{1,0:T(8,128)(2,1)S(1)}, bf16[1152,128]{1,0:T(8,128)(2,1)S(1)}, u32[]{:S(2)}, u32[]{:S(2)}) collective-permute-start(bf16[1152,128]{1,0:T(8,128)(2,1)S(1)} %attention.3.refs_2_), channel_id=1, source_target_pairs={{0,8},{4,12},{8,0},{12,4},{1,9},{5,13},{9,1},{13,5},{2,10},{6,14},... | collective-permute-start | bytes 884744 | tf_op jit(solution)/shard_map/ppermute | solution.py:264
  32.5 0.0 collective-permute-done.7.side_b_ref
  32.5 5.1 %attention.4.refs_6_ = bf16[1152,128]{1,0:T(8,128)(2,1)S(1)} custom-call(s32[5]{0:T(128)S(1)} %pad_add_fusion.1.info_ref, bf16[1152,128]{1,0:T(8,128)(2,1)S(1)} %get-tuple-element.58.q_ref, bf16[2,1152,128]{2,1,0:T(8,128)(2,1)S(1)} %get-tuple-element.59.own_ref, bf16[2,1152,128]{2,1,0:T(8,128)(2,1)} %collective-permute-done.6.side_a_ref, ...), custom_call_target="tpu_custom_call" | custom-call | bytes 1024 | tf_op jit(solution)/shard_map/attention/pallas_call | solution.py:102
  37.7 0.0 copy-start.5
  37.7 0.3 collective-permute-start.8
  38.0 0.0 collective-permute-done.4.refs_3_
  38.0 0.8 %collective-permute-start.13 = (bf16[1152,128]{1,0:T(8,128)(2,1)S(1)}, bf16[1152,128]{1,0:T(8,128)(2,1)}, u32[]{:S(2)}, u32[]{:S(2)}) collective-permute-start(bf16[1152,128]{1,0:T(8,128)(2,1)S(1)} %attention.4.refs_6_), channel_id=1, source_target_pairs={{0,16},{16,0},{1,17},{17,1},{2,18},{18,2},{3,19},{19,3},{4,20},{20... | collective-permute-start | bytes 884744 | tf_op jit(solution)/shard_map/ppermute | solution.py:262
  38.8 0.0 collective-permute-done.5.refs_4_
  38.8 0.7 copy-done.3
  39.5 0.7 collective-permute-start.12
  40.2 0.0 collective-permute-done.10.side_a_ref
  40.2 4.8 %collective-permute-done.11.side_b_ref = bf16[2,1152,128]{2,1,0:T(8,128)(2,1)S(1)} collective-permute-done((bf16[2,1152,128]{2,1,0:T(8,128)(2,1)S(1)}, bf16[2,1152,128]{2,1,0:T(8,128)(2,1)S(1)}, u32[]{:S(2)}, u32[]{:S(2)}) %collective-permute-start.11) | collective-permute-done | bytes 589856 | tf_op jit(solution)/shard_map/ppermute | solution.py:305
  45.0 4.6 %attention.5.refs_3_ = bf16[1152,128]{1,0:T(8,128)(2,1)S(1)} custom-call(s32[5]{0:T(128)S(1)} %pad_add_fusion.1.info_ref, bf16[1152,128]{1,0:T(8,128)(2,1)S(1)} %get-tuple-element.60.q_ref, bf16[2,1152,128]{2,1,0:T(8,128)(2,1)S(1)} %get-tuple-element.61.own_ref, bf16[2,1152,128]{2,1,0:T(8,128)(2,1)S(1)} %collective-permute-done.10.side_a_ref, ...), custom_call_target="tpu_custom_call" | custom-call | bytes 1024 | tf_op jit(solution)/shard_map/attention/pallas_call | solution.py:102
  49.6 1.3 %collective-permute-start.14 = (bf16[1152,128]{1,0:T(8,128)(2,1)S(1)}, bf16[1152,128]{1,0:T(8,128)(2,1)}, u32[]{:S(2)}, u32[]{:S(2)}) collective-permute-start(bf16[1152,128]{1,0:T(8,128)(2,1)S(1)} %attention.5.refs_3_), channel_id=1, source_target_pairs={{0,16},{16,0},{1,17},{17,1},{2,18},{18,2},{3,19},{19,3},{4,20},{20... | collective-permute-start | bytes 884744 | tf_op jit(solution)/shard_map/ppermute | solution.py:262
  50.9 1.3 %concatenate.6.info_ref = s32[22]{0:T(128)} concatenate(s32[1]{0:T(128)} %bitcast.info_ref, s32[1]{0:T(128)} %bitcast.1, s32[1]{0:T(128)} %bitcast.2, s32[1]{0:T(128)} %bitcast.3, s32[18]{0:T(128)} %param.15), dimensions={0} | concatenate | bytes 176 | tf_op jit(solution)/shard_map/concatenate | solution.py:320
  52.2 1.2 %collective-permute-start.15 = (bf16[1152,128]{1,0:T(8,128)(2,1)S(1)}, bf16[1152,128]{1,0:T(8,128)(2,1)S(1)}, u32[]{:S(2)}, u32[]{:S(2)}) collective-permute-start(bf16[1152,128]{1,0:T(8,128)(2,1)S(1)} %attention.5.refs_3_), channel_id=1, source_target_pairs={{0,8},{4,12},{8,0},{12,4},{1,9},{5,13},{9,1},{13,5},{2,10},{6,14},... | collective-permute-start | bytes 884744 | tf_op jit(solution)/shard_map/ppermute | solution.py:264
  53.4 0.0 collective-permute-done.8.refs_8_
  53.4 0.3 collective-permute-start.9
  53.7 0.0 collective-permute-done.12.refs_5_
  53.7 0.0 collective-permute-done.13.refs_7_
  53.7 0.0 copy-done.5
  53.7 0.0 copy-done.4
  53.7 0.0 copy-start.6
  53.7 0.6 copy-done.6
  54.3 3.6 %partial_projection.2 = (f32[1152,384]{1,0:T(8,128)S(1)}, f32[1152,384]{1,0:T(8,128)S(1)}) custom-call(s32[22]{0:T(128)S(1)} %copy-done.6, bf16[384,768]{1,0:T(8,128)(2,1)S(1)} %get-tuple-element.43.refs_0_, bf16[384,768]{1,0:T(8,128)(2,1)S(1)} %collective-permute-done.2.refs_1_, bf16[1152,128]{1,0:T(8,128)(2,1)S(1)} %attention.3.refs_2_, ...), custom_call_target="tpu_custom_call" | custom-call | bytes 1024 | tf_op jit(solution)/shard_map/partial_projection/pallas_call | solution.py:167
  57.9 0.0 collective-permute-done.14.refs_4_
  58.0 0.3 collective-permute-start.16
  58.2 4.2 %collective-permute-done.9.refs_2_ = bf16[1152,128]{1,0:T(8,128)(2,1)S(1)} collective-permute-done((bf16[1152,128]{1,0:T(8,128)(2,1)S(1)}, bf16[1152,128]{1,0:T(8,128)(2,1)S(1)}, u32[]{:S(2)}, u32[]{:S(2)}) %collective-permute-start.9) | collective-permute-done | bytes 294944 | tf_op jit(solution)/shard_map/ppermute | solution.py:262
  62.4 0.0 collective-permute-done.15.refs_5_
  62.4 1.9 %collective-permute-done.16.refs_6_ = bf16[1152,128]{1,0:T(8,128)(2,1)S(1)} collective-permute-done((bf16[1152,128]{1,0:T(8,128)(2,1)}, bf16[1152,128]{1,0:T(8,128)(2,1)S(1)}, u32[]{:S(2)}, u32[]{:S(2)}) %collective-permute-start.16) | collective-permute-done | bytes 294944 | tf_op jit(solution)/shard_map/ppermute | solution.py:264
  64.3 2.7 %partial_projection.3 = (f32[1152,384]{1,0:T(8,128)S(1)}, bf16[1152,384]{1,0:T(8,128)(2,1)S(1)}) custom-call(s32[22]{0:T(128)S(1)} %copy-done.6, bf16[384,768]{1,0:T(8,128)(2,1)S(1)} %get-tuple-element.43.refs_0_, bf16[384,768]{1,0:T(8,128)(2,1)S(1)} %collective-permute-done.2.refs_1_, bf16[1152,128]{1,0:T(8,128)(2,1)S(1)} %collective-permute-done.9.refs_2_, ...), custom_call_target="tpu_custom_call" | custom-call | bytes 1024 | tf_op jit(solution)/shard_map/partial_projection/pallas_call | solution.py:167
  67.1 4.5 %collective-permute-start.17 = (bf16[1152,384]{1,0:T(8,128)(2,1)S(1)}, bf16[1152,384]{1,0:T(8,128)(2,1)S(1)}, u32[]{:S(2)}, u32[]{:S(2)}) collective-permute-start(bf16[1152,384]{1,0:T(8,128)(2,1)S(1)} %get-tuple-element.72), channel_id=1, source_target_pairs={{0,4},{4,0},{8,12},{12,8},{1,5},{5,1},{9,13},{13,9},{2,6},{6,2},{1... | collective-permute-start | bytes 2654216 | tf_op jit(solution)/shard_map/ppermute | solution.py:264
  71.5 2.1 %collective-permute-done.17 = bf16[1152,384]{1,0:T(8,128)(2,1)S(1)} collective-permute-done((bf16[1152,384]{1,0:T(8,128)(2,1)S(1)}, bf16[1152,384]{1,0:T(8,128)(2,1)S(1)}, u32[]{:S(2)}, u32[]{:S(2)}) %collective-permute-start.17) | collective-permute-done | bytes 884768 | tf_op jit(solution)/shard_map/ppermute | solution.py:264
  73.6 1.2 %add_convert_fusion = bf16[1152,384]{1,0:T(8,128)(2,1)} fusion(f32[1152,384]{1,0:T(8,128)S(1)} %get-tuple-element.71, bf16[1152,384]{1,0:T(8,128)(2,1)S(1)} %collective-permute-done.17), kind=kLoop, calls=%fused_computation.1 | loop fusion | flops 1327104 | bytes 3538944 | tf_op jit(solution)/shard_map/convert_element_type | solution.py:374
  (4 shorter events, 0.0 us)
Async XLA Ops:
  0.0 13.3 %copy-start = (s32[3,4]{1,0:T(4,128)S(1)}, s32[3,4]{1,0:T(4,128)}, u32[]{:S(2)}) copy-start(s32[3,4]{1,0:T(4,128)} %param.14) | copy-start | bytes 148
  0.0 6.4 %copy-start.7 = (bf16[1,1152,2,384]{3,2,1,0:T(2,128)(2,1)S(1)}, bf16[1,1152,2,384]{3,2,1,0:T(2,128)(2,1)}, u32[]{:S(2)}) copy-start(bf16[1,1152,2,384]{3,2,1,0:T(2,128)(2,1)} %param.11) | copy-start | bytes 5308420
  1.8 14.4 %collective-permute-start = (bf16[2,1152,128]{2,1,0:T(8,128)(2,1)S(1)}, bf16[2,1152,128]{2,1,0:T(8,128)(2,1)S(1)}, u32[]{:S(2)}, u32[]{:S(2)}) collective-permute-start(bf16[2,1152,128]{2,1,0:T(8,128)(2,1)S(1)} %copy_columns.3.own_ref), channel_id=1, source_target_pairs={{0,1},{1,0},{2,3},{3,2},{4,5},{5,4},{6,7},{7,6},{8,9},{9,8},{10,11... | collective-permute-start | bytes 1769480 | tf_op jit(solution)/shard_map/ppermute | solution.py:305
  1.9 18.3 %collective-permute-start.1 = (bf16[2,1152,128]{2,1,0:T(8,128)(2,1)S(1)}, bf16[2,1152,128]{2,1,0:T(8,128)(2,1)}, u32[]{:S(2)}, u32[]{:S(2)}) collective-permute-start(bf16[2,1152,128]{2,1,0:T(8,128)(2,1)S(1)} %copy_columns.3.own_ref), channel_id=1, source_target_pairs={{1,2},{2,1},{5,6},{6,5},{9,10},{10,9},{13,14},{14,13},{17,18},{18,... | collective-permute-start | bytes 1769480 | tf_op jit(solution)/shard_map/ppermute | solution.py:305
  7.9 23.3 %collective-permute-start.3 = (bf16[1152,384]{1,0:T(8,128)(2,1)}, bf16[1152,384]{1,0:T(8,128)(2,1)}, u32[]{:S(2)}, u32[]{:S(2)}) collective-permute-start(bf16[1152,384]{1,0:T(8,128)(2,1)} %get-tuple-element.47), channel_id=1, source_target_pairs={{0,16},{16,0},{1,17},{17,1},{2,18},{18,2},{3,19},{19,3},{4,20},{20... | collective-permute-start | bytes 2654216 | tf_op jit(solution)/shard_map/ppermute | solution.py:262
  12.0 15.7 %collective-permute-start.2 = (bf16[384,768]{1,0:T(8,128)(2,1)}, bf16[384,768]{1,0:T(8,128)(2,1)S(1)}, u32[]{:S(2)}, u32[]{:S(2)}) collective-permute-start(bf16[384,768]{1,0:T(8,128)(2,1)} %get-tuple-element.51), channel_id=1, source_target_pairs={{0,8},{4,12},{8,0},{12,4},{1,9},{5,13},{9,1},{13,5},{2,10},{6,14},... | collective-permute-start | bytes 1769480 | tf_op jit(solution)/shard_map/ppermute | solution.py:264
  13.3 16.7 %collective-permute-start.6 = (bf16[2,1152,128]{2,1,0:T(8,128)(2,1)S(1)}, bf16[2,1152,128]{2,1,0:T(8,128)(2,1)}, u32[]{:S(2)}, u32[]{:S(2)}) collective-permute-start(bf16[2,1152,128]{2,1,0:T(8,128)(2,1)S(1)} %get-tuple-element.59.own_ref), channel_id=1, source_target_pairs={{0,1},{1,0},{2,3},{3,2},{4,5},{5,4},{6,7},{7,6},{8,9},{9,8},{10,11... | collective-permute-start | bytes 1769480 | tf_op jit(solution)/shard_map/ppermute | solution.py:305
  16.2 0.8 %copy-start.1 = (bf16[2,1152,128]{2,1,0:T(8,128)(2,1)}, bf16[2,1152,128]{2,1,0:T(8,128)(2,1)S(1)}, u32[]{:S(2)}) copy-start(bf16[2,1152,128]{2,1,0:T(8,128)(2,1)S(1)} %collective-permute-done.side_a_ref) | copy-start | bytes 1769476
  17.0 15.5 %collective-permute-start.7 = (bf16[2,1152,128]{2,1,0:T(8,128)(2,1)S(1)}, bf16[2,1152,128]{2,1,0:T(8,128)(2,1)S(1)}, u32[]{:S(2)}, u32[]{:S(2)}) collective-permute-start(bf16[2,1152,128]{2,1,0:T(8,128)(2,1)S(1)} %get-tuple-element.59.own_ref), channel_id=1, source_target_pairs={{1,2},{2,1},{5,6},{6,5},{9,10},{10,9},{13,14},{14,13},{17,18},{18,... | collective-permute-start | bytes 1769480 | tf_op jit(solution)/shard_map/ppermute | solution.py:305
  20.2 2.3 %copy-start.2 = (bf16[2,1152,128]{2,1,0:T(8,128)(2,1)S(1)}, bf16[2,1152,128]{2,1,0:T(8,128)(2,1)}, u32[]{:S(2)}) copy-start(bf16[2,1152,128]{2,1,0:T(8,128)(2,1)} %copy-done.1) | copy-start | bytes 1769476
  27.6 12.5 %collective-permute-start.10 = (bf16[2,1152,128]{2,1,0:T(8,128)(2,1)S(1)}, bf16[2,1152,128]{2,1,0:T(8,128)(2,1)S(1)}, u32[]{:S(2)}, u32[]{:S(2)}) collective-permute-start(bf16[2,1152,128]{2,1,0:T(8,128)(2,1)S(1)} %get-tuple-element.61.own_ref), channel_id=1, source_target_pairs={{0,1},{1,0},{2,3},{3,2},{4,5},{5,4},{6,7},{7,6},{8,9},{9,8},{10,11... | collective-permute-start | bytes 1769480 | tf_op jit(solution)/shard_map/ppermute | solution.py:305
  27.7 17.3 %collective-permute-start.11 = (bf16[2,1152,128]{2,1,0:T(8,128)(2,1)S(1)}, bf16[2,1152,128]{2,1,0:T(8,128)(2,1)S(1)}, u32[]{:S(2)}, u32[]{:S(2)}) collective-permute-start(bf16[2,1152,128]{2,1,0:T(8,128)(2,1)S(1)} %get-tuple-element.61.own_ref), channel_id=1, source_target_pairs={{1,2},{2,1},{5,6},{6,5},{9,10},{10,9},{13,14},{14,13},{17,18},{18,... | collective-permute-start | bytes 1769480 | tf_op jit(solution)/shard_map/ppermute | solution.py:305
  30.0 8.0 %collective-permute-start.4 = (bf16[1152,128]{1,0:T(8,128)(2,1)S(1)}, bf16[1152,128]{1,0:T(8,128)(2,1)}, u32[]{:S(2)}, u32[]{:S(2)}) collective-permute-start(bf16[1152,128]{1,0:T(8,128)(2,1)S(1)} %attention.3.refs_2_), channel_id=1, source_target_pairs={{0,16},{16,0},{1,17},{17,1},{2,18},{18,2},{3,19},{19,3},{4,20},{20... | collective-permute-start | bytes 884744 | tf_op jit(solution)/shard_map/ppermute | solution.py:262
  31.3 7.5 %collective-permute-start.5 = (bf16[1152,128]{1,0:T(8,128)(2,1)S(1)}, bf16[1152,128]{1,0:T(8,128)(2,1)S(1)}, u32[]{:S(2)}, u32[]{:S(2)}) collective-permute-start(bf16[1152,128]{1,0:T(8,128)(2,1)S(1)} %attention.3.refs_2_), channel_id=1, source_target_pairs={{0,8},{4,12},{8,0},{12,4},{1,9},{5,13},{9,1},{13,5},{2,10},{6,14},... | collective-permute-start | bytes 884744 | tf_op jit(solution)/shard_map/ppermute | solution.py:264
  37.7 16.0 %copy-start.5 = (bf16[2,2,1536]{2,1,0:T(2,128)(2,1)S(1)}, bf16[2,2,1536]{2,1,0:T(2,128)(2,1)}, u32[]{:S(2)}) copy-start(bf16[2,2,1536]{2,1,0:T(2,128)(2,1)} %refs_7_.1) | copy-start | bytes 36868
  37.7 15.7 %collective-permute-start.8 = (bf16[1152,128]{1,0:T(8,128)(2,1)S(1)}, bf16[1152,128]{1,0:T(8,128)(2,1)S(1)}, u32[]{:S(2)}, u32[]{:S(2)}) collective-permute-start(bf16[1152,128]{1,0:T(8,128)(2,1)S(1)} %attention.4.refs_6_), channel_id=1, source_target_pairs={{0,8},{4,12},{8,0},{12,4},{1,9},{5,13},{9,1},{13,5},{2,10},{6,14},... | collective-permute-start | bytes 884744 | tf_op jit(solution)/shard_map/ppermute | solution.py:264
  38.0 15.7 %collective-permute-start.13 = (bf16[1152,128]{1,0:T(8,128)(2,1)S(1)}, bf16[1152,128]{1,0:T(8,128)(2,1)}, u32[]{:S(2)}, u32[]{:S(2)}) collective-permute-start(bf16[1152,128]{1,0:T(8,128)(2,1)S(1)} %attention.4.refs_6_), channel_id=1, source_target_pairs={{0,16},{16,0},{1,17},{17,1},{2,18},{18,2},{3,19},{19,3},{4,20},{20... | collective-permute-start | bytes 884744 | tf_op jit(solution)/shard_map/ppermute | solution.py:262
  38.8 0.7 copy-start.3
  39.5 14.2 %collective-permute-start.12 = (bf16[1152,128]{1,0:T(8,128)(2,1)}, bf16[1152,128]{1,0:T(8,128)(2,1)}, u32[]{:S(2)}, u32[]{:S(2)}) collective-permute-start(bf16[1152,128]{1,0:T(8,128)(2,1)} %collective-permute-done.4.refs_3_), channel_id=1, source_target_pairs={{0,8},{4,12},{8,0},{12,4},{1,9},{5,13},{9,1},{13,5},{2,10},{6,14},... | collective-permute-start | bytes 884744 | tf_op jit(solution)/shard_map/ppermute | solution.py:264
  40.2 13.5 %copy-start.4 = (bf16[1152,128]{1,0:T(8,128)(2,1)S(1)}, bf16[1152,128]{1,0:T(8,128)(2,1)}, u32[]{:S(2)}) copy-start(bf16[1152,128]{1,0:T(8,128)(2,1)} %copy-done.3) | copy-start | bytes 884740
  49.6 8.3 %collective-permute-start.14 = (bf16[1152,128]{1,0:T(8,128)(2,1)S(1)}, bf16[1152,128]{1,0:T(8,128)(2,1)}, u32[]{:S(2)}, u32[]{:S(2)}) collective-permute-start(bf16[1152,128]{1,0:T(8,128)(2,1)S(1)} %attention.5.refs_3_), channel_id=1, source_target_pairs={{0,16},{16,0},{1,17},{17,1},{2,18},{18,2},{3,19},{19,3},{4,20},{20... | collective-permute-start | bytes 884744 | tf_op jit(solution)/shard_map/ppermute | solution.py:262
  52.2 10.3 %collective-permute-start.15 = (bf16[1152,128]{1,0:T(8,128)(2,1)S(1)}, bf16[1152,128]{1,0:T(8,128)(2,1)S(1)}, u32[]{:S(2)}, u32[]{:S(2)}) collective-permute-start(bf16[1152,128]{1,0:T(8,128)(2,1)S(1)} %attention.5.refs_3_), channel_id=1, source_target_pairs={{0,8},{4,12},{8,0},{12,4},{1,9},{5,13},{9,1},{13,5},{2,10},{6,14},... | collective-permute-start | bytes 884744 | tf_op jit(solution)/shard_map/ppermute | solution.py:264
  53.4 9.0 %collective-permute-start.9 = (bf16[1152,128]{1,0:T(8,128)(2,1)S(1)}, bf16[1152,128]{1,0:T(8,128)(2,1)S(1)}, u32[]{:S(2)}, u32[]{:S(2)}) collective-permute-start(bf16[1152,128]{1,0:T(8,128)(2,1)S(1)} %collective-permute-done.8.refs_8_), channel_id=1, source_target_pairs={{0,16},{16,0},{1,17},{17,1},{2,18},{18,2},{3,19},{19,3},{4,20},{20... | collective-permute-start | bytes 884744 | tf_op jit(solution)/shard_map/ppermute | solution.py:262
  53.7 0.6 copy-start.6
  58.0 6.4 %collective-permute-start.16 = (bf16[1152,128]{1,0:T(8,128)(2,1)}, bf16[1152,128]{1,0:T(8,128)(2,1)S(1)}, u32[]{:S(2)}, u32[]{:S(2)}) collective-permute-start(bf16[1152,128]{1,0:T(8,128)(2,1)} %collective-permute-done.14.refs_4_), channel_id=1, source_target_pairs={{0,8},{4,12},{8,0},{12,4},{1,9},{5,13},{9,1},{13,5},{2,10},{6,14},... | collective-permute-start | bytes 884744 | tf_op jit(solution)/shard_map/ppermute | solution.py:264
  67.1 6.5 %collective-permute-start.17 = (bf16[1152,384]{1,0:T(8,128)(2,1)S(1)}, bf16[1152,384]{1,0:T(8,128)(2,1)S(1)}, u32[]{:S(2)}, u32[]{:S(2)}) collective-permute-start(bf16[1152,384]{1,0:T(8,128)(2,1)S(1)} %get-tuple-element.72), channel_id=1, source_target_pairs={{0,4},{4,0},{8,12},{12,8},{1,5},{5,1},{9,13},{13,9},{2,6},{6,2},{1... | collective-permute-start | bytes 2654216 | tf_op jit(solution)/shard_map/ppermute | solution.py:264

commit v12 on v11

--- a/solution.py
+++ b/solution.py
@@ -18,7 +18,8 @@
 LATE_PACK = True
 RESIDUAL_FIRST = True
 SPLIT = 0
-TIE_PARTIAL = True
+TIE_PARTIAL = False
+BEFORE_LAST = ((1, 1, 0), (1, 0, 1), (0, 1, 1))
 BEFORE_X = {1: (), 2: ()}
 BEFORE_Y = {1: (), 2: ()}
 RESIDUAL_AFTER = 0
@@ -31,7 +32,7 @@
 
 
 def attention_kernel(first, last, info_ref, q_ref, own_ref, side_a_ref, side_b_ref, *refs):
-    *earlier, out_ref, turned_ref = refs
+    *earlier, out_ref = refs
     tiles_time = info_ref.shape[0] - 2
     tile = q_ref.shape[0] // tiles_time
     width_oks = (None, info_ref[tiles_time] == 1, info_ref[tiles_time + 1] == 1)
@@ -43,14 +44,13 @@
         return pl.ds(pl.multiple_of(base * tile, tile), 2 * tile), inside
 
     refs = (own_ref, side_a_ref, side_b_ref)
-    for side, ref in enumerate(refs):
-        turned_ref[side] = ref[0].T
 
     def score(t, side):
         rows, inside = window(t)
-        scores = jnp.dot(
+        scores = lax.dot_general(
             q_ref[t * tile : (t + 1) * tile, :],
-            turned_ref[side, :, rows],
+            refs[side][0, rows, :],
+            (((1,), (1,)), ((), ())),
             preferred_element_type=jnp.float32,
         )
         blocks, largest = [], None
@@ -104,7 +104,6 @@
         out_shape=jax.ShapeDtypeStruct(operands[0].shape, jnp.bfloat16),
         in_specs=[SCALARS] + [IN_VMEM] * len(operands),
         out_specs=IN_VMEM,
-        scratch_shapes=[pltpu.VMEM((3,) + operands[0].shape[::-1], jnp.bfloat16)],
         compiler_params=pltpu.CompilerParams(vmem_limit_bytes=VMEM_LIMIT),
         cost_estimate=SMALL_COST,
         name="attention",
@@ -319,6 +318,7 @@
     place = head_pos & 1
     projection_info = jnp.concatenate([jnp.stack([branch_pos, place, place ^ 1, head_pos]), guidance_index])
 
+    head_queries[0], projection_info = lax.optimization_barrier((head_queries[0], projection_info))
     def relay(head):
         if RELAY[head] == "x":
             store[1, 1, head] = swap(store[0, 1, head], 1, 0)
@@ -369,6 +369,9 @@
     if TIE_PARTIAL:
         name = (1, 0, heads - 1) if RELAY[-1] == "y" else (0, 1, heads - 1)
         base, store[name] = lax.optimization_barrier((base, store[name]))
+    if BEFORE_LAST:
+        name = (1, 0, heads - 1) if RELAY[-1] == "y" else (0, 1, heads - 1)
+        store[name] = await_names(BEFORE_LAST, store[name])
     relay(heads - 1)
     base = partial(late + [(1, 1, heads - 1)], base)
     return (base[0] + swap(base[1], 0, 1).astype(jnp.float32)).astype(jnp.bfloat16)

time: 76.1 us -> 73.4 us (0.965); the launches traced: 74.7 us -> 73.1 us
  local copies, waits for them, and re-layouts: 3.82 us -> 1.04 us
  starting transfers between devices: 24.5 us -> 26.8 us
  Pallas kernels: 29.3 us -> 27.5 us
    unnamed x16 -> x8, local copies, waits for them, and re-layouts: 2.15 us -> 0.02 us
    ppermute x7, starting transfers between devices: 9.51 us -> 11.6 us  [swap(): lax.ppermute(value, 'head', [(i, i ^ head_bits) for i in range(head_count)])]
    ppermute x5, waiting for transfers between devices: 4.2 us -> 5.83 us  [swap(): return lax.ppermute(value, 'branch', [(0, 1), (1, 0)])]
    pallas_call x2, Pallas kernels: 6.36 us -> 5.07 us  [partial_projection(): pl.pallas_call(functools.partial(partial_kernel, first, tuple(pieces), ti...]
    concatenate x1, local copies, waits for them, and re-layouts: 1.26 us -> 0.08 us  [local(): jnp.concatenate([jnp.stack([branch_pos, place, place ^ 1, head_pos]), gui...]
    ppermute x6, waiting for transfers between devices: 7.38 us -> 6.35 us  [halo(): return [lax.ppermute(part, 'tokens', pairs) for pairs in rounds]]
    ppermute x6, starting transfers between devices: 10.1 us -> 10.8 us  [halo(): return [lax.ppermute(part, 'tokens', pairs) for pairs in rounds]]
  transfers between devices with their start and end apart: 18 -> 18, of which waited for: 5 -> 7; matrix products, arithmetic and copies ran while one was open for 2% -> 2% of each run, Pallas kernels for 33% -> 32%
where the time goes in v12:
time: 73.4 us; the launch traced here: 73.1 us
  Pallas kernels  27.5 us (37%)
  starting transfers between devices  26.8 us (37%)
  waiting for transfers between devices  15.6 us (21%)
  other arithmetic  1.95 us (3%)
  local copies, waits for them, and re-layouts  1.04 us (1%)
    pallas_call x3, Pallas kernels, attention(): pl.pallas_call(functools.partial(attention_kernel, *tiles), out_shape=jax...  14.3 us
    ppermute x7, starting transfers between devices, swap(): lax.ppermute(value, 'head', [(i, i ^ head_bits) for i in range(head_count)])  11.6 us
    ppermute x6, starting transfers between devices, halo(): return [lax.ppermute(part, 'tokens', pairs) for pairs in rounds]  10.8 us
    pallas_call x3, Pallas kernels, copy_columns(): pl.pallas_call(functools.partial(copy_kernel, plan), out_shape=[jax.Shape...  6.81 us
    ppermute x6, waiting for transfers between devices, halo(): return [lax.ppermute(part, 'tokens', pairs) for pairs in rounds]  6.35 us
    ppermute x5, waiting for transfers between devices, swap(): return lax.ppermute(value, 'branch', [(0, 1), (1, 0)])  5.83 us
    pallas_call x2, Pallas kernels, partial_projection(): pl.pallas_call(functools.partial(partial_kernel, first, tuple(pieces), ti...  5.07 us
    ppermute x5, starting transfers between devices, swap(): return lax.ppermute(value, 'branch', [(0, 1), (1, 0)])  4.4 us
  transfers between devices with their start and end apart: 18, of which 7 were waited for; matrix products, arithmetic and copies ran while one was open for 2% of the time, Pallas kernels for 32%

profile of v12, /device:TPU:9, one launch (start us, length us, event | category | flops | bytes accessed | tf_op | source)
XLA Modules:
  0.0 73.1 jit_solution(5069631722384275760)
XLA Ops:
  0.0 0.0 copy-start
  0.0 0.0 copy-start.2
  0.0 0.1 pad_add_fusion.info_ref
  0.1 1.7 %copy_columns.3.own_ref = bf16[2,1152,128]{2,1,0:T(8,128)(2,1)S(1)} custom-call(s32[2]{0:T(128)S(1)} %pad_add_fusion.info_ref, bf16[1152,384]{1,0:T(8,128)(2,1)} %bitcast.17, bf16[1152,384]{1,0:T(8,128)(2,1)} %bitcast.20), custom_call_target="tpu_custom_call" | custom-call | bytes 1024 | tf_op jit(solution)/shard_map/copy_columns/pallas_call | solution.py:203
  1.8 0.1 collective-permute-start
  1.9 4.5 %collective-permute-start.1 = (bf16[2,1152,128]{2,1,0:T(8,128)(2,1)S(1)}, bf16[2,1152,128]{2,1,0:T(8,128)(2,1)}, u32[]{:S(2)}, u32[]{:S(2)}) collective-permute-start(bf16[2,1152,128]{2,1,0:T(8,128)(2,1)S(1)} %copy_columns.3.own_ref), channel_id=1, source_target_pairs={{1,2},{2,1},{5,6},{6,5},{9,10},{10,9},{13,14},{14,13},{17,18},{18,... | collective-permute-start | bytes 1769480 | tf_op jit(solution)/shard_map/ppermute | solution.py:304
  6.4 0.0 copy-done.2
  6.4 0.2 copy.11
  6.6 1.3 %split_halves.1 = (bf16[1152,384]{1,0:T(8,128)(2,1)S(1)}, bf16[1152,384]{1,0:T(8,128)(2,1)}) custom-call(s32[1]{0:T(128)} %bitcast.5.info_ref, bf16[2,1152,384]{2,1,0:T(8,128)(2,1)S(1)} %bitcast.16), custom_call_target="tpu_custom_call" | custom-call | bytes 1024 | tf_op jit(solution)/shard_map/split_halves/pallas_call | solution.py:227
  7.9 1.3 %collective-permute-start.3 = (bf16[1152,384]{1,0:T(8,128)(2,1)}, bf16[1152,384]{1,0:T(8,128)(2,1)S(1)}, u32[]{:S(2)}, u32[]{:S(2)}) collective-permute-start(bf16[1152,384]{1,0:T(8,128)(2,1)} %get-tuple-element.49), channel_id=1, source_target_pairs={{0,16},{16,0},{1,17},{17,1},{2,18},{18,2},{3,19},{19,3},{4,20},{20... | collective-permute-start | bytes 2654216 | tf_op jit(solution)/shard_map/ppermute | solution.py:261
  9.2 0.0 copy-start.3
  9.2 2.8 %copy_columns.5 = (bf16[2,1152,128]{2,1,0:T(8,128)(2,1)S(1)}, bf16[384,768]{1,0:T(8,128)(2,1)}) custom-call(s32[2]{0:T(128)S(1)} %pad_add_fusion.info_ref, bf16[1152,384]{1,0:T(8,128)(2,1)} %bitcast.18, bf16[1152,384]{1,0:T(8,128)(2,1)} %bitcast.21, bf16[384,3072]{1,0:T(8,128)(2,1)} %refs_2_), custom_call_target="tpu_custom_call" | custom-call | bytes 1024 | tf_op jit(solution)/shard_map/copy_columns/pallas_call | solution.py:203
  12.0 1.3 %collective-permute-start.2 = (bf16[384,768]{1,0:T(8,128)(2,1)}, bf16[384,768]{1,0:T(8,128)(2,1)S(1)}, u32[]{:S(2)}, u32[]{:S(2)}) collective-permute-start(bf16[384,768]{1,0:T(8,128)(2,1)} %get-tuple-element.53), channel_id=1, source_target_pairs={{0,8},{4,12},{8,0},{12,4},{1,9},{5,13},{9,1},{13,5},{2,10},{6,14},... | collective-permute-start | bytes 1769480 | tf_op jit(solution)/shard_map/ppermute | solution.py:263
  13.3 0.0 collective-permute-start.6
  13.3 0.0 copy-done
  13.3 0.7 dynamic-slice_reduce_fusion
  14.0 0.0 copy-done.3
  14.0 0.1 concatenate.6.info_ref
  14.1 0.1 add_convert_fusion.1
  14.2 0.7 pad_add_fusion.1.info_ref
  14.9 1.3 %collective-permute-done.side_a_ref = bf16[2,1152,128]{2,1,0:T(8,128)(2,1)} collective-permute-done((bf16[2,1152,128]{2,1,0:T(8,128)(2,1)S(1)}, bf16[2,1152,128]{2,1,0:T(8,128)(2,1)}, u32[]{:S(2)}, u32[]{:S(2)}) %collective-permute-start) | collective-permute-done | bytes 589856 | tf_op jit(solution)/shard_map/ppermute | solution.py:304
  16.2 3.2 %collective-permute-start.7 = (bf16[2,1152,128]{2,1,0:T(8,128)(2,1)S(1)}, bf16[2,1152,128]{2,1,0:T(8,128)(2,1)S(1)}, u32[]{:S(2)}, u32[]{:S(2)}) collective-permute-start(bf16[2,1152,128]{2,1,0:T(8,128)(2,1)S(1)} %get-tuple-element.61.own_ref), channel_id=1, source_target_pairs={{1,2},{2,1},{5,6},{6,5},{9,10},{10,9},{13,14},{14,13},{17,18},{18,... | collective-permute-start | bytes 1769480 | tf_op jit(solution)/shard_map/ppermute | solution.py:304
  19.4 0.0 collective-permute-done.1.side_b_ref
  19.4 2.3 %copy_columns.4 = (bf16[384,768]{1,0:T(8,128)(2,1)S(1)}, bf16[1152,128]{1,0:T(8,128)(2,1)S(1)}, bf16[1152,128]{1,0:T(8,128)(2,1)S(1)}, bf16[1152,128]{1,0:T(8,128)(2,1)S(1)}, bf16[2,1152,128]{2,1,0:T(8,128)(2,1)S(1)}) custom-call(s32[2]{0:T(128)S(1)} %pad_add_fusion.info_ref, bf16[1152,384]{1,0:T(8,128)(2,1)} %bitcast.23, bf16[1152,384]{1,0:T(8,128)(2,1)} %bitcast.19, ...), custom_call_target="tpu_custom_call" | custom-call | bytes 1024 | tf_op jit(solution)/shard_map/copy_columns/pallas_call | solution.py:203
  21.7 5.1 %attention.3.refs_2_ = bf16[1152,128]{1,0:T(8,128)(2,1)S(1)} custom-call(s32[5]{0:T(128)S(1)} %pad_add_fusion.1.info_ref, bf16[1152,128]{1,0:T(8,128)(2,1)S(1)} %get-tuple-element.56.q_ref, bf16[2,1152,128]{2,1,0:T(8,128)(2,1)S(1)} %copy_columns.3.own_ref, bf16[2,1152,128]{2,1,0:T(8,128)(2,1)} %collective-permute-done.side_a_ref, ...), custom_call_target="tpu_custom_call" | custom-call | bytes 1024 | tf_op jit(solution)/shard_map/attention/pallas_call | solution.py:102
  26.8 0.1 collective-permute-start.10
  26.9 0.0 collective-permute-done.2.refs_1_
  26.9 3.0 %collective-permute-start.11 = (bf16[2,1152,128]{2,1,0:T(8,128)(2,1)S(1)}, bf16[2,1152,128]{2,1,0:T(8,128)(2,1)S(1)}, u32[]{:S(2)}, u32[]{:S(2)}) collective-permute-start(bf16[2,1152,128]{2,1,0:T(8,128)(2,1)S(1)} %get-tuple-element.63.own_ref), channel_id=1, source_target_pairs={{1,2},{2,1},{5,6},{6,5},{9,10},{10,9},{13,14},{14,13},{17,18},{18,... | collective-permute-start | bytes 1769480 | tf_op jit(solution)/shard_map/ppermute | solution.py:304
  29.9 0.0 collective-permute-done.6.side_a_ref
  29.9 1.3 %collective-permute-start.4 = (bf16[1152,128]{1,0:T(8,128)(2,1)S(1)}, bf16[1152,128]{1,0:T(8,128)(2,1)S(1)}, u32[]{:S(2)}, u32[]{:S(2)}) collective-permute-start(bf16[1152,128]{1,0:T(8,128)(2,1)S(1)} %attention.3.refs_2_), channel_id=1, source_target_pairs={{0,16},{16,0},{1,17},{17,1},{2,18},{18,2},{3,19},{19,3},{4,20},{20... | collective-permute-start | bytes 884744 | tf_op jit(solution)/shard_map/ppermute | solution.py:261
  31.2 0.0 collective-permute-done.3.refs_11_
  31.2 1.2 %collective-permute-start.5 = (bf16[1152,128]{1,0:T(8,128)(2,1)S(1)}, bf16[1152,128]{1,0:T(8,128)(2,1)S(1)}, u32[]{:S(2)}, u32[]{:S(2)}) collective-permute-start(bf16[1152,128]{1,0:T(8,128)(2,1)S(1)} %attention.3.refs_2_), channel_id=1, source_target_pairs={{0,8},{4,12},{8,0},{12,4},{1,9},{5,13},{9,1},{13,5},{2,10},{6,14},... | collective-permute-start | bytes 884744 | tf_op jit(solution)/shard_map/ppermute | solution.py:263
  32.5 0.0 collective-permute-done.7.side_b_ref
  32.5 4.9 %attention.4.refs_6_ = bf16[1152,128]{1,0:T(8,128)(2,1)S(1)} custom-call(s32[5]{0:T(128)S(1)} %pad_add_fusion.1.info_ref, bf16[1152,128]{1,0:T(8,128)(2,1)S(1)} %get-tuple-element.60.q_ref, bf16[2,1152,128]{2,1,0:T(8,128)(2,1)S(1)} %get-tuple-element.61.own_ref, bf16[2,1152,128]{2,1,0:T(8,128)(2,1)} %collective-permute-done.6.side_a_ref, ...), custom_call_target="tpu_custom_call" | custom-call | bytes 1024 | tf_op jit(solution)/shard_map/attention/pallas_call | solution.py:102
  37.4 0.0 copy-start.1
  37.4 0.3 collective-permute-start.14
  37.7 0.0 collective-permute-done.4.refs_3_
  37.7 0.2 collective-permute-start.8
  37.9 0.0 collective-permute-done.5.refs_4_
  37.9 1.2 %collective-permute-start.13 = (bf16[1152,128]{1,0:T(8,128)(2,1)S(1)}, bf16[1152,128]{1,0:T(8,128)(2,1)S(1)}, u32[]{:S(2)}, u32[]{:S(2)}) collective-permute-start(bf16[1152,128]{1,0:T(8,128)(2,1)S(1)} %collective-permute-done.4.refs_3_), channel_id=1, source_target_pairs={{0,8},{4,12},{8,0},{12,4},{1,9},{5,13},{9,1},{13,5},{2,10},{6,14},... | collective-permute-start | bytes 884744 | tf_op jit(solution)/shard_map/ppermute | solution.py:263
  39.2 0.1 collective-permute-done.10.side_a_ref
  39.3 4.9 %collective-permute-done.11.side_b_ref = bf16[2,1152,128]{2,1,0:T(8,128)(2,1)S(1)} collective-permute-done((bf16[2,1152,128]{2,1,0:T(8,128)(2,1)S(1)}, bf16[2,1152,128]{2,1,0:T(8,128)(2,1)S(1)}, u32[]{:S(2)}, u32[]{:S(2)}) %collective-permute-start.11) | collective-permute-done | bytes 589856 | tf_op jit(solution)/shard_map/ppermute | solution.py:304
  44.2 4.4 %attention.5.refs_3_ = bf16[1152,128]{1,0:T(8,128)(2,1)S(1)} custom-call(s32[5]{0:T(128)S(1)} %pad_add_fusion.1.info_ref, bf16[1152,128]{1,0:T(8,128)(2,1)S(1)} %get-tuple-element.62.q_ref, bf16[2,1152,128]{2,1,0:T(8,128)(2,1)S(1)} %get-tuple-element.63.own_ref, bf16[2,1152,128]{2,1,0:T(8,128)(2,1)S(1)} %collective-permute-done.10.side_a_ref, ...), custom_call_target="tpu_custom_call" | custom-call | bytes 1024 | tf_op jit(solution)/shard_map/attention/pallas_call | solution.py:102
  48.5 1.3 %collective-permute-start.12 = (bf16[1152,128]{1,0:T(8,128)(2,1)S(1)}, bf16[1152,128]{1,0:T(8,128)(2,1)S(1)}, u32[]{:S(2)}, u32[]{:S(2)}) collective-permute-start(bf16[1152,128]{1,0:T(8,128)(2,1)S(1)} %attention.5.refs_3_), channel_id=1, source_target_pairs={{0,16},{16,0},{1,17},{17,1},{2,18},{18,2},{3,19},{19,3},{4,20},{20... | collective-permute-start | bytes 884744 | tf_op jit(solution)/shard_map/ppermute | solution.py:261
  49.8 1.2 %collective-permute-start.15 = (bf16[1152,128]{1,0:T(8,128)(2,1)S(1)}, bf16[1152,128]{1,0:T(8,128)(2,1)S(1)}, u32[]{:S(2)}, u32[]{:S(2)}) collective-permute-start(bf16[1152,128]{1,0:T(8,128)(2,1)S(1)} %attention.5.refs_3_), channel_id=1, source_target_pairs={{0,8},{4,12},{8,0},{12,4},{1,9},{5,13},{9,1},{13,5},{2,10},{6,14},... | collective-permute-start | bytes 884744 | tf_op jit(solution)/shard_map/ppermute | solution.py:263
  51.1 0.0 collective-permute-done.8.refs_8_
  51.1 0.3 collective-permute-start.9
  51.3 0.0 collective-permute-done.14.refs_7_
  51.3 0.0 collective-permute-done.13.refs_5_
  51.3 3.5 %collective-permute-done.12.refs_4_ = bf16[1152,128]{1,0:T(8,128)(2,1)S(1)} collective-permute-done((bf16[1152,128]{1,0:T(8,128)(2,1)S(1)}, bf16[1152,128]{1,0:T(8,128)(2,1)S(1)}, u32[]{:S(2)}, u32[]{:S(2)}) %collective-permute-start.12) | collective-permute-done | bytes 294944 | tf_op jit(solution)/shard_map/ppermute | solution.py:261
  54.9 1.2 %collective-permute-start.16 = (bf16[1152,128]{1,0:T(8,128)(2,1)S(1)}, bf16[1152,128]{1,0:T(8,128)(2,1)S(1)}, u32[]{:S(2)}, u32[]{:S(2)}) collective-permute-start(bf16[1152,128]{1,0:T(8,128)(2,1)S(1)} %collective-permute-done.12.refs_4_), channel_id=1, source_target_pairs={{0,8},{4,12},{8,0},{12,4},{1,9},{5,13},{9,1},{13,5},{2,10},{6,14},... | collective-permute-start | bytes 884744 | tf_op jit(solution)/shard_map/ppermute | solution.py:263
  56.1 0.0 copy-done.1
  56.1 2.8 %partial_projection.2 = (f32[1152,384]{1,0:T(8,128)S(1)}, f32[1152,384]{1,0:T(8,128)S(1)}) custom-call(s32[22]{0:T(128)S(1)} %concatenate.6.info_ref, bf16[384,768]{1,0:T(8,128)(2,1)S(1)} %get-tuple-element.45.refs_0_, bf16[384,768]{1,0:T(8,128)(2,1)S(1)} %collective-permute-done.2.refs_1_, bf16[1152,128]{1,0:T(8,128)(2,1)S(1)} %attention.3.refs_2_, ...), custom_call_target="tpu_custom_call" | custom-call | bytes 1024 | tf_op jit(solution)/shard_map/partial_projection/pallas_call | solution.py:166
  58.9 0.0 collective-permute-done.15.refs_5_
  58.9 2.3 %collective-permute-done.9.refs_2_ = bf16[1152,128]{1,0:T(8,128)(2,1)S(1)} collective-permute-done((bf16[1152,128]{1,0:T(8,128)(2,1)S(1)}, bf16[1152,128]{1,0:T(8,128)(2,1)S(1)}, u32[]{:S(2)}, u32[]{:S(2)}) %collective-permute-start.9) | collective-permute-done | bytes 294944 | tf_op jit(solution)/shard_map/ppermute | solution.py:261
  61.2 1.3 %collective-permute-done.16.refs_6_ = bf16[1152,128]{1,0:T(8,128)(2,1)S(1)} collective-permute-done((bf16[1152,128]{1,0:T(8,128)(2,1)S(1)}, bf16[1152,128]{1,0:T(8,128)(2,1)S(1)}, u32[]{:S(2)}, u32[]{:S(2)}) %collective-permute-start.16) | collective-permute-done | bytes 294944 | tf_op jit(solution)/shard_map/ppermute | solution.py:263
  62.5 2.3 %partial_projection.3 = (f32[1152,384]{1,0:T(8,128)S(1)}, bf16[1152,384]{1,0:T(8,128)(2,1)S(1)}) custom-call(s32[22]{0:T(128)S(1)} %concatenate.6.info_ref, bf16[384,768]{1,0:T(8,128)(2,1)S(1)} %get-tuple-element.45.refs_0_, bf16[384,768]{1,0:T(8,128)(2,1)S(1)} %collective-permute-done.2.refs_1_, bf16[1152,128]{1,0:T(8,128)(2,1)S(1)} %collective-permute-done.9.refs_2_, ...), custom_call_target="tpu_custom_call" | custom-call | bytes 1024 | tf_op jit(solution)/shard_map/partial_projection/pallas_call | solution.py:166
  64.8 5.1 %collective-permute-start.17 = (bf16[1152,384]{1,0:T(8,128)(2,1)S(1)}, bf16[1152,384]{1,0:T(8,128)(2,1)S(1)}, u32[]{:S(2)}, u32[]{:S(2)}) collective-permute-start(bf16[1152,384]{1,0:T(8,128)(2,1)S(1)} %get-tuple-element.72), channel_id=1, source_target_pairs={{0,4},{4,0},{8,12},{12,8},{1,5},{5,1},{9,13},{13,9},{2,6},{6,2},{1... | collective-permute-start | bytes 2654216 | tf_op jit(solution)/shard_map/ppermute | solution.py:263
  69.9 2.1 %collective-permute-done.17 = bf16[1152,384]{1,0:T(8,128)(2,1)S(1)} collective-permute-done((bf16[1152,384]{1,0:T(8,128)(2,1)S(1)}, bf16[1152,384]{1,0:T(8,128)(2,1)S(1)}, u32[]{:S(2)}, u32[]{:S(2)}) %collective-permute-start.17) | collective-permute-done | bytes 884768 | tf_op jit(solution)/shard_map/ppermute | solution.py:263
  72.0 1.1 %add_convert_fusion = bf16[1152,384]{1,0:T(8,128)(2,1)} fusion(f32[1152,384]{1,0:T(8,128)S(1)} %get-tuple-element.71, bf16[1152,384]{1,0:T(8,128)(2,1)S(1)} %collective-permute-done.17), kind=kLoop, calls=%fused_computation.1 | loop fusion | flops 1327104 | bytes 3538944 | tf_op jit(solution)/shard_map/convert_element_type | solution.py:377
Async XLA Ops:
  0.0 13.3 %copy-start = (s32[3,4]{1,0:T(4,128)S(1)}, s32[3,4]{1,0:T(4,128)}, u32[]{:S(2)}) copy-start(s32[3,4]{1,0:T(4,128)} %param.14) | copy-start | bytes 148
  0.0 6.4 %copy-start.2 = (bf16[1,1152,2,384]{3,2,1,0:T(2,128)(2,1)S(1)}, bf16[1,1152,2,384]{3,2,1,0:T(2,128)(2,1)}, u32[]{:S(2)}) copy-start(bf16[1,1152,2,384]{3,2,1,0:T(2,128)(2,1)} %param.11) | copy-start | bytes 5308420
  1.8 14.4 %collective-permute-start = (bf16[2,1152,128]{2,1,0:T(8,128)(2,1)S(1)}, bf16[2,1152,128]{2,1,0:T(8,128)(2,1)}, u32[]{:S(2)}, u32[]{:S(2)}) collective-permute-start(bf16[2,1152,128]{2,1,0:T(8,128)(2,1)S(1)} %copy_columns.3.own_ref), channel_id=1, source_target_pairs={{0,1},{1,0},{2,3},{3,2},{4,5},{5,4},{6,7},{7,6},{8,9},{9,8},{10,11... | collective-permute-start | bytes 1769480 | tf_op jit(solution)/shard_map/ppermute | solution.py:304
  1.9 17.5 %collective-permute-start.1 = (bf16[2,1152,128]{2,1,0:T(8,128)(2,1)S(1)}, bf16[2,1152,128]{2,1,0:T(8,128)(2,1)}, u32[]{:S(2)}, u32[]{:S(2)}) collective-permute-start(bf16[2,1152,128]{2,1,0:T(8,128)(2,1)S(1)} %copy_columns.3.own_ref), channel_id=1, source_target_pairs={{1,2},{2,1},{5,6},{6,5},{9,10},{10,9},{13,14},{14,13},{17,18},{18,... | collective-permute-start | bytes 1769480 | tf_op jit(solution)/shard_map/ppermute | solution.py:304
  7.9 23.3 %collective-permute-start.3 = (bf16[1152,384]{1,0:T(8,128)(2,1)}, bf16[1152,384]{1,0:T(8,128)(2,1)S(1)}, u32[]{:S(2)}, u32[]{:S(2)}) collective-permute-start(bf16[1152,384]{1,0:T(8,128)(2,1)} %get-tuple-element.49), channel_id=1, source_target_pairs={{0,16},{16,0},{1,17},{17,1},{2,18},{18,2},{3,19},{19,3},{4,20},{20... | collective-permute-start | bytes 2654216 | tf_op jit(solution)/shard_map/ppermute | solution.py:261
  9.2 4.8 %copy-start.3 = (s32[18]{0:T(128)S(1)}, s32[18]{0:T(128)}, u32[]{:S(2)}) copy-start(s32[18]{0:T(128)} %param.15) | copy-start | bytes 220
  12.0 14.9 %collective-permute-start.2 = (bf16[384,768]{1,0:T(8,128)(2,1)}, bf16[384,768]{1,0:T(8,128)(2,1)S(1)}, u32[]{:S(2)}, u32[]{:S(2)}) collective-permute-start(bf16[384,768]{1,0:T(8,128)(2,1)} %get-tuple-element.53), channel_id=1, source_target_pairs={{0,8},{4,12},{8,0},{12,4},{1,9},{5,13},{9,1},{13,5},{2,10},{6,14},... | collective-permute-start | bytes 1769480 | tf_op jit(solution)/shard_map/ppermute | solution.py:263
  13.3 16.6 %collective-permute-start.6 = (bf16[2,1152,128]{2,1,0:T(8,128)(2,1)S(1)}, bf16[2,1152,128]{2,1,0:T(8,128)(2,1)}, u32[]{:S(2)}, u32[]{:S(2)}) collective-permute-start(bf16[2,1152,128]{2,1,0:T(8,128)(2,1)S(1)} %get-tuple-element.61.own_ref), channel_id=1, source_target_pairs={{0,1},{1,0},{2,3},{3,2},{4,5},{5,4},{6,7},{7,6},{8,9},{9,8},{10,11... | collective-permute-start | bytes 1769480 | tf_op jit(solution)/shard_map/ppermute | solution.py:304
  16.2 16.3 %collective-permute-start.7 = (bf16[2,1152,128]{2,1,0:T(8,128)(2,1)S(1)}, bf16[2,1152,128]{2,1,0:T(8,128)(2,1)S(1)}, u32[]{:S(2)}, u32[]{:S(2)}) collective-permute-start(bf16[2,1152,128]{2,1,0:T(8,128)(2,1)S(1)} %get-tuple-element.61.own_ref), channel_id=1, source_target_pairs={{1,2},{2,1},{5,6},{6,5},{9,10},{10,9},{13,14},{14,13},{17,18},{18,... | collective-permute-start | bytes 1769480 | tf_op jit(solution)/shard_map/ppermute | solution.py:304
  26.8 12.5 %collective-permute-start.10 = (bf16[2,1152,128]{2,1,0:T(8,128)(2,1)S(1)}, bf16[2,1152,128]{2,1,0:T(8,128)(2,1)S(1)}, u32[]{:S(2)}, u32[]{:S(2)}) collective-permute-start(bf16[2,1152,128]{2,1,0:T(8,128)(2,1)S(1)} %get-tuple-element.63.own_ref), channel_id=1, source_target_pairs={{0,1},{1,0},{2,3},{3,2},{4,5},{5,4},{6,7},{7,6},{8,9},{9,8},{10,11... | collective-permute-start | bytes 1769480 | tf_op jit(solution)/shard_map/ppermute | solution.py:304
  26.9 17.3 %collective-permute-start.11 = (bf16[2,1152,128]{2,1,0:T(8,128)(2,1)S(1)}, bf16[2,1152,128]{2,1,0:T(8,128)(2,1)S(1)}, u32[]{:S(2)}, u32[]{:S(2)}) collective-permute-start(bf16[2,1152,128]{2,1,0:T(8,128)(2,1)S(1)} %get-tuple-element.63.own_ref), channel_id=1, source_target_pairs={{1,2},{2,1},{5,6},{6,5},{9,10},{10,9},{13,14},{14,13},{17,18},{18,... | collective-permute-start | bytes 1769480 | tf_op jit(solution)/shard_map/ppermute | solution.py:304
  29.9 7.8 %collective-permute-start.4 = (bf16[1152,128]{1,0:T(8,128)(2,1)S(1)}, bf16[1152,128]{1,0:T(8,128)(2,1)S(1)}, u32[]{:S(2)}, u32[]{:S(2)}) collective-permute-start(bf16[1152,128]{1,0:T(8,128)(2,1)S(1)} %attention.3.refs_2_), channel_id=1, source_target_pairs={{0,16},{16,0},{1,17},{17,1},{2,18},{18,2},{3,19},{19,3},{4,20},{20... | collective-permute-start | bytes 884744 | tf_op jit(solution)/shard_map/ppermute | solution.py:261
  31.2 6.7 %collective-permute-start.5 = (bf16[1152,128]{1,0:T(8,128)(2,1)S(1)}, bf16[1152,128]{1,0:T(8,128)(2,1)S(1)}, u32[]{:S(2)}, u32[]{:S(2)}) collective-permute-start(bf16[1152,128]{1,0:T(8,128)(2,1)S(1)} %attention.3.refs_2_), channel_id=1, source_target_pairs={{0,8},{4,12},{8,0},{12,4},{1,9},{5,13},{9,1},{13,5},{2,10},{6,14},... | collective-permute-start | bytes 884744 | tf_op jit(solution)/shard_map/ppermute | solution.py:263
  37.4 18.7 %copy-start.1 = (bf16[2,2,1536]{2,1,0:T(2,128)(2,1)S(1)}, bf16[2,2,1536]{2,1,0:T(2,128)(2,1)}, u32[]{:S(2)}) copy-start(bf16[2,2,1536]{2,1,0:T(2,128)(2,1)} %refs_7_.1) | copy-start | bytes 36868
  37.4 14.0 %collective-permute-start.14 = (bf16[1152,128]{1,0:T(8,128)(2,1)S(1)}, bf16[1152,128]{1,0:T(8,128)(2,1)S(1)}, u32[]{:S(2)}, u32[]{:S(2)}) collective-permute-start(bf16[1152,128]{1,0:T(8,128)(2,1)S(1)} %attention.4.refs_6_), channel_id=1, source_target_pairs={{0,16},{16,0},{1,17},{17,1},{2,18},{18,2},{3,19},{19,3},{4,20},{20... | collective-permute-start | bytes 884744 | tf_op jit(solution)/shard_map/ppermute | solution.py:261
  37.7 13.4 %collective-permute-start.8 = (bf16[1152,128]{1,0:T(8,128)(2,1)S(1)}, bf16[1152,128]{1,0:T(8,128)(2,1)S(1)}, u32[]{:S(2)}, u32[]{:S(2)}) collective-permute-start(bf16[1152,128]{1,0:T(8,128)(2,1)S(1)} %attention.4.refs_6_), channel_id=1, source_target_pairs={{0,8},{4,12},{8,0},{12,4},{1,9},{5,13},{9,1},{13,5},{2,10},{6,14},... | collective-permute-start | bytes 884744 | tf_op jit(solution)/shard_map/ppermute | solution.py:263
  37.9 13.4 %collective-permute-start.13 = (bf16[1152,128]{1,0:T(8,128)(2,1)S(1)}, bf16[1152,128]{1,0:T(8,128)(2,1)S(1)}, u32[]{:S(2)}, u32[]{:S(2)}) collective-permute-start(bf16[1152,128]{1,0:T(8,128)(2,1)S(1)} %collective-permute-done.4.refs_3_), channel_id=1, source_target_pairs={{0,8},{4,12},{8,0},{12,4},{1,9},{5,13},{9,1},{13,5},{2,10},{6,14},... | collective-permute-start | bytes 884744 | tf_op jit(solution)/shard_map/ppermute | solution.py:263
  48.5 6.3 %collective-permute-start.12 = (bf16[1152,128]{1,0:T(8,128)(2,1)S(1)}, bf16[1152,128]{1,0:T(8,128)(2,1)S(1)}, u32[]{:S(2)}, u32[]{:S(2)}) collective-permute-start(bf16[1152,128]{1,0:T(8,128)(2,1)S(1)} %attention.5.refs_3_), channel_id=1, source_target_pairs={{0,16},{16,0},{1,17},{17,1},{2,18},{18,2},{3,19},{19,3},{4,20},{20... | collective-permute-start | bytes 884744 | tf_op jit(solution)/shard_map/ppermute | solution.py:261
  49.8 9.1 %collective-permute-start.15 = (bf16[1152,128]{1,0:T(8,128)(2,1)S(1)}, bf16[1152,128]{1,0:T(8,128)(2,1)S(1)}, u32[]{:S(2)}, u32[]{:S(2)}) collective-permute-start(bf16[1152,128]{1,0:T(8,128)(2,1)S(1)} %attention.5.refs_3_), channel_id=1, source_target_pairs={{0,8},{4,12},{8,0},{12,4},{1,9},{5,13},{9,1},{13,5},{2,10},{6,14},... | collective-permute-start | bytes 884744 | tf_op jit(solution)/shard_map/ppermute | solution.py:263
  51.1 10.1 %collective-permute-start.9 = (bf16[1152,128]{1,0:T(8,128)(2,1)S(1)}, bf16[1152,128]{1,0:T(8,128)(2,1)S(1)}, u32[]{:S(2)}, u32[]{:S(2)}) collective-permute-start(bf16[1152,128]{1,0:T(8,128)(2,1)S(1)} %collective-permute-done.8.refs_8_), channel_id=1, source_target_pairs={{0,16},{16,0},{1,17},{17,1},{2,18},{18,2},{3,19},{19,3},{4,20},{20... | collective-permute-start | bytes 884744 | tf_op jit(solution)/shard_map/ppermute | solution.py:261
  54.9 7.7 %collective-permute-start.16 = (bf16[1152,128]{1,0:T(8,128)(2,1)S(1)}, bf16[1152,128]{1,0:T(8,128)(2,1)S(1)}, u32[]{:S(2)}, u32[]{:S(2)}) collective-permute-start(bf16[1152,128]{1,0:T(8,128)(2,1)S(1)} %collective-permute-done.12.refs_4_), channel_id=1, source_target_pairs={{0,8},{4,12},{8,0},{12,4},{1,9},{5,13},{9,1},{13,5},{2,10},{6,14},... | collective-permute-start | bytes 884744 | tf_op jit(solution)/shard_map/ppermute | solution.py:263
  64.8 7.1 %collective-permute-start.17 = (bf16[1152,384]{1,0:T(8,128)(2,1)S(1)}, bf16[1152,384]{1,0:T(8,128)(2,1)S(1)}, u32[]{:S(2)}, u32[]{:S(2)}) collective-permute-start(bf16[1152,384]{1,0:T(8,128)(2,1)S(1)} %get-tuple-element.72), channel_id=1, source_target_pairs={{0,4},{4,0},{8,12},{12,8},{1,5},{5,1},{9,13},{13,9},{2,6},{6,2},{1... | collective-permute-start | bytes 2654216 | tf_op jit(solution)/shard_map/ppermute | solution.py:263

commit v13 on v12

--- a/solution.py
+++ b/solution.py
@@ -14,7 +14,7 @@
 EXP2_SCALE = math.log2(math.e) / math.sqrt(HD)
 VMEM_LIMIT = 14 * 1024 * 1024
 COPY_LIMIT = 8 * 1024 * 1024
-COPY_PARTS = 3
+COPY_PARTS = 8
 LATE_PACK = True
 RESIDUAL_FIRST = True
 SPLIT = 0

time: 73.4 us -> 73.5 us (level)
  transfers between devices with their start and end apart: 18 -> 18, of which waited for: 7 -> 6; matrix products, arithmetic and copies ran while one was open for 2% -> 2% of each run, Pallas kernels for 32% -> 33%
where the time goes in v13:
time: 73.5 us; the launch traced here: 73.1 us
  Pallas kernels  27.9 us (38%)
  starting transfers between devices  26.8 us (36%)
  waiting for transfers between devices  15.3 us (21%)
  other arithmetic  1.95 us (3%)
  local copies, waits for them, and re-layouts  1.04 us (1%)
    pallas_call x3, Pallas kernels, attention(): pl.pallas_call(functools.partial(attention_kernel, *tiles), out_shape=jax...  14.3 us
    ppermute x7, starting transfers between devices, swap(): lax.ppermute(value, 'head', [(i, i ^ head_bits) for i in range(head_count)])  11.5 us
    ppermute x6, starting transfers between devices, halo(): return [lax.ppermute(part, 'tokens', pairs) for pairs in rounds]  10.8 us
    pallas_call x3, Pallas kernels, copy_columns(): pl.pallas_call(functools.partial(copy_kernel, plan), out_shape=[jax.Shape...  7.18 us
    ppermute x6, waiting for transfers between devices, halo(): return [lax.ppermute(part, 'tokens', pairs) for pairs in rounds]  6.08 us
    ppermute x5, waiting for transfers between devices, swap(): return lax.ppermute(value, 'branch', [(0, 1), (1, 0)])  5.73 us
    pallas_call x2, Pallas kernels, partial_projection(): pl.pallas_call(functools.partial(partial_kernel, first, tuple(pieces), ti...  5.06 us
    ppermute x5, starting transfers between devices, swap(): return lax.ppermute(value, 'branch', [(0, 1), (1, 0)])  4.41 us
  transfers between devices with their start and end apart: 18, of which 6 were waited for; matrix products, arithmetic and copies ran while one was open for 2% of the time, Pallas kernels for 33%

profile of v13, /device:TPU:9, one launch (start us, length us, event | category | flops | bytes accessed | tf_op | source)
XLA Modules:
  0.0 73.1 jit_solution(1083881742508740159)
XLA Ops:
  0.0 0.0 copy-start
  0.0 0.0 copy-start.2
  0.0 0.1 pad_add_fusion.info_ref
  0.1 1.7 %copy_columns.3.own_ref = bf16[2,1152,128]{2,1,0:T(8,128)(2,1)S(1)} custom-call(s32[2]{0:T(128)S(1)} %pad_add_fusion.info_ref, bf16[1152,384]{1,0:T(8,128)(2,1)} %bitcast.17, bf16[1152,384]{1,0:T(8,128)(2,1)} %bitcast.20), custom_call_target="tpu_custom_call" | custom-call | bytes 1024 | tf_op jit(solution)/shard_map/copy_columns/pallas_call | solution.py:203
  1.8 0.1 collective-permute-start
  1.9 4.5 %collective-permute-start.1 = (bf16[2,1152,128]{2,1,0:T(8,128)(2,1)S(1)}, bf16[2,1152,128]{2,1,0:T(8,128)(2,1)}, u32[]{:S(2)}, u32[]{:S(2)}) collective-permute-start(bf16[2,1152,128]{2,1,0:T(8,128)(2,1)S(1)} %copy_columns.3.own_ref), channel_id=1, source_target_pairs={{1,2},{2,1},{5,6},{6,5},{9,10},{10,9},{13,14},{14,13},{17,18},{18,... | collective-permute-start | bytes 1769480 | tf_op jit(solution)/shard_map/ppermute | solution.py:304
  6.4 0.0 copy-done.2
  6.4 0.2 copy.11
  6.6 1.3 %split_halves.1 = (bf16[1152,384]{1,0:T(8,128)(2,1)S(1)}, bf16[1152,384]{1,0:T(8,128)(2,1)}) custom-call(s32[1]{0:T(128)} %bitcast.5.info_ref, bf16[2,1152,384]{2,1,0:T(8,128)(2,1)S(1)} %bitcast.16), custom_call_target="tpu_custom_call" | custom-call | bytes 1024 | tf_op jit(solution)/shard_map/split_halves/pallas_call | solution.py:227
  7.9 1.3 %collective-permute-start.3 = (bf16[1152,384]{1,0:T(8,128)(2,1)}, bf16[1152,384]{1,0:T(8,128)(2,1)S(1)}, u32[]{:S(2)}, u32[]{:S(2)}) collective-permute-start(bf16[1152,384]{1,0:T(8,128)(2,1)} %get-tuple-element.49), channel_id=1, source_target_pairs={{0,16},{16,0},{1,17},{17,1},{2,18},{18,2},{3,19},{19,3},{4,20},{20... | collective-permute-start | bytes 2654216 | tf_op jit(solution)/shard_map/ppermute | solution.py:261
  9.2 0.0 copy-start.3
  9.2 2.9 %copy_columns.5 = (bf16[2,1152,128]{2,1,0:T(8,128)(2,1)S(1)}, bf16[384,768]{1,0:T(8,128)(2,1)}) custom-call(s32[2]{0:T(128)S(1)} %pad_add_fusion.info_ref, bf16[1152,384]{1,0:T(8,128)(2,1)} %bitcast.18, bf16[1152,384]{1,0:T(8,128)(2,1)} %bitcast.21, bf16[384,3072]{1,0:T(8,128)(2,1)} %refs_2_), custom_call_target="tpu_custom_call" | custom-call | bytes 1024 | tf_op jit(solution)/shard_map/copy_columns/pallas_call | solution.py:203
  12.1 1.3 %collective-permute-start.2 = (bf16[384,768]{1,0:T(8,128)(2,1)}, bf16[384,768]{1,0:T(8,128)(2,1)S(1)}, u32[]{:S(2)}, u32[]{:S(2)}) collective-permute-start(bf16[384,768]{1,0:T(8,128)(2,1)} %get-tuple-element.53), channel_id=1, source_target_pairs={{0,8},{4,12},{8,0},{12,4},{1,9},{5,13},{9,1},{13,5},{2,10},{6,14},... | collective-permute-start | bytes 1769480 | tf_op jit(solution)/shard_map/ppermute | solution.py:263
  13.4 0.0 collective-permute-start.6
  13.4 0.0 copy-done
  13.5 0.7 dynamic-slice_reduce_fusion
  14.2 0.0 copy-done.3
  14.2 0.1 concatenate.6.info_ref
  14.2 0.1 add_convert_fusion.1
  14.3 0.7 pad_add_fusion.1.info_ref
  15.0 1.2 %collective-permute-done.side_a_ref = bf16[2,1152,128]{2,1,0:T(8,128)(2,1)} collective-permute-done((bf16[2,1152,128]{2,1,0:T(8,128)(2,1)S(1)}, bf16[2,1152,128]{2,1,0:T(8,128)(2,1)}, u32[]{:S(2)}, u32[]{:S(2)}) %collective-permute-start) | collective-permute-done | bytes 589856 | tf_op jit(solution)/shard_map/ppermute | solution.py:304
  16.2 3.2 %collective-permute-start.7 = (bf16[2,1152,128]{2,1,0:T(8,128)(2,1)S(1)}, bf16[2,1152,128]{2,1,0:T(8,128)(2,1)S(1)}, u32[]{:S(2)}, u32[]{:S(2)}) collective-permute-start(bf16[2,1152,128]{2,1,0:T(8,128)(2,1)S(1)} %get-tuple-element.61.own_ref), channel_id=1, source_target_pairs={{1,2},{2,1},{5,6},{6,5},{9,10},{10,9},{13,14},{14,13},{17,18},{18,... | collective-permute-start | bytes 1769480 | tf_op jit(solution)/shard_map/ppermute | solution.py:304
  19.4 0.0 collective-permute-done.1.side_b_ref
  19.4 2.5 %copy_columns.4 = (bf16[384,768]{1,0:T(8,128)(2,1)S(1)}, bf16[1152,128]{1,0:T(8,128)(2,1)S(1)}, bf16[1152,128]{1,0:T(8,128)(2,1)S(1)}, bf16[1152,128]{1,0:T(8,128)(2,1)S(1)}, bf16[2,1152,128]{2,1,0:T(8,128)(2,1)S(1)}) custom-call(s32[2]{0:T(128)S(1)} %pad_add_fusion.info_ref, bf16[1152,384]{1,0:T(8,128)(2,1)} %bitcast.23, bf16[1152,384]{1,0:T(8,128)(2,1)} %bitcast.19, ...), custom_call_target="tpu_custom_call" | custom-call | bytes 1024 | tf_op jit(solution)/shard_map/copy_columns/pallas_call | solution.py:203
  21.9 5.1 %attention.3.refs_2_ = bf16[1152,128]{1,0:T(8,128)(2,1)S(1)} custom-call(s32[5]{0:T(128)S(1)} %pad_add_fusion.1.info_ref, bf16[1152,128]{1,0:T(8,128)(2,1)S(1)} %get-tuple-element.56.q_ref, bf16[2,1152,128]{2,1,0:T(8,128)(2,1)S(1)} %copy_columns.3.own_ref, bf16[2,1152,128]{2,1,0:T(8,128)(2,1)} %collective-permute-done.side_a_ref, ...), custom_call_target="tpu_custom_call" | custom-call | bytes 1024 | tf_op jit(solution)/shard_map/attention/pallas_call | solution.py:102
  27.0 0.1 collective-permute-start.10
  27.1 0.0 collective-permute-done.2.refs_1_
  27.1 3.0 %collective-permute-start.11 = (bf16[2,1152,128]{2,1,0:T(8,128)(2,1)S(1)}, bf16[2,1152,128]{2,1,0:T(8,128)(2,1)S(1)}, u32[]{:S(2)}, u32[]{:S(2)}) collective-permute-start(bf16[2,1152,128]{2,1,0:T(8,128)(2,1)S(1)} %get-tuple-element.63.own_ref), channel_id=1, source_target_pairs={{1,2},{2,1},{5,6},{6,5},{9,10},{10,9},{13,14},{14,13},{17,18},{18,... | collective-permute-start | bytes 1769480 | tf_op jit(solution)/shard_map/ppermute | solution.py:304
  30.1 0.0 collective-permute-done.6.side_a_ref
  30.2 1.2 %collective-permute-start.4 = (bf16[1152,128]{1,0:T(8,128)(2,1)S(1)}, bf16[1152,128]{1,0:T(8,128)(2,1)S(1)}, u32[]{:S(2)}, u32[]{:S(2)}) collective-permute-start(bf16[1152,128]{1,0:T(8,128)(2,1)S(1)} %attention.3.refs_2_), channel_id=1, source_target_pairs={{0,16},{16,0},{1,17},{17,1},{2,18},{18,2},{3,19},{19,3},{4,20},{20... | collective-permute-start | bytes 884744 | tf_op jit(solution)/shard_map/ppermute | solution.py:261
  31.4 0.0 collective-permute-done.3.refs_11_
  31.4 1.2 %collective-permute-start.5 = (bf16[1152,128]{1,0:T(8,128)(2,1)S(1)}, bf16[1152,128]{1,0:T(8,128)(2,1)S(1)}, u32[]{:S(2)}, u32[]{:S(2)}) collective-permute-start(bf16[1152,128]{1,0:T(8,128)(2,1)S(1)} %attention.3.refs_2_), channel_id=1, source_target_pairs={{0,8},{4,12},{8,0},{12,4},{1,9},{5,13},{9,1},{13,5},{2,10},{6,14},... | collective-permute-start | bytes 884744 | tf_op jit(solution)/shard_map/ppermute | solution.py:263
  32.6 0.0 collective-permute-done.7.side_b_ref
  32.6 4.9 %attention.4.refs_6_ = bf16[1152,128]{1,0:T(8,128)(2,1)S(1)} custom-call(s32[5]{0:T(128)S(1)} %pad_add_fusion.1.info_ref, bf16[1152,128]{1,0:T(8,128)(2,1)S(1)} %get-tuple-element.60.q_ref, bf16[2,1152,128]{2,1,0:T(8,128)(2,1)S(1)} %get-tuple-element.61.own_ref, bf16[2,1152,128]{2,1,0:T(8,128)(2,1)} %collective-permute-done.6.side_a_ref, ...), custom_call_target="tpu_custom_call" | custom-call | bytes 1024 | tf_op jit(solution)/shard_map/attention/pallas_call | solution.py:102
  37.5 0.0 copy-start.1
  37.5 0.3 collective-permute-start.14
  37.9 0.0 collective-permute-done.4.refs_3_
  37.9 0.3 collective-permute-start.8
  38.1 0.0 collective-permute-done.5.refs_4_
  38.1 1.2 %collective-permute-start.13 = (bf16[1152,128]{1,0:T(8,128)(2,1)S(1)}, bf16[1152,128]{1,0:T(8,128)(2,1)S(1)}, u32[]{:S(2)}, u32[]{:S(2)}) collective-permute-start(bf16[1152,128]{1,0:T(8,128)(2,1)S(1)} %collective-permute-done.4.refs_3_), channel_id=1, source_target_pairs={{0,8},{4,12},{8,0},{12,4},{1,9},{5,13},{9,1},{13,5},{2,10},{6,14},... | collective-permute-start | bytes 884744 | tf_op jit(solution)/shard_map/ppermute | solution.py:263
  39.3 0.0 collective-permute-done.10.side_a_ref
  39.3 4.9 %collective-permute-done.11.side_b_ref = bf16[2,1152,128]{2,1,0:T(8,128)(2,1)S(1)} collective-permute-done((bf16[2,1152,128]{2,1,0:T(8,128)(2,1)S(1)}, bf16[2,1152,128]{2,1,0:T(8,128)(2,1)S(1)}, u32[]{:S(2)}, u32[]{:S(2)}) %collective-permute-start.11) | collective-permute-done | bytes 589856 | tf_op jit(solution)/shard_map/ppermute | solution.py:304
  44.2 4.4 %attention.5.refs_3_ = bf16[1152,128]{1,0:T(8,128)(2,1)S(1)} custom-call(s32[5]{0:T(128)S(1)} %pad_add_fusion.1.info_ref, bf16[1152,128]{1,0:T(8,128)(2,1)S(1)} %get-tuple-element.62.q_ref, bf16[2,1152,128]{2,1,0:T(8,128)(2,1)S(1)} %get-tuple-element.63.own_ref, bf16[2,1152,128]{2,1,0:T(8,128)(2,1)S(1)} %collective-permute-done.10.side_a_ref, ...), custom_call_target="tpu_custom_call" | custom-call | bytes 1024 | tf_op jit(solution)/shard_map/attention/pallas_call | solution.py:102
  48.6 1.3 %collective-permute-start.12 = (bf16[1152,128]{1,0:T(8,128)(2,1)S(1)}, bf16[1152,128]{1,0:T(8,128)(2,1)S(1)}, u32[]{:S(2)}, u32[]{:S(2)}) collective-permute-start(bf16[1152,128]{1,0:T(8,128)(2,1)S(1)} %attention.5.refs_3_), channel_id=1, source_target_pairs={{0,16},{16,0},{1,17},{17,1},{2,18},{18,2},{3,19},{19,3},{4,20},{20... | collective-permute-start | bytes 884744 | tf_op jit(solution)/shard_map/ppermute | solution.py:261
  49.9 1.3 %collective-permute-start.15 = (bf16[1152,128]{1,0:T(8,128)(2,1)S(1)}, bf16[1152,128]{1,0:T(8,128)(2,1)S(1)}, u32[]{:S(2)}, u32[]{:S(2)}) collective-permute-start(bf16[1152,128]{1,0:T(8,128)(2,1)S(1)} %attention.5.refs_3_), channel_id=1, source_target_pairs={{0,8},{4,12},{8,0},{12,4},{1,9},{5,13},{9,1},{13,5},{2,10},{6,14},... | collective-permute-start | bytes 884744 | tf_op jit(solution)/shard_map/ppermute | solution.py:263
  51.2 0.0 collective-permute-done.8.refs_8_
  51.2 0.3 collective-permute-start.9
  51.4 0.0 collective-permute-done.14.refs_7_
  51.4 0.0 collective-permute-done.13.refs_5_
  51.4 3.5 %collective-permute-done.12.refs_4_ = bf16[1152,128]{1,0:T(8,128)(2,1)S(1)} collective-permute-done((bf16[1152,128]{1,0:T(8,128)(2,1)S(1)}, bf16[1152,128]{1,0:T(8,128)(2,1)S(1)}, u32[]{:S(2)}, u32[]{:S(2)}) %collective-permute-start.12) | collective-permute-done | bytes 294944 | tf_op jit(solution)/shard_map/ppermute | solution.py:261
  55.0 1.3 %collective-permute-start.16 = (bf16[1152,128]{1,0:T(8,128)(2,1)S(1)}, bf16[1152,128]{1,0:T(8,128)(2,1)S(1)}, u32[]{:S(2)}, u32[]{:S(2)}) collective-permute-start(bf16[1152,128]{1,0:T(8,128)(2,1)S(1)} %collective-permute-done.12.refs_4_), channel_id=1, source_target_pairs={{0,8},{4,12},{8,0},{12,4},{1,9},{5,13},{9,1},{13,5},{2,10},{6,14},... | collective-permute-start | bytes 884744 | tf_op jit(solution)/shard_map/ppermute | solution.py:263
  56.3 0.0 copy-done.1
  56.3 2.8 %partial_projection.2 = (f32[1152,384]{1,0:T(8,128)S(1)}, f32[1152,384]{1,0:T(8,128)S(1)}) custom-call(s32[22]{0:T(128)S(1)} %concatenate.6.info_ref, bf16[384,768]{1,0:T(8,128)(2,1)S(1)} %get-tuple-element.45.refs_0_, bf16[384,768]{1,0:T(8,128)(2,1)S(1)} %collective-permute-done.2.refs_1_, bf16[1152,128]{1,0:T(8,128)(2,1)S(1)} %attention.3.refs_2_, ...), custom_call_target="tpu_custom_call" | custom-call | bytes 1024 | tf_op jit(solution)/shard_map/partial_projection/pallas_call | solution.py:166
  59.1 0.0 collective-permute-done.15.refs_5_
  59.1 2.2 %collective-permute-done.9.refs_2_ = bf16[1152,128]{1,0:T(8,128)(2,1)S(1)} collective-permute-done((bf16[1152,128]{1,0:T(8,128)(2,1)S(1)}, bf16[1152,128]{1,0:T(8,128)(2,1)S(1)}, u32[]{:S(2)}, u32[]{:S(2)}) %collective-permute-start.9) | collective-permute-done | bytes 294944 | tf_op jit(solution)/shard_map/ppermute | solution.py:261
  61.3 1.4 %collective-permute-done.16.refs_6_ = bf16[1152,128]{1,0:T(8,128)(2,1)S(1)} collective-permute-done((bf16[1152,128]{1,0:T(8,128)(2,1)S(1)}, bf16[1152,128]{1,0:T(8,128)(2,1)S(1)}, u32[]{:S(2)}, u32[]{:S(2)}) %collective-permute-start.16) | collective-permute-done | bytes 294944 | tf_op jit(solution)/shard_map/ppermute | solution.py:263
  62.7 2.3 %partial_projection.3 = (f32[1152,384]{1,0:T(8,128)S(1)}, bf16[1152,384]{1,0:T(8,128)(2,1)S(1)}) custom-call(s32[22]{0:T(128)S(1)} %concatenate.6.info_ref, bf16[384,768]{1,0:T(8,128)(2,1)S(1)} %get-tuple-element.45.refs_0_, bf16[384,768]{1,0:T(8,128)(2,1)S(1)} %collective-permute-done.2.refs_1_, bf16[1152,128]{1,0:T(8,128)(2,1)S(1)} %collective-permute-done.9.refs_2_, ...), custom_call_target="tpu_custom_call" | custom-call | bytes 1024 | tf_op jit(solution)/shard_map/partial_projection/pallas_call | solution.py:166
  65.0 4.9 %collective-permute-start.17 = (bf16[1152,384]{1,0:T(8,128)(2,1)S(1)}, bf16[1152,384]{1,0:T(8,128)(2,1)S(1)}, u32[]{:S(2)}, u32[]{:S(2)}) collective-permute-start(bf16[1152,384]{1,0:T(8,128)(2,1)S(1)} %get-tuple-element.72), channel_id=1, source_target_pairs={{0,4},{4,0},{8,12},{12,8},{1,5},{5,1},{9,13},{13,9},{2,6},{6,2},{1... | collective-permute-start | bytes 2654216 | tf_op jit(solution)/shard_map/ppermute | solution.py:263
  69.9 2.1 %collective-permute-done.17 = bf16[1152,384]{1,0:T(8,128)(2,1)S(1)} collective-permute-done((bf16[1152,384]{1,0:T(8,128)(2,1)S(1)}, bf16[1152,384]{1,0:T(8,128)(2,1)S(1)}, u32[]{:S(2)}, u32[]{:S(2)}) %collective-permute-start.17) | collective-permute-done | bytes 884768 | tf_op jit(solution)/shard_map/ppermute | solution.py:263
  72.0 1.1 %add_convert_fusion = bf16[1152,384]{1,0:T(8,128)(2,1)} fusion(f32[1152,384]{1,0:T(8,128)S(1)} %get-tuple-element.71, bf16[1152,384]{1,0:T(8,128)(2,1)S(1)} %collective-permute-done.17), kind=kLoop, calls=%fused_computation.1 | loop fusion | flops 1327104 | bytes 3538944 | tf_op jit(solution)/shard_map/convert_element_type | solution.py:377
Async XLA Ops:
  0.0 13.5 %copy-start = (s32[3,4]{1,0:T(4,128)S(1)}, s32[3,4]{1,0:T(4,128)}, u32[]{:S(2)}) copy-start(s32[3,4]{1,0:T(4,128)} %param.14) | copy-start | bytes 148
  0.0 6.4 %copy-start.2 = (bf16[1,1152,2,384]{3,2,1,0:T(2,128)(2,1)S(1)}, bf16[1,1152,2,384]{3,2,1,0:T(2,128)(2,1)}, u32[]{:S(2)}) copy-start(bf16[1,1152,2,384]{3,2,1,0:T(2,128)(2,1)} %param.11) | copy-start | bytes 5308420
  1.8 14.4 %collective-permute-start = (bf16[2,1152,128]{2,1,0:T(8,128)(2,1)S(1)}, bf16[2,1152,128]{2,1,0:T(8,128)(2,1)}, u32[]{:S(2)}, u32[]{:S(2)}) collective-permute-start(bf16[2,1152,128]{2,1,0:T(8,128)(2,1)S(1)} %copy_columns.3.own_ref), channel_id=1, source_target_pairs={{0,1},{1,0},{2,3},{3,2},{4,5},{5,4},{6,7},{7,6},{8,9},{9,8},{10,11... | collective-permute-start | bytes 1769480 | tf_op jit(solution)/shard_map/ppermute | solution.py:304
  1.9 17.5 %collective-permute-start.1 = (bf16[2,1152,128]{2,1,0:T(8,128)(2,1)S(1)}, bf16[2,1152,128]{2,1,0:T(8,128)(2,1)}, u32[]{:S(2)}, u32[]{:S(2)}) collective-permute-start(bf16[2,1152,128]{2,1,0:T(8,128)(2,1)S(1)} %copy_columns.3.own_ref), channel_id=1, source_target_pairs={{1,2},{2,1},{5,6},{6,5},{9,10},{10,9},{13,14},{14,13},{17,18},{18,... | collective-permute-start | bytes 1769480 | tf_op jit(solution)/shard_map/ppermute | solution.py:304
  7.9 23.5 %collective-permute-start.3 = (bf16[1152,384]{1,0:T(8,128)(2,1)}, bf16[1152,384]{1,0:T(8,128)(2,1)S(1)}, u32[]{:S(2)}, u32[]{:S(2)}) collective-permute-start(bf16[1152,384]{1,0:T(8,128)(2,1)} %get-tuple-element.49), channel_id=1, source_target_pairs={{0,16},{16,0},{1,17},{17,1},{2,18},{18,2},{3,19},{19,3},{4,20},{20... | collective-permute-start | bytes 2654216 | tf_op jit(solution)/shard_map/ppermute | solution.py:261
  9.2 5.0 %copy-start.3 = (s32[18]{0:T(128)S(1)}, s32[18]{0:T(128)}, u32[]{:S(2)}) copy-start(s32[18]{0:T(128)} %param.15) | copy-start | bytes 220
  12.1 15.0 %collective-permute-start.2 = (bf16[384,768]{1,0:T(8,128)(2,1)}, bf16[384,768]{1,0:T(8,128)(2,1)S(1)}, u32[]{:S(2)}, u32[]{:S(2)}) collective-permute-start(bf16[384,768]{1,0:T(8,128)(2,1)} %get-tuple-element.53), channel_id=1, source_target_pairs={{0,8},{4,12},{8,0},{12,4},{1,9},{5,13},{9,1},{13,5},{2,10},{6,14},... | collective-permute-start | bytes 1769480 | tf_op jit(solution)/shard_map/ppermute | solution.py:263
  13.4 16.7 %collective-permute-start.6 = (bf16[2,1152,128]{2,1,0:T(8,128)(2,1)S(1)}, bf16[2,1152,128]{2,1,0:T(8,128)(2,1)}, u32[]{:S(2)}, u32[]{:S(2)}) collective-permute-start(bf16[2,1152,128]{2,1,0:T(8,128)(2,1)S(1)} %get-tuple-element.61.own_ref), channel_id=1, source_target_pairs={{0,1},{1,0},{2,3},{3,2},{4,5},{5,4},{6,7},{7,6},{8,9},{9,8},{10,11... | collective-permute-start | bytes 1769480 | tf_op jit(solution)/shard_map/ppermute | solution.py:304
  16.2 16.5 %collective-permute-start.7 = (bf16[2,1152,128]{2,1,0:T(8,128)(2,1)S(1)}, bf16[2,1152,128]{2,1,0:T(8,128)(2,1)S(1)}, u32[]{:S(2)}, u32[]{:S(2)}) collective-permute-start(bf16[2,1152,128]{2,1,0:T(8,128)(2,1)S(1)} %get-tuple-element.61.own_ref), channel_id=1, source_target_pairs={{1,2},{2,1},{5,6},{6,5},{9,10},{10,9},{13,14},{14,13},{17,18},{18,... | collective-permute-start | bytes 1769480 | tf_op jit(solution)/shard_map/ppermute | solution.py:304
  27.0 12.3 %collective-permute-start.10 = (bf16[2,1152,128]{2,1,0:T(8,128)(2,1)S(1)}, bf16[2,1152,128]{2,1,0:T(8,128)(2,1)S(1)}, u32[]{:S(2)}, u32[]{:S(2)}) collective-permute-start(bf16[2,1152,128]{2,1,0:T(8,128)(2,1)S(1)} %get-tuple-element.63.own_ref), channel_id=1, source_target_pairs={{0,1},{1,0},{2,3},{3,2},{4,5},{5,4},{6,7},{7,6},{8,9},{9,8},{10,11... | collective-permute-start | bytes 1769480 | tf_op jit(solution)/shard_map/ppermute | solution.py:304
  27.1 17.1 %collective-permute-start.11 = (bf16[2,1152,128]{2,1,0:T(8,128)(2,1)S(1)}, bf16[2,1152,128]{2,1,0:T(8,128)(2,1)S(1)}, u32[]{:S(2)}, u32[]{:S(2)}) collective-permute-start(bf16[2,1152,128]{2,1,0:T(8,128)(2,1)S(1)} %get-tuple-element.63.own_ref), channel_id=1, source_target_pairs={{1,2},{2,1},{5,6},{6,5},{9,10},{10,9},{13,14},{14,13},{17,18},{18,... | collective-permute-start | bytes 1769480 | tf_op jit(solution)/shard_map/ppermute | solution.py:304
  30.2 7.7 %collective-permute-start.4 = (bf16[1152,128]{1,0:T(8,128)(2,1)S(1)}, bf16[1152,128]{1,0:T(8,128)(2,1)S(1)}, u32[]{:S(2)}, u32[]{:S(2)}) collective-permute-start(bf16[1152,128]{1,0:T(8,128)(2,1)S(1)} %attention.3.refs_2_), channel_id=1, source_target_pairs={{0,16},{16,0},{1,17},{17,1},{2,18},{18,2},{3,19},{19,3},{4,20},{20... | collective-permute-start | bytes 884744 | tf_op jit(solution)/shard_map/ppermute | solution.py:261
  31.4 6.7 %collective-permute-start.5 = (bf16[1152,128]{1,0:T(8,128)(2,1)S(1)}, bf16[1152,128]{1,0:T(8,128)(2,1)S(1)}, u32[]{:S(2)}, u32[]{:S(2)}) collective-permute-start(bf16[1152,128]{1,0:T(8,128)(2,1)S(1)} %attention.3.refs_2_), channel_id=1, source_target_pairs={{0,8},{4,12},{8,0},{12,4},{1,9},{5,13},{9,1},{13,5},{2,10},{6,14},... | collective-permute-start | bytes 884744 | tf_op jit(solution)/shard_map/ppermute | solution.py:263
  37.5 18.8 %copy-start.1 = (bf16[2,2,1536]{2,1,0:T(2,128)(2,1)S(1)}, bf16[2,2,1536]{2,1,0:T(2,128)(2,1)}, u32[]{:S(2)}) copy-start(bf16[2,2,1536]{2,1,0:T(2,128)(2,1)} %refs_7_.1) | copy-start | bytes 36868
  37.5 13.9 %collective-permute-start.14 = (bf16[1152,128]{1,0:T(8,128)(2,1)S(1)}, bf16[1152,128]{1,0:T(8,128)(2,1)S(1)}, u32[]{:S(2)}, u32[]{:S(2)}) collective-permute-start(bf16[1152,128]{1,0:T(8,128)(2,1)S(1)} %attention.4.refs_6_), channel_id=1, source_target_pairs={{0,16},{16,0},{1,17},{17,1},{2,18},{18,2},{3,19},{19,3},{4,20},{20... | collective-permute-start | bytes 884744 | tf_op jit(solution)/shard_map/ppermute | solution.py:261
  37.9 13.3 %collective-permute-start.8 = (bf16[1152,128]{1,0:T(8,128)(2,1)S(1)}, bf16[1152,128]{1,0:T(8,128)(2,1)S(1)}, u32[]{:S(2)}, u32[]{:S(2)}) collective-permute-start(bf16[1152,128]{1,0:T(8,128)(2,1)S(1)} %attention.4.refs_6_), channel_id=1, source_target_pairs={{0,8},{4,12},{8,0},{12,4},{1,9},{5,13},{9,1},{13,5},{2,10},{6,14},... | collective-permute-start | bytes 884744 | tf_op jit(solution)/shard_map/ppermute | solution.py:263
  38.1 13.3 %collective-permute-start.13 = (bf16[1152,128]{1,0:T(8,128)(2,1)S(1)}, bf16[1152,128]{1,0:T(8,128)(2,1)S(1)}, u32[]{:S(2)}, u32[]{:S(2)}) collective-permute-start(bf16[1152,128]{1,0:T(8,128)(2,1)S(1)} %collective-permute-done.4.refs_3_), channel_id=1, source_target_pairs={{0,8},{4,12},{8,0},{12,4},{1,9},{5,13},{9,1},{13,5},{2,10},{6,14},... | collective-permute-start | bytes 884744 | tf_op jit(solution)/shard_map/ppermute | solution.py:263
  48.6 6.4 %collective-permute-start.12 = (bf16[1152,128]{1,0:T(8,128)(2,1)S(1)}, bf16[1152,128]{1,0:T(8,128)(2,1)S(1)}, u32[]{:S(2)}, u32[]{:S(2)}) collective-permute-start(bf16[1152,128]{1,0:T(8,128)(2,1)S(1)} %attention.5.refs_3_), channel_id=1, source_target_pairs={{0,16},{16,0},{1,17},{17,1},{2,18},{18,2},{3,19},{19,3},{4,20},{20... | collective-permute-start | bytes 884744 | tf_op jit(solution)/shard_map/ppermute | solution.py:261
  49.9 9.2 %collective-permute-start.15 = (bf16[1152,128]{1,0:T(8,128)(2,1)S(1)}, bf16[1152,128]{1,0:T(8,128)(2,1)S(1)}, u32[]{:S(2)}, u32[]{:S(2)}) collective-permute-start(bf16[1152,128]{1,0:T(8,128)(2,1)S(1)} %attention.5.refs_3_), channel_id=1, source_target_pairs={{0,8},{4,12},{8,0},{12,4},{1,9},{5,13},{9,1},{13,5},{2,10},{6,14},... | collective-permute-start | bytes 884744 | tf_op jit(solution)/shard_map/ppermute | solution.py:263
  51.2 10.1 %collective-permute-start.9 = (bf16[1152,128]{1,0:T(8,128)(2,1)S(1)}, bf16[1152,128]{1,0:T(8,128)(2,1)S(1)}, u32[]{:S(2)}, u32[]{:S(2)}) collective-permute-start(bf16[1152,128]{1,0:T(8,128)(2,1)S(1)} %collective-permute-done.8.refs_8_), channel_id=1, source_target_pairs={{0,16},{16,0},{1,17},{17,1},{2,18},{18,2},{3,19},{19,3},{4,20},{20... | collective-permute-start | bytes 884744 | tf_op jit(solution)/shard_map/ppermute | solution.py:261
  55.0 7.7 %collective-permute-start.16 = (bf16[1152,128]{1,0:T(8,128)(2,1)S(1)}, bf16[1152,128]{1,0:T(8,128)(2,1)S(1)}, u32[]{:S(2)}, u32[]{:S(2)}) collective-permute-start(bf16[1152,128]{1,0:T(8,128)(2,1)S(1)} %collective-permute-done.12.refs_4_), channel_id=1, source_target_pairs={{0,8},{4,12},{8,0},{12,4},{1,9},{5,13},{9,1},{13,5},{2,10},{6,14},... | collective-permute-start | bytes 884744 | tf_op jit(solution)/shard_map/ppermute | solution.py:263
  65.0 7.0 %collective-permute-start.17 = (bf16[1152,384]{1,0:T(8,128)(2,1)S(1)}, bf16[1152,384]{1,0:T(8,128)(2,1)S(1)}, u32[]{:S(2)}, u32[]{:S(2)}) collective-permute-start(bf16[1152,384]{1,0:T(8,128)(2,1)S(1)} %get-tuple-element.72), channel_id=1, source_target_pairs={{0,4},{4,0},{8,12},{12,8},{1,5},{5,1},{9,13},{13,9},{2,6},{6,2},{1... | collective-permute-start | bytes 2654216 | tf_op jit(solution)/shard_map/ppermute | solution.py:263

commit v14 on v12

--- a/solution.py
+++ b/solution.py
@@ -304,8 +304,8 @@
         return [lax.ppermute(part, "tokens", pairs) for pairs in rounds]
 
     sides = [halo(part) for part in packed]
-    near, *late = pack(pair_weight[:1] + query + key_value[2:], sides[0] if LATE_PACK else packed)
-    head_queries, packed = late[:heads], packed + late[heads:]
+    late = pack(query + key_value[2:], sides[0] if LATE_PACK else packed)
+    head_queries, packed = list(late[:heads]), packed + list(late[heads:])
     store = {"far": swap(far, 0, 2)}
 
     if RESIDUAL_AFTER:
@@ -350,6 +350,7 @@
         if head < heads - 1:
             relay(head)
 
+    (near,) = pack(pair_weight[:1], store[0, 0, heads - 1])
     names = [name for name in store if isinstance(name, tuple)]
     late = [name for name in names if name[2] == heads - 1 or name in LATE]
     base = (mine, store["other"])

time: 73.4 us -> 73.4 us (level)
  waiting for transfers between devices: 15.6 us -> 13.8 us
  Pallas kernels: 27.5 us -> 28.9 us
    ppermute x5, waiting for transfers between devices: 5.83 us -> 3.84 us  [swap(): return lax.ppermute(value, 'branch', [(0, 1), (1, 0)])]
    pallas_call x3 -> x4, Pallas kernels: 6.81 us -> 8.28 us  [copy_columns(): pl.pallas_call(functools.partial(copy_kernel, plan), out_shape=[jax.Shape...]
  transfers between devices with their start and end apart: 18 -> 18, of which waited for: 7 -> 7; matrix products, arithmetic and copies ran while one was open for 2% -> 2% of each run, Pallas kernels for 32% -> 34%
where the time goes in v14:
time: 73.4 us; the launch traced here: 73.1 us
  Pallas kernels  28.9 us (39%)
  starting transfers between devices  27.2 us (37%)
  waiting for transfers between devices  13.8 us (19%)
  other arithmetic  1.97 us (3%)
  local copies, waits for them, and re-layouts  1.03 us (1%)
    pallas_call x3, Pallas kernels, attention(): pl.pallas_call(functools.partial(attention_kernel, *tiles), out_shape=jax...  14.3 us
    ppermute x7, starting transfers between devices, swap(): lax.ppermute(value, 'head', [(i, i ^ head_bits) for i in range(head_count)])  11.9 us
    ppermute x6, starting transfers between devices, halo(): return [lax.ppermute(part, 'tokens', pairs) for pairs in rounds]  10.8 us
    pallas_call x4, Pallas kernels, copy_columns(): pl.pallas_call(functools.partial(copy_kernel, plan), out_shape=[jax.Shape...  8.28 us
    ppermute x6, waiting for transfers between devices, halo(): return [lax.ppermute(part, 'tokens', pairs) for pairs in rounds]  6.39 us
    pallas_call x2, Pallas kernels, partial_projection(): pl.pallas_call(functools.partial(partial_kernel, first, tuple(pieces), ti...  5.1 us
    ppermute x5, starting transfers between devices, swap(): return lax.ppermute(value, 'branch', [(0, 1), (1, 0)])  4.39 us
    ppermute x5, waiting for transfers between devices, swap(): return lax.ppermute(value, 'branch', [(0, 1), (1, 0)])  3.84 us
  transfers between devices with their start and end apart: 18, of which 7 were waited for; matrix products, arithmetic and copies ran while one was open for 2% of the time, Pallas kernels for 34%

profile of v14, /device:TPU:9, one launch (start us, length us, event | category | flops | bytes accessed | tf_op | source)
XLA Modules:
  0.0 73.1 jit_solution(10399074106045324266)
XLA Ops:
  0.0 0.0 copy-start
  0.0 0.0 copy-start.2
  0.0 0.1 pad_add_fusion.info_ref
  0.1 1.7 %copy_columns.4.own_ref = bf16[2,1152,128]{2,1,0:T(8,128)(2,1)S(1)} custom-call(s32[2]{0:T(128)S(1)} %pad_add_fusion.info_ref, bf16[1152,384]{1,0:T(8,128)(2,1)} %bitcast.17, bf16[1152,384]{1,0:T(8,128)(2,1)} %bitcast.20), custom_call_target="tpu_custom_call" | custom-call | bytes 1024 | tf_op jit(solution)/shard_map/copy_columns/pallas_call | solution.py:203
  1.8 0.1 collective-permute-start
  1.9 4.5 %collective-permute-start.1 = (bf16[2,1152,128]{2,1,0:T(8,128)(2,1)S(1)}, bf16[2,1152,128]{2,1,0:T(8,128)(2,1)}, u32[]{:S(2)}, u32[]{:S(2)}) collective-permute-start(bf16[2,1152,128]{2,1,0:T(8,128)(2,1)S(1)} %copy_columns.4.own_ref), channel_id=1, source_target_pairs={{1,2},{2,1},{5,6},{6,5},{9,10},{10,9},{13,14},{14,13},{17,18},{18,... | collective-permute-start | bytes 1769480 | tf_op jit(solution)/shard_map/ppermute | solution.py:304
  6.4 0.0 copy-done.2
  6.4 0.2 copy.11
  6.6 1.3 %split_halves.1 = (bf16[1152,384]{1,0:T(8,128)(2,1)S(1)}, bf16[1152,384]{1,0:T(8,128)(2,1)}) custom-call(s32[1]{0:T(128)} %bitcast.5.info_ref, bf16[2,1152,384]{2,1,0:T(8,128)(2,1)S(1)} %bitcast.16), custom_call_target="tpu_custom_call" | custom-call | bytes 1024 | tf_op jit(solution)/shard_map/split_halves/pallas_call | solution.py:227
  7.9 1.3 %collective-permute-start.3 = (bf16[1152,384]{1,0:T(8,128)(2,1)}, bf16[1152,384]{1,0:T(8,128)(2,1)S(1)}, u32[]{:S(2)}, u32[]{:S(2)}) collective-permute-start(bf16[1152,384]{1,0:T(8,128)(2,1)} %get-tuple-element.46), channel_id=1, source_target_pairs={{0,16},{16,0},{1,17},{17,1},{2,18},{18,2},{3,19},{19,3},{4,20},{20... | collective-permute-start | bytes 2654216 | tf_op jit(solution)/shard_map/ppermute | solution.py:261
  9.2 0.0 copy-start.3
  9.2 2.8 %copy_columns.6 = (bf16[2,1152,128]{2,1,0:T(8,128)(2,1)S(1)}, bf16[384,768]{1,0:T(8,128)(2,1)}) custom-call(s32[2]{0:T(128)S(1)} %pad_add_fusion.info_ref, bf16[1152,384]{1,0:T(8,128)(2,1)} %bitcast.18, bf16[1152,384]{1,0:T(8,128)(2,1)} %bitcast.21, bf16[384,3072]{1,0:T(8,128)(2,1)} %refs_0_), custom_call_target="tpu_custom_call" | custom-call | bytes 1024 | tf_op jit(solution)/shard_map/copy_columns/pallas_call | solution.py:203
  12.0 1.3 %collective-permute-start.2 = (bf16[384,768]{1,0:T(8,128)(2,1)}, bf16[384,768]{1,0:T(8,128)(2,1)S(1)}, u32[]{:S(2)}, u32[]{:S(2)}) collective-permute-start(bf16[384,768]{1,0:T(8,128)(2,1)} %get-tuple-element.50), channel_id=1, source_target_pairs={{0,8},{4,12},{8,0},{12,4},{1,9},{5,13},{9,1},{13,5},{2,10},{6,14},... | collective-permute-start | bytes 1769480 | tf_op jit(solution)/shard_map/ppermute | solution.py:263
  13.3 0.0 collective-permute-start.8
  13.3 0.0 copy-done
  13.3 0.7 dynamic-slice_reduce_fusion
  14.0 0.0 copy-done.3
  14.0 0.1 concatenate.6.info_ref
  14.1 0.1 add_convert_fusion.1
  14.2 0.7 pad_add_fusion.1.info_ref
  14.9 1.3 %collective-permute-done.side_a_ref = bf16[2,1152,128]{2,1,0:T(8,128)(2,1)} collective-permute-done((bf16[2,1152,128]{2,1,0:T(8,128)(2,1)S(1)}, bf16[2,1152,128]{2,1,0:T(8,128)(2,1)}, u32[]{:S(2)}, u32[]{:S(2)}) %collective-permute-start) | collective-permute-done | bytes 589856 | tf_op jit(solution)/shard_map/ppermute | solution.py:304
  16.2 3.2 %collective-permute-start.9 = (bf16[2,1152,128]{2,1,0:T(8,128)(2,1)S(1)}, bf16[2,1152,128]{2,1,0:T(8,128)(2,1)S(1)}, u32[]{:S(2)}, u32[]{:S(2)}) collective-permute-start(bf16[2,1152,128]{2,1,0:T(8,128)(2,1)S(1)} %get-tuple-element.61.own_ref), channel_id=1, source_target_pairs={{1,2},{2,1},{5,6},{6,5},{9,10},{10,9},{13,14},{14,13},{17,18},{18,... | collective-permute-start | bytes 1769480 | tf_op jit(solution)/shard_map/ppermute | solution.py:304
  19.4 0.0 collective-permute-done.1.side_b_ref
  19.4 2.1 %copy_columns.5 = (bf16[1152,128]{1,0:T(8,128)(2,1)S(1)}, bf16[1152,128]{1,0:T(8,128)(2,1)S(1)}, bf16[1152,128]{1,0:T(8,128)(2,1)S(1)}, bf16[2,1152,128]{2,1,0:T(8,128)(2,1)S(1)}) custom-call(s32[2]{0:T(128)S(1)} %pad_add_fusion.info_ref, bf16[1152,384]{1,0:T(8,128)(2,1)} %bitcast.23, bf16[1152,384]{1,0:T(8,128)(2,1)} %bitcast.19, bf16[1152,384]{1,0:T(8,128)(2,1)} %bitcast.22), custom_call_target="tpu_custom_call" | custom-call | bytes 1024 | tf_op jit(solution)/shard_map/copy_columns/pallas_call | solution.py:203
  21.5 5.1 %attention.3.refs_2_ = bf16[1152,128]{1,0:T(8,128)(2,1)S(1)} custom-call(s32[5]{0:T(128)S(1)} %pad_add_fusion.1.info_ref, bf16[1152,128]{1,0:T(8,128)(2,1)S(1)} %get-tuple-element.53.q_ref, bf16[2,1152,128]{2,1,0:T(8,128)(2,1)S(1)} %copy_columns.4.own_ref, bf16[2,1152,128]{2,1,0:T(8,128)(2,1)} %collective-permute-done.side_a_ref, ...), custom_call_target="tpu_custom_call" | custom-call | bytes 1024 | tf_op jit(solution)/shard_map/attention/pallas_call | solution.py:102
  26.6 0.1 collective-permute-start.6
  26.6 0.0 collective-permute-done.2.refs_1_
  26.6 3.0 %collective-permute-start.7 = (bf16[2,1152,128]{2,1,0:T(8,128)(2,1)S(1)}, bf16[2,1152,128]{2,1,0:T(8,128)(2,1)S(1)}, u32[]{:S(2)}, u32[]{:S(2)}) collective-permute-start(bf16[2,1152,128]{2,1,0:T(8,128)(2,1)S(1)} %get-tuple-element.57.own_ref), channel_id=1, source_target_pairs={{1,2},{2,1},{5,6},{6,5},{9,10},{10,9},{13,14},{14,13},{17,18},{18,... | collective-permute-start | bytes 1769480 | tf_op jit(solution)/shard_map/ppermute | solution.py:304
  29.7 0.0 collective-permute-done.8.side_a_ref
  29.7 1.3 %collective-permute-start.4 = (bf16[1152,128]{1,0:T(8,128)(2,1)S(1)}, bf16[1152,128]{1,0:T(8,128)(2,1)S(1)}, u32[]{:S(2)}, u32[]{:S(2)}) collective-permute-start(bf16[1152,128]{1,0:T(8,128)(2,1)S(1)} %attention.3.refs_2_), channel_id=1, source_target_pairs={{0,16},{16,0},{1,17},{17,1},{2,18},{18,2},{3,19},{19,3},{4,20},{20... | collective-permute-start | bytes 884744 | tf_op jit(solution)/shard_map/ppermute | solution.py:261
  31.0 0.0 collective-permute-done.3.refs_11_
  31.0 1.2 %collective-permute-start.5 = (bf16[1152,128]{1,0:T(8,128)(2,1)S(1)}, bf16[1152,128]{1,0:T(8,128)(2,1)S(1)}, u32[]{:S(2)}, u32[]{:S(2)}) collective-permute-start(bf16[1152,128]{1,0:T(8,128)(2,1)S(1)} %attention.3.refs_2_), channel_id=1, source_target_pairs={{0,8},{4,12},{8,0},{12,4},{1,9},{5,13},{9,1},{13,5},{2,10},{6,14},... | collective-permute-start | bytes 884744 | tf_op jit(solution)/shard_map/ppermute | solution.py:263
  32.2 0.0 collective-permute-done.9.side_b_ref
  32.2 4.9 %attention.5.refs_6_ = bf16[1152,128]{1,0:T(8,128)(2,1)S(1)} custom-call(s32[5]{0:T(128)S(1)} %pad_add_fusion.1.info_ref, bf16[1152,128]{1,0:T(8,128)(2,1)S(1)} %get-tuple-element.60.q_ref, bf16[2,1152,128]{2,1,0:T(8,128)(2,1)S(1)} %get-tuple-element.61.own_ref, bf16[2,1152,128]{2,1,0:T(8,128)(2,1)} %collective-permute-done.8.side_a_ref, ...), custom_call_target="tpu_custom_call" | custom-call | bytes 1024 | tf_op jit(solution)/shard_map/attention/pallas_call | solution.py:102
  37.1 0.3 collective-permute-start.10
  37.4 0.0 collective-permute-done.4.refs_3_
  37.4 0.3 collective-permute-start.14
  37.7 0.0 collective-permute-done.5.refs_4_
  37.7 1.2 %collective-permute-start.13 = (bf16[1152,128]{1,0:T(8,128)(2,1)S(1)}, bf16[1152,128]{1,0:T(8,128)(2,1)S(1)}, u32[]{:S(2)}, u32[]{:S(2)}) collective-permute-start(bf16[1152,128]{1,0:T(8,128)(2,1)S(1)} %collective-permute-done.4.refs_3_), channel_id=1, source_target_pairs={{0,8},{4,12},{8,0},{12,4},{1,9},{5,13},{9,1},{13,5},{2,10},{6,14},... | collective-permute-start | bytes 884744 | tf_op jit(solution)/shard_map/ppermute | solution.py:263
  38.9 0.6 collective-permute-done.6.side_a_ref
  39.5 4.4 %collective-permute-done.7.side_b_ref = bf16[2,1152,128]{2,1,0:T(8,128)(2,1)S(1)} collective-permute-done((bf16[2,1152,128]{2,1,0:T(8,128)(2,1)S(1)}, bf16[2,1152,128]{2,1,0:T(8,128)(2,1)S(1)}, u32[]{:S(2)}, u32[]{:S(2)}) %collective-permute-start.7) | collective-permute-done | bytes 589856 | tf_op jit(solution)/shard_map/ppermute | solution.py:304
  44.0 4.3 %attention.4.refs_3_ = bf16[1152,128]{1,0:T(8,128)(2,1)S(1)} custom-call(s32[5]{0:T(128)S(1)} %pad_add_fusion.1.info_ref, bf16[1152,128]{1,0:T(8,128)(2,1)S(1)} %get-tuple-element.56.q_ref, bf16[2,1152,128]{2,1,0:T(8,128)(2,1)S(1)} %get-tuple-element.57.own_ref, bf16[2,1152,128]{2,1,0:T(8,128)(2,1)S(1)} %collective-permute-done.6.side_a_ref, ...), custom_call_target="tpu_custom_call" | custom-call | bytes 1024 | tf_op jit(solution)/shard_map/attention/pallas_call | solution.py:102
  48.3 0.0 copy-start.1
  48.3 1.3 %collective-permute-start.12 = (bf16[1152,128]{1,0:T(8,128)(2,1)S(1)}, bf16[1152,128]{1,0:T(8,128)(2,1)S(1)}, u32[]{:S(2)}, u32[]{:S(2)}) collective-permute-start(bf16[1152,128]{1,0:T(8,128)(2,1)S(1)} %attention.4.refs_3_), channel_id=1, source_target_pairs={{0,16},{16,0},{1,17},{17,1},{2,18},{18,2},{3,19},{19,3},{4,20},{20... | collective-permute-start | bytes 884744 | tf_op jit(solution)/shard_map/ppermute | solution.py:261
  49.6 1.2 %collective-permute-start.15 = (bf16[1152,128]{1,0:T(8,128)(2,1)S(1)}, bf16[1152,128]{1,0:T(8,128)(2,1)S(1)}, u32[]{:S(2)}, u32[]{:S(2)}) collective-permute-start(bf16[1152,128]{1,0:T(8,128)(2,1)S(1)} %attention.4.refs_3_), channel_id=1, source_target_pairs={{0,8},{4,12},{8,0},{12,4},{1,9},{5,13},{9,1},{13,5},{2,10},{6,14},... | collective-permute-start | bytes 884744 | tf_op jit(solution)/shard_map/ppermute | solution.py:263
  50.8 0.0 collective-permute-done.10.refs_8_
  50.8 0.3 collective-permute-start.11
  51.1 0.0 collective-permute-done.14.refs_7_
  51.1 0.0 collective-permute-done.13.refs_5_
  51.1 3.3 %collective-permute-done.12.refs_4_ = bf16[1152,128]{1,0:T(8,128)(2,1)S(1)} collective-permute-done((bf16[1152,128]{1,0:T(8,128)(2,1)S(1)}, bf16[1152,128]{1,0:T(8,128)(2,1)S(1)}, u32[]{:S(2)}, u32[]{:S(2)}) %collective-permute-start.12) | collective-permute-done | bytes 294944 | tf_op jit(solution)/shard_map/ppermute | solution.py:261
  54.4 1.3 %collective-permute-start.16 = (bf16[1152,128]{1,0:T(8,128)(2,1)S(1)}, bf16[1152,128]{1,0:T(8,128)(2,1)S(1)}, u32[]{:S(2)}, u32[]{:S(2)}) collective-permute-start(bf16[1152,128]{1,0:T(8,128)(2,1)S(1)} %collective-permute-done.12.refs_4_), channel_id=1, source_target_pairs={{0,8},{4,12},{8,0},{12,4},{1,9},{5,13},{9,1},{13,5},{2,10},{6,14},... | collective-permute-start | bytes 884744 | tf_op jit(solution)/shard_map/ppermute | solution.py:263
  55.6 1.7 %copy_columns.7.refs_0_ = bf16[384,768]{1,0:T(8,128)(2,1)S(1)} custom-call(s32[2]{0:T(128)S(1)} %pad_add_fusion.info_ref, bf16[384,3072]{1,0:T(8,128)(2,1)} %refs_0_), custom_call_target="tpu_custom_call" | custom-call | bytes 1024 | tf_op jit(solution)/shard_map/copy_columns/pallas_call | solution.py:203
  57.3 0.0 copy-done.1
  57.3 2.8 %partial_projection.2 = (f32[1152,384]{1,0:T(8,128)S(1)}, f32[1152,384]{1,0:T(8,128)S(1)}) custom-call(s32[22]{0:T(128)S(1)} %concatenate.6.info_ref, bf16[384,768]{1,0:T(8,128)(2,1)S(1)} %copy_columns.7.refs_0_, bf16[384,768]{1,0:T(8,128)(2,1)S(1)} %collective-permute-done.2.refs_1_, bf16[1152,128]{1,0:T(8,128)(2,1)S(1)} %attention.3.refs_2_, ...), custom_call_target="tpu_custom_call" | custom-call | bytes 1024 | tf_op jit(solution)/shard_map/partial_projection/pallas_call | solution.py:166
  60.1 0.5 collective-permute-done.11.refs_2_
  60.7 0.0 collective-permute-done.15.refs_5_
  60.7 1.5 %collective-permute-done.16.refs_6_ = bf16[1152,128]{1,0:T(8,128)(2,1)S(1)} collective-permute-done((bf16[1152,128]{1,0:T(8,128)(2,1)S(1)}, bf16[1152,128]{1,0:T(8,128)(2,1)S(1)}, u32[]{:S(2)}, u32[]{:S(2)}) %collective-permute-start.16) | collective-permute-done | bytes 294944 | tf_op jit(solution)/shard_map/ppermute | solution.py:263
  62.2 2.3 %partial_projection.3 = (f32[1152,384]{1,0:T(8,128)S(1)}, bf16[1152,384]{1,0:T(8,128)(2,1)S(1)}) custom-call(s32[22]{0:T(128)S(1)} %concatenate.6.info_ref, bf16[384,768]{1,0:T(8,128)(2,1)S(1)} %copy_columns.7.refs_0_, bf16[384,768]{1,0:T(8,128)(2,1)S(1)} %collective-permute-done.2.refs_1_, bf16[1152,128]{1,0:T(8,128)(2,1)S(1)} %collective-permute-done.11.refs_2_, ...), custom_call_target="tpu_custom_call" | custom-call | bytes 1024 | tf_op jit(solution)/shard_map/partial_projection/pallas_call | solution.py:166
  64.5 5.4 %collective-permute-start.17 = (bf16[1152,384]{1,0:T(8,128)(2,1)S(1)}, bf16[1152,384]{1,0:T(8,128)(2,1)S(1)}, u32[]{:S(2)}, u32[]{:S(2)}) collective-permute-start(bf16[1152,384]{1,0:T(8,128)(2,1)S(1)} %get-tuple-element.70), channel_id=1, source_target_pairs={{0,4},{4,0},{8,12},{12,8},{1,5},{5,1},{9,13},{13,9},{2,6},{6,2},{1... | collective-permute-start | bytes 2654216 | tf_op jit(solution)/shard_map/ppermute | solution.py:263
  69.9 2.1 %collective-permute-done.17 = bf16[1152,384]{1,0:T(8,128)(2,1)S(1)} collective-permute-done((bf16[1152,384]{1,0:T(8,128)(2,1)S(1)}, bf16[1152,384]{1,0:T(8,128)(2,1)S(1)}, u32[]{:S(2)}, u32[]{:S(2)}) %collective-permute-start.17) | collective-permute-done | bytes 884768 | tf_op jit(solution)/shard_map/ppermute | solution.py:263
  71.9 1.1 %add_convert_fusion = bf16[1152,384]{1,0:T(8,128)(2,1)} fusion(f32[1152,384]{1,0:T(8,128)S(1)} %get-tuple-element.69, bf16[1152,384]{1,0:T(8,128)(2,1)S(1)} %collective-permute-done.17), kind=kLoop, calls=%fused_computation.1 | loop fusion | flops 1327104 | bytes 3538944 | tf_op jit(solution)/shard_map/convert_element_type | solution.py:378
Async XLA Ops:
  0.0 13.3 %copy-start = (s32[3,4]{1,0:T(4,128)S(1)}, s32[3,4]{1,0:T(4,128)}, u32[]{:S(2)}) copy-start(s32[3,4]{1,0:T(4,128)} %param.14) | copy-start | bytes 148
  0.0 6.4 %copy-start.2 = (bf16[1,1152,2,384]{3,2,1,0:T(2,128)(2,1)S(1)}, bf16[1,1152,2,384]{3,2,1,0:T(2,128)(2,1)}, u32[]{:S(2)}) copy-start(bf16[1,1152,2,384]{3,2,1,0:T(2,128)(2,1)} %param.11) | copy-start | bytes 5308420
  1.8 14.4 %collective-permute-start = (bf16[2,1152,128]{2,1,0:T(8,128)(2,1)S(1)}, bf16[2,1152,128]{2,1,0:T(8,128)(2,1)}, u32[]{:S(2)}, u32[]{:S(2)}) collective-permute-start(bf16[2,1152,128]{2,1,0:T(8,128)(2,1)S(1)} %copy_columns.4.own_ref), channel_id=1, source_target_pairs={{0,1},{1,0},{2,3},{3,2},{4,5},{5,4},{6,7},{7,6},{8,9},{9,8},{10,11... | collective-permute-start | bytes 1769480 | tf_op jit(solution)/shard_map/ppermute | solution.py:304
  1.9 17.5 %collective-permute-start.1 = (bf16[2,1152,128]{2,1,0:T(8,128)(2,1)S(1)}, bf16[2,1152,128]{2,1,0:T(8,128)(2,1)}, u32[]{:S(2)}, u32[]{:S(2)}) collective-permute-start(bf16[2,1152,128]{2,1,0:T(8,128)(2,1)S(1)} %copy_columns.4.own_ref), channel_id=1, source_target_pairs={{1,2},{2,1},{5,6},{6,5},{9,10},{10,9},{13,14},{14,13},{17,18},{18,... | collective-permute-start | bytes 1769480 | tf_op jit(solution)/shard_map/ppermute | solution.py:304
  7.9 23.1 %collective-permute-start.3 = (bf16[1152,384]{1,0:T(8,128)(2,1)}, bf16[1152,384]{1,0:T(8,128)(2,1)S(1)}, u32[]{:S(2)}, u32[]{:S(2)}) collective-permute-start(bf16[1152,384]{1,0:T(8,128)(2,1)} %get-tuple-element.46), channel_id=1, source_target_pairs={{0,16},{16,0},{1,17},{17,1},{2,18},{18,2},{3,19},{19,3},{4,20},{20... | collective-permute-start | bytes 2654216 | tf_op jit(solution)/shard_map/ppermute | solution.py:261
  9.2 4.8 %copy-start.3 = (s32[18]{0:T(128)S(1)}, s32[18]{0:T(128)}, u32[]{:S(2)}) copy-start(s32[18]{0:T(128)} %param.15) | copy-start | bytes 220
  12.0 14.6 %collective-permute-start.2 = (bf16[384,768]{1,0:T(8,128)(2,1)}, bf16[384,768]{1,0:T(8,128)(2,1)S(1)}, u32[]{:S(2)}, u32[]{:S(2)}) collective-permute-start(bf16[384,768]{1,0:T(8,128)(2,1)} %get-tuple-element.50), channel_id=1, source_target_pairs={{0,8},{4,12},{8,0},{12,4},{1,9},{5,13},{9,1},{13,5},{2,10},{6,14},... | collective-permute-start | bytes 1769480 | tf_op jit(solution)/shard_map/ppermute | solution.py:263
  13.3 16.4 %collective-permute-start.8 = (bf16[2,1152,128]{2,1,0:T(8,128)(2,1)S(1)}, bf16[2,1152,128]{2,1,0:T(8,128)(2,1)}, u32[]{:S(2)}, u32[]{:S(2)}) collective-permute-start(bf16[2,1152,128]{2,1,0:T(8,128)(2,1)S(1)} %get-tuple-element.61.own_ref), channel_id=1, source_target_pairs={{0,1},{1,0},{2,3},{3,2},{4,5},{5,4},{6,7},{7,6},{8,9},{9,8},{10,11... | collective-permute-start | bytes 1769480 | tf_op jit(solution)/shard_map/ppermute | solution.py:304
  16.2 16.0 %collective-permute-start.9 = (bf16[2,1152,128]{2,1,0:T(8,128)(2,1)S(1)}, bf16[2,1152,128]{2,1,0:T(8,128)(2,1)S(1)}, u32[]{:S(2)}, u32[]{:S(2)}) collective-permute-start(bf16[2,1152,128]{2,1,0:T(8,128)(2,1)S(1)} %get-tuple-element.61.own_ref), channel_id=1, source_target_pairs={{1,2},{2,1},{5,6},{6,5},{9,10},{10,9},{13,14},{14,13},{17,18},{18,... | collective-permute-start | bytes 1769480 | tf_op jit(solution)/shard_map/ppermute | solution.py:304
  26.6 13.0 %collective-permute-start.6 = (bf16[2,1152,128]{2,1,0:T(8,128)(2,1)S(1)}, bf16[2,1152,128]{2,1,0:T(8,128)(2,1)S(1)}, u32[]{:S(2)}, u32[]{:S(2)}) collective-permute-start(bf16[2,1152,128]{2,1,0:T(8,128)(2,1)S(1)} %get-tuple-element.57.own_ref), channel_id=1, source_target_pairs={{0,1},{1,0},{2,3},{3,2},{4,5},{5,4},{6,7},{7,6},{8,9},{9,8},{10,11... | collective-permute-start | bytes 1769480 | tf_op jit(solution)/shard_map/ppermute | solution.py:304
  26.6 17.3 %collective-permute-start.7 = (bf16[2,1152,128]{2,1,0:T(8,128)(2,1)S(1)}, bf16[2,1152,128]{2,1,0:T(8,128)(2,1)S(1)}, u32[]{:S(2)}, u32[]{:S(2)}) collective-permute-start(bf16[2,1152,128]{2,1,0:T(8,128)(2,1)S(1)} %get-tuple-element.57.own_ref), channel_id=1, source_target_pairs={{1,2},{2,1},{5,6},{6,5},{9,10},{10,9},{13,14},{14,13},{17,18},{18,... | collective-permute-start | bytes 1769480 | tf_op jit(solution)/shard_map/ppermute | solution.py:304
  29.7 7.7 %collective-permute-start.4 = (bf16[1152,128]{1,0:T(8,128)(2,1)S(1)}, bf16[1152,128]{1,0:T(8,128)(2,1)S(1)}, u32[]{:S(2)}, u32[]{:S(2)}) collective-permute-start(bf16[1152,128]{1,0:T(8,128)(2,1)S(1)} %attention.3.refs_2_), channel_id=1, source_target_pairs={{0,16},{16,0},{1,17},{17,1},{2,18},{18,2},{3,19},{19,3},{4,20},{20... | collective-permute-start | bytes 884744 | tf_op jit(solution)/shard_map/ppermute | solution.py:261
  31.0 6.7 %collective-permute-start.5 = (bf16[1152,128]{1,0:T(8,128)(2,1)S(1)}, bf16[1152,128]{1,0:T(8,128)(2,1)S(1)}, u32[]{:S(2)}, u32[]{:S(2)}) collective-permute-start(bf16[1152,128]{1,0:T(8,128)(2,1)S(1)} %attention.3.refs_2_), channel_id=1, source_target_pairs={{0,8},{4,12},{8,0},{12,4},{1,9},{5,13},{9,1},{13,5},{2,10},{6,14},... | collective-permute-start | bytes 884744 | tf_op jit(solution)/shard_map/ppermute | solution.py:263
  37.1 13.7 %collective-permute-start.10 = (bf16[1152,128]{1,0:T(8,128)(2,1)S(1)}, bf16[1152,128]{1,0:T(8,128)(2,1)S(1)}, u32[]{:S(2)}, u32[]{:S(2)}) collective-permute-start(bf16[1152,128]{1,0:T(8,128)(2,1)S(1)} %attention.5.refs_6_), channel_id=1, source_target_pairs={{0,8},{4,12},{8,0},{12,4},{1,9},{5,13},{9,1},{13,5},{2,10},{6,14},... | collective-permute-start | bytes 884744 | tf_op jit(solution)/shard_map/ppermute | solution.py:263
  37.4 13.7 %collective-permute-start.14 = (bf16[1152,128]{1,0:T(8,128)(2,1)S(1)}, bf16[1152,128]{1,0:T(8,128)(2,1)S(1)}, u32[]{:S(2)}, u32[]{:S(2)}) collective-permute-start(bf16[1152,128]{1,0:T(8,128)(2,1)S(1)} %attention.5.refs_6_), channel_id=1, source_target_pairs={{0,16},{16,0},{1,17},{17,1},{2,18},{18,2},{3,19},{19,3},{4,20},{20... | collective-permute-start | bytes 884744 | tf_op jit(solution)/shard_map/ppermute | solution.py:261
  37.7 13.4 %collective-permute-start.13 = (bf16[1152,128]{1,0:T(8,128)(2,1)S(1)}, bf16[1152,128]{1,0:T(8,128)(2,1)S(1)}, u32[]{:S(2)}, u32[]{:S(2)}) collective-permute-start(bf16[1152,128]{1,0:T(8,128)(2,1)S(1)} %collective-permute-done.4.refs_3_), channel_id=1, source_target_pairs={{0,8},{4,12},{8,0},{12,4},{1,9},{5,13},{9,1},{13,5},{2,10},{6,14},... | collective-permute-start | bytes 884744 | tf_op jit(solution)/shard_map/ppermute | solution.py:263
  48.3 9.0 %copy-start.1 = (bf16[2,2,1536]{2,1,0:T(2,128)(2,1)S(1)}, bf16[2,2,1536]{2,1,0:T(2,128)(2,1)}, u32[]{:S(2)}) copy-start(bf16[2,2,1536]{2,1,0:T(2,128)(2,1)} %refs_7_.1) | copy-start | bytes 36868
  48.3 6.1 %collective-permute-start.12 = (bf16[1152,128]{1,0:T(8,128)(2,1)S(1)}, bf16[1152,128]{1,0:T(8,128)(2,1)S(1)}, u32[]{:S(2)}, u32[]{:S(2)}) collective-permute-start(bf16[1152,128]{1,0:T(8,128)(2,1)S(1)} %attention.4.refs_3_), channel_id=1, source_target_pairs={{0,16},{16,0},{1,17},{17,1},{2,18},{18,2},{3,19},{19,3},{4,20},{20... | collective-permute-start | bytes 884744 | tf_op jit(solution)/shard_map/ppermute | solution.py:261
  49.6 11.1 %collective-permute-start.15 = (bf16[1152,128]{1,0:T(8,128)(2,1)S(1)}, bf16[1152,128]{1,0:T(8,128)(2,1)S(1)}, u32[]{:S(2)}, u32[]{:S(2)}) collective-permute-start(bf16[1152,128]{1,0:T(8,128)(2,1)S(1)} %attention.4.refs_3_), channel_id=1, source_target_pairs={{0,8},{4,12},{8,0},{12,4},{1,9},{5,13},{9,1},{13,5},{2,10},{6,14},... | collective-permute-start | bytes 884744 | tf_op jit(solution)/shard_map/ppermute | solution.py:263
  50.8 9.9 %collective-permute-start.11 = (bf16[1152,128]{1,0:T(8,128)(2,1)S(1)}, bf16[1152,128]{1,0:T(8,128)(2,1)S(1)}, u32[]{:S(2)}, u32[]{:S(2)}) collective-permute-start(bf16[1152,128]{1,0:T(8,128)(2,1)S(1)} %collective-permute-done.10.refs_8_), channel_id=1, source_target_pairs={{0,16},{16,0},{1,17},{17,1},{2,18},{18,2},{3,19},{19,3},{4,20},{20... | collective-permute-start | bytes 884744 | tf_op jit(solution)/shard_map/ppermute | solution.py:261
  54.4 7.8 %collective-permute-start.16 = (bf16[1152,128]{1,0:T(8,128)(2,1)S(1)}, bf16[1152,128]{1,0:T(8,128)(2,1)S(1)}, u32[]{:S(2)}, u32[]{:S(2)}) collective-permute-start(bf16[1152,128]{1,0:T(8,128)(2,1)S(1)} %collective-permute-done.12.refs_4_), channel_id=1, source_target_pairs={{0,8},{4,12},{8,0},{12,4},{1,9},{5,13},{9,1},{13,5},{2,10},{6,14},... | collective-permute-start | bytes 884744 | tf_op jit(solution)/shard_map/ppermute | solution.py:263
  64.5 7.4 %collective-permute-start.17 = (bf16[1152,384]{1,0:T(8,128)(2,1)S(1)}, bf16[1152,384]{1,0:T(8,128)(2,1)S(1)}, u32[]{:S(2)}, u32[]{:S(2)}) collective-permute-start(bf16[1152,384]{1,0:T(8,128)(2,1)S(1)} %get-tuple-element.70), channel_id=1, source_target_pairs={{0,4},{4,0},{8,12},{12,8},{1,5},{5,1},{9,13},{13,9},{2,6},{6,2},{1... | collective-permute-start | bytes 2654216 | tf_op jit(solution)/shard_map/ppermute | solution.py:263
